TPU v7x, 32 devices: a whole 2x2x4 slice. The times are simulated.
32 devices in a mesh: dp: 8 (over z, x), seq: 4 (over y, core).
Axes of the slice: x: 2, y: 2, z: 4, core: 2. Of those that a mesh axis runs over, the one named last changes fastest.
Arguments:
- tokens: bfloat16 [16, 512, 768], P('dp', 'seq'), may hold values from -6 to 6
- lengths: int32 [16], P('dp'), may hold values from 20 to 512, as said below
- query_key_value: bfloat16 [768, 2304], replicated, may hold values from -0.21875 to 0.21875
- query_bias: bfloat16 [768], replicated, may hold values from -3 to 3
- value_bias: bfloat16 [768], replicated, may hold values from -0.59765625 to 0.59765625
- attn_weight: bfloat16 [768, 768], replicated, may hold values from -1.75 to 1.75
- attn_bias: bfloat16 [768], replicated, may hold values from -2 to 2
- attn_gain: bfloat16 [768], replicated, may hold values from 0.5 to 1.5
- attn_shift: bfloat16 [768], replicated, may hold values from -2 to 2
- inner_weight: bfloat16 [768, 3072], replicated, may hold values from -0.21875 to 0.21875
- inner_bias: bfloat16 [3072], replicated, may hold values from -3 to 3
- outer_weight: bfloat16 [3072, 768], replicated, may hold values from -0.109375 to 0.109375
- outer_bias: bfloat16 [768], replicated, may hold values from -2 to 2
- ffn_gain: bfloat16 [768], replicated, may hold values from 0.5 to 1.5
- ffn_shift: bfloat16 [768], replicated, may hold values from -2 to 2
- cotangent: bfloat16 [16, 512, 768], P('dp', 'seq'), may hold values from -6 to 6
Outputs:
- layer_out: bfloat16 [16, 512, 768], P('dp', 'seq')
- input_grad: bfloat16 [16, 512, 768], P('dp', 'seq')
- grad_query_key_value: float32 [768, 2304], P('seq')
- grad_query_bias: float32 [768], P('seq')
- grad_value_bias: float32 [768], P('seq')
- grad_attn_weight: float32 [768, 768], P('seq')
- grad_attn_bias: float32 [768], P('seq')
- grad_attn_gain: float32 [768], P('seq')
- grad_attn_shift: float32 [768], P('seq')
- grad_inner_weight: float32 [768, 3072], P('seq')
- grad_inner_bias: float32 [3072], P('seq')
- grad_outer_weight: float32 [3072, 768], P('seq')
- grad_outer_bias: float32 [768], P('seq')
- grad_ffn_gain: float32 [768], P('seq')
- grad_ffn_shift: float32 [768], P('seq')
Inputs may be any that keep to these rules, and one draw needn't show every extreme that they name: `lengths`: slots at or beyond a passage's length are padding. In every aligned group of 2 passages one has length 512, and some passage has length 20.
All inputs are finite; a program needn't handle non-finite values.
Results may differ from a plain program's by a relative error of at most 0.018.
Values may be sent and summed in bfloat16 or wider, within the bound.
No kernel may reach another device: no remote copies, remote signals or barrier semaphores. Data moves between devices by JAX's collectives and lax.ppermute only.
A program may use at most 192 MiB of HBM per device.

v0:
```python
import jax
import jax.numpy as jnp
from jax import lax
from jax.sharding import PartitionSpec as P

H = 12
HD = 64


EPS = 1e-12


def layer_norm(field):
    centre = field - jnp.mean(field, -1, keepdims=True)
    spread = jnp.mean(centre * centre, -1, keepdims=True)
    return centre * lax.rsqrt(spread + EPS)


def norm_affine(field, gain, shift):
    return layer_norm(field) * gain + shift


def gelu_exact(field):
    return jax.nn.gelu(field, approximate=False)


def masked_logits(query_part, key_part, usable_part, score_scale):
    logits = (
        jnp.einsum("qhe,khe->hqk", query_part, key_part, preferred_element_type=jnp.float32)
        * score_scale
    )
    return jnp.where(usable_part[None, None, :], logits, -1000000000.0)


def reduce_grads(gradients):
    groups = lax.axis_size("seq")
    lanes = lax.axis_size("dp")
    pieces = [grad_item.reshape(groups, -1) for grad_item in gradients]
    joined = jnp.concatenate(pieces, 1)
    count = joined.shape[1]
    padded = -(-count // lanes) * lanes
    share = lax.psum_scatter(
        joined.astype(jnp.bfloat16), "seq", scatter_dimension=0, tiled=True
    ).astype(jnp.float32)
    share = share.reshape(-1).reshape(lanes, padded // lanes)
    piece = lax.psum_scatter(share, "dp", scatter_dimension=0, tiled=True)
    summed = (
        lax.all_gather(piece.astype(jnp.bfloat16), "dp", axis=0, tiled=True)
        .astype(piece.dtype)
        .reshape(-1)
    )
    results = []
    offset = 0
    for grad_item, piece_item in zip(gradients, pieces):
        length_here = piece_item.shape[1]
        local_shape = (grad_item.shape[0] // groups,) + grad_item.shape[1:]
        results.append(summed[offset : offset + length_here].reshape(local_shape))
        offset = offset + length_here
    return results


def local(
    tokens,
    lengths,
    query_key_value,
    query_bias,
    value_bias,
    attn_weight,
    attn_bias,
    attn_gain,
    attn_shift,
    inner_weight,
    inner_bias,
    outer_weight,
    outer_bias,
    ffn_gain,
    ffn_shift,
    cotangent,
):
    groups = lax.axis_size("seq")
    passages, quarter, model_width = tokens.shape
    heads_here = H // groups
    passage_len = quarter * groups
    row_count = passages * quarter
    score_scale = HD ** (-0.5)
    flat_in = tokens.reshape(row_count, model_width)
    project = jnp.dot(flat_in, query_key_value, preferred_element_type=jnp.float32)
    queries = (project[:, :model_width] + query_bias).astype(jnp.bfloat16)
    key_rows = project[:, model_width : 2 * model_width].astype(jnp.bfloat16)
    values = (project[:, 2 * model_width :] + value_bias).astype(jnp.bfloat16)

    def to_heads(field):
        return field.reshape(passages, quarter, groups, heads_here * HD)

    query_h, key_h, value_h = (
        lax.all_to_all(to_heads(queries), "seq", split_axis=2, concat_axis=1, tiled=True),
        lax.all_to_all(to_heads(key_rows), "seq", split_axis=2, concat_axis=1, tiled=True),
        lax.all_to_all(to_heads(values), "seq", split_axis=2, concat_axis=1, tiled=True),
    )
    query_h = query_h.reshape(passages, passage_len, heads_here, HD)
    key_h = key_h.reshape(passages, passage_len, heads_here, HD)
    value_h = value_h.reshape(passages, passage_len, heads_here, HD)
    usable = lax.broadcasted_iota(jnp.int32, (passages, passage_len), 1) < lengths[:, None]

    def attend(element):
        query_part, key_part, value_part, usable_part = element
        logits = masked_logits(query_part, key_part, usable_part, score_scale)
        highest = jnp.max(logits, -1, keepdims=True)
        total = jnp.sum(jnp.exp(logits - highest), -1, keepdims=True)
        lse_part = highest + jnp.log(total)
        chance_low = jnp.exp(logits - lse_part).astype(jnp.bfloat16)
        context_part = jnp.einsum(
            "hqk,khe->qhe", chance_low, value_part, preferred_element_type=jnp.float32
        )
        return (context_part.astype(jnp.bfloat16), lse_part)

    context_h, lse_all = lax.map(attend, (query_h, key_h, value_h, usable))
    context = lax.all_to_all(
        context_h.reshape(passages, passage_len, 1, heads_here * HD),
        "seq",
        split_axis=1,
        concat_axis=2,
        tiled=True,
    )
    context = context.reshape(row_count, model_width)
    attended = jnp.dot(context, attn_weight, preferred_element_type=jnp.float32) + attn_bias
    pre_one = flat_in.astype(jnp.float32) + attended
    hidden, pull_one = jax.vjp(
        norm_affine, pre_one, attn_gain.astype(jnp.float32), attn_shift.astype(jnp.float32)
    )
    hidden_low = hidden.astype(jnp.bfloat16)
    inner_pre = jnp.dot(hidden_low, inner_weight, preferred_element_type=jnp.float32) + inner_bias
    active_full, pull_gelu = jax.vjp(gelu_exact, inner_pre)
    active = active_full.astype(jnp.bfloat16)
    outer_out = jnp.dot(active, outer_weight, preferred_element_type=jnp.float32) + outer_bias
    pre_two = hidden + outer_out
    result, pull_two = jax.vjp(
        norm_affine, pre_two, ffn_gain.astype(jnp.float32), ffn_shift.astype(jnp.float32)
    )
    layer_out = result.astype(jnp.bfloat16).reshape(passages, quarter, model_width)
    grad_two, grad_ffn_gain, grad_ffn_shift = pull_two(
        cotangent.reshape(row_count, model_width).astype(jnp.float32)
    )
    grad_outer = grad_two.astype(jnp.bfloat16)
    grad_outer_weight = jnp.einsum(
        "tf,td->fd", active, grad_outer, preferred_element_type=jnp.float32
    )
    grad_outer_bias = jnp.sum(grad_outer, 0, dtype=jnp.float32)
    grad_active = jnp.einsum(
        "td,fd->tf", grad_outer, outer_weight, preferred_element_type=jnp.float32
    )
    (grad_inner_full,) = pull_gelu(grad_active)
    grad_inner = grad_inner_full.astype(jnp.bfloat16)
    grad_inner_weight = jnp.einsum(
        "td,tf->df", hidden_low, grad_inner, preferred_element_type=jnp.float32
    )
    grad_inner_bias = jnp.sum(grad_inner, 0, dtype=jnp.float32)
    grad_hidden = grad_two + jnp.einsum(
        "tf,df->td", grad_inner, inner_weight, preferred_element_type=jnp.float32
    )
    grad_one, grad_attn_gain, grad_attn_shift = pull_one(grad_hidden)
    grad_attn = grad_one.astype(jnp.bfloat16)
    grad_attn_weight = jnp.einsum(
        "td,te->de", context, grad_attn, preferred_element_type=jnp.float32
    )
    grad_attn_bias = jnp.sum(grad_attn, 0, dtype=jnp.float32)
    grad_context = jnp.einsum(
        "te,de->td", grad_attn, attn_weight, preferred_element_type=jnp.float32
    ).astype(jnp.bfloat16)
    grad_context_h = lax.all_to_all(
        to_heads(grad_context), "seq", split_axis=2, concat_axis=1, tiled=True
    )
    grad_context_h = grad_context_h.reshape(passages, passage_len, heads_here, HD)

    def attend_back(element):
        query_part, key_part, value_part, usable_part, lse_part, grad_part = element
        logits = masked_logits(query_part, key_part, usable_part, score_scale)
        chance = jnp.exp(logits - lse_part)
        chance_low = chance.astype(jnp.bfloat16)
        grad_chance = jnp.einsum(
            "qhe,khe->hqk", grad_part, value_part, preferred_element_type=jnp.float32
        )
        row_inner = jnp.sum(grad_chance * chance, -1, keepdims=True)
        grad_logits = (chance * (grad_chance - row_inner)).astype(jnp.bfloat16)
        grad_q = (
            jnp.einsum("hqk,khe->qhe", grad_logits, key_part, preferred_element_type=jnp.float32)
            * score_scale
        )
        grad_k = (
            jnp.einsum("hqk,qhe->khe", grad_logits, query_part, preferred_element_type=jnp.float32)
            * score_scale
        )
        grad_v = jnp.einsum(
            "hqk,qhe->khe", chance_low, grad_part, preferred_element_type=jnp.float32
        )
        return (
            grad_q.astype(jnp.bfloat16),
            grad_k.astype(jnp.bfloat16),
            grad_v.astype(jnp.bfloat16),
        )

    grad_q_h, grad_k_h, grad_v_h = lax.map(
        attend_back, (query_h, key_h, value_h, usable, lse_all, grad_context_h)
    )

    def to_slots(field):
        return field.reshape(passages, passage_len, 1, heads_here * HD)

    grad_queries, grad_keys, grad_values = (
        lax.all_to_all(to_slots(grad_q_h), "seq", split_axis=1, concat_axis=2, tiled=True),
        lax.all_to_all(to_slots(grad_k_h), "seq", split_axis=1, concat_axis=2, tiled=True),
        lax.all_to_all(to_slots(grad_v_h), "seq", split_axis=1, concat_axis=2, tiled=True),
    )
    grad_project = jnp.concatenate(
        [
            grad_queries.reshape(row_count, model_width),
            grad_keys.reshape(row_count, model_width),
            grad_values.reshape(row_count, model_width),
        ],
        1,
    )
    grad_query_key_value = jnp.einsum(
        "td,te->de", flat_in, grad_project, preferred_element_type=jnp.float32
    )
    grad_query_bias = jnp.sum(grad_project[:, :model_width], 0, dtype=jnp.float32)
    grad_value_bias = jnp.sum(grad_project[:, 2 * model_width :], 0, dtype=jnp.float32)
    input_full = grad_one + jnp.einsum(
        "te,de->td", grad_project, query_key_value, preferred_element_type=jnp.float32
    )
    input_grad = input_full.astype(jnp.bfloat16).reshape(passages, quarter, model_width)
    reduced = reduce_grads(
        [
            grad_query_key_value,
            grad_query_bias,
            grad_value_bias,
            grad_attn_weight,
            grad_attn_bias,
            grad_attn_gain,
            grad_attn_shift,
            grad_inner_weight,
            grad_inner_bias,
            grad_outer_weight,
            grad_outer_bias,
            grad_ffn_gain,
            grad_ffn_shift,
        ]
    )
    return (
        layer_out,
        input_grad,
        reduced[0],
        reduced[1],
        reduced[2],
        reduced[3],
        reduced[4],
        reduced[5],
        reduced[6],
        reduced[7],
        reduced[8],
        reduced[9],
        reduced[10],
        reduced[11],
        reduced[12],
    )


def solution(mesh):
    placed = (
        P("dp", "seq", None),
        P("dp"),
        P(),
        P(),
        P(),
        P(),
        P(),
        P(),
        P(),
        P(),
        P(),
        P(),
        P(),
        P(),
        P(),
        P("dp", "seq", None),
    )
    return jax.shard_map(
        local,
        mesh=mesh,
        in_specs=placed,
        out_specs=(
            P("dp", "seq", None),
            P("dp", "seq", None),
            P("seq", None),
            P("seq"),
            P("seq"),
            P("seq", None),
            P("seq"),
            P("seq"),
            P("seq"),
            P("seq", None),
            P("seq"),
            P("seq", None),
            P("seq"),
            P("seq"),
            P("seq"),
        ),
        check_vma=False,
    )
```

profile of v0, /device:TPU:0, one launch (start us, length us, event | category | flops | bytes accessed | tf_op | source)
XLA Modules:
  0.0 1190.6 jit_solution(2588954487593814598)
XLA Ops:
  17.5 4.4 all-to-all-start
  25.6 4.3 all-to-all-done
  29.9 4.1 all-to-all-start.1
  41.5 4.1 all-to-all-start.2
  58.3 8.6 while.26
  68.9 4.1 all-to-all-start.3
  78.8 3.1 all-to-all-done.3
  81.9 2.1 copy.123
  85.5 2.1 fusion.89
  88.0 10.0 multiply_convert_fusion.1
  102.6 2.7 fusion.82
  105.3 2.2 multiply_reduce_fusion.1
  114.8 4.3 all-to-all-start.4
  122.2 2.6 convolution_convert_fusion.3
  124.8 3.2 reshape.292
  137.6 13.9 %while.27 = (s32[]{:T(128)}, bf16[2,512,3,64]{1,3,2,0:T(8,128)(2,1)}, bf16[2,512,3,64]{1,3,2,0:T(8,128)(2,1)}, bf16[2,512,3,64]{1,3,2,0:T(8,128)(2,1)}, bf16[2,5...) while((s32[]{:T(128)}, ...), condition=%wide.region_14.15_spmd, body=%wide.region_12.14_spmd.sunk | while | flops 510884352 | bytes 41325460 | solution.py:202
  153.5 4.1 all-to-all-start.5
  157.7 5.4 convolution_convert_fusion.1
  163.1 8.1 reshape.296
  173.2 4.4 all-to-all-start.6
  177.6 5.0 convolution_convert_fusion
  182.6 8.2 reshape.298
  196.3 4.1 all-to-all-start.7
  202.4 2.1 copy.109
  204.5 2.6 copy.125
  207.1 2.1 copy.112
  211.0 2.1 copy.126
  219.1 4.2 fusion.55
  223.3 5.8 copy.116
  229.1 6.6 reshape.291
  235.7 4.8 constant_dynamic-update-slice_fusion.1
  245.1 2.3 constant_dynamic-update-slice_fusion
  251.6 45.4 %dynamic-update-slice.7 = bf16[4,1771776]{1,0:T(4,128)(2,1)} dynamic-update-slice(bf16[4,1771776]{1,0:T(4,128)(2,1)} %dynamic-update-slice.6, bf16[4,589824]{1,0:T(4,128)(2,1)} %reshape.296, s32[]{} %constant.149, s32[]{} %constant.156) | dynamic-update-slice | bytes 9437188
  298.5 45.2 %dynamic-update-slice.9 = bf16[4,1771776]{1,0:T(4,128)(2,1)} dynamic-update-slice(bf16[4,1771776]{1,0:T(4,128)(2,1)} %dynamic-update-slice.8, bf16[4,589824]{1,0:T(4,128)(2,1)} %reshape.298, s32[]{} %constant.149, s32[]{} %constant.158) | dynamic-update-slice | bytes 9437188
  349.6 247.8 %all-reduce.5.cloned.1.call-done = bf16[4,1771776]{1,0:T(4,128)(2,1)} async-done(((bf16[4,1771776]{1,0:T(4,128)(2,1)}), bf16[4,1771776]{1,0:T(4,128)(2,1)}) %all-reduce.5.cloned.1.call-update) | async-done | bytes 14174224
  597.4 66.4 %fusion.54 = f32[1771776]{0:T(1024)} fusion(bf16[4,1771776]{1,0:T(4,128)(2,1)} %all-reduce.5.cloned.1.call-done, u32[]{:T(128)} %bitcast.52), kind=kLoop, calls=%fused_computation.63 | loop fusion | flops 1771776 | bytes 10630660 | tf_op jit(solution)/shard_map/reshape;reshape | solution.py:45
  663.8 9.7 reshape.307
  673.5 279.5 %all-reduce.6 = bf16[8,221472]{1,0:T(8,128)(2,1)} all-reduce(f32[8,221472]{1,0:T(8,128)} %reshape.307), channel_id=3, replica_groups=mesh['dp'=8,'seq'=4] {'dp'}, use_global_device_ids=true, to_apply=%region_25.26.clone | all-reduce | flops 1771776 | bytes 10630656
  953.0 3.9 fusion.67
  956.9 3.4 fusion.64
  960.3 103.2 %all-gather.3.cloned.1.call-done = bf16[8,1,221472]{2,1,0:T(2,128)(2,1)} async-done(((bf16[1,1,221472]{2,1,0:T(2,128)(2,1)}), bf16[8,1,221472]{2,1,0:T(2,128)(2,1)}) %all-gather.3.cloned.1.call-update) | async-done | bytes 3543568 | tf_op jit(solution)/shard_map/all_gather | solution.py:48
  1063.5 77.5 %convert_reduce_fusion = f32[8,221472]{1,0:T(8,128)} fusion(bf16[8,1,221472]{2,1,0:T(2,128)(2,1)} %all-gather.3.cloned.1.call-done), kind=kLoop, calls=%fused_computation.61 | loop fusion | flops 1771776 | bytes 10630656 | tf_op jit(solution)/shard_map/convert_element_type | solution.py:49
  1141.0 10.8 slice.55
  1151.8 9.5 reshape.302
  1164.7 5.8 fusion.88
  1171.9 2.8 slice.72
  1176.7 3.2 reshape.304
  1179.9 3.4 reshape.305
  (254 shorter events, 132.1 us)
Async XLA Ops:
  7.2 2.0 copy-start
  17.5 28.2 %copy-start.42 = (s32[2]{0:T(128)S(1)}, s32[2]{0:T(128)}, u32[]{:S(2)}) copy-start(s32[2]{0:T(128)} %param.21) | copy-start | bytes 28
  17.5 12.4 %all-to-all-start = ((bf16[2,128,4,192]{1,0,3,2:T(2,128)(2,1)}), bf16[2,128,4,192]{1,0,3,2:T(2,128)(2,1)}, u32[]{:S(2)}, u32[]{:S(2)}) async-start(bf16[2,128,4,192]{1,0,3,2:T(2,128)(2,1)} %reshape.273), calls=%async_computation | async-start | bytes 786432 | tf_op jit(solution)/shard_map/all_to_all | solution.py:98
  29.9 11.6 all-to-all-start.1
  41.5 12.1 %all-to-all-start.2 = ((bf16[2,128,4,192]{1,0,3,2:T(2,128)(2,1)}), bf16[2,128,4,192]{1,0,3,2:T(2,128)(2,1)}, u32[]{:S(2)}, u32[]{:S(2)}) async-start(bf16[2,128,4,192]{1,0,3,2:T(2,128)(2,1)} %reshape.277), calls=%async_computation.2 | async-start | bytes 786432 | tf_op jit(solution)/shard_map/all_to_all | solution.py:97
  58.3 14.7 %copy-start.41 = (bf16[768]{0:T(1024)(128)(2,1)S(1)}, bf16[768]{0:T(1024)(128)(2,1)}, u32[]{:S(2)}) copy-start(bf16[768]{0:T(1024)(128)(2,1)} %param.32) | copy-start | bytes 4612
  58.3 15.3 %copy-start.37 = (bf16[3072]{0:T(1024)(128)(2,1)S(1)}, bf16[3072]{0:T(1024)(128)(2,1)}, u32[]{:S(2)}) copy-start(bf16[3072]{0:T(1024)(128)(2,1)} %param.30) | copy-start | bytes 18436
  58.4 2.6 copy-start.24
  58.4 2.6 copy-start.6
  58.4 2.6 copy-start.19
  62.6 2.6 copy-start.24
  62.6 2.6 copy-start.6
  62.6 2.6 copy-start.19
  68.9 13.1 %all-to-all-start.3 = ((bf16[2,512,1,192]{3,0,2,1:T(2,128)(2,1)}), bf16[2,512,1,192]{3,0,2,1:T(2,128)(2,1)}, u32[]{:S(2)}, u32[]{:S(2)}) async-start(bf16[2,512,1,192]{3,0,2,1:T(2,128)(2,1)} %copy.102), calls=%async_computation.3 | async-start | bytes 1048576 | tf_op jit(solution)/shard_map/all_to_all | solution.py:118
  84.1 3.9 copy-start.30
  85.5 2.4 copy-start.21
  85.5 12.5 %slice-start = ((s8[4718592]{0:T(1024)(128)(4,1)}), s8[4194304]{0:T(1024)(128)(4,1)S(1)}, s32[]{:S(2)}) async-start(s8[4718592]{0:T(1024)(128)(4,1)} %bitcast.224), calls=%async_computation.10 | async-start | bytes 8388608
  87.6 19.9 %copy-start.4 = (f32[256,768]{1,0:T(8,128)}, f32[256,768]{1,0:T(8,128)S(1)}, u32[]{:S(2)}) copy-start(f32[256,768]{1,0:T(8,128)S(1)} %get-tuple-element.183) | copy-start | bytes 2359300
  87.7 19.9 %copy-start.26 = (f32[256]{0:T(256)}, f32[256]{0:T(256)S(1)}, u32[]{:S(2)}) copy-start(f32[256]{0:T(256)S(1)} %broadcast_multiply_fusion.1) | copy-start | bytes 3076
  87.9 19.7 %copy-start.29 = (f32[256]{0:T(256)}, f32[256]{0:T(256)S(1)}, u32[]{:S(2)}) copy-start(f32[256]{0:T(256)S(1)} %fusion.77) | copy-start | bytes 3076
  87.9 10.0 copy-start.38
  88.0 10.0 slice-start.1
  97.9 1.6 copy-start.9
  98.0 1.8 copy-start.8
  98.0 2.7 copy-start.28
  100.7 4.6 slice-start.2
  102.6 2.7 copy-start.12
  102.6 2.7 slice-start.3
  105.3 2.3 copy-start.22
  107.6 2.3 copy-start.23
  114.8 16.5 %all-to-all-start.4 = ((bf16[2,128,4,192]{1,0,3,2:T(2,128)(2,1)}), bf16[2,128,4,192]{1,0,3,2:T(2,128)(2,1)}, u32[]{:S(2)}, u32[]{:S(2)}) async-start(bf16[2,128,4,192]{1,0,3,2:T(2,128)(2,1)} %reshape.282), calls=%async_computation.4 | async-start | bytes 786432 | tf_op jit(solution)/shard_map/all_to_all | solution.py:170
  137.6 20.1 %copy-start.27 = (f32[256]{0:T(256)S(1)}, f32[256]{0:T(256)}, u32[]{:S(2)}) copy-start(f32[256]{0:T(256)} %copy-done.26) | copy-start | bytes 3076
  137.6 2.8 copy-start.3
  137.6 2.8 copy-start.7
  144.6 2.7 copy-start.3
  144.6 2.8 copy-start.7
  153.5 19.7 %all-to-all-start.5 = ((bf16[2,512,1,192]{3,0,2,1:T(2,128)(2,1)}), bf16[2,512,1,192]{3,0,2,1:T(2,128)(2,1)}, u32[]{:S(2)}, u32[]{:S(2)}) async-start(bf16[2,512,1,192]{3,0,2,1:T(2,128)(2,1)} %copy.107), calls=%async_computation.5 | async-start | bytes 1048576 | tf_op jit(solution)/shard_map/all_to_all | solution.py:210
  163.1 8.1 copy-start.36
  173.2 23.1 %all-to-all-start.6 = ((bf16[2,512,1,192]{3,0,2,1:T(2,128)(2,1)}), bf16[2,512,1,192]{3,0,2,1:T(2,128)(2,1)}, u32[]{:S(2)}, u32[]{:S(2)}) async-start(bf16[2,512,1,192]{3,0,2,1:T(2,128)(2,1)} %copy.110), calls=%async_computation.6 | async-start | bytes 1048576 | tf_op jit(solution)/shard_map/all_to_all | solution.py:211
  182.6 8.2 copy-start.32
  182.6 8.8 copy-start.31
  196.3 14.8 %all-to-all-start.7 = ((bf16[2,512,1,192]{3,0,2,1:T(2,128)(2,1)}), bf16[2,512,1,192]{3,0,2,1:T(2,128)(2,1)}, u32[]{:S(2)}, u32[]{:S(2)}) async-start(bf16[2,512,1,192]{3,0,2,1:T(2,128)(2,1)} %copy.113), calls=%async_computation.7 | async-start | bytes 1048576 | tf_op jit(solution)/shard_map/all_to_all | solution.py:212
  200.4 397.0 %all-reduce.5.cloned.1.call-start = ((), (), s32[]{:S(2)}) async-start(), calls=%async_computation.9 | async-start | bytes 28348416
  298.5 45.2 %copy-start.35 = (bf16[4,192]{1,0:T(4,128)(2,1)S(1)}, bf16[4,192]{1,0:T(4,128)(2,1)}, u32[]{:S(2)}) copy-start(bf16[4,192]{1,0:T(4,128)(2,1)} %reshape.299) | copy-start | bytes 4612
  298.5 46.6 %copy-start.34 = (bf16[4,192]{1,0:T(4,128)(2,1)S(1)}, bf16[4,192]{1,0:T(4,128)(2,1)}, u32[]{:S(2)}) copy-start(bf16[4,192]{1,0:T(4,128)(2,1)} %reshape.300) | copy-start | bytes 4612
  298.5 48.0 %copy-start.33 = (bf16[4,192]{1,0:T(4,128)(2,1)S(1)}, bf16[4,192]{1,0:T(4,128)(2,1)}, u32[]{:S(2)}) copy-start(bf16[4,192]{1,0:T(4,128)(2,1)} %reshape.301) | copy-start | bytes 4612
  347.8 715.7 %all-gather.3.cloned.1.call-start = ((), (), s32[]{:S(2)}) async-start(), calls=%async_computation.8 | async-start | bytes 7976448 | tf_op jit(solution)/shard_map/all_gather | solution.py:48
  673.5 283.4 %copy-start.40 = (f32[256]{0:T(256)S(1)}, f32[256]{0:T(256)}, u32[]{:S(2)}) copy-start(f32[256]{0:T(256)} %copy-done.39) | copy-start | bytes 3076
  (26 other events, 27.3 us)
Sparse Core Ops, SparseCore 0:
  347.9 249.3 all-reduce.4
  957.0 106.4 all-gather.2
where the time goes:
time: 1210 us; the launch traced here: 1190 us
  waiting for transfers between devices  360 us (30%)
  local copies, waits for them, and re-layouts  281 us (23%)
  blocking collectives  279 us (23%)
  other arithmetic  165 us (14%)
  matrix products  56.3 us (5%)
  starting transfers between devices  33.8 us (3%)
  between operations  15 us (1%)
    unnamed x1, blocking collectives  279 us
    unnamed x3, waiting for transfers between devices  248 us
    unnamed x85, local copies, waits for them, and re-layouts  122 us
    all_gather x1, waiting for transfers between devices, reduce_grads(): lax.all_gather(piece.astype(jnp.bfloat16), 'dp', axis=0, tiled=True)  103 us
    convert_element_type x1, other arithmetic, reduce_grads(): summed = lax.all_gather(piece.astype(jnp.bfloat16), 'dp', axis=0, tiled=T...  77.5 us
    another operation x1, other arithmetic, reduce_grads(): share = share.reshape(-1).reshape(lanes, padded // lanes)  66.4 us
    reshape x11, local copies, waits for them, and re-layouts, reduce_grads(): pieces = [grad_item.reshape(groups, -1) for grad_item in gradients]  32.1 us
    slice x6, local copies, waits for them, and re-layouts, reduce_grads(): results.append(summed[offset:offset + length_here].reshape(local_shape))  24.2 us
  transfers between devices with their start and end apart: 10, of which 5 were waited for; matrix products, arithmetic and copies ran while one was open for 7% of the time, Pallas kernels for 0%

commit v1 on v0

v1 whole, which is shorter than its diff:
```python
import jax
import jax.numpy as jnp
from jax import lax
from jax.experimental import pallas as pl
from jax.experimental.pallas import tpu as pltpu
from jax.sharding import PartitionSpec as P

H = 12
HD = 64
EPS = 1e-12
F32 = jnp.float32
LOW = jnp.bfloat16
MIB = 1 << 20
PIECES = 8


def dot(a, b):
    return lax.dot_general(a, b, (((1,), (0,)), ((), ())), preferred_element_type=F32)


def dot_nt(a, b):
    return lax.dot_general(a, b, (((1,), (1,)), ((), ())), preferred_element_type=F32)


def dot_tn(a, b):
    return lax.dot_general(a, b, (((0,), (0,)), ((), ())), preferred_element_type=F32)


def vmem(shape=None, index=None):
    if shape is None:
        return pl.BlockSpec(memory_space=pltpu.VMEM)
    return pl.BlockSpec(shape, index)


SMEM = pl.BlockSpec(memory_space=pltpu.SMEM)


def key_mask(me, length, rows, quarter):
    slot = lax.broadcasted_iota(jnp.int32, (rows, 1), 0)
    block = slot // quarter
    return ((block ^ me) * quarter + (slot - block * quarter)) < length


def attend_kernel(where, lengths, x0, x1, x2, x3, w, qb, vb, qkv_out, lse_out, *context_out):
    p = pl.program_id(0)
    quarter = x0.shape[1]
    rows = 4 * quarter
    hw = w.shape[1] // 3
    heads = hw // HD
    x = jnp.concatenate([x0[0], x1[0], x2[0], x3[0]], 0)
    proj = dot(x, w[...])
    q = ((proj[:, :hw] + qb[...]).astype(LOW).astype(F32) * HD ** (-0.5)).astype(LOW)
    k = proj[:, hw : 2 * hw].astype(LOW)
    v = (proj[:, 2 * hw :] + vb[...]).astype(LOW)
    qkv_out[0] = jnp.concatenate([q, k, v], 1)
    usable = key_mask(where[0], lengths[p], rows, quarter)
    parts = []
    for h in range(heads):
        cols = slice(h * HD, (h + 1) * HD)
        logits = jnp.where(usable, dot_nt(k[:, cols], q[:, cols]), -1e9)
        highest = jnp.max(logits, 0, keepdims=True)
        weight = jnp.exp(logits - highest)
        total = jnp.sum(weight, 0, keepdims=True)
        lse_out[0, h : h + 1, :] = highest + jnp.log(total)
        parts.append(dot_tn(v[:, cols], weight.astype(LOW)) * (1.0 / total))
    context = jnp.concatenate(parts, 0).T.astype(LOW)
    for j in range(4):
        context_out[j][0] = context[j * quarter : (j + 1) * quarter]


def attend(where, lengths, shards, w, qb, vb):
    passages, quarter, width = shards[0].shape
    rows = 4 * quarter
    hw = w.shape[1] // 3
    heads = hw // HD
    block = vmem((1, quarter, width), lambda p: (p, 0, 0))
    whole = lambda *shape: vmem(shape, lambda p: (0,) * len(shape))
    return pl.pallas_call(
        attend_kernel,
        grid=(passages,),
        in_specs=[SMEM, SMEM] + [block] * 4 + [whole(width, 3 * hw), whole(1, hw), whole(1, hw)],
        out_specs=[
            vmem((1, rows, 3 * hw), lambda p: (p, 0, 0)),
            vmem((1, heads, rows), lambda p: (p, 0, 0)),
        ]
        + [vmem((1, quarter, hw), lambda p: (p, 0, 0))] * 4,
        out_shape=[
            jax.ShapeDtypeStruct((passages, rows, 3 * hw), LOW),
            jax.ShapeDtypeStruct((passages, heads, rows), F32),
        ]
        + [jax.ShapeDtypeStruct((passages, quarter, hw), LOW)] * 4,
        compiler_params=pltpu.CompilerParams(vmem_limit_bytes=40 * MIB),
        cost_estimate=pl.CostEstimate(flops=3 * 10**9, bytes_accessed=6 * 10**6, transcendentals=10**6),
        name="attend",
    )(where, lengths, *shards, w, qb, vb)


def attend_back_kernel(
    where, lengths, x0, x1, x2, x3, w, qkv, lse, g0, g1, g2, g3,
    keep_out, send_out, weight_out, bias_out, acc,
):
    p = pl.program_id(0)
    me = where[0]
    quarter = x0.shape[1]
    rows = 4 * quarter
    hw = w.shape[1] // 3
    heads = hw // HD
    scale = HD ** (-0.5)
    x = jnp.concatenate([x0[0], x1[0], x2[0], x3[0]], 0)
    g = jnp.concatenate([g0[0], g1[0], g2[0], g3[0]], 0)
    usable = key_mask(me, lengths[p], rows, quarter)
    q = qkv[0, :, :hw]
    k = qkv[0, :, hw : 2 * hw]
    v = qkv[0, :, 2 * hw :]
    grad_q, grad_k, grad_v = [], [], []
    for h in range(heads):
        cols = slice(h * HD, (h + 1) * HD)
        qh, kh, vh, gh = q[:, cols], k[:, cols], v[:, cols], g[:, cols]
        logits = jnp.where(usable, dot_nt(kh, qh), -1e9)
        chance = jnp.exp(logits - lse[0, h : h + 1, :])
        grad_chance = dot_nt(vh, gh)
        inner = jnp.sum(grad_chance * chance, 0, keepdims=True)
        grad_logits = (chance * (grad_chance - inner)).astype(LOW)
        grad_q.append(dot_tn(kh, grad_logits) * scale)
        grad_k.append(dot(grad_logits, qh))
        grad_v.append(dot(chance.astype(LOW), gh))
    gq = jnp.concatenate(grad_q, 0).T.astype(LOW)
    gk = jnp.concatenate(grad_k, 1).astype(LOW)
    gv = jnp.concatenate(grad_v, 1).astype(LOW)
    joined = jnp.concatenate([gq, gk, gv], 1)
    part = dot_tn(x, joined)
    sums = jnp.concatenate(
        [
            jnp.sum(gq.astype(F32), 0, keepdims=True),
            jnp.sum(gv.astype(F32), 0, keepdims=True),
        ],
        0,
    )

    @pl.when(p == 0)
    def _():
        acc[...] = part
        bias_out[...] = sums

    @pl.when(p > 0)
    def _():
        acc[...] += part
        bias_out[...] += sums

    back = dot_nt(joined, w[...]).astype(LOW)
    for j in range(4):
        out = send_out if j % 2 else keep_out
        out[j // 2, 0] = back[j * quarter : (j + 1) * quarter]

    @pl.when(p == pl.num_programs(0) - 1)
    def _():
        n = weight_out.shape[2]
        for j in range(4):
            for e in range(PIECES):
                start = pl.multiple_of((me ^ j) * (n * PIECES) + e * n, 8)
                weight_out[e, j] = acc[pl.ds(start, n), :].astype(LOW)


def attend_back(where, lengths, shards, w, qkv, lse, grads):
    passages, quarter, width = shards[0].shape
    rows = 4 * quarter
    hw = w.shape[1] // 3
    heads = hw // HD
    n = width // (4 * PIECES)
    block = vmem((1, quarter, width), lambda p: (p, 0, 0))
    gblock = vmem((1, quarter, hw), lambda p: (p, 0, 0))
    whole = lambda *shape: vmem(shape, lambda p: (0,) * len(shape))
    return pl.pallas_call(
        attend_back_kernel,
        grid=(passages,),
        in_specs=[SMEM, SMEM]
        + [block] * 4
        + [
            whole(width, 3 * hw),
            vmem((1, rows, 3 * hw), lambda p: (p, 0, 0)),
            vmem((1, heads, rows), lambda p: (p, 0, 0)),
        ]
        + [gblock] * 4,
        out_specs=[
            vmem((2, 1, quarter, width), lambda p: (0, p, 0, 0)),
            vmem((2, 1, quarter, width), lambda p: (0, p, 0, 0)),
            whole(PIECES, 4, n, 3 * hw),
            whole(2, hw),
        ],
        out_shape=[
            jax.ShapeDtypeStruct((2, passages, quarter, width), LOW),
            jax.ShapeDtypeStruct((2, passages, quarter, width), LOW),
            jax.ShapeDtypeStruct((PIECES, 4, n, 3 * hw), LOW),
            jax.ShapeDtypeStruct((2, hw), F32),
        ],
        scratch_shapes=[pltpu.VMEM((width, 3 * hw), F32)],
        compiler_params=pltpu.CompilerParams(vmem_limit_bytes=48 * MIB),
        cost_estimate=pl.CostEstimate(flops=5 * 10**9, bytes_accessed=10**7, transcendentals=10**6),
        name="attend_back",
    )(where, lengths, *shards, w, qkv, lse, *grads)


def normalise(field):
    centre = field - jnp.mean(field, -1, keepdims=True)
    scale = lax.rsqrt(jnp.mean(centre * centre, -1, keepdims=True) + EPS)
    return centre * scale, scale


def normalise_back(grad, normal, scale):
    return (
        grad
        - jnp.mean(grad, -1, keepdims=True)
        - normal * jnp.mean(grad * normal, -1, keepdims=True)
    ) * scale


def rows_kernel(
    where, x, c0, c1, c2, c3, cot, wa, vec, ib, wi_hbm, wo_hbm,
    layer_out, grad_one_out, hidden_out, active_out, inner_out, outer_out, attn_out,
    h0, h1, h2, h3, sums_out, inner_bias_out,
    wi, wo, slope, sem,
):
    me = where[0]
    width = x.shape[1]
    ff = ib.shape[1]
    chunk = width
    chunks = ff // chunk
    hw = c0.shape[1]

    def copies(c):
        cols = pl.ds(c * chunk, chunk)
        return (
            pltpu.make_async_copy(wi_hbm.at[:, cols], wi.at[:, cols], sem.at[2 * c]),
            pltpu.make_async_copy(wo_hbm.at[cols, :], wo.at[cols, :], sem.at[2 * c + 1]),
        )

    for c in range(chunks):
        for copy in copies(c):
            copy.start()
    row = lambda r: vec[r : r + 1, :]
    attn_bias, attn_gain, attn_shift, outer_bias, ffn_gain, ffn_shift = (row(r) for r in range(6))
    attended = attn_bias + x[...].astype(F32)
    for j, part in enumerate((c0, c1, c2, c3)):
        attended += dot(part[...], wa[me ^ j])
    normal_one, scale_one = normalise(attended)
    hidden = normal_one * attn_gain + attn_shift
    hidden_low = hidden.astype(LOW)
    hidden_out[...] = hidden_low
    pre_two = hidden + outer_bias
    for c in range(chunks):
        cols = slice(c * chunk, (c + 1) * chunk)
        first, second = copies(c)
        first.wait()
        u = dot(hidden_low, wi[:, cols]) + ib[:, cols]
        below = 0.5 * (1.0 + lax.erf(u * (0.5**0.5)))
        density = jnp.exp(-0.5 * u * u) * 0.3989422804014327
        active = (u * below).astype(LOW)
        slope[:, cols] = below + u * density
        active_out[:, cols] = active
        second.wait()
        pre_two += dot(active, wo[cols, :])
    normal_two, scale_two = normalise(pre_two)
    layer_out[...] = (normal_two * ffn_gain + ffn_shift).astype(LOW)
    dy = cot[...].astype(F32)
    sums_out[4:5, :] = jnp.sum(dy * normal_two, 0, keepdims=True)
    sums_out[5:6, :] = jnp.sum(dy, 0, keepdims=True)
    grad_two = normalise_back(dy * ffn_gain, normal_two, scale_two)
    grad_outer = grad_two.astype(LOW)
    outer_out[...] = grad_outer
    sums_out[3:4, :] = jnp.sum(grad_outer.astype(F32), 0, keepdims=True)
    grad_hidden = grad_two
    for c in range(chunks):
        cols = slice(c * chunk, (c + 1) * chunk)
        grad_inner = (dot_nt(grad_outer, wo[cols, :]) * slope[:, cols]).astype(LOW)
        inner_out[:, cols] = grad_inner
        inner_bias_out[:, cols] = jnp.sum(grad_inner.astype(F32), 0, keepdims=True)
        grad_hidden += dot_nt(grad_inner, wi[:, cols])
    sums_out[1:2, :] = jnp.sum(grad_hidden * normal_one, 0, keepdims=True)
    sums_out[2:3, :] = jnp.sum(grad_hidden, 0, keepdims=True)
    grad_one = normalise_back(grad_hidden * attn_gain, normal_one, scale_one)
    grad_one_out[...] = grad_one
    grad_attn = grad_one.astype(LOW)
    attn_out[...] = grad_attn
    sums_out[0:1, :] = jnp.sum(grad_attn.astype(F32), 0, keepdims=True)
    sums_out[6:8, :] = jnp.zeros((2, width), F32)
    for j, out in enumerate((h0, h1, h2, h3)):
        out[...] = dot_nt(grad_attn, wa[me ^ j]).astype(LOW)


def rows_pass(where, x, context, cot, wa, vec, ib, wi, wo):
    rows, width = x.shape
    ff = ib.shape[1]
    hw = context[0].shape[1]
    hbm = pl.BlockSpec(memory_space=pl.ANY)
    low = lambda *s: jax.ShapeDtypeStruct(s, LOW)
    full = lambda *s: jax.ShapeDtypeStruct(s, F32)
    return pl.pallas_call(
        rows_kernel,
        in_specs=[SMEM] + [vmem()] * 9 + [hbm, hbm],
        out_specs=[vmem()] * 13,
        out_shape=[
            low(rows, width), full(rows, width), low(rows, width), low(rows, ff), low(rows, ff),
            low(rows, width), low(rows, width),
            low(rows, hw), low(rows, hw), low(rows, hw), low(rows, hw),
            full(8, width), full(1, ff),
        ],
        scratch_shapes=[
            pltpu.VMEM(wi.shape, LOW),
            pltpu.VMEM(wo.shape, LOW),
            pltpu.VMEM((rows, ff), F32),
            pltpu.SemaphoreType.DMA((2 * (ff // width),)),
        ],
        compiler_params=pltpu.CompilerParams(vmem_limit_bytes=48 * MIB),
        cost_estimate=pl.CostEstimate(flops=6 * 10**9, bytes_accessed=2 * 10**7, transcendentals=10**6),
        name="rows_pass",
    )(where, x, *context, cot, wa, vec, ib, wi, wo)


def outer_grad_kernel(where, active, grad, send_out, keep_out):
    j = pl.program_id(0)
    width = grad.shape[1]
    n = width // PIECES
    relative = jnp.where(j < 2, 2 * j + 1, 2 * j - 4)
    cols = pl.ds(pl.multiple_of((where[0] ^ relative) * width, 128), width)
    product = dot_tn(active[:, cols], grad[...]).astype(LOW)

    def store(out):
        for e in range(PIECES):
            out[0, e] = product[e * n : (e + 1) * n]

    pl.when(j < 2)(lambda: store(send_out))
    pl.when(j >= 2)(lambda: store(keep_out))


def outer_grad(where, active, grad):
    rows, width = grad.shape
    ff = active.shape[1]
    shape = (2, PIECES, width // PIECES, width)
    return pl.pallas_call(
        outer_grad_kernel,
        grid=(4,),
        in_specs=[
            SMEM,
            vmem((rows, ff), lambda j: (0, 0)),
            vmem((rows, width), lambda j: (0, 0)),
        ],
        out_specs=[
            vmem((1,) + shape[1:], lambda j: (jnp.minimum(j, 1), 0, 0, 0)),
            vmem((1,) + shape[1:], lambda j: (jnp.maximum(j - 2, 0), 0, 0, 0)),
        ],
        out_shape=[jax.ShapeDtypeStruct(shape, LOW)] * 2,
        compiler_params=pltpu.CompilerParams(vmem_limit_bytes=32 * MIB),
        cost_estimate=pl.CostEstimate(flops=2 * rows * ff * width, bytes_accessed=8 * 10**6, transcendentals=0),
        name="outer_grad",
    )(where, active, grad)


def inner_grad_kernel(where, hidden, grad_inner, c0, c1, c2, c3, grad_attn, send_out, keep_out, left):
    c = pl.program_id(0)
    me = where[0]
    hw = c0.shape[1]
    n = hw // PIECES
    width = hidden.shape[1]

    @pl.when(c == 0)
    def _():
        flipped = hidden[...].astype(F32).T.astype(LOW)
        left[...] = flipped

    def store(j, rows, value):
        out = send_out if j % 2 else keep_out
        out[j // 2, 0, rows, :] = value

    for j in range(4):
        rows = pl.ds(pl.multiple_of((me ^ j) * hw, 64), hw)
        store(j, slice(0, hw), dot(left[rows, :], grad_inner[...]).astype(LOW))
    for j, part in enumerate((c0, c1, c2, c3)):
        half = width // 2
        mine = dot_tn(part[...], grad_attn[...])
        for e in range(PIECES):
            @pl.when(c == e)
            def _(e=e, j=j, mine=mine):
                piece = mine[e * n : (e + 1) * n]
                store(j, slice(hw, hw + 2 * n), jnp.concatenate([piece[:, :half], piece[:, half:]], 0).astype(LOW))


def inner_grad(where, hidden, grad_inner, context, grad_attn):
    rows, width = hidden.shape
    ff = grad_inner.shape[1]
    hw = context[0].shape[1]
    n = hw // PIECES
    cols = ff // PIECES
    shape = (2, PIECES, hw + 2 * n, cols)
    whole = lambda *s: vmem(s, lambda c: (0,) * len(s))
    return pl.pallas_call(
        inner_grad_kernel,
        grid=(PIECES,),
        in_specs=[SMEM, whole(rows, width), vmem((rows, cols), lambda c: (0, c))]
        + [whole(rows, hw)] * 4
        + [whole(rows, width)],
        out_specs=[vmem((2, 1, hw + 2 * n, cols), lambda c: (0, c, 0, 0))] * 2,
        out_shape=[jax.ShapeDtypeStruct(shape, LOW)] * 2,
        scratch_shapes=[pltpu.VMEM((width, rows), LOW)],
        compiler_params=pltpu.CompilerParams(vmem_limit_bytes=32 * MIB),
        cost_estimate=pl.CostEstimate(flops=2 * rows * ff * width, bytes_accessed=8 * 10**6, transcendentals=0),
        name="inner_grad",
    )(where, hidden, grad_inner, *context, grad_attn)


def outer_place_kernel(place, piece, out):
    out[...] = piece[0].astype(F32)


def outer_place(place, pieces):
    count, n, width = pieces.shape
    return pl.pallas_call(
        outer_place_kernel,
        grid_spec=pltpu.PrefetchScalarGridSpec(
            num_scalar_prefetch=1,
            grid=(count,),
            in_specs=[vmem((1, n, width), lambda a, place: (a ^ place[0], 0, 0))],
            out_specs=vmem((n, width), lambda a, place: (a, 0)),
        ),
        out_shape=jax.ShapeDtypeStruct((count * n, width), F32),
        name="outer_place",
    )(place, pieces)


def inner_place_kernel(place, piece, inner, attn):
    hw = inner.shape[0]
    n = attn.shape[0]
    inner[...] = piece[0, :hw, :].astype(F32)
    rest = piece[0, hw:, :].astype(F32)
    attn[...] = jnp.concatenate([rest[:n], rest[n:]], 1)


def inner_place(place, pieces, hw):
    count, tall, cols = pieces.shape
    n = (tall - hw) // 2
    return pl.pallas_call(
        inner_place_kernel,
        grid_spec=pltpu.PrefetchScalarGridSpec(
            num_scalar_prefetch=1,
            grid=(count,),
            in_specs=[vmem((1, tall, cols), lambda a, place: (a ^ place[0], 0, 0))],
            out_specs=[
                vmem((hw, cols), lambda a, place: (0, a)),
                vmem((n, 2 * cols), lambda a, place: (a, 0)),
            ],
        ),
        out_shape=[
            jax.ShapeDtypeStruct((hw, count * cols), F32),
            jax.ShapeDtypeStruct((count * n, 2 * cols), F32),
        ],
        name="inner_place",
    )(place, pieces)


def project_place_kernel(place, piece, out):
    hw = piece.shape[3] // 3
    for owner in range(4):
        block = piece[0, owner ^ place[1]].astype(F32)
        for t in range(3):
            start = t * 4 * hw + owner * hw
            out[:, start : start + hw] = block[:, t * hw : (t + 1) * hw]


def project_place(place, pieces):
    count, groups, n, wide = pieces.shape
    return pl.pallas_call(
        project_place_kernel,
        grid_spec=pltpu.PrefetchScalarGridSpec(
            num_scalar_prefetch=1,
            grid=(count,),
            in_specs=[vmem((1, groups, n, wide), lambda a, place: (a ^ place[0], 0, 0, 0))],
            out_specs=vmem((n, groups * wide), lambda a, place: (a, 0)),
        ),
        out_shape=jax.ShapeDtypeStruct((count * n, groups * wide), F32),
        name="project_place",
    )(place, pieces)


def swap(field, axis, bit):
    count = lax.axis_size(axis)
    return lax.ppermute(field, axis, [(i, i ^ bit) for i in range(count)])


def halve(left, right, axis, bit, dim=0):
    n = left.shape[dim] // 2
    mine = jnp.where(lax.axis_index(axis) & bit, 1, 0)
    cut = lambda f, i: lax.dynamic_slice_in_dim(f, i * n, n, dim)
    both = lambda i: cut(left, i) if right is None else (cut(left, i).astype(F32) + cut(right, i).astype(F32)).astype(LOW)
    got = swap(both(1 - mine), axis, bit)
    return both(mine), got


def spread(piece, bits):
    for bit in reversed(bits):
        piece = jnp.concatenate([piece, swap(piece, "dp", bit)], 0)
    return piece


def add(left, right):
    return (left.astype(F32) + right.astype(F32)).astype(LOW)


def sum_lanes(left, right, bits, rest):
    for bit in bits:
        left, right = halve(left, right, "dp", bit)
    total = add(left, right)
    for bit in rest:
        total = add(total, swap(total, "dp", bit))
    return total


def local(
    tokens, lengths, query_key_value, query_bias, value_bias, attn_weight, attn_bias, attn_gain,
    attn_shift, inner_weight, inner_bias, outer_weight, outer_bias, ffn_gain, ffn_shift, cotangent,
):
    groups = lax.axis_size("seq")
    lanes = lax.axis_size("dp")
    me = lax.axis_index("seq")
    lane = lax.axis_index("dp")
    passages, quarter, width = tokens.shape
    hw = H // groups * HD
    rows = passages * quarter
    ff = inner_bias.shape[0]
    bits = [1, 2, 4]
    rest = [1 << i for i in range(3, lanes.bit_length() - 1)]
    where = me.astype(jnp.int32).reshape(1)
    piece_of = ((lane & 1) * 4 + (lane & 2) + (lane >> 2 & 1)).astype(jnp.int32)
    place = jnp.stack([piece_of, me.astype(jnp.int32)])

    across = swap(tokens, "seq", 2)
    beside = swap(tokens, "seq", 1)
    corner = swap(across, "seq", 1)
    shards = (tokens, beside, across, corner)

    cut = lambda f, start: lax.dynamic_slice_in_dim(f, start + me * hw, hw, f.ndim - 1)
    w = jnp.concatenate([cut(query_key_value, t * width) for t in range(3)], 1)
    qb = cut(query_bias, 0).astype(F32).reshape(1, hw)
    vb = cut(value_bias, 0).astype(F32).reshape(1, hw)
    qkv, lse, *context_h = attend(where, lengths, shards, w, qb, vb)
    context = [context_h[0]] + [swap(context_h[j], "seq", j) for j in (1, 2, 3)]
    context = [part.reshape(rows, hw) for part in context]

    vec = jnp.stack([attn_bias, attn_gain, attn_shift, outer_bias, ffn_gain, ffn_shift, ffn_shift, ffn_shift])
    (
        layer_out, grad_one, hidden, active, grad_inner, grad_outer, grad_attn,
        h0, h1, h2, h3, sums, inner_sums,
    ) = rows_pass(
        where,
        tokens.reshape(rows, width),
        context,
        cotangent.reshape(rows, width),
        attn_weight.reshape(groups, hw, width),
        vec.astype(F32),
        inner_bias.astype(F32).reshape(1, ff),
        inner_weight,
        outer_weight,
    )
    grads_h = [h0] + [swap(part, "seq", j) for j, part in ((1, h1), (2, h2), (3, h3))]
    grads_h = [part.reshape(passages, quarter, hw) for part in grads_h]

    outer_send, outer_keep = outer_grad(where, active, grad_outer)
    inner_send, inner_keep = inner_grad(where, hidden, grad_inner, context, grad_attn)

    keep, send, project_grad, bias_sums = attend_back(where, lengths, shards, w, qkv, lse, grads_h)

    def sum_groups(kept, sent):
        got = swap(sent, "seq", 1)
        over = swap(add(kept[1], got[1]), "seq", 2)
        return add(kept[0], got[0]), over

    outer_total = spread(sum_lanes(*sum_groups(outer_keep, outer_send), bits, rest), bits)
    inner_total = spread(sum_lanes(*sum_groups(inner_keep, inner_send), bits, rest), bits)
    project = sum_lanes(project_grad, None, bits, rest)
    got = [project[:, 0]] + [swap(project[:, j], "seq", j) for j in (1, 2, 3)]
    project_total = spread(jnp.stack(got, 1), bits)

    grad_outer_weight = outer_place(place, outer_total)
    grad_inner_weight, grad_attn_weight = inner_place(place, inner_total, hw)
    grad_query_key_value = project_place(place, project_total)

    back, over = sum_groups(keep, send)
    input_grad = (
        grad_one.reshape(passages, quarter, width) + back.astype(F32) + over.astype(F32)
    ).astype(LOW)

    vectors = lax.psum(jnp.concatenate([sums[:6].reshape(-1), inner_sums.reshape(-1)]), ("dp", "seq"))
    mine = lambda r: lax.dynamic_slice(vectors, (r * width + me * hw,), (hw,))
    inner_bias_sum = lax.dynamic_slice(vectors, (6 * width + me * (ff // groups),), (ff // groups,))
    head_sums = lax.psum(bias_sums, "dp")
    return (
        layer_out.reshape(passages, quarter, width),
        input_grad,
        grad_query_key_value,
        head_sums[0],
        head_sums[1],
        grad_attn_weight,
        mine(0),
        mine(1),
        mine(2),
        grad_inner_weight,
        inner_bias_sum,
        grad_outer_weight,
        mine(3),
        mine(4),
        mine(5),
    )


def solution(mesh):
    rows = P("dp", "seq", None)
    return jax.shard_map(
        local,
        mesh=mesh,
        in_specs=(rows, P("dp")) + (P(),) * 13 + (rows,),
        out_specs=(
            rows,
            rows,
            P("seq", None),
            P("seq"),
            P("seq"),
            P("seq", None),
            P("seq"),
            P("seq"),
            P("seq"),
            P("seq", None),
            P("seq"),
            P("seq", None),
            P("seq"),
            P("seq"),
            P("seq"),
        ),
        check_vma=False,
    )
```

time: 1210 us -> 325 us (0.27); the launches traced: 1190 us -> 324 us
  local copies, waits for them, and re-layouts: 281 us -> 21.8 us
  waiting for transfers between devices: 360 us -> 104 us
  blocking collectives: 279 us -> 81.2 us
  other arithmetic: 165 us -> 29.8 us
  Pallas kernels: 0 us -> 62.1 us
  matrix products: 56.3 us -> 0 us
  between operations: 15 us -> 1.23 us
    unnamed x1 -> x0, blocking collectives: 279 us -> none
    unnamed x3 -> x0, waiting for transfers between devices: 248 us -> none
    ppermute x0 -> x36, waiting for transfers between devices: none -> 104 us  [swap(): return lax.ppermute(field, axis, [(i, i ^ bit) for i in range(count)])]
    unnamed x85 -> x88, local copies, waits for them, and re-layouts: 122 us -> 17.8 us
    all_gather x1 -> x0, waiting for transfers between devices: 103 us -> none  [reduce_grads(): lax.all_gather(piece.astype(jnp.bfloat16), 'dp', axis=0, tiled=True)]
    psum x0 -> x2, blocking collectives: none -> 81.2 us  [the longest x1 60.1 us: local(): lax.psum(jnp.concatenate([sums[:6].reshape(-1), inner_sums.reshape(-1)]),...]
    reshape x27 -> x1, local copies, waits for them, and re-layouts: 73 us -> 0.01 us  [local(): sums[:6].reshape(-1)]
    convert_element_type x13 -> x16, other arithmetic: 87.7 us -> 20.2 us  [the longest x8 11.5 us: halve(): (cut(left, i).astype(F32) + cut(right, i).astype(F32)).astype(LOW)]
  transfers between devices with their start and end apart: 10 -> 36, of which waited for: 5 -> 18; matrix products, arithmetic and copies ran while one was open for 7% -> 10% of each run, Pallas kernels for 0% -> 8%
where the time goes in v1:
time: 325 us; the launch traced here: 324 us
  waiting for transfers between devices  104 us (32%)
  blocking collectives  81.2 us (25%)
  Pallas kernels  62.1 us (19%)
  other arithmetic  29.8 us (9%)
  starting transfers between devices  23.5 us (7%)
  local copies, waits for them, and re-layouts  21.8 us (7%)
    ppermute x36, waiting for transfers between devices, swap(): return lax.ppermute(field, axis, [(i, i ^ bit) for i in range(count)])  104 us
    psum x1, blocking collectives, local(): lax.psum(jnp.concatenate([sums[:6].reshape(-1), inner_sums.reshape(-1)]),...  60.1 us
    ppermute x36, starting transfers between devices, swap(): return lax.ppermute(field, axis, [(i, i ^ bit) for i in range(count)])  23.5 us
    psum x1, blocking collectives, local(): head_sums = lax.psum(bias_sums, 'dp')  21.2 us
    unnamed x88, local copies, waits for them, and re-layouts  17.8 us
    pallas_call x1, Pallas kernels, inner_grad(): pl.pallas_call(inner_grad_kernel, grid=(PIECES,), in_specs=[SMEM, whole(r...  12.2 us
    pallas_call x1, Pallas kernels, rows_pass(): pl.pallas_call(rows_kernel, in_specs=[SMEM] + [vmem()] * 9 + [hbm, hbm],...  11.8 us
    convert_element_type x8, other arithmetic, halve(): (cut(left, i).astype(F32) + cut(right, i).astype(F32)).astype(LOW)  11.5 us
  transfers between devices with their start and end apart: 36, of which 18 were waited for; matrix products, arithmetic and copies ran while one was open for 10% of the time, Pallas kernels for 8%

profile of v1, /device:TPU:0, one launch (start us, length us, event | category | flops | bytes accessed | tf_op | source)
XLA Modules:
  0.0 323.6 jit_solution(5114369791096186400)
XLA Ops:
  0.6 3.0 collective-permute-start.1
  3.7 9.3 %collective-permute-done.1.x2 = bf16[2,128,768]{2,1,0:T(8,128)(2,1)S(1)} collective-permute-done((bf16[2,128,768]{2,1,0:T(8,128)(2,1)}, bf16[2,128,768]{2,1,0:T(8,128)(2,1)S(1)}, u32[]{:S(2)}, u32[]{:S(2)}) %collective-permute-start.1) | collective-permute-done | bytes 393248 | tf_op jit(solution)/shard_map/ppermute | solution.py:485
  13.8 2.0 constant_dynamic-slice_fusion.3
  16.9 5.2 %attend.1 = (bf16[2,512,576]{2,1,0:T(8,128)(2,1)S(1)}, f32[2,3,512]{2,1,0:T(4,128)S(1)}, bf16[2,128,192]{2,1,0:T(8,128)(2,1)S(1)}, bf16[2,128,192]{2,1,0:T(8,128...) custom-call(s32[1]{0:T(128)} %bitcast.where, s32[2]{0:T(128)S(1)} %copy-done.20, ...), custom_call_target="tpu_custom_call" | custom-call | flops 3000000000 | bytes 6000000 | tf_op jit(solution)/shard_map/attend/pallas_call | solution.py:78
  24.2 1.7 collective-permute-start.4
  26.1 4.3 %collective-permute-done.4 = bf16[2,128,192]{2,1,0:T(8,128)(2,1)S(1)} collective-permute-done((bf16[2,128,192]{2,1,0:T(8,128)(2,1)S(1)}, bf16[2,128,192]{2,1,0:T(8,128)(2,1)S(1)}, u32[]{:S(2)}, u32[]{:S(2)}) %collective-permute-start.4) | collective-permute-done | bytes 98336 | tf_op jit(solution)/shard_map/ppermute | solution.py:485
  30.5 1.3 collective-permute-done.5
  31.8 1.3 copy-done.2
  33.9 11.8 %rows_pass.1 = (bf16[256,768]{1,0:T(8,128)(2,1)}, f32[256,768]{1,0:T(8,128)S(1)}, bf16[256,768]{1,0:T(8,128)(2,1)S(1)}, bf16[256,3072]{1,0:T(8,128)(2,1)}, bf16[...) custom-call(s32[1]{0:T(128)} %bitcast.where, ...), custom_call_target="tpu_custom_call" | custom-call | flops 6000000000 | bytes 20000000 | tf_op jit(solution)/shard_map/rows_pass/pallas_call | solution.py:297
  45.8 1.4 copy-done.26
  47.3 12.2 %inner_grad.1 = (bf16[2,8,240,384]{3,2,1,0:T(8,128)(2,1)S(1)}, bf16[2,8,240,384]{3,2,1,0:T(8,128)(2,1)S(1)}) custom-call(s32[1]{0:T(128)} %bitcast.where, bf16[256,768]{1,0:T(8,128)(2,1)S(1)} %get-tuple-element.60.hidden, bf16[256,3072]{1,0:T(8,128)(2,1)S(1)} %copy-done.26, bf16[256,192]{1,0:T(8,128)(2,1)S(1)} %bitcast.74, bf16[256,192]{1,0:T(8,128)(2,1)S(1)} %bitcast.67, ...), custom_call_target="tpu_custom_call" | custom-call | flops 1207959552 | bytes 8000000 | tf_op jit(solution)/shard_map/inner_grad/pallas_call | solution.py:395
  60.1 2.6 outer_grad.1
  63.3 1.7 collective-permute-start.7
  65.1 2.4 add_convert_fusion.1
  67.5 1.8 collective-permute-start.21
  69.3 2.2 add_convert_fusion.3
  83.4 11.4 %attend_back.1 = (bf16[2,2,128,768]{3,2,1,0:T(8,128)(2,1)S(1)}, bf16[2,2,128,768]{3,2,1,0:T(8,128)(2,1)S(1)}, bf16[8,4,24,576]{3,2,1,0:T(8,128)(2,1)S(1)}, f32[2,192]{1,0:T(2,128)S(1)}) custom-call(s32[1]{0:T(128)} %bitcast.where, s32[2]{0:T(128)S(1)} %copy-done.21, bf16[2,128,768]{2,1,0:T(8,128)(2,1)S(1)} %copy-done.7, bf16[2,128,768]{2,1,0:T(8,128)(2,1)S(1)} %copy-done.11, ...), custom_call_target="tpu_custom_call" | custom-call | flops 5000000000 | bytes 10000000 | tf_op jit(solution)/shard_map/attend_back/pallas_call | solution.py:173
  95.7 1.6 collective-permute-start.11
  97.3 11.8 %collective-permute-done.11 = bf16[4,4,24,576]{3,2,1,0:T(8,128)(2,1)} collective-permute-done((bf16[4,4,24,576]{3,2,1,0:T(8,128)(2,1)S(1)}, bf16[4,4,24,576]{3,2,1,0:T(8,128)(2,1)}, u32[]{:S(2)}, u32[]{:S(2)}) %collective-permute-start.11) | collective-permute-done | bytes 442400 | tf_op jit(solution)/shard_map/ppermute | solution.py:485
  109.1 1.9 add_convert_fusion.11
  111.0 1.6 collective-permute-start.12
  112.5 16.2 %collective-permute-done.29 = bf16[8,96,768]{2,1,0:T(8,128)(2,1)} collective-permute-done((bf16[8,96,768]{2,1,0:T(8,128)(2,1)}, bf16[8,96,768]{2,1,0:T(8,128)(2,1)}, u32[]{:S(2)}, u32[]{:S(2)}) %collective-permute-start.29) | collective-permute-done | bytes 1179680 | tf_op jit(solution)/shard_map/ppermute | solution.py:485
  128.7 2.7 fusion.5
  131.4 1.7 collective-permute-start.30
  133.1 2.7 fusion.2
  136.7 60.1 %psum.15 = f32[7680]{0:T(1024)S(1)} all-reduce(f32[7680]{0:T(1024)S(1)} %pad_maximum_fusion.11), channel_id=1, replica_groups=mesh['dp'=8,'seq'=4] {'dp','seq'}, use_global_device_ids=true, to_apply=%region_1.2 | all-reduce | flops 7680 | bytes 61440 | tf_op jit(solution)/shard_map/psum | solution.py:590
  197.5 1.6 add_convert_fusion.19
  200.2 21.2 %psum.14 = f32[2,192]{1,0:T(2,128)S(1)} all-reduce(f32[2,192]{1,0:T(2,128)S(1)} %get-tuple-element.59), channel_id=1, replica_groups=mesh['dp'=8,'seq'=4] {'dp'}, use_global_device_ids=true, to_apply=%region_0.1 | all-reduce | flops 384 | bytes 3072 | tf_op jit(solution)/shard_map/psum | solution.py:593
  222.4 1.4 add_convert_fusion.9
  223.9 1.3 add_convert_fusion.7
  225.2 2.1 collective-permute-start.23
  227.8 5.5 %collective-permute-done.31 = bf16[2,96,768]{2,1,0:T(8,128)(2,1)S(1)} collective-permute-done((bf16[2,96,768]{2,1,0:T(8,128)(2,1)S(1)}, bf16[2,96,768]{2,1,0:T(8,128)(2,1)S(1)}, u32[]{:S(2)}, u32[]{:S(2)}) %collective-permute-start.31) | collective-permute-done | bytes 294944 | tf_op jit(solution)/shard_map/ppermute | solution.py:485
  234.6 1.9 collective-permute-start.17
  237.7 12.4 %collective-permute-done.32 = bf16[1,96,768]{2,1,0:T(8,128)(2,1)S(1)} collective-permute-done((bf16[1,96,768]{2,1,0:T(8,128)(2,1)S(1)}, bf16[1,96,768]{2,1,0:T(8,128)(2,1)S(1)}, u32[]{:S(2)}, u32[]{:S(2)}) %collective-permute-start.32) | collective-permute-done | bytes 147488 | tf_op jit(solution)/shard_map/ppermute | solution.py:485
  250.3 9.6 %collective-permute-done.24 = bf16[1,240,384]{2,1,0:T(8,128)(2,1)S(1)} collective-permute-done((bf16[1,240,384]{2,1,0:T(8,128)(2,1)S(1)}, bf16[1,240,384]{2,1,0:T(8,128)(2,1)S(1)}, u32[]{:S(2)}, u32[]{:S(2)}) %collective-permute-start.24) | collective-permute-done | bytes 184352 | tf_op jit(solution)/shard_map/ppermute | solution.py:485
  261.1 6.0 %collective-permute-done.33 = bf16[1,96,768]{2,1,0:T(8,128)(2,1)S(1)} collective-permute-done((bf16[1,96,768]{2,1,0:T(8,128)(2,1)S(1)}, bf16[1,96,768]{2,1,0:T(8,128)(2,1)S(1)}, u32[]{:S(2)}, u32[]{:S(2)}) %collective-permute-start.33) | collective-permute-done | bytes 147488 | tf_op jit(solution)/shard_map/ppermute | solution.py:485
  267.2 3.8 %collective-permute-done.25 = bf16[1,240,384]{2,1,0:T(8,128)(2,1)S(1)} collective-permute-done((bf16[1,240,384]{2,1,0:T(8,128)(2,1)S(1)}, bf16[1,240,384]{2,1,0:T(8,128)(2,1)S(1)}, u32[]{:S(2)}, u32[]{:S(2)}) %collective-permute-start.25) | collective-permute-done | bytes 184352 | tf_op jit(solution)/shard_map/ppermute | solution.py:485
  272.8 2.0 collective-permute-done.18
  274.9 6.1 %collective-permute-done.34 = bf16[2,96,768]{2,1,0:T(8,128)(2,1)S(1)} collective-permute-done((bf16[2,96,768]{2,1,0:T(8,128)(2,1)S(1)}, bf16[2,96,768]{2,1,0:T(8,128)(2,1)S(1)}, u32[]{:S(2)}, u32[]{:S(2)}) %collective-permute-start.34) | collective-permute-done | bytes 294944 | tf_op jit(solution)/shard_map/ppermute | solution.py:485
  282.0 6.1 %collective-permute-done.26 = bf16[2,240,384]{2,1,0:T(8,128)(2,1)S(1)} collective-permute-done((bf16[2,240,384]{2,1,0:T(8,128)(2,1)S(1)}, bf16[2,240,384]{2,1,0:T(8,128)(2,1)S(1)}, u32[]{:S(2)}, u32[]{:S(2)}) %collective-permute-start.26) | collective-permute-done | bytes 368672 | tf_op jit(solution)/shard_map/ppermute | solution.py:485
  289.6 1.9 fusion.7
  292.6 6.4 %project_place.1 = f32[192,2304]{1,0:T(8,128)} custom-call(s32[2]{0:T(128)} %pad_add_fusion.place, bf16[8,4,24,576]{3,2,1,0:T(8,128)(2,1)} %pad_maximum_fusion.3.piece), custom_call_target="tpu_custom_call" | custom-call | tf_op jit(solution)/shard_map/project_place/pallas_call | solution.py:470
  299.0 2.8 collective-permute-done.35
  301.8 2.2 pad_maximum_fusion.1.piece
  304.0 6.2 %outer_place.1 = f32[768,768]{1,0:T(8,128)} custom-call(s32[2]{0:T(128)} %pad_add_fusion.place, bf16[8,96,768]{2,1,0:T(8,128)(2,1)} %pad_maximum_fusion.1.piece), custom_call_target="tpu_custom_call" | custom-call | tf_op jit(solution)/shard_map/outer_place/pallas_call | solution.py:416
  310.2 4.7 %collective-permute-done.27 = bf16[4,240,384]{2,1,0:T(8,128)(2,1)} collective-permute-done((bf16[4,240,384]{2,1,0:T(8,128)(2,1)}, bf16[4,240,384]{2,1,0:T(8,128)(2,1)}, u32[]{:S(2)}, u32[]{:S(2)}) %collective-permute-start.27) | collective-permute-done | bytes 737312 | tf_op jit(solution)/shard_map/ppermute | solution.py:485
  314.9 2.4 pad_maximum_fusion.piece
  317.3 6.4 %inner_place.1 = (f32[192,3072]{1,0:T(8,128)}, f32[192,768]{1,0:T(8,128)}) custom-call(s32[2]{0:T(128)} %pad_add_fusion.place, bf16[8,240,384]{2,1,0:T(8,128)(2,1)} %pad_maximum_fusion.piece), custom_call_target="tpu_custom_call" | custom-call | tf_op jit(solution)/shard_map/inner_place/pallas_call | solution.py:440
  (167 shorter events, 32.9 us)
Async XLA Ops:
  0.6 12.4 %collective-permute-start.1 = (bf16[2,128,768]{2,1,0:T(8,128)(2,1)}, bf16[2,128,768]{2,1,0:T(8,128)(2,1)S(1)}, u32[]{:S(2)}, u32[]{:S(2)}) collective-permute-start(bf16[2,128,768]{2,1,0:T(8,128)(2,1)} %x0.3), channel_id=1, source_target_pairs={{0,2},{1,3},{2,0},{3,1},{4,6},{5,7},{6,4},{7,5},{8,10},{9,11},{10,... | collective-permute-start | bytes 1179656 | tf_op jit(solution)/shard_map/ppermute | solution.py:485
  3.7 12.5 %collective-permute-start = (bf16[2,128,768]{2,1,0:T(8,128)(2,1)}, bf16[2,128,768]{2,1,0:T(8,128)(2,1)S(1)}, u32[]{:S(2)}, u32[]{:S(2)}) collective-permute-start(bf16[2,128,768]{2,1,0:T(8,128)(2,1)} %x0.3), channel_id=1, source_target_pairs={{0,1},{1,0},{2,3},{3,2},{4,5},{5,4},{6,7},{7,6},{8,9},{9,8},{10,11... | collective-permute-start | bytes 1179656 | tf_op jit(solution)/shard_map/ppermute | solution.py:485
  13.0 3.2 collective-permute-start.2
  16.8 9.2 %copy-start.43 = (bf16[768]{0:T(1024)(128)(2,1)S(1)}, bf16[768]{0:T(1024)(128)(2,1)}, u32[]{:S(2)}) copy-start(bf16[768]{0:T(1024)(128)(2,1)} %param.30) | copy-start | bytes 4612
  16.9 9.3 %copy-start.37 = (bf16[3072]{0:T(1024)(128)(2,1)S(1)}, bf16[3072]{0:T(1024)(128)(2,1)}, u32[]{:S(2)}) copy-start(bf16[3072]{0:T(1024)(128)(2,1)} %param.26) | copy-start | bytes 18436
  16.9 14.9 %copy-start.5 = (bf16[2,128,768]{2,1,0:T(8,128)(2,1)S(1)}, bf16[2,128,768]{2,1,0:T(8,128)(2,1)}, u32[]{:S(2)}) copy-start(bf16[2,128,768]{2,1,0:T(8,128)(2,1)} %param.31) | copy-start | bytes 1179652
  23.8 22.0 %copy-start.29 = (f32[2,3,512]{2,1,0:T(4,128)}, f32[2,3,512]{2,1,0:T(4,128)S(1)}, u32[]{:S(2)}) copy-start(f32[2,3,512]{2,1,0:T(4,128)S(1)} %get-tuple-element.51.lse) | copy-start | bytes 36868
  23.8 2.4 collective-permute-start.3
  24.2 6.2 %collective-permute-start.4 = (bf16[2,128,192]{2,1,0:T(8,128)(2,1)S(1)}, bf16[2,128,192]{2,1,0:T(8,128)(2,1)S(1)}, u32[]{:S(2)}, u32[]{:S(2)}) collective-permute-start(bf16[2,128,192]{2,1,0:T(8,128)(2,1)S(1)} %get-tuple-element.46), channel_id=1, source_target_pairs={{0,2},{1,3},{2,0},{3,1},{4,6},{5,7},{6,4},{7,5},{8,10},{9,11},{10,... | collective-permute-start | bytes 294920 | tf_op jit(solution)/shard_map/ppermute | solution.py:485
  25.9 5.8 %collective-permute-start.5 = (bf16[2,128,192]{2,1,0:T(8,128)(2,1)S(1)}, bf16[2,128,192]{2,1,0:T(8,128)(2,1)S(1)}, u32[]{:S(2)}, u32[]{:S(2)}) collective-permute-start(bf16[2,128,192]{2,1,0:T(8,128)(2,1)S(1)} %get-tuple-element.47), channel_id=1, source_target_pairs={{0,3},{1,2},{2,1},{3,0},{4,7},{5,6},{6,5},{7,4},{8,11},{9,10},{10,... | collective-permute-start | bytes 294920 | tf_op jit(solution)/shard_map/ppermute | solution.py:485
  45.8 13.7 %copy-start = (f32[8,768]{1,0:T(8,128)}, f32[8,768]{1,0:T(8,128)S(1)}, u32[]{:S(2)}) copy-start(f32[8,768]{1,0:T(8,128)S(1)} %get-tuple-element.66) | copy-start | bytes 73732
  45.8 13.7 %copy-start.22 = (bf16[256,192]{1,0:T(8,128)(2,1)}, bf16[256,192]{1,0:T(8,128)(2,1)S(1)}, u32[]{:S(2)}) copy-start(bf16[256,192]{1,0:T(8,128)(2,1)S(1)} %get-tuple-element.52) | copy-start | bytes 294916
  47.3 12.9 %copy-start.27 = (bf16[256,3072]{1,0:T(8,128)(2,1)S(1)}, bf16[256,3072]{1,0:T(8,128)(2,1)}, u32[]{:S(2)}) copy-start(bf16[256,3072]{1,0:T(8,128)(2,1)} %get-tuple-element.69.active) | copy-start | bytes 4718596
  59.5 5.6 %collective-permute-start.20 = (bf16[2,8,240,384]{3,2,1,0:T(8,128)(2,1)S(1)}, bf16[2,8,240,384]{3,2,1,0:T(8,128)(2,1)S(1)}, u32[]{:S(2)}, u32[]{:S(2)}) collective-permute-start(bf16[2,8,240,384]{3,2,1,0:T(8,128)(2,1)S(1)} %get-tuple-element.64), channel_id=1, source_target_pairs={{0,1},{1,0},{2,3},{3,2},{4,5},{5,4},{6,7},{7,6},{8,9},{9,8},{10,11... | collective-permute-start | bytes 8847368 | tf_op jit(solution)/shard_map/ppermute | solution.py:485
  62.7 6.5 %collective-permute-start.28 = (bf16[2,8,96,768]{3,2,1,0:T(8,128)(2,1)S(1)}, bf16[2,8,96,768]{3,2,1,0:T(8,128)(2,1)S(1)}, u32[]{:S(2)}, u32[]{:S(2)}) collective-permute-start(bf16[2,8,96,768]{3,2,1,0:T(8,128)(2,1)S(1)} %get-tuple-element.72), channel_id=1, source_target_pairs={{0,1},{1,0},{2,3},{3,2},{4,5},{5,4},{6,7},{7,6},{8,9},{9,8},{10,11... | collective-permute-start | bytes 7077896 | tf_op jit(solution)/shard_map/ppermute | solution.py:485
  63.0 9.4 %collective-permute-start.6 = (bf16[256,192]{1,0:T(8,128)(2,1)S(1)}, bf16[256,192]{1,0:T(8,128)(2,1)S(1)}, u32[]{:S(2)}, u32[]{:S(2)}) collective-permute-start(bf16[256,192]{1,0:T(8,128)(2,1)S(1)} %get-tuple-element.53), channel_id=1, source_target_pairs={{0,1},{1,0},{2,3},{3,2},{4,5},{5,4},{6,7},{7,6},{8,9},{9,8},{10,11... | collective-permute-start | bytes 294920 | tf_op jit(solution)/shard_map/ppermute | solution.py:485
  63.3 9.8 %collective-permute-start.7 = (bf16[256,192]{1,0:T(8,128)(2,1)S(1)}, bf16[256,192]{1,0:T(8,128)(2,1)S(1)}, u32[]{:S(2)}, u32[]{:S(2)}) collective-permute-start(bf16[256,192]{1,0:T(8,128)(2,1)S(1)} %get-tuple-element.54), channel_id=1, source_target_pairs={{0,2},{1,3},{2,0},{3,1},{4,6},{5,7},{6,4},{7,5},{8,10},{9,11},{10,... | collective-permute-start | bytes 294920 | tf_op jit(solution)/shard_map/ppermute | solution.py:485
  65.0 8.7 %collective-permute-start.8 = (bf16[256,192]{1,0:T(8,128)(2,1)S(1)}, bf16[256,192]{1,0:T(8,128)(2,1)S(1)}, u32[]{:S(2)}, u32[]{:S(2)}) collective-permute-start(bf16[256,192]{1,0:T(8,128)(2,1)S(1)} %get-tuple-element.55), channel_id=1, source_target_pairs={{0,3},{1,2},{2,1},{3,0},{4,7},{5,6},{6,5},{7,4},{8,11},{9,10},{10,... | collective-permute-start | bytes 294920 | tf_op jit(solution)/shard_map/ppermute | solution.py:485
  67.5 65.6 %collective-permute-start.21 = (bf16[8,240,384]{2,1,0:T(8,128)(2,1)}, bf16[8,240,384]{2,1,0:T(8,128)(2,1)}, u32[]{:S(2)}, u32[]{:S(2)}) collective-permute-start(bf16[8,240,384]{2,1,0:T(8,128)(2,1)} %get-tuple-element.74), channel_id=1, source_target_pairs={{0,2},{1,3},{2,0},{3,1},{4,6},{5,7},{6,4},{7,5},{8,10},{9,11},{10,... | collective-permute-start | bytes 4423688 | tf_op jit(solution)/shard_map/ppermute | solution.py:485
  71.4 57.3 %collective-permute-start.29 = (bf16[8,96,768]{2,1,0:T(8,128)(2,1)}, bf16[8,96,768]{2,1,0:T(8,128)(2,1)}, u32[]{:S(2)}, u32[]{:S(2)}) collective-permute-start(bf16[8,96,768]{2,1,0:T(8,128)(2,1)} %get-tuple-element.76), channel_id=1, source_target_pairs={{0,2},{1,3},{2,0},{3,1},{4,6},{5,7},{6,4},{7,5},{8,10},{9,11},{10,... | collective-permute-start | bytes 3538952 | tf_op jit(solution)/shard_map/ppermute | solution.py:485
  95.7 13.4 %collective-permute-start.11 = (bf16[4,4,24,576]{3,2,1,0:T(8,128)(2,1)S(1)}, bf16[4,4,24,576]{3,2,1,0:T(8,128)(2,1)}, u32[]{:S(2)}, u32[]{:S(2)}) collective-permute-start(bf16[4,4,24,576]{3,2,1,0:T(8,128)(2,1)S(1)} %constant_dynamic-slice_fusion), channel_id=1, source_target_pairs={{0,4},{4,0},{8,12},{12,8},{16,20},{20,16},{24,28},{28,24},{1,5},{5... | collective-permute-start | bytes 1327112 | tf_op jit(solution)/shard_map/ppermute | solution.py:485
  97.3 31.4 %copy-start.32 = (bf16[1,8,96,768]{3,2,1,0:T(8,128)(2,1)S(1)}, bf16[1,8,96,768]{3,2,1,0:T(8,128)(2,1)}, u32[]{:S(2)}) copy-start(bf16[1,8,96,768]{3,2,1,0:T(8,128)(2,1)} %get-tuple-element.75) | copy-start | bytes 3538948
  111.0 86.5 %collective-permute-start.12 = (bf16[2,4,24,576]{3,2,1,0:T(8,128)(2,1)}, bf16[2,4,24,576]{3,2,1,0:T(8,128)(2,1)}, u32[]{:S(2)}, u32[]{:S(2)}) collective-permute-start(bf16[2,4,24,576]{3,2,1,0:T(8,128)(2,1)} %get-tuple-element.87), channel_id=1, source_target_pairs={{0,8},{4,12},{8,0},{12,4},{16,24},{20,28},{24,16},{28,20},{1,9},{5... | collective-permute-start | bytes 663560 | tf_op jit(solution)/shard_map/ppermute | solution.py:485
  131.4 91.0 %collective-permute-start.30 = (bf16[4,96,768]{2,1,0:T(8,128)(2,1)}, bf16[4,96,768]{2,1,0:T(8,128)(2,1)}, u32[]{:S(2)}, u32[]{:S(2)}) collective-permute-start(bf16[4,96,768]{2,1,0:T(8,128)(2,1)} %get-tuple-element.83), channel_id=1, source_target_pairs={{0,4},{4,0},{8,12},{12,8},{16,20},{20,16},{24,28},{28,24},{1,5},{5... | collective-permute-start | bytes 1769480 | tf_op jit(solution)/shard_map/ppermute | solution.py:485
  133.1 67.1 %copy-start.4 = (bf16[2,2,128,768]{3,2,1,0:T(8,128)(2,1)S(1)}, bf16[2,2,128,768]{3,2,1,0:T(8,128)(2,1)}, u32[]{:S(2)}) copy-start(bf16[2,2,128,768]{3,2,1,0:T(8,128)(2,1)} %copy-done.3) | copy-start | bytes 2359300
  135.8 88.1 %collective-permute-start.22 = (bf16[4,240,384]{2,1,0:T(8,128)(2,1)}, bf16[4,240,384]{2,1,0:T(8,128)(2,1)}, u32[]{:S(2)}, u32[]{:S(2)}) collective-permute-start(bf16[4,240,384]{2,1,0:T(8,128)(2,1)} %get-tuple-element.81), channel_id=1, source_target_pairs={{0,4},{4,0},{8,12},{12,8},{16,20},{20,16},{24,28},{28,24},{1,5},{5... | collective-permute-start | bytes 2211848 | tf_op jit(solution)/shard_map/ppermute | solution.py:485
  199.1 22.4 %collective-permute-start.13 = (bf16[1,4,24,576]{3,2,1,0:T(8,128)(2,1)}, bf16[1,4,24,576]{3,2,1,0:T(8,128)(2,1)S(1)}, u32[]{:S(2)}, u32[]{:S(2)}) collective-permute-start(bf16[1,4,24,576]{3,2,1,0:T(8,128)(2,1)} %add_convert_fusion.19), channel_id=1, source_target_pairs={{0,16},{4,20},{8,24},{12,28},{16,0},{20,4},{24,8},{28,12},{1,17},{... | collective-permute-start | bytes 331784 | tf_op jit(solution)/shard_map/ppermute | solution.py:485
  200.2 70.9 %collective-permute-start.9 = (bf16[2,2,128,768]{3,2,1,0:T(8,128)(2,1)S(1)}, bf16[2,2,128,768]{3,2,1,0:T(8,128)(2,1)}, u32[]{:S(2)}, u32[]{:S(2)}) collective-permute-start(bf16[2,2,128,768]{3,2,1,0:T(8,128)(2,1)S(1)} %copy-done.4), channel_id=1, source_target_pairs={{0,1},{1,0},{2,3},{3,2},{4,5},{5,4},{6,7},{7,6},{8,9},{9,8},{10,11... | collective-permute-start | bytes 2359304 | tf_op jit(solution)/shard_map/ppermute | solution.py:485
  223.8 9.6 %collective-permute-start.31 = (bf16[2,96,768]{2,1,0:T(8,128)(2,1)S(1)}, bf16[2,96,768]{2,1,0:T(8,128)(2,1)S(1)}, u32[]{:S(2)}, u32[]{:S(2)}) collective-permute-start(bf16[2,96,768]{2,1,0:T(8,128)(2,1)S(1)} %get-tuple-element.89), channel_id=1, source_target_pairs={{0,8},{4,12},{8,0},{12,4},{16,24},{20,28},{24,16},{28,20},{1,9},{5... | collective-permute-start | bytes 884744 | tf_op jit(solution)/shard_map/ppermute | solution.py:485
  225.2 12.1 %collective-permute-start.23 = (bf16[2,240,384]{2,1,0:T(8,128)(2,1)S(1)}, bf16[2,240,384]{2,1,0:T(8,128)(2,1)S(1)}, u32[]{:S(2)}, u32[]{:S(2)}) collective-permute-start(bf16[2,240,384]{2,1,0:T(8,128)(2,1)S(1)} %get-tuple-element.85), channel_id=1, source_target_pairs={{0,8},{4,12},{8,0},{12,4},{16,24},{20,28},{24,16},{28,20},{1,9},{5... | collective-permute-start | bytes 1105928 | tf_op jit(solution)/shard_map/ppermute | solution.py:485
  227.3 6.1 %collective-permute-start.16 = (bf16[1,24,576]{2,1,0:T(8,128)(2,1)S(1)}, bf16[1,24,576]{2,1,0:T(8,128)(2,1)S(1)}, u32[]{:S(2)}, u32[]{:S(2)}) collective-permute-start(bf16[1,24,576]{2,1,0:T(8,128)(2,1)S(1)} %get-tuple-element.91), channel_id=1, source_target_pairs={{0,3},{1,2},{2,1},{3,0},{4,7},{5,6},{6,5},{7,4},{8,11},{9,10},{10,... | collective-permute-start | bytes 82952 | tf_op jit(solution)/shard_map/ppermute | solution.py:485
  227.3 6.1 %collective-permute-start.15 = (bf16[1,24,576]{2,1,0:T(8,128)(2,1)S(1)}, bf16[1,24,576]{2,1,0:T(8,128)(2,1)S(1)}, u32[]{:S(2)}, u32[]{:S(2)}) collective-permute-start(bf16[1,24,576]{2,1,0:T(8,128)(2,1)S(1)} %get-tuple-element.92), channel_id=1, source_target_pairs={{0,2},{1,3},{2,0},{3,1},{4,6},{5,7},{6,4},{7,5},{8,10},{9,11},{10,... | collective-permute-start | bytes 82952 | tf_op jit(solution)/shard_map/ppermute | solution.py:485
  233.3 1.2 collective-permute-start.14
  233.4 16.7 %collective-permute-start.32 = (bf16[1,96,768]{2,1,0:T(8,128)(2,1)S(1)}, bf16[1,96,768]{2,1,0:T(8,128)(2,1)S(1)}, u32[]{:S(2)}, u32[]{:S(2)}) collective-permute-start(bf16[1,96,768]{2,1,0:T(8,128)(2,1)S(1)} %add_convert_fusion.16), channel_id=1, source_target_pairs={{0,16},{4,20},{8,24},{12,28},{16,0},{20,4},{24,8},{28,12},{1,17},{... | collective-permute-start | bytes 442376 | tf_op jit(solution)/shard_map/ppermute | solution.py:485
  234.6 25.5 %collective-permute-start.17 = (bf16[1,4,24,576]{3,2,1,0:T(8,128)(2,1)S(1)}, bf16[1,4,24,576]{3,2,1,0:T(8,128)(2,1)S(1)}, u32[]{:S(2)}, u32[]{:S(2)}) collective-permute-start(bf16[1,4,24,576]{3,2,1,0:T(8,128)(2,1)S(1)} %pad_maximum_fusion.10), channel_id=1, source_target_pairs={{0,16},{4,20},{8,24},{12,28},{16,0},{20,4},{24,8},{28,12},{1,17},{... | collective-permute-start | bytes 331784 | tf_op jit(solution)/shard_map/ppermute | solution.py:485
  237.3 22.5 %collective-permute-start.24 = (bf16[1,240,384]{2,1,0:T(8,128)(2,1)S(1)}, bf16[1,240,384]{2,1,0:T(8,128)(2,1)S(1)}, u32[]{:S(2)}, u32[]{:S(2)}) collective-permute-start(bf16[1,240,384]{2,1,0:T(8,128)(2,1)S(1)} %add_convert_fusion.13), channel_id=1, source_target_pairs={{0,16},{4,20},{8,24},{12,28},{16,0},{20,4},{24,8},{28,12},{1,17},{... | collective-permute-start | bytes 552968 | tf_op jit(solution)/shard_map/ppermute | solution.py:485
  250.2 16.9 %collective-permute-start.33 = (bf16[1,96,768]{2,1,0:T(8,128)(2,1)S(1)}, bf16[1,96,768]{2,1,0:T(8,128)(2,1)S(1)}, u32[]{:S(2)}, u32[]{:S(2)}) collective-permute-start(bf16[1,96,768]{2,1,0:T(8,128)(2,1)S(1)} %add_convert_fusion.15), channel_id=1, source_target_pairs={{0,16},{4,20},{8,24},{12,28},{16,0},{20,4},{24,8},{28,12},{1,17},{... | collective-permute-start | bytes 442376 | tf_op jit(solution)/shard_map/ppermute | solution.py:485
  259.9 11.1 %collective-permute-start.25 = (bf16[1,240,384]{2,1,0:T(8,128)(2,1)S(1)}, bf16[1,240,384]{2,1,0:T(8,128)(2,1)S(1)}, u32[]{:S(2)}, u32[]{:S(2)}) collective-permute-start(bf16[1,240,384]{2,1,0:T(8,128)(2,1)S(1)} %add_convert_fusion.12), channel_id=1, source_target_pairs={{0,16},{4,20},{8,24},{12,28},{16,0},{20,4},{24,8},{28,12},{1,17},{... | collective-permute-start | bytes 552968 | tf_op jit(solution)/shard_map/ppermute | solution.py:485
  260.1 14.7 %collective-permute-start.18 = (bf16[2,4,24,576]{3,2,1,0:T(8,128)(2,1)S(1)}, bf16[2,4,24,576]{3,2,1,0:T(8,128)(2,1)S(1)}, u32[]{:S(2)}, u32[]{:S(2)}) collective-permute-start(bf16[2,4,24,576]{3,2,1,0:T(8,128)(2,1)S(1)} %pad_maximum_fusion.9), channel_id=1, source_target_pairs={{0,8},{4,12},{8,0},{12,4},{16,24},{20,28},{24,16},{28,20},{1,9},{5... | collective-permute-start | bytes 663560 | tf_op jit(solution)/shard_map/ppermute | solution.py:485
  267.1 14.0 %copy-start.33 = (bf16[1,96,768]{2,1,0:T(8,128)(2,1)}, bf16[1,96,768]{2,1,0:T(8,128)(2,1)S(1)}, u32[]{:S(2)}) copy-start(bf16[1,96,768]{2,1,0:T(8,128)(2,1)S(1)} %collective-permute-done.33) | copy-start | bytes 442372
  267.1 14.0 %collective-permute-start.34 = (bf16[2,96,768]{2,1,0:T(8,128)(2,1)S(1)}, bf16[2,96,768]{2,1,0:T(8,128)(2,1)S(1)}, u32[]{:S(2)}, u32[]{:S(2)}) collective-permute-start(bf16[2,96,768]{2,1,0:T(8,128)(2,1)S(1)} %pad_maximum_fusion.8), channel_id=1, source_target_pairs={{0,8},{4,12},{8,0},{12,4},{16,24},{20,28},{24,16},{28,20},{1,9},{5... | collective-permute-start | bytes 884744 | tf_op jit(solution)/shard_map/ppermute | solution.py:485
  271.0 17.0 %collective-permute-start.26 = (bf16[2,240,384]{2,1,0:T(8,128)(2,1)S(1)}, bf16[2,240,384]{2,1,0:T(8,128)(2,1)S(1)}, u32[]{:S(2)}, u32[]{:S(2)}) collective-permute-start(bf16[2,240,384]{2,1,0:T(8,128)(2,1)S(1)} %pad_maximum_fusion.7), channel_id=1, source_target_pairs={{0,8},{4,12},{8,0},{12,4},{16,24},{20,28},{24,16},{28,20},{1,9},{5... | collective-permute-start | bytes 1105928 | tf_op jit(solution)/shard_map/ppermute | solution.py:485
  272.2 17.4 %collective-permute-start.10 = (bf16[2,128,768]{2,1,0:T(8,128)(2,1)S(1)}, bf16[2,128,768]{2,1,0:T(8,128)(2,1)S(1)}, u32[]{:S(2)}, u32[]{:S(2)}) collective-permute-start(bf16[2,128,768]{2,1,0:T(8,128)(2,1)S(1)} %fusion.9), channel_id=1, source_target_pairs={{0,2},{1,3},{2,0},{3,1},{4,6},{5,7},{6,4},{7,5},{8,10},{9,11},{10,... | collective-permute-start | bytes 1179656 | tf_op jit(solution)/shard_map/ppermute | solution.py:485
  274.8 16.7 %collective-permute-start.19 = (bf16[4,4,24,576]{3,2,1,0:T(8,128)(2,1)S(1)}, bf16[4,4,24,576]{3,2,1,0:T(8,128)(2,1)S(1)}, u32[]{:S(2)}, u32[]{:S(2)}) collective-permute-start(bf16[4,4,24,576]{3,2,1,0:T(8,128)(2,1)S(1)} %pad_maximum_fusion.6), channel_id=1, source_target_pairs={{0,4},{4,0},{8,12},{12,8},{16,20},{20,16},{24,28},{28,24},{1,5},{5... | collective-permute-start | bytes 1327112 | tf_op jit(solution)/shard_map/ppermute | solution.py:485
  282.0 19.8 %collective-permute-start.35 = (bf16[4,96,768]{2,1,0:T(8,128)(2,1)}, bf16[4,96,768]{2,1,0:T(8,128)(2,1)}, u32[]{:S(2)}, u32[]{:S(2)}) collective-permute-start(bf16[4,96,768]{2,1,0:T(8,128)(2,1)} %pad_maximum_fusion.5), channel_id=1, source_target_pairs={{0,4},{4,0},{8,12},{12,8},{16,20},{20,16},{24,28},{28,24},{1,5},{5... | collective-permute-start | bytes 1769480 | tf_op jit(solution)/shard_map/ppermute | solution.py:485
  289.0 25.8 %collective-permute-start.27 = (bf16[4,240,384]{2,1,0:T(8,128)(2,1)}, bf16[4,240,384]{2,1,0:T(8,128)(2,1)}, u32[]{:S(2)}, u32[]{:S(2)}) collective-permute-start(bf16[4,240,384]{2,1,0:T(8,128)(2,1)} %pad_maximum_fusion.4), channel_id=1, source_target_pairs={{0,4},{4,0},{8,12},{12,8},{16,20},{20,16},{24,28},{28,24},{1,5},{5... | collective-permute-start | bytes 2211848 | tf_op jit(solution)/shard_map/ppermute | solution.py:485
  292.6 9.2 %copy-start.34 = (bf16[1,96,768]{2,1,0:T(8,128)(2,1)S(1)}, bf16[1,96,768]{2,1,0:T(8,128)(2,1)}, u32[]{:S(2)}) copy-start(bf16[1,96,768]{2,1,0:T(8,128)(2,1)} %copy-done.33) | copy-start | bytes 442372
  292.6 9.2 %copy-start.36 = (bf16[2,96,768]{2,1,0:T(8,128)(2,1)S(1)}, bf16[2,96,768]{2,1,0:T(8,128)(2,1)}, u32[]{:S(2)}) copy-start(bf16[2,96,768]{2,1,0:T(8,128)(2,1)} %copy-done.35) | copy-start | bytes 884740
  (32 other events, 88.7 us)

commit v2 on v1

v2 whole, which is shorter than its diff:
```python
import jax
import jax.numpy as jnp
from jax import lax
from jax.experimental import pallas as pl
from jax.experimental.pallas import tpu as pltpu
from jax.sharding import PartitionSpec as P

H = 12
HD = 64
EPS = 1e-12
F32 = jnp.float32
LOW = jnp.bfloat16
MIB = 1 << 20
PIECES = 8


def cost(us):
    return pl.CostEstimate(flops=int(us * 1.15e9), bytes_accessed=int(us * 3.69e6), transcendentals=0)


def dot(a, b):
    return lax.dot_general(a, b, (((1,), (0,)), ((), ())), preferred_element_type=F32)


def dot_nt(a, b):
    return lax.dot_general(a, b, (((1,), (1,)), ((), ())), preferred_element_type=F32)


def dot_tn(a, b):
    return lax.dot_general(a, b, (((0,), (0,)), ((), ())), preferred_element_type=F32)


def vmem(shape=None, index=None):
    if shape is None:
        return pl.BlockSpec(memory_space=pltpu.VMEM)
    return pl.BlockSpec(shape, index)


SMEM = pl.BlockSpec(memory_space=pltpu.SMEM)
HBM = pl.BlockSpec(memory_space=pltpu.HBM)


def far(array):
    return pltpu.with_memory_space_constraint(array, pltpu.HBM)


def key_mask(me, length, rows, quarter):
    slot = lax.broadcasted_iota(jnp.int32, (rows, 1), 0)
    block = slot // quarter
    return ((block ^ me) * quarter + (slot - block * quarter)) < length


def attend_kernel(where, lengths, x0, x1, x2, x3, w_hbm, qb, vb, qkv_out, lse_out, w, *refs):
    near_out, across_out, wide, sem = refs
    p = pl.program_id(0)
    me = where[0]
    quarter, width = x0.shape[1:]
    rows = 4 * quarter
    hw = w.shape[1] // 3
    window = wide.shape[2]
    odd = (me & 1) == 1
    first = pl.multiple_of(me * hw - (me & 1) * HD, 128)
    choose = lambda f: jnp.where(odd, f[:, HD : HD + hw], f[:, :hw])

    @pl.when(p == 0)
    def _():
        copies = [
            pltpu.make_async_copy(
                w_hbm.at[:, pl.ds(pl.multiple_of(t * width + first, 128), window)], wide.at[t], sem.at[t]
            )
            for t in range(3)
        ]
        for copy in copies:
            copy.start()
        for t, copy in enumerate(copies):
            copy.wait()
            w[:, t * hw : (t + 1) * hw] = choose(wide[t])

    heads = hw // HD
    x = jnp.concatenate([x0[0], x1[0], x2[0], x3[0]], 0)
    proj = dot(x, w[...])
    here = pl.ds(first, window)
    q = ((proj[:, :hw] + choose(qb[:, here].astype(F32))).astype(LOW).astype(F32) * HD ** (-0.5)).astype(LOW)
    k = proj[:, hw : 2 * hw].astype(LOW)
    v = (proj[:, 2 * hw :] + choose(vb[:, here].astype(F32))).astype(LOW)
    qkv_out[0] = jnp.concatenate([q, k, v], 1)
    usable = key_mask(me, lengths[p], rows, quarter)
    parts = []
    for h in range(heads):
        cols = slice(h * HD, (h + 1) * HD)
        logits = jnp.where(usable, dot_nt(k[:, cols], q[:, cols]), -1e9)
        highest = jnp.max(logits, 0, keepdims=True)
        weight = jnp.exp(logits - highest)
        total = jnp.sum(weight, 0, keepdims=True)
        lse_out[0, h : h + 1, :] = highest + jnp.log(total)
        parts.append(dot_tn(v[:, cols], weight.astype(LOW)) * (1.0 / total))
    context = jnp.concatenate(parts, 0).T.astype(LOW)
    for j in range(4):
        out = across_out if j > 1 else near_out
        out[j & 1, 0] = context[j * quarter : (j + 1) * quarter]


def attend(where, lengths, shards, w, qb, vb):
    passages, quarter, width = shards[0].shape
    rows = 4 * quarter
    hw = width // 4
    window = hw + HD
    heads = hw // HD
    block = vmem((1, quarter, width), lambda p: (p, 0, 0))
    whole = lambda *shape: vmem(shape, lambda p: (0,) * len(shape))
    return pl.pallas_call(
        attend_kernel,
        grid=(passages,),
        in_specs=[SMEM, SMEM] + [block] * 4 + [HBM, whole(1, width), whole(1, width)],
        out_specs=[
            vmem((1, rows, 3 * hw), lambda p: (p, 0, 0)),
            vmem((1, heads, rows), lambda p: (p, 0, 0)),
            whole(width, 3 * hw),
        ]
        + [vmem((2, 1, quarter, hw), lambda p: (0, p, 0, 0))] * 2,
        out_shape=[
            pltpu.HBM((passages, rows, 3 * hw), LOW),
            pltpu.HBM((passages, heads, rows), F32),
            pltpu.HBM((width, 3 * hw), LOW),
        ]
        + [jax.ShapeDtypeStruct((2, passages, quarter, hw), LOW)] * 2,
        scratch_shapes=[pltpu.VMEM((3, width, window), LOW), pltpu.SemaphoreType.DMA((3,))],
        compiler_params=pltpu.CompilerParams(vmem_limit_bytes=16 * MIB),
        cost_estimate=cost(5.5),
        name="attend",
    )(where, lengths, *map(far, shards), far(w), qb, vb)


def attend_back_kernel(
    place, lengths, x0, x1, x2, x3, w, qkv, lse, near, near_got, far_got, vectors, *refs
):
    keep_out, send_out, weight_send, weight_keep, acc, bias = refs[-6:]
    p = pl.program_id(0)
    me = place[1]
    quarter = x0.shape[1]
    rows = 4 * quarter
    hw = w.shape[1] // 3
    heads = hw // HD
    scale = HD ** (-0.5)
    x = jnp.concatenate([x0[0], x1[0], x2[0], x3[0]], 0)
    g = jnp.concatenate([near[0, 0], near_got[0, 0], far_got[0, 0], near_got[1, 0]], 0)
    usable = key_mask(me, lengths[p], rows, quarter)
    q = qkv[0, :, :hw]
    k = qkv[0, :, hw : 2 * hw]
    v = qkv[0, :, 2 * hw :]
    grad_q, grad_k, grad_v = [], [], []
    for h in range(heads):
        cols = slice(h * HD, (h + 1) * HD)
        qh, kh, vh, gh = q[:, cols], k[:, cols], v[:, cols], g[:, cols]
        logits = jnp.where(usable, dot_nt(kh, qh), -1e9)
        chance = jnp.exp(logits - lse[0, h : h + 1, :])
        grad_chance = dot_nt(vh, gh)
        inner = jnp.sum(grad_chance * chance, 0, keepdims=True)
        grad_logits = (chance * (grad_chance - inner)).astype(LOW)
        grad_q.append(dot_tn(kh, grad_logits) * scale)
        grad_k.append(dot(grad_logits, qh))
        grad_v.append(dot(chance.astype(LOW), gh))
    gq = jnp.concatenate(grad_q, 0).T.astype(LOW)
    gk = jnp.concatenate(grad_k, 1).astype(LOW)
    gv = jnp.concatenate(grad_v, 1).astype(LOW)
    joined = jnp.concatenate([gq, gk, gv], 1)
    part = dot_tn(x, joined)
    sums = [jnp.sum(f.astype(F32), 0, keepdims=True) for f in (gq, gv)]
    wide = 3 * hw

    @pl.when(p == 0)
    def _():
        acc[:, :wide] = part
        bias[...] = jnp.zeros_like(bias)

    @pl.when(p > 0)
    def _():
        acc[:, :wide] += part

    here = pl.ds(pl.multiple_of(me * 256, 128), hw)
    for i in range(2):
        bias[i : i + 1, here] += sums[i]

    back = dot_nt(joined, w[...]).astype(LOW)
    for j in range(4):
        out = send_out if j % 2 else keep_out
        out[j // 2, 0] = back[j * quarter : (j + 1) * quarter]

    @pl.when(p == pl.num_programs(0) - 1)
    def _():
        n = weight_send.shape[2] // 4
        rows_of = jnp.concatenate([bias[:, i * 256 : i * 256 + hw] for i in range(4)], 1)
        extra = jnp.concatenate([vectors[:10, :], rows_of[:2, :], jnp.zeros((52, vectors.shape[1]), F32)], 0)
        acc[:, wide:] = extra.T
        half = PIECES // 2
        spot = place[0] & half
        for out, first in ((weight_send, spot ^ half), (weight_keep, spot)):
            for j in range(4):
                for e in range(half):
                    start = pl.multiple_of((me ^ j) * (n * PIECES) + (first + e) * n, 8)
                    out[0, e, j * n : (j + 1) * n, :] = acc[pl.ds(start, n), :].astype(LOW)


def attend_back(place, lengths, shards, w, qkv, lse, grads, vectors, after=()):
    passages, quarter, width = shards[0].shape
    rows = 4 * quarter
    hw = w.shape[1] // 3
    heads = hw // HD
    n = width // (4 * PIECES)
    block = vmem((1, quarter, width), lambda p: (p, 0, 0))
    gblock = vmem((2, 1, quarter, hw), lambda p: (0, p, 0, 0))
    whole = lambda *shape: vmem(shape, lambda p: (0,) * len(shape))
    return pl.pallas_call(
        attend_back_kernel,
        grid=(passages,),
        in_specs=[SMEM, SMEM]
        + [block] * 4
        + [
            whole(width, 3 * hw),
            vmem((1, rows, 3 * hw), lambda p: (p, 0, 0)),
            vmem((1, heads, rows), lambda p: (p, 0, 0)),
        ]
        + [gblock] * 3
        + [whole(*vectors.shape)]
        + [ANYWHERE] * len(after),
        out_specs=[
            vmem((2, 1, quarter, width), lambda p: (0, p, 0, 0)),
            vmem((2, 1, quarter, width), lambda p: (0, p, 0, 0)),
            whole(1, PIECES // 2, 4 * n, 3 * hw + 64),
            whole(1, PIECES // 2, 4 * n, 3 * hw + 64),
        ],
        out_shape=[
            jax.ShapeDtypeStruct((2, passages, quarter, width), LOW),
            jax.ShapeDtypeStruct((2, passages, quarter, width), LOW),
            jax.ShapeDtypeStruct((1, PIECES // 2, 4 * n, 3 * hw + 64), LOW),
            jax.ShapeDtypeStruct((1, PIECES // 2, 4 * n, 3 * hw + 64), LOW),
        ],
        scratch_shapes=[pltpu.VMEM((width, 3 * hw + 64), F32), pltpu.VMEM((8, 1024), F32)],
        compiler_params=pltpu.CompilerParams(vmem_limit_bytes=24 * MIB),
        cost_estimate=cost(11),
        name="attend_back",
    )(place, lengths, *map(far, shards), far(w), far(qkv), far(lse), *grads, vectors, *after)


def normalise(field):
    centre = field - jnp.mean(field, -1, keepdims=True)
    scale = lax.rsqrt(jnp.mean(centre * centre, -1, keepdims=True) + EPS)
    return centre * scale, scale


def normalise_back(grad, normal, scale):
    return (
        grad
        - jnp.mean(grad, -1, keepdims=True)
        - normal * jnp.mean(grad * normal, -1, keepdims=True)
    ) * scale


def rows_kernel(
    where, x, near, near_got, far_got, cot, wa, vec, ib, wi_hbm, wo_hbm,
    layer_out, hidden_own, hidden_send, active_own, active_send, slope, outer_out, grad_out, normal_out, scale_out,
    sums_out, wi, wo, flipped, sem,
):
    me = where[0]
    width = x.shape[1]
    chunk = width
    hw = near.shape[2]

    def copies(c):
        cols = pl.ds(pl.multiple_of((me ^ c) * chunk, 128), chunk)
        return (
            pltpu.make_async_copy(wi_hbm.at[:, cols], wi.at[:, cols], sem.at[2 * c]),
            pltpu.make_async_copy(wo_hbm.at[cols, :], wo.at[cols, :], sem.at[2 * c + 1]),
        )

    for c in range(4):
        for copy in copies(c):
            copy.start()
    row = lambda r: vec[r : r + 1, :]
    attn_bias, attn_gain, attn_shift, outer_bias, ffn_gain, ffn_shift = (row(r) for r in range(6))
    attended = attn_bias + x[...].astype(F32)
    for j, part in enumerate((near[0], near_got[0], far_got[0], near_got[1])):
        attended += dot(part, wa[me ^ j])
    normal_one, scale_one = normalise(attended)
    normal_out[...] = normal_one
    scale_out[...] = scale_one
    hidden = normal_one * attn_gain + attn_shift
    hidden_low = hidden.astype(LOW)
    pre_two = hidden + outer_bias
    for c in range(4):
        cols = pl.ds(pl.multiple_of((me ^ c) * chunk, 128), chunk)
        first, second = copies(c)
        first.wait()
        u = dot(hidden_low, wi[:, cols]) + ib[:, cols]
        below = 0.5 * (1.0 + lax.erf(u * (0.5**0.5)))
        density = jnp.exp(-0.5 * u * u) * 0.3989422804014327
        active = (u * below).astype(LOW)
        slope[c] = below + u * density
        here = active_send if c & 1 else active_own
        here[:, (c >> 1) * chunk : ((c >> 1) + 1) * chunk] = active
        second.wait()
        pre_two += dot(active, wo[cols, :])
    flipped[...] = hidden.T
    for j in range(4):
        start = pl.multiple_of((me ^ j) * hw, 64)
        here = hidden_send if j & 1 else hidden_own
        here[j >> 1] = flipped[pl.ds(start, hw), :].astype(LOW)
    normal_two, scale_two = normalise(pre_two)
    layer_out[...] = (normal_two * ffn_gain + ffn_shift).astype(LOW)
    dy = cot[...].astype(F32)
    sums_out[...] = jnp.zeros_like(sums_out)
    sums_out[4:5, :] = jnp.sum(dy * normal_two, 0, keepdims=True)
    sums_out[5:6, :] = jnp.sum(dy, 0, keepdims=True)
    grad_two = normalise_back(dy * ffn_gain, normal_two, scale_two)
    grad_outer = grad_two.astype(LOW)
    outer_out[...] = grad_outer
    sums_out[3:4, :] = jnp.sum(grad_outer.astype(F32), 0, keepdims=True)
    grad_out[...] = grad_two


def rows_pass(where, x, near, near_got, far_got, cot, wa, vec, ib, wi, wo):
    rows, width = x.shape
    ff = ib.shape[1]
    hw = near.shape[2]
    low = lambda *s: jax.ShapeDtypeStruct(s, LOW)
    full = lambda *s: jax.ShapeDtypeStruct(s, F32)
    return pl.pallas_call(
        rows_kernel,
        in_specs=[SMEM] + [vmem()] * 8 + [HBM, HBM],
        out_specs=[vmem()] * 13,
        out_shape=[
            low(rows, width), low(2, hw, rows), low(2, hw, rows), low(rows, 2 * width), low(rows, 2 * width),
            full(4, rows, width), low(rows, width), full(rows, width), full(rows, width), full(rows, 1),
            full(8, width), low(width, ff), low(ff, width),
        ],
        scratch_shapes=[pltpu.VMEM((width, rows), F32), pltpu.SemaphoreType.DMA((8,))],
        compiler_params=pltpu.CompilerParams(vmem_limit_bytes=16 * MIB),
        cost_estimate=cost(7),
        name="rows_pass",
    )(where, x, near, near_got, far_got, cot, wa, vec, ib, far(wi), far(wo))


def rows_back_kernel(
    where, slope, outer, grad_two, normal, scale, sums, wa, gain, wi, wo,
    grad_one_out, inner_out, attn_out, near_out, across_out, sums_out,
):
    me = where[0]
    rows, width = outer.shape
    chunk = width
    hw = wa.shape[1]
    sums_out[...] = jnp.zeros_like(sums_out)
    sums_out[3:6, :] = sums[3:6, :]
    grad_outer = outer[...]
    grad_hidden = grad_two[...]
    for c in range(4):
        cols = slice(c * chunk, (c + 1) * chunk)
        grad_inner = (dot_nt(grad_outer, wo[cols, :]) * slope[me ^ c]).astype(LOW)
        inner_out[:, cols] = grad_inner
        column = jnp.sum(grad_inner.astype(F32), 0, keepdims=True)
        for i in range(4):
            sums_out[6 + i : 7 + i, c * hw : (c + 1) * hw] = column[:, i * hw : (i + 1) * hw]
        grad_hidden += dot_nt(grad_inner, wi[:, cols])
    normal_one = normal[...]
    sums_out[1:2, :] = jnp.sum(grad_hidden * normal_one, 0, keepdims=True)
    sums_out[2:3, :] = jnp.sum(grad_hidden, 0, keepdims=True)
    grad_one = normalise_back(grad_hidden * gain[1:2, :], normal_one, scale[...])
    grad_one_out[...] = grad_one
    grad_attn = grad_one.astype(LOW)
    attn_out[...] = grad_attn
    sums_out[0:1, :] = jnp.sum(grad_attn.astype(F32), 0, keepdims=True)
    for j in range(4):
        out = across_out if j > 1 else near_out
        out[j & 1] = dot_nt(grad_attn, wa[me ^ j]).astype(LOW)


def rows_back(where, slope, outer, grad_two, normal, scale, sums, wa, vec, wi, wo):
    rows, width = outer.shape
    ff = wi.shape[1]
    hw = wa.shape[1]
    low = lambda *s: jax.ShapeDtypeStruct(s, LOW)
    full = lambda *s: jax.ShapeDtypeStruct(s, F32)
    return pl.pallas_call(
        rows_back_kernel,
        in_specs=[SMEM] + [vmem()] * 10,
        out_specs=[vmem()] * 6,
        out_shape=[
            full(rows, width), low(rows, ff), low(rows, width), low(2, rows, hw), low(2, rows, hw), full(16, width),
        ],
        compiler_params=pltpu.CompilerParams(vmem_limit_bytes=12 * MIB),
        cost_estimate=cost(5),
        name="rows_back",
    )(where, slope, outer, grad_two, normal, scale, sums, wa, vec, wi, wo)


def outer_grad_kernel(active, active_got, grad, grad_got, send_out, keep_out):
    width = grad.shape[1]
    n = width // PIECES
    right = jnp.concatenate([grad[...], grad_got[...]], 0)
    for y, out in ((1, send_out), (0, keep_out)):
        cols = slice(y * width, (y + 1) * width)
        product = dot_tn(jnp.concatenate([active[:, cols], active_got[:, cols]], 0), right)
        for e in range(PIECES):
            out[0, e] = product[e * n : (e + 1) * n].astype(LOW)


def outer_grad(active, active_got, grad, grad_got):
    width = grad.shape[1]
    shape = (1, PIECES, width // PIECES, width)
    return pl.pallas_call(
        outer_grad_kernel,
        in_specs=[vmem()] * 4,
        out_specs=[vmem()] * 2,
        out_shape=[jax.ShapeDtypeStruct(shape, LOW)] * 2,
        compiler_params=pltpu.CompilerParams(vmem_limit_bytes=12 * MIB),
        cost_estimate=cost(3),
        name="outer_grad",
    )(active, active_got, grad, grad_got)


def inner_grad_kernel(
    place, hidden, hidden_got, inner, inner_got, near, far_got, context_got, attn, attn_got, send_out, keep_out, rest
):
    hw = hidden.shape[1]
    rows, width = attn.shape
    half = PIECES // 2
    n = hw // PIECES
    cols = inner.shape[1] // PIECES
    left = jnp.concatenate(
        [jnp.concatenate([hidden[y], hidden_got[y]], 1) for y in range(2)], 0
    )
    grads = jnp.concatenate([attn[...], attn_got[...]], 0)
    for y, mine in enumerate((near[0], far_got[0])):
        rest[y] = dot_tn(jnp.concatenate([mine, context_got[y]], 0), grads)
    me = place[0] & half
    for out, first in ((send_out, me ^ half), (keep_out, me)):
        for e in range(half):
            piece = first + e
            here = pl.ds(pl.multiple_of(piece * cols, 128), cols)
            product = dot(left, jnp.concatenate([inner[:, here], inner_got[:, here]], 0))
            for y in range(2):
                out[y, e, :hw, :] = product[y * hw : (y + 1) * hw].astype(LOW)
                more = rest[y, pl.ds(pl.multiple_of(piece * n, 8), n), :]
                more = jnp.concatenate([more[:, : width // 2], more[:, width // 2 :]], 0)
                out[y, e, hw:, :] = more.astype(LOW)


def inner_grad(place, hidden, hidden_got, inner, inner_got, near, far_got, context_got, attn, attn_got):
    hw = hidden.shape[1]
    width = attn.shape[1]
    shape = (2, PIECES // 2, hw + 2 * hw // PIECES, inner.shape[1] // PIECES)
    return pl.pallas_call(
        inner_grad_kernel,
        in_specs=[SMEM] + [vmem()] * 9,
        out_specs=[vmem()] * 2,
        out_shape=[jax.ShapeDtypeStruct(shape, LOW)] * 2,
        scratch_shapes=[pltpu.VMEM((2, hw, width), F32)],
        compiler_params=pltpu.CompilerParams(vmem_limit_bytes=12 * MIB),
        cost_estimate=cost(3),
        name="inner_grad",
    )(place, hidden, hidden_got, inner, inner_got, near, far_got, context_got, attn, attn_got)


ANYWHERE = pl.BlockSpec(memory_space=pl.ANY)


def sum_kernel(spec, place, *refs):
    leads, count, flip, inputs, splits = spec
    ins = refs[: len(inputs)]
    outs = refs[-splits:]
    first = (place[0] // count) * count
    if flip:
        first = first ^ count
    for y, lead in enumerate(leads):
        for r in range(count):
            total = None
            for ref in ins:
                pieces = ref.shape[1]
                base = first & (pieces - 1) if count < pieces else 0
                term = ref[lead if ref.shape[0] > 1 else 0, base + r].astype(F32)
                total = term if total is None else total + term
            if splits == 1:
                outs[0][y, r] = total.astype(LOW)
            else:
                n = total.shape[0] // splits
                for j in range(splits):
                    outs[j][...] = total[j * n : (j + 1) * n].astype(LOW)


def sum_pieces(place, inputs, leads, count, flip, after=(), splits=1, name="sum_pieces"):
    tall, wide = inputs[0].shape[2:]
    spec = (tuple(leads), count, flip, tuple(range(len(inputs))), splits)
    if splits == 1:
        out_shape = [jax.ShapeDtypeStruct((len(leads), count, tall, wide), LOW)]
    else:
        out_shape = [jax.ShapeDtypeStruct((tall // splits, wide), LOW)] * splits
    return pl.pallas_call(
        lambda *refs: sum_kernel(spec, *refs),
        in_specs=[SMEM] + [vmem()] * len(inputs) + [ANYWHERE] * len(after),
        out_specs=[vmem()] * splits,
        out_shape=out_shape,
        compiler_params=pltpu.CompilerParams(vmem_limit_bytes=4 * MIB),
        cost_estimate=cost(0.3 + 0.3 * len(leads) * count * len(inputs) / 4),
        name=name,
    )(place, *inputs, *after)


def outer_place_kernel(spots, place, own, got, *refs):
    out = refs[-1]
    n = own.shape[1]
    for i, spot in enumerate(spots):
        piece = own[i] if i < 4 else got[i - 4]
        out[pl.ds(pl.multiple_of((place[0] ^ spot) * n, 8), n), :] = piece.astype(F32)


def outer_place(spots, place, own, got, after=()):
    n, width = own.shape[1:]
    return pl.pallas_call(
        lambda *refs: outer_place_kernel(spots, *refs),
        in_specs=[SMEM, vmem(), vmem()] + [ANYWHERE] * len(after),
        out_specs=vmem(),
        out_shape=jax.ShapeDtypeStruct((PIECES * n, width), F32),
        compiler_params=pltpu.CompilerParams(vmem_limit_bytes=4 * MIB),
        cost_estimate=cost(2),
        name="outer_place",
    )(place, own, got, *after)


def inner_place_kernel(spots, place, own, got, *refs):
    inner, attn = refs[-2:]
    hw, cols = inner.shape[0], own.shape[2]
    n = attn.shape[0] // PIECES
    for i, spot in enumerate(spots):
        piece = (own[i] if i < 4 else got[i - 4]).astype(F32)
        here = place[0] ^ spot
        inner[:, pl.ds(pl.multiple_of(here * cols, 128), cols)] = piece[:hw]
        attn[pl.ds(pl.multiple_of(here * n, 8), n), :] = jnp.concatenate([piece[hw : hw + n], piece[hw + n :]], 1)


def inner_place(spots, place, own, got, hw, after=()):
    _, tall, cols = own.shape
    n = (tall - hw) // 2
    return pl.pallas_call(
        lambda *refs: inner_place_kernel(spots, *refs),
        in_specs=[SMEM, vmem(), vmem()] + [ANYWHERE] * len(after),
        out_specs=[vmem(), vmem()],
        out_shape=[
            jax.ShapeDtypeStruct((hw, PIECES * cols), F32),
            jax.ShapeDtypeStruct((PIECES * n, 2 * cols), F32),
        ],
        compiler_params=pltpu.CompilerParams(vmem_limit_bytes=4 * MIB),
        cost_estimate=cost(2),
        name="inner_place",
    )(place, own, got, *after)


def project_place_kernel(spots, place, own, got, *refs):
    out, vectors, tall = refs[-3:]
    n = own.shape[1] // 4
    hw = out.shape[1] // 12
    wide = 3 * hw
    for i, spot in enumerate(spots):
        ref, k = (own, i) if i < 4 else (got, i - 4)
        rows = pl.ds(pl.multiple_of((place[0] ^ spot) * n, 8), n)
        total = None
        for owner in range(4):
            start = pl.multiple_of((owner ^ place[1]) * n, 8)
            block = ref[k, pl.ds(start, n), :].astype(F32)
            for t in range(3):
                at = t * 4 * hw + owner * hw
                out[rows, at : at + hw] = block[:, t * hw : (t + 1) * hw]
            extra = block[:, wide:]
            total = extra if total is None else total + extra
        tall[rows, : total.shape[1]] = total
    vectors[...] = tall[...].T[: vectors.shape[0]]


def project_place(spots, place, own, got, hw, after=()):
    _, tall, wide = own.shape
    n = tall // 4
    return pl.pallas_call(
        lambda *refs: project_place_kernel(spots, *refs),
        in_specs=[SMEM, vmem(), vmem()] + [ANYWHERE] * len(after),
        out_specs=[vmem(), vmem()],
        out_shape=[
            jax.ShapeDtypeStruct((PIECES * n, 12 * hw), F32),
            jax.ShapeDtypeStruct((16, PIECES * n), F32),
        ],
        scratch_shapes=[pltpu.VMEM((PIECES * n, 128), F32)],
        compiler_params=pltpu.CompilerParams(vmem_limit_bytes=4 * MIB),
        cost_estimate=cost(2),
        name="project_place",
    )(place, own, got, *after)


def pair_kernel(near, far, *refs):
    out = refs[len(refs) // 2]
    out[0] = near[1]
    out[1] = far[1]


def pair(near, far, gated):
    return pl.pallas_call(
        pair_kernel,
        in_specs=[vmem(), vmem()] + [ANYWHERE] * len(gated),
        out_specs=[vmem()] + [ANYWHERE] * len(gated),
        out_shape=[jax.ShapeDtypeStruct(f.shape, f.dtype) for f in (near, *gated)],
        input_output_aliases={2 + i: 1 + i for i in range(len(gated))},
        compiler_params=pltpu.CompilerParams(vmem_limit_bytes=2 * MIB),
        cost_estimate=cost(0.5),
        name="pair",
    )(near, far, *gated)


def swap(field, axis, bit):
    count = lax.axis_size(axis)
    return lax.ppermute(field, axis, [(i, i ^ bit) for i in range(count)])


def add(left, right):
    return (left.astype(F32) + right.astype(F32)).astype(LOW)


class Reduction:
    def __init__(self, order, back, lane, me, rest):
        self.order = list(order)
        self.back = list(back)
        self.rest = rest
        bits = [o for o in order if o != "y"]
        weight = {bit: PIECES >> (k + 1) for k, bit in enumerate(bits)}
        spot = sum(jnp.where(lane & bit, w, 0) for bit, w in weight.items())
        self.spots = [sum(weight[bit] for t, bit in enumerate(back) if i >> t & 1) for i in range(PIECES)]
        self.place = jnp.stack([spot.astype(jnp.int32), me.astype(jnp.int32)])

    def begin(self, keep, send):
        axis = self.order.pop(0)
        got = swap(send, "seq", 2) if axis == "y" else swap(send, "dp", axis)
        self.arrays = [keep, got]
        self.left = keep.shape[1]
        self.folded = keep.shape[0] == 1

    def step(self, after=(), splits=1, name="sum"):
        leads = [0] if self.folded else [0, 1]
        if not self.order:
            return sum_pieces(self.place, self.arrays, [0], 1, False, after, splits, name)
        axis = self.order.pop(0)
        if axis == "y":
            (sent,) = sum_pieces(self.place, self.arrays, [1], self.left, False, after, name=name)
            self.folded = True
            got = swap(sent, "seq", 2)
        else:
            self.left //= 2
            (sent,) = sum_pieces(self.place, self.arrays, leads, self.left, True, after, name=name)
            got = swap(sent, "dp", axis)
        self.arrays = self.arrays + [got]
        return sent


def local(
    tokens, lengths, query_key_value, query_bias, value_bias, attn_weight, attn_bias, attn_gain,
    attn_shift, inner_weight, inner_bias, outer_weight, outer_bias, ffn_gain, ffn_shift, cotangent,
):
    groups = lax.axis_size("seq")
    lanes = lax.axis_size("dp")
    me = lax.axis_index("seq")
    lane = lax.axis_index("dp")
    passages, quarter, width = tokens.shape
    hw = H // groups * HD
    rows = passages * quarter
    ff = inner_bias.shape[0]
    rest = [1 << i for i in range(3, lanes.bit_length() - 1)]
    where = me.astype(jnp.int32).reshape(1)

    across = swap(tokens, "seq", 2)
    beside = swap(tokens, "seq", 1)
    corner = swap(across, "seq", 1)
    shards = (tokens, beside, across, corner)
    vec = jnp.stack([attn_bias, attn_gain, attn_shift, outer_bias, ffn_gain, ffn_shift, ffn_shift, ffn_shift])
    vec = vec.astype(F32)
    ib = inner_bias.astype(F32).reshape(1, ff)

    biases = (query_bias.reshape(1, width), value_bias.reshape(1, width))
    qkv, lse, w, near, across_heads = attend(where, lengths, shards, query_key_value, *biases)
    far_got = swap(across_heads, "seq", 2)
    (near_send,) = pair(near, far_got, [])
    near_got = swap(near_send, "seq", 1)
    context_got = swap(near_got, "seq", 1)
    flat = lambda f: f.reshape(2, rows, hw)
    context = [flat(f) for f in (near, near_got, far_got)]

    wa = attn_weight.reshape(groups, hw, width)
    (
        layer_out, hidden_own, hidden_send, active_own, active_send, slope, grad_outer, grad_two, normal, scale,
        row_sums, wi, wo,
    ) = rows_pass(
        where, tokens.reshape(rows, width), *context, cotangent.reshape(rows, width), wa, vec, ib, inner_weight,
        outer_weight,
    )
    active_got = swap(active_send, "seq", 1)
    outer_got = swap(grad_outer, "seq", 1)
    hidden_got = swap(hidden_send, "seq", 1)
    grad_one, grad_inner, grad_attn, near, across_heads, vectors = rows_back(
        where, slope, grad_outer, grad_two, normal, scale, row_sums, wa, vec, wi, wo
    )
    a = Reduction(["y", 1, 2, 4], [4, 2, 1], lane, me, rest)
    b = Reduction([2, "y", 1, 4], [4, 1, 2], lane, me, rest)
    d = Reduction([1, 2, 4], [4, 2, 1], lane, me, rest)
    far_got = swap(across_heads, "seq", 2)
    inner_got = swap(grad_inner, "seq", 1)
    attn_got = swap(grad_attn, "seq", 1)
    outer_send, outer_keep = outer_grad(active_own, active_got, grad_outer, outer_got)
    near_send, outer_send = pair(near, far_got, [outer_send])
    near_got = swap(near_send, "seq", 1)
    a.begin(outer_keep, outer_send)
    inner_send, inner_keep = inner_grad(
        b.place, hidden_own, hidden_got, grad_inner, inner_got, context[0], context[2], flat(context_got),
        grad_attn, attn_got,
    )
    b.begin(inner_keep, inner_send)
    grads_h = [f.reshape(2, passages, quarter, hw) for f in (near, near_got, far_got)]
    back_keep, back_send, project_send, project_keep = attend_back(
        d.place, lengths, shards, w, qkv, lse, grads_h, vectors, [inner_send]
    )
    d.begin(project_keep, project_send)
    back_got = swap(back_send, "seq", 1)
    (back_sum,) = sum_pieces(
        d.place,
        [f.reshape(2, 1, rows, width) for f in (back_keep, back_got)],
        [1], 1, False, name="back_y",
    )
    back_over = swap(back_sum, "seq", 2)
    t = a.step([back_sum], name="outer_x")
    t = d.step([t], name="project_z")
    t = b.step([t], name="inner_y")
    t = a.step([t], name="outer_z")
    t = d.step([t], name="project_zz")
    t = b.step([t], name="inner_x")
    t = a.step([t], name="outer_zz")
    project = d.step([t], splits=4, name="project_sum")
    t = b.step([project[0]], name="inner_zz")
    (outer_total,) = a.step([t], name="outer_sum")

    def finish(total):
        for bit in rest:
            total = add(total, swap(total, "dp", bit))
        return total

    def spread(piece, back):
        for bit in back[:-1]:
            piece = jnp.concatenate([piece, swap(piece, "dp", bit)], 0)
        return piece, swap(piece, "dp", back[-1])

    outer_total = spread(finish(outer_total)[0], a.back)
    project = [finish(p) for p in project]
    project = [project[0]] + [swap(project[j], "seq", j) for j in (1, 2, 3)]
    project_total = spread(jnp.concatenate(project, 0)[None], d.back)
    (inner_total,) = b.step(name="inner_sum")
    inner_total = spread(finish(inner_total)[0], b.back)

    grad_query_key_value, summed = project_place(d.spots, d.place, *project_total, hw)
    grad_outer_weight = outer_place(a.spots, a.place, *outer_total)
    grad_inner_weight, grad_attn_weight = inner_place(b.spots, b.place, *inner_total, hw)
    input_grad = (
        grad_one + back_keep[0].reshape(rows, width).astype(F32)
        + back_got[0].reshape(rows, width).astype(F32)
        + back_over[0, 0].astype(F32)
    ).astype(LOW)
    return (
        layer_out.reshape(passages, quarter, width),
        input_grad.reshape(passages, quarter, width),
        grad_query_key_value,
        summed[10],
        summed[11],
        grad_attn_weight,
        summed[0],
        summed[1],
        summed[2],
        grad_inner_weight,
        summed[6:10].reshape(-1),
        grad_outer_weight,
        summed[3],
        summed[4],
        summed[5],
    )


def solution(mesh):
    rows = P("dp", "seq", None)
    return jax.shard_map(
        local,
        mesh=mesh,
        in_specs=(rows, P("dp")) + (P(),) * 13 + (rows,),
        out_specs=(
            rows,
            rows,
            P("seq", None),
            P("seq"),
            P("seq"),
            P("seq", None),
            P("seq"),
            P("seq"),
            P("seq"),
            P("seq", None),
            P("seq"),
            P("seq", None),
            P("seq"),
            P("seq"),
            P("seq"),
        ),
        check_vma=False,
    )
```

time: 325 us -> 213 us (0.66)
  blocking collectives: 81.2 us -> 0 us
  other arithmetic: 29.8 us -> 1.46 us
  local copies, waits for them, and re-layouts: 21.8 us -> 11.6 us
  starting transfers between devices: 23.5 us -> 31 us
  waiting for transfers between devices: 104 us -> 111 us
  Pallas kernels: 62.1 us -> 55.8 us
    psum x2 -> x0, blocking collectives: 81.2 us -> none  [the longest x1 60.1 us: local(): lax.psum(jnp.concatenate([sums[:6].reshape(-1), inner_sums.reshape(-1)]),...]
    convert_element_type x16 -> x2, other arithmetic: 20.2 us -> 0.97 us  [the longest x1 0.97 us: local(): input_grad = (grad_one + back_keep[0].reshape(rows, width).astype(F32) +...]
    pallas_call x6 -> x21, Pallas kernels: 45.6 us -> 35.4 us  [the longest x1 8.44 us: rows_pass(): pl.pallas_call(rows_kernel, in_specs=[SMEM] + [vmem()] * 8 + [HBM, HBM],...]
    unnamed x88 -> x64, local copies, waits for them, and re-layouts: 17.8 us -> 8.78 us
    ppermute x36 -> x38, waiting for transfers between devices: 104 us -> 111 us  [swap(): return lax.ppermute(field, axis, [(i, i ^ bit) for i in range(count)])]
    concatenate x9 -> x6, other arithmetic: 7.82 us -> 0.32 us  [spread(): piece = jnp.concatenate([piece, swap(piece, 'dp', bit)], 0)]
    ppermute x36 -> x38, starting transfers between devices: 23.5 us -> 31 us  [swap(): return lax.ppermute(field, axis, [(i, i ^ bit) for i in range(count)])]
    dynamic_slice x4 -> x0, local copies, waits for them, and re-layouts: 3.35 us -> none  [the longest x1 1.97 us: local(): lax.dynamic_slice_in_dim(f, start + me * hw, hw, f.ndim - 1)]
  transfers between devices with their start and end apart: 36 -> 38, of which waited for: 18 -> 24; matrix products, arithmetic and copies ran while one was open for 10% -> 2% of each run, Pallas kernels for 8% -> 14%
where the time goes in v2:
time: 213 us
  waiting for transfers between devices  111 us (52%)
  Pallas kernels  55.8 us (26%)
  starting transfers between devices  31 us (15%)
  local copies, waits for them, and re-layouts  11.6 us (5%)
    ppermute x38, waiting for transfers between devices, swap(): return lax.ppermute(field, axis, [(i, i ^ bit) for i in range(count)])  111 us
    ppermute x38, starting transfers between devices, swap(): return lax.ppermute(field, axis, [(i, i ^ bit) for i in range(count)])  31 us
    pallas_call x1, Pallas kernels, attend_back(): pl.pallas_call(attend_back_kernel, grid=(passages,), in_specs=[SMEM, SMEM...  12.3 us
    unnamed x64, local copies, waits for them, and re-layouts  8.78 us
    pallas_call x1, Pallas kernels, rows_pass(): pl.pallas_call(rows_kernel, in_specs=[SMEM] + [vmem()] * 8 + [HBM, HBM],...  8.44 us
    pallas_call x1, Pallas kernels, attend(): pl.pallas_call(attend_kernel, grid=(passages,), in_specs=[SMEM, SMEM] + [...  8.08 us
    pallas_call x12, Pallas kernels, sum_pieces(): pl.pallas_call(lambda *refs: sum_kernel(spec, *refs), in_specs=[SMEM] + [...  7.85 us
    pallas_call x1, Pallas kernels, rows_back(): pl.pallas_call(rows_back_kernel, in_specs=[SMEM] + [vmem()] * 10, out_spe...  5.72 us
  transfers between devices with their start and end apart: 38, of which 24 were waited for; matrix products, arithmetic and copies ran while one was open for 2% of the time, Pallas kernels for 14%

profile of v2, /device:TPU:0, one launch (start us, length us, event | category | flops | bytes accessed | tf_op | source)
XLA Modules:
  0.0 212.5 jit_solution(9981519842691837476)
XLA Ops:
  0.6 3.0 %collective-permute-start.1 = (bf16[2,128,768]{2,1,0:T(8,128)(2,1)}, bf16[2,128,768]{2,1,0:T(8,128)(2,1)S(1)}, u32[]{:S(2)}, u32[]{:S(2)}) collective-permute-start(bf16[2,128,768]{2,1,0:T(8,128)(2,1)} %x0.3), channel_id=1, source_target_pairs={{0,2},{1,3},{2,0},{3,1},{4,6},{5,7},{6,4},{7,5},{8,10},{9,11},{10,... | collective-permute-start | bytes 1179656 | tf_op jit(solution)/shard_map/ppermute | solution.py:616
  3.7 9.3 %collective-permute-done.1.x2 = bf16[2,128,768]{2,1,0:T(8,128)(2,1)S(1)} collective-permute-done((bf16[2,128,768]{2,1,0:T(8,128)(2,1)}, bf16[2,128,768]{2,1,0:T(8,128)(2,1)S(1)}, u32[]{:S(2)}, u32[]{:S(2)}) %collective-permute-start.1) | collective-permute-done | bytes 393248 | tf_op jit(solution)/shard_map/ppermute | solution.py:616
  16.2 8.1 %attend.1 = (bf16[2,512,576]{2,1,0:T(8,128)(2,1)}, f32[2,3,512]{2,1,0:T(4,128)}, bf16[768,576]{1,0:T(8,128)(2,1)}, bf16[2,2,128,192]{3,2,1,0:T(8,128)(2,1)S(1)}, bf16[2,2,128,192]{3,2,1,0:T(8,128)(2,1)S(1)}) custom-call(s32[1]{0:T(128)} %bitcast.where, s32[2]{0:T(128)S(1)} %copy-done.11, bf16[2,128,768]{2,1,0:T(8,128)(2,1)} %x0.3, ...), custom_call_target="tpu_custom_call" | custom-call | flops 6325000192 | bytes 20295000 | tf_op jit(solution)/shard_map/attend/pallas_call | solution.py:111
  24.4 1.8 collective-permute-start.3
  26.2 6.8 %collective-permute-done.3.far = bf16[2,2,128,192]{3,2,1,0:T(8,128)(2,1)S(1)} collective-permute-done((bf16[2,2,128,192]{3,2,1,0:T(8,128)(2,1)S(1)}, bf16[2,2,128,192]{3,2,1,0:T(8,128)(2,1)S(1)}, u32[]{:S(2)}, u32[]{:S(2)}) %collective-permute-start.3) | collective-permute-done | bytes 196640 | tf_op jit(solution)/shard_map/ppermute | solution.py:616
  33.3 1.3 collective-permute-done.4
  35.5 8.4 %rows_pass.1 = (bf16[256,768]{1,0:T(8,128)(2,1)}, bf16[2,192,256]{2,1,0:T(8,128)(2,1)S(1)}, bf16[2,192,256]{2,1,0:T(8,128)(2,1)S(1)}, bf16[256,1536]{1,0:T(8,128...) custom-call(s32[1]{0:T(128)} %bitcast.where, ...), custom_call_target="tpu_custom_call" | custom-call | flops 8049999872 | bytes 25830000 | tf_op jit(solution)/shard_map/rows_pass/pallas_call | solution.py:327
  44.0 5.7 %rows_back.1 = (f32[256,768]{1,0:T(8,128)S(1)}, bf16[256,3072]{1,0:T(8,128)(2,1)}, bf16[256,768]{1,0:T(8,128)(2,1)S(1)}, bf16[2,256,192]{2,1,0:T(8,128)(2,1)S(1)...) custom-call(s32[1]{0:T(128)} %bitcast.where, f32[4,256,768]{2,1,0:T(8,128)S(1)} %get-tuple-element.60.slope, ...), custom_call_target="tpu_custom_call" | custom-call | flops 5750000128 | bytes 18450000 | tf_op jit(solution)/shard_map/rows_back/pallas_call | solution.py:382
  52.5 4.3 %collective-permute-done.7.grad_got = bf16[256,768]{1,0:T(8,128)(2,1)S(1)} collective-permute-done((bf16[256,768]{1,0:T(8,128)(2,1)}, bf16[256,768]{1,0:T(8,128)(2,1)S(1)}, u32[]{:S(2)}, u32[]{:S(2)}) %collective-permute-start.7) | collective-permute-done | bytes 393248 | tf_op jit(solution)/shard_map/ppermute | solution.py:616
  57.5 1.9 collective-permute-start.5
  60.3 1.1 copy-done.2
  61.5 1.0 copy-done.6
  62.5 1.1 copy-done.19
  63.6 2.4 %outer_grad.1 = (bf16[1,8,96,768]{3,2,1,0:T(8,128)(2,1)S(1)}, bf16[1,8,96,768]{3,2,1,0:T(8,128)(2,1)S(1)}) custom-call(bf16[256,1536]{1,0:T(8,128)(2,1)S(1)} %copy-done.19, bf16[256,1536]{1,0:T(8,128)(2,1)S(1)} %copy-done.2, bf16[256,768]{1,0:T(8,128)(2,1)} %get-tuple-element.61.outer.grad, bf16[256,768]{1,0:T(8,128)(2,1)S(1)} %copy-done.6), custom_call_target="tpu_custom_call" | custom-call | flops 3449999872 | bytes 11070000 | tf_op jit(solution)/shard_map/outer_grad/pallas_call | solution.py:409
  66.7 1.5 collective-permute-start.16
  68.2 4.4 %inner_grad.1 = (bf16[2,4,240,384]{3,2,1,0:T(8,128)(2,1)S(1)}, bf16[2,4,240,384]{3,2,1,0:T(8,128)(2,1)S(1)}) custom-call(s32[2]{0:T(128)S(1)} %pad_add_fusion.1.place.refs_0_, bf16[2,192,256]{2,1,0:T(8,128)(2,1)S(1)} %copy-done.21, bf16[2,192,256]{2,1,0:T(8,128)(2,1)S(1)} %collective-permute-done.9.hidden_got, bf16[256,3072]{1,0:T(8,128)(2,1)} %get-tuple-element.81.inner, ...), custom_call_target="tpu_custom_call" | custom-call | flops 3449999872 | bytes 11070000 | tf_op jit(solution)/shard_map/inner_grad/pallas_call | solution.py:451
  72.6 1.6 collective-permute-start.19
  74.2 12.3 %attend_back.1 = (bf16[2,2,128,768]{3,2,1,0:T(8,128)(2,1)S(1)}, bf16[2,2,128,768]{3,2,1,0:T(8,128)(2,1)S(1)}, bf16[1,4,96,640]{3,2,1,0:T(8,128)(2,1)S(1)}, bf16[1,4,96,640]{3,2,1,0:T(8,128)(2,1)S(1)}) custom-call(s32[2]{0:T(128)S(1)} %pad_add_fusion.place.refs_0_, s32[2]{0:T(128)S(1)} %copy-done.12, bf16[2,128,768]{2,1,0:T(8,128)(2,1)} %x0.3, ...), custom_call_target="tpu_custom_call" | custom-call | flops 12650000384 | bytes 40590000 | tf_op jit(solution)/shard_map/attend_back/pallas_call | solution.py:213
  86.7 1.7 collective-permute-start.15
  89.6 5.2 %collective-permute-done.16.refs_2_ = bf16[1,8,96,768]{3,2,1,0:T(8,128)(2,1)S(1)} collective-permute-done((bf16[1,8,96,768]{3,2,1,0:T(8,128)(2,1)S(1)}, bf16[1,8,96,768]{3,2,1,0:T(8,128)(2,1)S(1)}, u32[]{:S(2)}, u32[]{:S(2)}) %collective-permute-start.16) | collective-permute-done | bytes 1179680 | tf_op jit(solution)/shard_map/ppermute | solution.py:616
  95.4 4.9 %collective-permute-done.15.refs_2_ = bf16[1,4,96,640]{3,2,1,0:T(8,128)(2,1)S(1)} collective-permute-done((bf16[1,4,96,640]{3,2,1,0:T(8,128)(2,1)S(1)}, bf16[1,4,96,640]{3,2,1,0:T(8,128)(2,1)S(1)}, u32[]{:S(2)}, u32[]{:S(2)}) %collective-permute-start.15) | collective-permute-done | bytes 491552 | tf_op jit(solution)/shard_map/ppermute | solution.py:616
  100.9 6.2 %collective-permute-done.19.refs_2_ = bf16[2,4,240,384]{3,2,1,0:T(8,128)(2,1)S(1)} collective-permute-done((bf16[2,4,240,384]{3,2,1,0:T(8,128)(2,1)S(1)}, bf16[2,4,240,384]{3,2,1,0:T(8,128)(2,1)S(1)}, u32[]{:S(2)}, u32[]{:S(2)}) %collective-permute-start.19) | collective-permute-done | bytes 1474592 | tf_op jit(solution)/shard_map/ppermute | solution.py:616
  108.1 1.7 collective-permute-start.18
  109.8 1.5 collective-permute-start.17
  111.3 11.2 %collective-permute-done.18.refs_3_ = bf16[1,4,96,768]{3,2,1,0:T(8,128)(2,1)S(1)} collective-permute-done((bf16[1,4,96,768]{3,2,1,0:T(8,128)(2,1)S(1)}, bf16[1,4,96,768]{3,2,1,0:T(8,128)(2,1)S(1)}, u32[]{:S(2)}, u32[]{:S(2)}) %collective-permute-start.18) | collective-permute-done | bytes 589856 | tf_op jit(solution)/shard_map/ppermute | solution.py:616
  123.2 1.6 collective-permute-start.21
  126.3 1.6 collective-permute-start.29
  127.9 2.6 %collective-permute-start.20 = (bf16[1,1,96,640]{3,2,1,0:T(8,128)(2,1)S(1)}, bf16[1,1,96,640]{3,2,1,0:T(8,128)(2,1)S(1)}, u32[]{:S(2)}, u32[]{:S(2)}) collective-permute-start(bf16[1,1,96,640]{3,2,1,0:T(8,128)(2,1)S(1)} %project_zz.1.refs_4_), channel_id=1, source_target_pairs={{0,16},{4,20},{8,24},{12,28},{16,0},{20,4},{24,8},{28,12},{1,17},{... | collective-permute-start | bytes 368648 | tf_op jit(solution)/shard_map/ppermute | solution.py:616
  130.5 1.3 collective-permute-done.21.refs_4_
  132.4 2.7 %collective-permute-start.34 = (bf16[1,1,96,768]{3,2,1,0:T(8,128)(2,1)S(1)}, bf16[1,1,96,768]{3,2,1,0:T(8,128)(2,1)S(1)}, u32[]{:S(2)}, u32[]{:S(2)}) collective-permute-start(bf16[1,1,96,768]{3,2,1,0:T(8,128)(2,1)S(1)} %outer_zz.1.refs_5_), channel_id=1, source_target_pairs={{0,16},{4,20},{8,24},{12,28},{16,0},{20,4},{24,8},{28,12},{1,17},{... | collective-permute-start | bytes 442376 | tf_op jit(solution)/shard_map/ppermute | solution.py:616
  135.1 4.7 %collective-permute-done.20.refs_4_ = bf16[1,1,96,640]{3,2,1,0:T(8,128)(2,1)S(1)} collective-permute-done((bf16[1,1,96,640]{3,2,1,0:T(8,128)(2,1)S(1)}, bf16[1,1,96,640]{3,2,1,0:T(8,128)(2,1)S(1)}, u32[]{:S(2)}, u32[]{:S(2)}) %collective-permute-start.20) | collective-permute-done | bytes 122912 | tf_op jit(solution)/shard_map/ppermute | solution.py:616
  140.6 1.8 collective-permute-start.25
  143.1 1.5 collective-permute-done.24
  144.6 1.5 collective-permute-start.26
  146.8 1.6 collective-permute-start.35
  148.3 12.2 %collective-permute-done.30.refs_5_ = bf16[1,1,240,384]{3,2,1,0:T(8,128)(2,1)S(1)} collective-permute-done((bf16[1,1,240,384]{3,2,1,0:T(8,128)(2,1)S(1)}, bf16[1,1,240,384]{3,2,1,0:T(8,128)(2,1)S(1)}, u32[]{:S(2)}, u32[]{:S(2)}) %collective-permute-start.30) | collective-permute-done | bytes 184352 | tf_op jit(solution)/shard_map/ppermute | solution.py:616
  161.3 1.9 collective-permute-done.26
  163.3 7.1 %collective-permute-done.35 = bf16[1,96,768]{2,1,0:T(8,128)(2,1)S(1)} collective-permute-done((bf16[1,96,768]{2,1,0:T(8,128)(2,1)S(1)}, bf16[1,96,768]{2,1,0:T(8,128)(2,1)S(1)}, u32[]{:S(2)}, u32[]{:S(2)}) %collective-permute-start.35) | collective-permute-done | bytes 147488 | tf_op jit(solution)/shard_map/ppermute | solution.py:616
  170.5 3.8 %collective-permute-done.31 = bf16[1,240,384]{2,1,0:T(8,128)(2,1)S(1)} collective-permute-done((bf16[1,240,384]{2,1,0:T(8,128)(2,1)S(1)}, bf16[1,240,384]{2,1,0:T(8,128)(2,1)S(1)}, u32[]{:S(2)}, u32[]{:S(2)}) %collective-permute-start.31) | collective-permute-done | bytes 184352 | tf_op jit(solution)/shard_map/ppermute | solution.py:616
  174.8 4.0 %collective-permute-done.27 = bf16[2,96,640]{2,1,0:T(8,128)(2,1)S(1)} collective-permute-done((bf16[2,96,640]{2,1,0:T(8,128)(2,1)S(1)}, bf16[2,96,640]{2,1,0:T(8,128)(2,1)S(1)}, u32[]{:S(2)}, u32[]{:S(2)}) %collective-permute-start.27) | collective-permute-done | bytes 245792 | tf_op jit(solution)/shard_map/ppermute | solution.py:616
  179.0 5.2 %collective-permute-done.36 = bf16[2,96,768]{2,1,0:T(8,128)(2,1)S(1)} collective-permute-done((bf16[2,96,768]{2,1,0:T(8,128)(2,1)S(1)}, bf16[2,96,768]{2,1,0:T(8,128)(2,1)S(1)}, u32[]{:S(2)}, u32[]{:S(2)}) %collective-permute-start.36) | collective-permute-done | bytes 294944 | tf_op jit(solution)/shard_map/ppermute | solution.py:616
  184.3 1.6 collective-permute-done.32
  186.1 1.0 fusion
  187.0 9.4 %collective-permute-done.28.refs_2_ = bf16[4,96,640]{2,1,0:T(8,128)(2,1)S(1)} collective-permute-done((bf16[4,96,640]{2,1,0:T(8,128)(2,1)S(1)}, bf16[4,96,640]{2,1,0:T(8,128)(2,1)S(1)}, u32[]{:S(2)}, u32[]{:S(2)}) %collective-permute-start.28) | collective-permute-done | bytes 491552 | tf_op jit(solution)/shard_map/ppermute | solution.py:616
  196.4 2.0 project_place.1
  199.7 8.4 %collective-permute-done.37.refs_2_ = bf16[4,96,768]{2,1,0:T(8,128)(2,1)S(1)} collective-permute-done((bf16[4,96,768]{2,1,0:T(8,128)(2,1)S(1)}, bf16[4,96,768]{2,1,0:T(8,128)(2,1)S(1)}, u32[]{:S(2)}, u32[]{:S(2)}) %collective-permute-start.37) | collective-permute-done | bytes 589856 | tf_op jit(solution)/shard_map/ppermute | solution.py:616
  208.1 2.1 outer_place.1
  210.2 2.3 %inner_place.1 = (f32[192,3072]{1,0:T(8,128)}, f32[192,768]{1,0:T(8,128)}) custom-call(s32[2]{0:T(128)S(1)} %pad_add_fusion.1.place.refs_0_, bf16[4,240,384]{2,1,0:T(8,128)(2,1)S(1)} %pad_maximum_fusion.refs_1_, bf16[4,240,384]{2,1,0:T(8,128)(2,1)S(1)} %collective-permute-done.33.refs_2_), custom_call_target="tpu_custom_call" | custom-call | flops 2300000000 | bytes 7380000 | tf_op jit(solution)/shard_map/inner_place/pallas_call | solution.py:542
  (141 shorter events, 21.1 us)
Async XLA Ops:
  0.6 12.4 %collective-permute-start.1 = (bf16[2,128,768]{2,1,0:T(8,128)(2,1)}, bf16[2,128,768]{2,1,0:T(8,128)(2,1)S(1)}, u32[]{:S(2)}, u32[]{:S(2)}) collective-permute-start(bf16[2,128,768]{2,1,0:T(8,128)(2,1)} %x0.3), channel_id=1, source_target_pairs={{0,2},{1,3},{2,0},{3,1},{4,6},{5,7},{6,4},{7,5},{8,10},{9,11},{10,... | collective-permute-start | bytes 1179656 | tf_op jit(solution)/shard_map/ppermute | solution.py:616
  3.7 10.7 %collective-permute-start = (bf16[2,128,768]{2,1,0:T(8,128)(2,1)}, bf16[2,128,768]{2,1,0:T(8,128)(2,1)S(1)}, u32[]{:S(2)}, u32[]{:S(2)}) collective-permute-start(bf16[2,128,768]{2,1,0:T(8,128)(2,1)} %x0.3), channel_id=1, source_target_pairs={{0,1},{1,0},{2,3},{3,2},{4,5},{5,4},{6,7},{7,6},{8,9},{9,8},{10,11... | collective-permute-start | bytes 1179656 | tf_op jit(solution)/shard_map/ppermute | solution.py:616
  13.0 1.7 collective-permute-start.2
  24.2 10.3 %copy-start.13 = (bf16[2,2,128,192]{3,2,1,0:T(8,128)(2,1)}, bf16[2,2,128,192]{3,2,1,0:T(8,128)(2,1)S(1)}, u32[]{:S(2)}) copy-start(bf16[2,2,128,192]{3,2,1,0:T(8,128)(2,1)S(1)} %get-tuple-element.57.near) | copy-start | bytes 589828
  24.3 8.8 %copy-start.25 = (bf16[768]{0:T(1024)(128)(2,1)S(1)}, bf16[768]{0:T(1024)(128)(2,1)}, u32[]{:S(2)}) copy-start(bf16[768]{0:T(1024)(128)(2,1)} %param.24) | copy-start | bytes 4612
  24.3 8.8 %copy-start.26 = (bf16[768]{0:T(1024)(128)(2,1)S(1)}, bf16[768]{0:T(1024)(128)(2,1)}, u32[]{:S(2)}) copy-start(bf16[768]{0:T(1024)(128)(2,1)} %param.28) | copy-start | bytes 4612
  24.3 8.8 %copy-start.27 = (bf16[768]{0:T(1024)(128)(2,1)S(1)}, bf16[768]{0:T(1024)(128)(2,1)}, u32[]{:S(2)}) copy-start(bf16[768]{0:T(1024)(128)(2,1)} %param.29) | copy-start | bytes 4612
  24.3 8.8 %copy-start.28 = (bf16[768]{0:T(1024)(128)(2,1)S(1)}, bf16[768]{0:T(1024)(128)(2,1)}, u32[]{:S(2)}) copy-start(bf16[768]{0:T(1024)(128)(2,1)} %param.30) | copy-start | bytes 4612
  24.3 8.9 %copy-start.22 = (bf16[3072]{0:T(1024)(128)(2,1)S(1)}, bf16[3072]{0:T(1024)(128)(2,1)}, u32[]{:S(2)}) copy-start(bf16[3072]{0:T(1024)(128)(2,1)} %param.26) | copy-start | bytes 18436
  24.3 10.2 %copy-start = (bf16[768,768]{1,0:T(8,128)(2,1)S(1)}, bf16[768,768]{1,0:T(8,128)(2,1)}, u32[]{:S(2)}) copy-start(bf16[768,768]{1,0:T(8,128)(2,1)} %param.21) | copy-start | bytes 3538948
  24.3 10.2 %copy-start.3 = (bf16[2,128,768]{2,1,0:T(8,128)(2,1)S(1)}, bf16[2,128,768]{2,1,0:T(8,128)(2,1)}, u32[]{:S(2)}) copy-start(bf16[2,128,768]{2,1,0:T(8,128)(2,1)} %param.31) | copy-start | bytes 1179652
  24.4 10.2 %copy-start.4 = (bf16[2,128,768]{2,1,0:T(8,128)(2,1)S(1)}, bf16[2,128,768]{2,1,0:T(8,128)(2,1)}, u32[]{:S(2)}) copy-start(bf16[2,128,768]{2,1,0:T(8,128)(2,1)} %x0.3) | copy-start | bytes 1179652
  24.4 8.6 %collective-permute-start.3 = (bf16[2,2,128,192]{3,2,1,0:T(8,128)(2,1)S(1)}, bf16[2,2,128,192]{3,2,1,0:T(8,128)(2,1)S(1)}, u32[]{:S(2)}, u32[]{:S(2)}) collective-permute-start(bf16[2,2,128,192]{3,2,1,0:T(8,128)(2,1)S(1)} %get-tuple-element.58), channel_id=1, source_target_pairs={{0,2},{1,3},{2,0},{3,1},{4,6},{5,7},{6,4},{7,5},{8,10},{9,11},{10,... | collective-permute-start | bytes 589832 | tf_op jit(solution)/shard_map/ppermute | solution.py:616
  32.9 11.1 %copy-start.7 = (bf16[2,2,128,192]{3,2,1,0:T(8,128)(2,1)}, bf16[2,2,128,192]{3,2,1,0:T(8,128)(2,1)S(1)}, u32[]{:S(2)}) copy-start(bf16[2,2,128,192]{3,2,1,0:T(8,128)(2,1)S(1)} %collective-permute-done.3.far) | copy-start | bytes 589828
  33.0 1.6 collective-permute-start.4
  51.2 17.0 %collective-permute-start.10 = (bf16[256,3072]{1,0:T(8,128)(2,1)}, bf16[256,3072]{1,0:T(8,128)(2,1)}, u32[]{:S(2)}, u32[]{:S(2)}) collective-permute-start(bf16[256,3072]{1,0:T(8,128)(2,1)} %get-tuple-element.81.inner), channel_id=1, source_target_pairs={{0,1},{1,0},{2,3},{3,2},{4,5},{5,4},{6,7},{7,6},{8,9},{9,8},{10,11... | collective-permute-start | bytes 4718600 | tf_op jit(solution)/shard_map/ppermute | solution.py:616
  51.3 8.1 %collective-permute-start.6 = (bf16[256,1536]{1,0:T(8,128)(2,1)S(1)}, bf16[256,1536]{1,0:T(8,128)(2,1)S(1)}, u32[]{:S(2)}, u32[]{:S(2)}) collective-permute-start(bf16[256,1536]{1,0:T(8,128)(2,1)S(1)} %get-tuple-element.75), channel_id=1, source_target_pairs={{0,1},{1,0},{2,3},{3,2},{4,5},{5,4},{6,7},{7,6},{8,9},{9,8},{10,11... | collective-permute-start | bytes 2359304 | tf_op jit(solution)/shard_map/ppermute | solution.py:616
  51.7 5.1 %collective-permute-start.7 = (bf16[256,768]{1,0:T(8,128)(2,1)}, bf16[256,768]{1,0:T(8,128)(2,1)S(1)}, u32[]{:S(2)}, u32[]{:S(2)}) collective-permute-start(bf16[256,768]{1,0:T(8,128)(2,1)} %get-tuple-element.61.outer.grad), channel_id=1, source_target_pairs={{0,1},{1,0},{2,3},{3,2},{4,5},{5,4},{6,7},{7,6},{8,9},{9,8},{10,11... | collective-permute-start | bytes 1179656 | tf_op jit(solution)/shard_map/ppermute | solution.py:616
  51.9 16.3 %collective-permute-start.12 = (bf16[256,768]{1,0:T(8,128)(2,1)S(1)}, bf16[256,768]{1,0:T(8,128)(2,1)S(1)}, u32[]{:S(2)}, u32[]{:S(2)}) collective-permute-start(bf16[256,768]{1,0:T(8,128)(2,1)S(1)} %get-tuple-element.82.attn), channel_id=1, source_target_pairs={{0,1},{1,0},{2,3},{3,2},{4,5},{5,4},{6,7},{7,6},{8,9},{9,8},{10,11... | collective-permute-start | bytes 1179656 | tf_op jit(solution)/shard_map/ppermute | solution.py:616
  52.3 14.4 %collective-permute-start.9 = (bf16[2,192,256]{2,1,0:T(8,128)(2,1)}, bf16[2,192,256]{2,1,0:T(8,128)(2,1)S(1)}, u32[]{:S(2)}, u32[]{:S(2)}) collective-permute-start(bf16[2,192,256]{2,1,0:T(8,128)(2,1)} %copy-done.10), channel_id=1, source_target_pairs={{0,1},{1,0},{2,3},{3,2},{4,5},{5,4},{6,7},{7,6},{8,9},{9,8},{10,11... | collective-permute-start | bytes 589832 | tf_op jit(solution)/shard_map/ppermute | solution.py:616
  57.5 8.7 %collective-permute-start.5 = (bf16[2,256,192]{2,1,0:T(8,128)(2,1)}, bf16[2,256,192]{2,1,0:T(8,128)(2,1)S(1)}, u32[]{:S(2)}, u32[]{:S(2)}) collective-permute-start(bf16[2,256,192]{2,1,0:T(8,128)(2,1)} %copy-done.9), channel_id=1, source_target_pairs={{0,2},{1,3},{2,0},{3,1},{4,6},{5,7},{6,4},{7,5},{8,10},{9,11},{10,... | collective-permute-start | bytes 589832 | tf_op jit(solution)/shard_map/ppermute | solution.py:616
  60.3 7.8 %collective-permute-start.11 = (bf16[2,2,128,192]{3,2,1,0:T(8,128)(2,1)S(1)}, bf16[2,2,128,192]{3,2,1,0:T(8,128)(2,1)S(1)}, u32[]{:S(2)}, u32[]{:S(2)}) collective-permute-start(bf16[2,2,128,192]{3,2,1,0:T(8,128)(2,1)S(1)} %collective-permute-done.4), channel_id=1, source_target_pairs={{0,1},{1,0},{2,3},{3,2},{4,5},{5,4},{6,7},{7,6},{8,9},{9,8},{10,11... | collective-permute-start | bytes 589832 | tf_op jit(solution)/shard_map/ppermute | solution.py:616
  66.3 8.0 %collective-permute-start.8 = (bf16[2,256,192]{2,1,0:T(8,128)(2,1)S(1)}, bf16[2,256,192]{2,1,0:T(8,128)(2,1)S(1)}, u32[]{:S(2)}, u32[]{:S(2)}) collective-permute-start(bf16[2,256,192]{2,1,0:T(8,128)(2,1)S(1)} %get-tuple-element.77), channel_id=1, source_target_pairs={{0,1},{1,0},{2,3},{3,2},{4,5},{5,4},{6,7},{7,6},{8,9},{9,8},{10,11... | collective-permute-start | bytes 589832 | tf_op jit(solution)/shard_map/ppermute | solution.py:616
  66.7 28.0 %collective-permute-start.16 = (bf16[1,8,96,768]{3,2,1,0:T(8,128)(2,1)S(1)}, bf16[1,8,96,768]{3,2,1,0:T(8,128)(2,1)S(1)}, u32[]{:S(2)}, u32[]{:S(2)}) collective-permute-start(bf16[1,8,96,768]{3,2,1,0:T(8,128)(2,1)S(1)} %get-tuple-element.89), channel_id=1, source_target_pairs={{0,2},{1,3},{2,0},{3,1},{4,6},{5,7},{6,4},{7,5},{8,10},{9,11},{10,... | collective-permute-start | bytes 3538952 | tf_op jit(solution)/shard_map/ppermute | solution.py:616
  72.6 34.4 %collective-permute-start.19 = (bf16[2,4,240,384]{3,2,1,0:T(8,128)(2,1)S(1)}, bf16[2,4,240,384]{3,2,1,0:T(8,128)(2,1)S(1)}, u32[]{:S(2)}, u32[]{:S(2)}) collective-permute-start(bf16[2,4,240,384]{3,2,1,0:T(8,128)(2,1)S(1)} %get-tuple-element.83.refs_0_), channel_id=1, source_target_pairs={{0,8},{4,12},{8,0},{12,4},{16,24},{20,28},{24,16},{28,20},{1,9},{5... | collective-permute-start | bytes 4423688 | tf_op jit(solution)/shard_map/ppermute | solution.py:616
  86.6 2.4 %collective-permute-start.13 = (bf16[2,2,128,768]{3,2,1,0:T(8,128)(2,1)S(1)}, bf16[2,2,128,768]{3,2,1,0:T(8,128)(2,1)S(1)}, u32[]{:S(2)}, u32[]{:S(2)}) collective-permute-start(bf16[2,2,128,768]{3,2,1,0:T(8,128)(2,1)S(1)} %get-tuple-element.85), channel_id=1, source_target_pairs={{0,1},{1,0},{2,3},{3,2},{4,5},{5,4},{6,7},{7,6},{8,9},{9,8},{10,11... | collective-permute-start | bytes 2359304 | tf_op jit(solution)/shard_map/ppermute | solution.py:616
  86.7 13.6 %collective-permute-start.15 = (bf16[1,4,96,640]{3,2,1,0:T(8,128)(2,1)S(1)}, bf16[1,4,96,640]{3,2,1,0:T(8,128)(2,1)S(1)}, u32[]{:S(2)}, u32[]{:S(2)}) collective-permute-start(bf16[1,4,96,640]{3,2,1,0:T(8,128)(2,1)S(1)} %get-tuple-element.87), channel_id=1, source_target_pairs={{0,4},{4,0},{8,12},{12,8},{16,20},{20,16},{24,28},{28,24},{1,5},{5... | collective-permute-start | bytes 1474568 | tf_op jit(solution)/shard_map/ppermute | solution.py:616
  107.8 17.8 %collective-permute-start.22 = (bf16[1,4,240,384]{3,2,1,0:T(8,128)(2,1)S(1)}, bf16[1,4,240,384]{3,2,1,0:T(8,128)(2,1)S(1)}, u32[]{:S(2)}, u32[]{:S(2)}) collective-permute-start(bf16[1,4,240,384]{3,2,1,0:T(8,128)(2,1)S(1)} %inner_y.1.refs_4_), channel_id=1, source_target_pairs={{0,2},{1,3},{2,0},{3,1},{4,6},{5,7},{6,4},{7,5},{8,10},{9,11},{10,... | collective-permute-start | bytes 2211848 | tf_op jit(solution)/shard_map/ppermute | solution.py:616
  108.1 14.4 %collective-permute-start.18 = (bf16[1,4,96,768]{3,2,1,0:T(8,128)(2,1)S(1)}, bf16[1,4,96,768]{3,2,1,0:T(8,128)(2,1)S(1)}, u32[]{:S(2)}, u32[]{:S(2)}) collective-permute-start(bf16[1,4,96,768]{3,2,1,0:T(8,128)(2,1)S(1)} %outer_x.1.refs_3_), channel_id=1, source_target_pairs={{0,4},{4,0},{8,12},{12,8},{16,20},{20,16},{24,28},{28,24},{1,5},{5... | collective-permute-start | bytes 1769480 | tf_op jit(solution)/shard_map/ppermute | solution.py:616
  109.8 15.0 %collective-permute-start.17 = (bf16[1,2,96,640]{3,2,1,0:T(8,128)(2,1)S(1)}, bf16[1,2,96,640]{3,2,1,0:T(8,128)(2,1)S(1)}, u32[]{:S(2)}, u32[]{:S(2)}) collective-permute-start(bf16[1,2,96,640]{3,2,1,0:T(8,128)(2,1)S(1)} %project_z.1.refs_3_), channel_id=1, source_target_pairs={{0,8},{4,12},{8,0},{12,4},{16,24},{20,28},{24,16},{28,20},{1,9},{5... | collective-permute-start | bytes 737288 | tf_op jit(solution)/shard_map/ppermute | solution.py:616
  123.2 8.5 %collective-permute-start.21 = (bf16[1,2,96,768]{3,2,1,0:T(8,128)(2,1)S(1)}, bf16[1,2,96,768]{3,2,1,0:T(8,128)(2,1)S(1)}, u32[]{:S(2)}, u32[]{:S(2)}) collective-permute-start(bf16[1,2,96,768]{3,2,1,0:T(8,128)(2,1)S(1)} %outer_z.1.refs_4_), channel_id=1, source_target_pairs={{0,8},{4,12},{8,0},{12,4},{16,24},{20,28},{24,16},{28,20},{1,9},{5... | collective-permute-start | bytes 884744 | tf_op jit(solution)/shard_map/ppermute | solution.py:616
  126.3 16.1 %collective-permute-start.29 = (bf16[1,2,240,384]{3,2,1,0:T(8,128)(2,1)S(1)}, bf16[1,2,240,384]{3,2,1,0:T(8,128)(2,1)S(1)}, u32[]{:S(2)}, u32[]{:S(2)}) collective-permute-start(bf16[1,2,240,384]{3,2,1,0:T(8,128)(2,1)S(1)} %inner_x.1.refs_5_), channel_id=1, source_target_pairs={{0,4},{4,0},{8,12},{12,8},{16,20},{20,16},{24,28},{28,24},{1,5},{5... | collective-permute-start | bytes 1105928 | tf_op jit(solution)/shard_map/ppermute | solution.py:616
  127.9 12.0 %collective-permute-start.20 = (bf16[1,1,96,640]{3,2,1,0:T(8,128)(2,1)S(1)}, bf16[1,1,96,640]{3,2,1,0:T(8,128)(2,1)S(1)}, u32[]{:S(2)}, u32[]{:S(2)}) collective-permute-start(bf16[1,1,96,640]{3,2,1,0:T(8,128)(2,1)S(1)} %project_zz.1.refs_4_), channel_id=1, source_target_pairs={{0,16},{4,20},{8,24},{12,28},{16,0},{20,4},{24,8},{28,12},{1,17},{... | collective-permute-start | bytes 368648 | tf_op jit(solution)/shard_map/ppermute | solution.py:616
  132.4 13.8 %collective-permute-start.34 = (bf16[1,1,96,768]{3,2,1,0:T(8,128)(2,1)S(1)}, bf16[1,1,96,768]{3,2,1,0:T(8,128)(2,1)S(1)}, u32[]{:S(2)}, u32[]{:S(2)}) collective-permute-start(bf16[1,1,96,768]{3,2,1,0:T(8,128)(2,1)S(1)} %outer_zz.1.refs_5_), channel_id=1, source_target_pairs={{0,16},{4,20},{8,24},{12,28},{16,0},{20,4},{24,8},{28,12},{1,17},{... | collective-permute-start | bytes 442376 | tf_op jit(solution)/shard_map/ppermute | solution.py:616
  140.4 2.7 %collective-permute-start.23 = (bf16[24,640]{1,0:T(8,128)(2,1)S(1)}, bf16[24,640]{1,0:T(8,128)(2,1)S(1)}, u32[]{:S(2)}, u32[]{:S(2)}) collective-permute-start(bf16[24,640]{1,0:T(8,128)(2,1)S(1)} %get-tuple-element.92), channel_id=1, source_target_pairs={{0,1},{1,0},{2,3},{3,2},{4,5},{5,4},{6,7},{7,6},{8,9},{9,8},{10,11... | collective-permute-start | bytes 92168 | tf_op jit(solution)/shard_map/ppermute | solution.py:616
  140.5 4.1 %collective-permute-start.24 = (bf16[24,640]{1,0:T(8,128)(2,1)S(1)}, bf16[24,640]{1,0:T(8,128)(2,1)S(1)}, u32[]{:S(2)}, u32[]{:S(2)}) collective-permute-start(bf16[24,640]{1,0:T(8,128)(2,1)S(1)} %get-tuple-element.93), channel_id=1, source_target_pairs={{0,2},{1,3},{2,0},{3,1},{4,6},{5,7},{6,4},{7,5},{8,10},{9,11},{10,... | collective-permute-start | bytes 92168 | tf_op jit(solution)/shard_map/ppermute | solution.py:616
  140.6 4.0 %collective-permute-start.25 = (bf16[24,640]{1,0:T(8,128)(2,1)S(1)}, bf16[24,640]{1,0:T(8,128)(2,1)S(1)}, u32[]{:S(2)}, u32[]{:S(2)}) collective-permute-start(bf16[24,640]{1,0:T(8,128)(2,1)S(1)} %get-tuple-element.94), channel_id=1, source_target_pairs={{0,3},{1,2},{2,1},{3,0},{4,7},{5,6},{6,5},{7,4},{8,11},{9,10},{10,... | collective-permute-start | bytes 92168 | tf_op jit(solution)/shard_map/ppermute | solution.py:616
  143.1 17.5 %collective-permute-start.30 = (bf16[1,1,240,384]{3,2,1,0:T(8,128)(2,1)S(1)}, bf16[1,1,240,384]{3,2,1,0:T(8,128)(2,1)S(1)}, u32[]{:S(2)}, u32[]{:S(2)}) collective-permute-start(bf16[1,1,240,384]{3,2,1,0:T(8,128)(2,1)S(1)} %inner_zz.1.refs_6_), channel_id=1, source_target_pairs={{0,16},{4,20},{8,24},{12,28},{16,0},{20,4},{24,8},{28,12},{1,17},{... | collective-permute-start | bytes 552968 | tf_op jit(solution)/shard_map/ppermute | solution.py:616
  144.6 18.6 %collective-permute-start.26 = (bf16[1,96,640]{2,1,0:T(8,128)(2,1)S(1)}, bf16[1,96,640]{2,1,0:T(8,128)(2,1)S(1)}, u32[]{:S(2)}, u32[]{:S(2)}) collective-permute-start(bf16[1,96,640]{2,1,0:T(8,128)(2,1)S(1)} %maximum_bitcast_fusion), channel_id=1, source_target_pairs={{0,16},{4,20},{8,24},{12,28},{16,0},{20,4},{24,8},{28,12},{1,17},{... | collective-permute-start | bytes 368648 | tf_op jit(solution)/shard_map/ppermute | solution.py:616
  146.8 23.6 %collective-permute-start.35 = (bf16[1,96,768]{2,1,0:T(8,128)(2,1)S(1)}, bf16[1,96,768]{2,1,0:T(8,128)(2,1)S(1)}, u32[]{:S(2)}, u32[]{:S(2)}) collective-permute-start(bf16[1,96,768]{2,1,0:T(8,128)(2,1)S(1)} %bitcast.44), channel_id=1, source_target_pairs={{0,16},{4,20},{8,24},{12,28},{16,0},{20,4},{24,8},{28,12},{1,17},{... | collective-permute-start | bytes 442376 | tf_op jit(solution)/shard_map/ppermute | solution.py:616
  161.3 13.1 %collective-permute-start.31 = (bf16[1,240,384]{2,1,0:T(8,128)(2,1)S(1)}, bf16[1,240,384]{2,1,0:T(8,128)(2,1)S(1)}, u32[]{:S(2)}, u32[]{:S(2)}) collective-permute-start(bf16[1,240,384]{2,1,0:T(8,128)(2,1)S(1)} %bitcast.41), channel_id=1, source_target_pairs={{0,16},{4,20},{8,24},{12,28},{16,0},{20,4},{24,8},{28,12},{1,17},{... | collective-permute-start | bytes 552968 | tf_op jit(solution)/shard_map/ppermute | solution.py:616
  163.2 15.6 %collective-permute-start.27 = (bf16[2,96,640]{2,1,0:T(8,128)(2,1)S(1)}, bf16[2,96,640]{2,1,0:T(8,128)(2,1)S(1)}, u32[]{:S(2)}, u32[]{:S(2)}) collective-permute-start(bf16[2,96,640]{2,1,0:T(8,128)(2,1)S(1)} %pad_maximum_fusion.5), channel_id=1, source_target_pairs={{0,8},{4,12},{8,0},{12,4},{16,24},{20,28},{24,16},{28,20},{1,9},{5... | collective-permute-start | bytes 737288 | tf_op jit(solution)/shard_map/ppermute | solution.py:616
  170.5 13.7 %collective-permute-start.36 = (bf16[2,96,768]{2,1,0:T(8,128)(2,1)S(1)}, bf16[2,96,768]{2,1,0:T(8,128)(2,1)S(1)}, u32[]{:S(2)}, u32[]{:S(2)}) collective-permute-start(bf16[2,96,768]{2,1,0:T(8,128)(2,1)S(1)} %pad_maximum_fusion.4), channel_id=1, source_target_pairs={{0,8},{4,12},{8,0},{12,4},{16,24},{20,28},{24,16},{28,20},{1,9},{5... | collective-permute-start | bytes 884744 | tf_op jit(solution)/shard_map/ppermute | solution.py:616
  174.4 11.5 %collective-permute-start.32 = (bf16[2,240,384]{2,1,0:T(8,128)(2,1)S(1)}, bf16[2,240,384]{2,1,0:T(8,128)(2,1)S(1)}, u32[]{:S(2)}, u32[]{:S(2)}) collective-permute-start(bf16[2,240,384]{2,1,0:T(8,128)(2,1)S(1)} %pad_maximum_fusion.3), channel_id=1, source_target_pairs={{0,4},{4,0},{8,12},{12,8},{16,20},{20,16},{24,28},{28,24},{1,5},{5... | collective-permute-start | bytes 1105928 | tf_op jit(solution)/shard_map/ppermute | solution.py:616
  174.5 11.6 %collective-permute-start.14 = (bf16[1,1,256,768]{3,2,1,0:T(8,128)(2,1)S(1)}, bf16[1,1,256,768]{3,2,1,0:T(8,128)(2,1)S(1)}, u32[]{:S(2)}, u32[]{:S(2)}) collective-permute-start(bf16[1,1,256,768]{3,2,1,0:T(8,128)(2,1)S(1)} %back_y.1.refs_3_), channel_id=1, source_target_pairs={{0,2},{1,3},{2,0},{3,1},{4,6},{5,7},{6,4},{7,5},{8,10},{9,11},{10,... | collective-permute-start | bytes 1179656 | tf_op jit(solution)/shard_map/ppermute | solution.py:616
  178.9 17.5 %collective-permute-start.28 = (bf16[4,96,640]{2,1,0:T(8,128)(2,1)S(1)}, bf16[4,96,640]{2,1,0:T(8,128)(2,1)S(1)}, u32[]{:S(2)}, u32[]{:S(2)}) collective-permute-start(bf16[4,96,640]{2,1,0:T(8,128)(2,1)S(1)} %pad_maximum_fusion.2.refs_1_), channel_id=1, source_target_pairs={{0,4},{4,0},{8,12},{12,8},{16,20},{20,16},{24,28},{28,24},{1,5},{5... | collective-permute-start | bytes 1474568 | tf_op jit(solution)/shard_map/ppermute | solution.py:616
  184.2 23.9 %collective-permute-start.37 = (bf16[4,96,768]{2,1,0:T(8,128)(2,1)S(1)}, bf16[4,96,768]{2,1,0:T(8,128)(2,1)S(1)}, u32[]{:S(2)}, u32[]{:S(2)}) collective-permute-start(bf16[4,96,768]{2,1,0:T(8,128)(2,1)S(1)} %pad_maximum_fusion.1.refs_1_), channel_id=1, source_target_pairs={{0,4},{4,0},{8,12},{12,8},{16,20},{20,16},{24,28},{28,24},{1,5},{5... | collective-permute-start | bytes 1769480 | tf_op jit(solution)/shard_map/ppermute | solution.py:616
  186.0 24.2 %collective-permute-start.33 = (bf16[4,240,384]{2,1,0:T(8,128)(2,1)S(1)}, bf16[4,240,384]{2,1,0:T(8,128)(2,1)S(1)}, u32[]{:S(2)}, u32[]{:S(2)}) collective-permute-start(bf16[4,240,384]{2,1,0:T(8,128)(2,1)S(1)} %pad_maximum_fusion.refs_1_), channel_id=1, source_target_pairs={{0,8},{4,12},{8,0},{12,4},{16,24},{20,28},{24,16},{28,20},{1,9},{5... | collective-permute-start | bytes 2211848 | tf_op jit(solution)/shard_map/ppermute | solution.py:616
  (22 other events, 61.1 us)

commit v3 on v2

--- a/solution.py
+++ b/solution.py
@@ -12,6 +12,7 @@
 LOW = jnp.bfloat16
 MIB = 1 << 20
 PIECES = 8
+STEP = 5.0
 
 
 def cost(us):
@@ -51,7 +52,7 @@
 
 
 def attend_kernel(where, lengths, x0, x1, x2, x3, w_hbm, qb, vb, qkv_out, lse_out, w, *refs):
-    near_out, across_out, wide, sem = refs
+    near_out, across_out, own_out, wide, sem = refs
     p = pl.program_id(0)
     me = where[0]
     quarter, width = x0.shape[1:]
@@ -98,6 +99,7 @@
     for j in range(4):
         out = across_out if j > 1 else near_out
         out[j & 1, 0] = context[j * quarter : (j + 1) * quarter]
+    own_out[0] = context[:quarter]
 
 
 def attend(where, lengths, shards, w, qb, vb):
@@ -117,13 +119,15 @@
             vmem((1, heads, rows), lambda p: (p, 0, 0)),
             whole(width, 3 * hw),
         ]
-        + [vmem((2, 1, quarter, hw), lambda p: (0, p, 0, 0))] * 2,
+        + [vmem((2, 1, quarter, hw), lambda p: (0, p, 0, 0))] * 2
+        + [vmem((1, quarter, hw), lambda p: (p, 0, 0))],
         out_shape=[
             pltpu.HBM((passages, rows, 3 * hw), LOW),
             pltpu.HBM((passages, heads, rows), F32),
             pltpu.HBM((width, 3 * hw), LOW),
         ]
-        + [jax.ShapeDtypeStruct((2, passages, quarter, hw), LOW)] * 2,
+        + [jax.ShapeDtypeStruct((2, passages, quarter, hw), LOW)] * 2
+        + [pltpu.HBM((passages, quarter, hw), LOW)],
         scratch_shapes=[pltpu.VMEM((3, width, window), LOW), pltpu.SemaphoreType.DMA((3,))],
         compiler_params=pltpu.CompilerParams(vmem_limit_bytes=16 * MIB),
         cost_estimate=cost(5.5),
@@ -239,7 +243,7 @@
         compiler_params=pltpu.CompilerParams(vmem_limit_bytes=24 * MIB),
         cost_estimate=cost(11),
         name="attend_back",
-    )(place, lengths, *map(far, shards), far(w), far(qkv), far(lse), *grads, vectors, *after)
+    )(place, lengths, *map(far, shards), far(w), far(qkv), far(lse), *map(far, grads), far(vectors), *after)
 
 
 def normalise(field):
@@ -257,54 +261,69 @@
 
 
 def rows_kernel(
-    where, x, near, near_got, far_got, cot, wa, vec, ib, wi_hbm, wo_hbm,
+    where, x, near_hbm, near_got_hbm, far_got_hbm, cot, wa, vec, ib, wi_hbm, wo_hbm,
     layer_out, hidden_own, hidden_send, active_own, active_send, slope, outer_out, grad_out, normal_out, scale_out,
-    sums_out, wi, wo, flipped, sem,
+    sums_out, wi, wo, parts, hidden_here, active_here, flipped, sem,
 ):
     me = where[0]
     width = x.shape[1]
     chunk = width
-    hw = near.shape[2]
-
-    def copies(c):
+    hw = parts.shape[2]
+    loads = [
+        pltpu.make_async_copy(f, parts.at[pl.ds(first, count)], sem.at[i])
+        for i, (f, first, count) in enumerate(
+            ((near_hbm.at[pl.ds(0, 1)], 0, 1), (near_got_hbm, 1, 2), (far_got_hbm.at[pl.ds(0, 1)], 3, 1))
+        )
+    ]
+    order = (0, 2, 1, 3)
+    weights = []
+    for k, c in enumerate(order):
         cols = pl.ds(pl.multiple_of((me ^ c) * chunk, 128), chunk)
-        return (
-            pltpu.make_async_copy(wi_hbm.at[:, cols], wi.at[:, cols], sem.at[2 * c]),
-            pltpu.make_async_copy(wo_hbm.at[cols, :], wo.at[cols, :], sem.at[2 * c + 1]),
-        )
-
-    for c in range(4):
-        for copy in copies(c):
-            copy.start()
+        weights.append(pltpu.make_async_copy(wi_hbm.at[:, cols], wi.at[:, cols], sem.at[5 + 2 * k]))
+        weights.append(pltpu.make_async_copy(wo_hbm.at[cols, :], wo.at[cols, :], sem.at[6 + 2 * k]))
+    for copy in loads + weights[:2]:
+        copy.start()
+    stores = [
+        pltpu.make_async_copy(hidden_here, hidden_own, sem.at[3]),
+        pltpu.make_async_copy(active_here, active_own, sem.at[4]),
+    ]
     row = lambda r: vec[r : r + 1, :]
     attn_bias, attn_gain, attn_shift, outer_bias, ffn_gain, ffn_shift = (row(r) for r in range(6))
     attended = attn_bias + x[...].astype(F32)
-    for j, part in enumerate((near[0], near_got[0], far_got[0], near_got[1])):
-        attended += dot(part, wa[me ^ j])
+    for copy in loads:
+        copy.wait()
+    weights[2].start()
+    weights[3].start()
+    for j, k in enumerate((0, 1, 3, 2)):
+        attended += dot(parts[k], wa[me ^ j])
     normal_one, scale_one = normalise(attended)
     normal_out[...] = normal_one
     scale_out[...] = scale_one
     hidden = normal_one * attn_gain + attn_shift
     hidden_low = hidden.astype(LOW)
+    flipped[...] = hidden.T
+    for j in range(4):
+        start = pl.multiple_of((me ^ j) * hw, 64)
+        here = hidden_send if j & 1 else hidden_here
+        here[j >> 1] = flipped[pl.ds(start, hw), :].astype(LOW)
+    stores[0].start()
     pre_two = hidden + outer_bias
-    for c in range(4):
+    for k, c in enumerate(order):
         cols = pl.ds(pl.multiple_of((me ^ c) * chunk, 128), chunk)
-        first, second = copies(c)
-        first.wait()
+        for copy in weights[2 * k + 4 : 2 * k + 6]:
+            copy.start()
+        weights[2 * k].wait()
         u = dot(hidden_low, wi[:, cols]) + ib[:, cols]
         below = 0.5 * (1.0 + lax.erf(u * (0.5**0.5)))
         density = jnp.exp(-0.5 * u * u) * 0.3989422804014327
         active = (u * below).astype(LOW)
         slope[c] = below + u * density
-        here = active_send if c & 1 else active_own
+        here = active_send if c & 1 else active_here
         here[:, (c >> 1) * chunk : ((c >> 1) + 1) * chunk] = active
-        second.wait()
+        weights[2 * k + 1].wait()
         pre_two += dot(active, wo[cols, :])
-    flipped[...] = hidden.T
-    for j in range(4):
-        start = pl.multiple_of((me ^ j) * hw, 64)
-        here = hidden_send if j & 1 else hidden_own
-        here[j >> 1] = flipped[pl.ds(start, hw), :].astype(LOW)
+        if c == 2:
+            stores[1].start()
     normal_two, scale_two = normalise(pre_two)
     layer_out[...] = (normal_two * ffn_gain + ffn_shift).astype(LOW)
     dy = cot[...].astype(F32)
@@ -316,6 +335,8 @@
     outer_out[...] = grad_outer
     sums_out[3:4, :] = jnp.sum(grad_outer.astype(F32), 0, keepdims=True)
     grad_out[...] = grad_two
+    for copy in stores:
+        copy.wait()
 
 
 def rows_pass(where, x, near, near_got, far_got, cot, wa, vec, ib, wi, wo):
@@ -326,138 +347,190 @@
     full = lambda *s: jax.ShapeDtypeStruct(s, F32)
     return pl.pallas_call(
         rows_kernel,
-        in_specs=[SMEM] + [vmem()] * 8 + [HBM, HBM],
-        out_specs=[vmem()] * 13,
+        in_specs=[SMEM, vmem(), HBM, HBM, HBM] + [vmem()] * 4 + [HBM, HBM],
+        out_specs=[vmem(), HBM, vmem(), HBM] + [vmem()] * 9,
         out_shape=[
-            low(rows, width), low(2, hw, rows), low(2, hw, rows), low(rows, 2 * width), low(rows, 2 * width),
+            low(rows, width), pltpu.HBM((2, hw, rows), LOW), low(2, hw, rows),
+            pltpu.HBM((rows, 2 * width), LOW), low(rows, 2 * width),
             full(4, rows, width), low(rows, width), full(rows, width), full(rows, width), full(rows, 1),
             full(8, width), low(width, ff), low(ff, width),
         ],
-        scratch_shapes=[pltpu.VMEM((width, rows), F32), pltpu.SemaphoreType.DMA((8,))],
-        compiler_params=pltpu.CompilerParams(vmem_limit_bytes=16 * MIB),
-        cost_estimate=cost(7),
+        scratch_shapes=[
+            pltpu.VMEM((4, rows, hw), LOW),
+            pltpu.VMEM((2, hw, rows), LOW),
+            pltpu.VMEM((rows, 2 * width), LOW),
+            pltpu.VMEM((width, rows), F32),
+            pltpu.SemaphoreType.DMA((13,)),
+        ],
+        compiler_params=pltpu.CompilerParams(vmem_limit_bytes=14 * MIB),
+        cost_estimate=cost(6),
         name="rows_pass",
-    )(where, x, near, near_got, far_got, cot, wa, vec, ib, far(wi), far(wo))
+    )(where, x, far(near), far(near_got), far(far_got), cot, wa, vec, ib, far(wi), far(wo))
 
 
 def rows_back_kernel(
     where, slope, outer, grad_two, normal, scale, sums, wa, gain, wi, wo,
     grad_one_out, inner_out, attn_out, near_out, across_out, sums_out,
+    grad_one_here, inner_here, attn_here, near_here, sums_here, sem,
 ):
     me = where[0]
     rows, width = outer.shape
     chunk = width
     hw = wa.shape[1]
-    sums_out[...] = jnp.zeros_like(sums_out)
-    sums_out[3:6, :] = sums[3:6, :]
+    pairs = ((grad_one_here, grad_one_out), (attn_here, attn_out), (near_here, near_out), (sums_here, sums_out))
+    stores = [pltpu.make_async_copy(here, out, sem.at[4 + i]) for i, (here, out) in enumerate(pairs)]
+    sums_here[...] = jnp.zeros_like(sums_here)
+    sums_here[3:6, :] = sums[3:6, :]
     grad_outer = outer[...]
     grad_hidden = grad_two[...]
+    moved = []
     for c in range(4):
         cols = slice(c * chunk, (c + 1) * chunk)
         grad_inner = (dot_nt(grad_outer, wo[cols, :]) * slope[me ^ c]).astype(LOW)
-        inner_out[:, cols] = grad_inner
+        inner_here[:, cols] = grad_inner
+        some = pl.ds(c * chunk, chunk)
+        moved.append(pltpu.make_async_copy(inner_here.at[:, some], inner_out.at[:, some], sem.at[c]))
+        moved[c].start()
         column = jnp.sum(grad_inner.astype(F32), 0, keepdims=True)
         for i in range(4):
-            sums_out[6 + i : 7 + i, c * hw : (c + 1) * hw] = column[:, i * hw : (i + 1) * hw]
+            sums_here[6 + i : 7 + i, c * hw : (c + 1) * hw] = column[:, i * hw : (i + 1) * hw]
         grad_hidden += dot_nt(grad_inner, wi[:, cols])
     normal_one = normal[...]
-    sums_out[1:2, :] = jnp.sum(grad_hidden * normal_one, 0, keepdims=True)
-    sums_out[2:3, :] = jnp.sum(grad_hidden, 0, keepdims=True)
+    sums_here[1:2, :] = jnp.sum(grad_hidden * normal_one, 0, keepdims=True)
+    sums_here[2:3, :] = jnp.sum(grad_hidden, 0, keepdims=True)
     grad_one = normalise_back(grad_hidden * gain[1:2, :], normal_one, scale[...])
-    grad_one_out[...] = grad_one
+    grad_one_here[...] = grad_one
+    stores[0].start()
     grad_attn = grad_one.astype(LOW)
-    attn_out[...] = grad_attn
-    sums_out[0:1, :] = jnp.sum(grad_attn.astype(F32), 0, keepdims=True)
-    for j in range(4):
-        out = across_out if j > 1 else near_out
-        out[j & 1] = dot_nt(grad_attn, wa[me ^ j]).astype(LOW)
+    attn_here[...] = grad_attn
+    stores[1].start()
+    sums_here[0:1, :] = jnp.sum(grad_attn.astype(F32), 0, keepdims=True)
+    stores[3].start()
+    for j in range(2):
+        near_here[j] = dot_nt(grad_attn, wa[me ^ j]).astype(LOW)
+    stores[2].start()
+    for j in range(2):
+        across_out[j] = dot_nt(grad_attn, wa[me ^ (j + 2)]).astype(LOW)
+    for copy in moved + stores:
+        copy.wait()
 
 
 def rows_back(where, slope, outer, grad_two, normal, scale, sums, wa, vec, wi, wo):
     rows, width = outer.shape
     ff = wi.shape[1]
     hw = wa.shape[1]
-    low = lambda *s: jax.ShapeDtypeStruct(s, LOW)
-    full = lambda *s: jax.ShapeDtypeStruct(s, F32)
+    kinds = [((rows, width), F32), ((rows, ff), LOW), ((rows, width), LOW), ((2, rows, hw), LOW), ((16, width), F32)]
+    outs = [pltpu.HBM(*kind) for kind in kinds]
     return pl.pallas_call(
         rows_back_kernel,
         in_specs=[SMEM] + [vmem()] * 10,
-        out_specs=[vmem()] * 6,
-        out_shape=[
-            full(rows, width), low(rows, ff), low(rows, width), low(2, rows, hw), low(2, rows, hw), full(16, width),
-        ],
-        compiler_params=pltpu.CompilerParams(vmem_limit_bytes=12 * MIB),
+        out_specs=[HBM] * 4 + [vmem(), HBM],
+        out_shape=outs[:4] + [jax.ShapeDtypeStruct((2, rows, hw), LOW)] + outs[4:],
+        scratch_shapes=[pltpu.VMEM(*kind) for kind in kinds] + [pltpu.SemaphoreType.DMA((8,))],
+        compiler_params=pltpu.CompilerParams(vmem_limit_bytes=14 * MIB),
         cost_estimate=cost(5),
         name="rows_back",
     )(where, slope, outer, grad_two, normal, scale, sums, wa, vec, wi, wo)
 
 
-def outer_grad_kernel(active, active_got, grad, grad_got, send_out, keep_out):
-    width = grad.shape[1]
-    n = width // PIECES
+def outer_grad_kernel(place, active, active_got, grad, grad_got, send_out, keep_out):
+    half = PIECES // 2
+    n = grad.shape[1] // PIECES
     right = jnp.concatenate([grad[...], grad_got[...]], 0)
-    for y, out in ((1, send_out), (0, keep_out)):
-        cols = slice(y * width, (y + 1) * width)
-        product = dot_tn(jnp.concatenate([active[:, cols], active_got[:, cols]], 0), right)
+    product = dot_tn(jnp.concatenate([active[...], active_got[...]], 0), right)
+
+    def store(low_out, high_out):
         for e in range(PIECES):
-            out[0, e] = product[e * n : (e + 1) * n].astype(LOW)
-
-
-def outer_grad(active, active_got, grad, grad_got):
-    width = grad.shape[1]
-    shape = (1, PIECES, width // PIECES, width)
+            out = high_out if e >= half else low_out
+            out[0, e % half] = product[e * n : (e + 1) * n].astype(LOW)
+
+    high = (place[0] & half) > 0
+    pl.when(high)(lambda: store(send_out, keep_out))
+    pl.when(jnp.logical_not(high))(lambda: store(keep_out, send_out))
+
+
+def outer_grad(place, active, active_got, grad, grad_got):
+    rows, width = grad.shape
+    block = (1, PIECES // 2, width // PIECES, width)
+    side = vmem((rows, width), lambda y: (0, y))
+    whole = lambda *s: vmem(s, lambda y: (0,) * len(s))
     return pl.pallas_call(
         outer_grad_kernel,
-        in_specs=[vmem()] * 4,
-        out_specs=[vmem()] * 2,
-        out_shape=[jax.ShapeDtypeStruct(shape, LOW)] * 2,
-        compiler_params=pltpu.CompilerParams(vmem_limit_bytes=12 * MIB),
-        cost_estimate=cost(3),
+        grid=(2,),
+        in_specs=[SMEM, side, side, whole(rows, width), whole(rows, width)],
+        out_specs=[vmem(block, lambda y: (y, 0, 0, 0))] * 2,
+        out_shape=[jax.ShapeDtypeStruct((2,) + block[1:], LOW)] * 2,
+        compiler_params=pltpu.CompilerParams(vmem_limit_bytes=16 * MIB),
+        cost_estimate=cost(6),
         name="outer_grad",
-    )(active, active_got, grad, grad_got)
+    )(place, far(active), far(active_got), far(grad), far(grad_got))
+
+
+SPLIT = 128
 
 
 def inner_grad_kernel(
-    place, hidden, hidden_got, inner, inner_got, near, far_got, context_got, attn, attn_got, send_out, keep_out, rest
+    place, hidden, hidden_got, inner, inner_got, near, far_got, context_got, attn, attn_got, *refs
 ):
+    first_send, first_keep, second_send, second_keep, left, rest = refs[-6:]
+    step = pl.program_id(0)
     hw = hidden.shape[1]
     rows, width = attn.shape
     half = PIECES // 2
     n = hw // PIECES
+    cols = inner.shape[1] // 2
+
+    @pl.when(step == 0)
+    def _():
+        grads = jnp.concatenate([attn[...], attn_got[...]], 0)
+        for y, mine in enumerate((near, far_got)):
+            left[y * hw : (y + 1) * hw, :rows] = hidden[y]
+            left[y * hw : (y + 1) * hw, rows:] = hidden_got[y]
+            rest[y] = dot_tn(jnp.concatenate([mine[0], context_got[y]], 0), grads)
+
+    product = dot(left[...], jnp.concatenate([inner[...], inner_got[...]], 0))
+
+    def store_first(out):
+        for k in range(2):
+            for y in range(2):
+                piece = product[y * hw : y * hw + SPLIT, k * cols : (k + 1) * cols]
+                out[y, 2 * (step & 1) + k] = piece.astype(LOW)
+
+    mine = (place[0] & half) == (step >> 1) * half
+    pl.when(mine)(lambda: store_first(first_keep))
+    pl.when(jnp.logical_not(mine))(lambda: store_first(first_send))
+    for k in range(2):
+        for y, out in enumerate((second_keep, second_send)):
+            piece = 2 * step + k
+            some = product[y * hw + SPLIT : (y + 1) * hw, k * cols : (k + 1) * cols]
+            more = rest[y, pl.ds(pl.multiple_of(piece * n, 8), n), :]
+            some = jnp.concatenate([some, more[:, : width // 2], more[:, width // 2 :]], 0)
+            out[0, piece] = some.astype(LOW)
+
+
+def inner_grad(place, hidden, hidden_got, inner, inner_got, near, far_got, context_got, attn, attn_got, after):
+    hw = hidden.shape[1]
+    rows, width = attn.shape
+    half = PIECES // 2
     cols = inner.shape[1] // PIECES
-    left = jnp.concatenate(
-        [jnp.concatenate([hidden[y], hidden_got[y]], 1) for y in range(2)], 0
-    )
-    grads = jnp.concatenate([attn[...], attn_got[...]], 0)
-    for y, mine in enumerate((near[0], far_got[0])):
-        rest[y] = dot_tn(jnp.concatenate([mine, context_got[y]], 0), grads)
-    me = place[0] & half
-    for out, first in ((send_out, me ^ half), (keep_out, me)):
-        for e in range(half):
-            piece = first + e
-            here = pl.ds(pl.multiple_of(piece * cols, 128), cols)
-            product = dot(left, jnp.concatenate([inner[:, here], inner_got[:, here]], 0))
-            for y in range(2):
-                out[y, e, :hw, :] = product[y * hw : (y + 1) * hw].astype(LOW)
-                more = rest[y, pl.ds(pl.multiple_of(piece * n, 8), n), :]
-                more = jnp.concatenate([more[:, : width // 2], more[:, width // 2 :]], 0)
-                out[y, e, hw:, :] = more.astype(LOW)
-
-
-def inner_grad(place, hidden, hidden_got, inner, inner_got, near, far_got, context_got, attn, attn_got):
-    hw = hidden.shape[1]
-    width = attn.shape[1]
-    shape = (2, PIECES // 2, hw + 2 * hw // PIECES, inner.shape[1] // PIECES)
+    first = (2, half, SPLIT, cols)
+    second = (1, PIECES, hw - SPLIT + 2 * hw // PIECES, cols)
+    whole = lambda *s: vmem(s, lambda t: (0,) * len(s))
+    side = vmem((rows, 2 * cols), lambda t: (0, t))
+    one = vmem((1, rows, hw), lambda t: (0, 0, 0))
     return pl.pallas_call(
         inner_grad_kernel,
-        in_specs=[SMEM] + [vmem()] * 9,
-        out_specs=[vmem()] * 2,
-        out_shape=[jax.ShapeDtypeStruct(shape, LOW)] * 2,
-        scratch_shapes=[pltpu.VMEM((2, hw, width), F32)],
-        compiler_params=pltpu.CompilerParams(vmem_limit_bytes=12 * MIB),
-        cost_estimate=cost(3),
+        grid=(half,),
+        in_specs=[SMEM, whole(2, hw, rows), whole(2, hw, rows), side, side, one, one, whole(2, rows, hw)]
+        + [whole(rows, width)] * 2
+        + [ANYWHERE] * len(after),
+        out_specs=[whole(*first)] * 2 + [whole(*second)] * 2,
+        out_shape=[jax.ShapeDtypeStruct(s, LOW) for s in (first, first, second, second)],
+        scratch_shapes=[pltpu.VMEM((2 * hw, 2 * rows), LOW), pltpu.VMEM((2, hw, width), F32)],
+        compiler_params=pltpu.CompilerParams(vmem_limit_bytes=20 * MIB),
+        cost_estimate=cost(4),
         name="inner_grad",
-    )(place, hidden, hidden_got, inner, inner_got, near, far_got, context_got, attn, attn_got)
+    )(place, *map(far, (hidden, hidden_got, inner, inner_got, near, far_got, context_got, attn, attn_got)), *after)
 
 
 ANYWHERE = pl.BlockSpec(memory_space=pl.ANY)
@@ -499,7 +572,7 @@
         out_specs=[vmem()] * splits,
         out_shape=out_shape,
         compiler_params=pltpu.CompilerParams(vmem_limit_bytes=4 * MIB),
-        cost_estimate=cost(0.3 + 0.3 * len(leads) * count * len(inputs) / 4),
+        cost_estimate=cost(STEP),
         name=name,
     )(place, *inputs, *after)
 
@@ -525,23 +598,28 @@
     )(place, own, got, *after)
 
 
-def inner_place_kernel(spots, place, own, got, *refs):
+def inner_place_kernel(spots_one, spots_two, one, two, own, got, own_two, got_two, *refs):
     inner, attn = refs[-2:]
     hw, cols = inner.shape[0], own.shape[2]
     n = attn.shape[0] // PIECES
-    for i, spot in enumerate(spots):
+    for i in range(PIECES):
         piece = (own[i] if i < 4 else got[i - 4]).astype(F32)
-        here = place[0] ^ spot
-        inner[:, pl.ds(pl.multiple_of(here * cols, 128), cols)] = piece[:hw]
-        attn[pl.ds(pl.multiple_of(here * n, 8), n), :] = jnp.concatenate([piece[hw : hw + n], piece[hw + n :]], 1)
-
-
-def inner_place(spots, place, own, got, hw, after=()):
-    _, tall, cols = own.shape
-    n = (tall - hw) // 2
-    return pl.pallas_call(
-        lambda *refs: inner_place_kernel(spots, *refs),
-        in_specs=[SMEM, vmem(), vmem()] + [ANYWHERE] * len(after),
+        here = one[0] ^ spots_one[i]
+        inner[:SPLIT, pl.ds(pl.multiple_of(here * cols, 128), cols)] = piece
+        piece = (own_two[i] if i < 4 else got_two[i - 4]).astype(F32)
+        here = two[0] ^ spots_two[i]
+        some = hw - SPLIT
+        inner[SPLIT:, pl.ds(pl.multiple_of(here * cols, 128), cols)] = piece[:some]
+        more = jnp.concatenate([piece[some : some + n], piece[some + n :]], 1)
+        attn[pl.ds(pl.multiple_of(here * n, 8), n), :] = more
+
+
+def inner_place(spots_one, spots_two, one, two, parts_one, parts_two, hw, after=()):
+    cols = parts_one[0].shape[2]
+    n = hw // PIECES
+    return pl.pallas_call(
+        lambda *refs: inner_place_kernel(spots_one, spots_two, *refs),
+        in_specs=[SMEM, SMEM] + [vmem()] * 4 + [ANYWHERE] * len(after),
         out_specs=[vmem(), vmem()],
         out_shape=[
             jax.ShapeDtypeStruct((hw, PIECES * cols), F32),
@@ -550,7 +628,7 @@
         compiler_params=pltpu.CompilerParams(vmem_limit_bytes=4 * MIB),
         cost_estimate=cost(2),
         name="inner_place",
-    )(place, own, got, *after)
+    )(one, two, *parts_one, *parts_two, *after)
 
 
 def project_place_kernel(spots, place, own, got, *refs):
@@ -592,23 +670,52 @@
     )(place, own, got, *after)
 
 
-def pair_kernel(near, far, *refs):
-    out = refs[len(refs) // 2]
-    out[0] = near[1]
-    out[1] = far[1]
-
-
-def pair(near, far, gated):
-    return pl.pallas_call(
-        pair_kernel,
-        in_specs=[vmem(), vmem()] + [ANYWHERE] * len(gated),
-        out_specs=[vmem()] + [ANYWHERE] * len(gated),
+def join_kernel(*refs):
+    out, sem = refs[-2:]
+    own, got = refs[:2]
+    n = own.shape[0]
+    copies = [pltpu.make_async_copy(f, out.at[pl.ds(i * n, n)], sem.at[i]) for i, f in enumerate((own, got))]
+    for copy in copies:
+        copy.start()
+    for copy in copies:
+        copy.wait()
+
+
+def join(own, got, after):
+    shape = (2 * own.shape[0],) + own.shape[1:]
+    return pl.pallas_call(
+        join_kernel,
+        in_specs=[ANYWHERE] * (2 + len(after)),
+        out_specs=ANYWHERE,
+        out_shape=jax.ShapeDtypeStruct(shape, own.dtype),
+        scratch_shapes=[pltpu.SemaphoreType.DMA((2,))],
+        compiler_params=pltpu.CompilerParams(vmem_limit_bytes=2 * MIB),
+        cost_estimate=cost(STEP),
+        name="join",
+    )(own, got, *after)
+
+
+def pair_kernel(gates, near, far, *refs):
+    out, sem = refs[-1 - gates - 1], refs[-1]
+    copies = [pltpu.make_async_copy(f.at[1], out.at[i], sem.at[i]) for i, f in enumerate((near, far))]
+    for copy in copies:
+        copy.start()
+    for copy in copies:
+        copy.wait()
+
+
+def pair(near, far, gated, after=()):
+    return pl.pallas_call(
+        lambda *refs: pair_kernel(len(gated), *refs),
+        in_specs=[ANYWHERE] * (2 + len(gated) + len(after)),
+        out_specs=[ANYWHERE] * (1 + len(gated)),
         out_shape=[jax.ShapeDtypeStruct(f.shape, f.dtype) for f in (near, *gated)],
         input_output_aliases={2 + i: 1 + i for i in range(len(gated))},
+        scratch_shapes=[pltpu.SemaphoreType.DMA((2,))],
         compiler_params=pltpu.CompilerParams(vmem_limit_bytes=2 * MIB),
         cost_estimate=cost(0.5),
         name="pair",
-    )(near, far, *gated)
+    )(near, far, *gated, *after)
 
 
 def swap(field, axis, bit):
@@ -654,6 +761,19 @@
         self.arrays = self.arrays + [got]
         return sent
 
+    def start(self, piece):
+        for bit in self.rest:
+            piece = add(piece, swap(piece, "dp", bit))
+        self.own = piece
+        self.got = swap(piece, "dp", self.back[0])
+        self.done = 1
+
+    def grow(self, after):
+        self.own = join(self.own, self.got, after)
+        self.got = swap(self.own, "dp", self.back[self.done])
+        self.done += 1
+        return self.own
+
 
 def local(
     tokens, lengths, query_key_value, query_bias, value_bias, attn_weight, attn_bias, attn_gain,
@@ -679,7 +799,7 @@
     ib = inner_bias.astype(F32).reshape(1, ff)
 
     biases = (query_bias.reshape(1, width), value_bias.reshape(1, width))
-    qkv, lse, w, near, across_heads = attend(where, lengths, shards, query_key_value, *biases)
+    qkv, lse, w, near, across_heads, own_context = attend(where, lengths, shards, query_key_value, *biases)
     far_got = swap(across_heads, "seq", 2)
     (near_send,) = pair(near, far_got, [])
     near_got = swap(near_send, "seq", 1)
@@ -692,8 +812,7 @@
         layer_out, hidden_own, hidden_send, active_own, active_send, slope, grad_outer, grad_two, normal, scale,
         row_sums, wi, wo,
     ) = rows_pass(
-        where, tokens.reshape(rows, width), *context, cotangent.reshape(rows, width), wa, vec, ib, inner_weight,
-        outer_weight,
+        where, tokens.reshape(rows, width), *context, cotangent.reshape(rows, width), wa, vec, ib, inner_weight, outer_weight,
     )
     active_got = swap(active_send, "seq", 1)
     outer_got = swap(grad_outer, "seq", 1)
@@ -701,64 +820,69 @@
     grad_one, grad_inner, grad_attn, near, across_heads, vectors = rows_back(
         where, slope, grad_outer, grad_two, normal, scale, row_sums, wa, vec, wi, wo
     )
-    a = Reduction(["y", 1, 2, 4], [4, 2, 1], lane, me, rest)
-    b = Reduction([2, "y", 1, 4], [4, 1, 2], lane, me, rest)
-    d = Reduction([1, 2, 4], [4, 2, 1], lane, me, rest)
+    a = Reduction([2, "y", 1, 4], [4, 2, 1], lane, me, rest)
+    b = Reduction([1, 2, "y", 4], [1, 2, 4], lane, me, rest)
+    c = Reduction(["y", 4, 1, 2], [4, 1, 2], lane, me, rest)
+    d = Reduction([2, 1, 4], [4, 1, 2], lane, me, rest)
     far_got = swap(across_heads, "seq", 2)
     inner_got = swap(grad_inner, "seq", 1)
     attn_got = swap(grad_attn, "seq", 1)
-    outer_send, outer_keep = outer_grad(active_own, active_got, grad_outer, outer_got)
+    outer_send, outer_keep = outer_grad(a.place, active_own, active_got, grad_outer, outer_got)
     near_send, outer_send = pair(near, far_got, [outer_send])
     near_got = swap(near_send, "seq", 1)
     a.begin(outer_keep, outer_send)
-    inner_send, inner_keep = inner_grad(
-        b.place, hidden_own, hidden_got, grad_inner, inner_got, context[0], context[2], flat(context_got),
-        grad_attn, attn_got,
+    first_send, first_keep, second_send, second_keep = inner_grad(
+        b.place, hidden_own, hidden_got, grad_inner, inner_got, own_context.reshape(1, rows, hw), context[2],
+        flat(context_got),
+        grad_attn, attn_got, [near_send],
     )
-    b.begin(inner_keep, inner_send)
+    b.begin(first_keep, first_send)
+    c.begin(second_keep, second_send)
     grads_h = [f.reshape(2, passages, quarter, hw) for f in (near, near_got, far_got)]
     back_keep, back_send, project_send, project_keep = attend_back(
-        d.place, lengths, shards, w, qkv, lse, grads_h, vectors, [inner_send]
+        d.place, lengths, shards, w, qkv, lse, grads_h, vectors, [second_send]
     )
     d.begin(project_keep, project_send)
     back_got = swap(back_send, "seq", 1)
+    t = a.step([back_keep], name="outer_y")
+    t = b.step([t], name="first_z")
+    t = c.step([t], name="second_m")
+    t = d.step([t], name="project_x")
+    t = a.step([t], name="outer_x")
+    t = b.step([t], name="first_y")
+    t = d.step([t], name="project_m")
+    t = c.step([t], name="second_x")
+    t = a.step([t], name="outer_m")
+    t = b.step([t], name="first_m")
+    project = d.step([t], splits=4, name="project_sum")
+    parts = [project[0]] + [swap(project[j], "seq", j) for j in (1, 2, 3)]
+    t = c.step([project[0]], name="second_z")
+    (t,) = a.step([t], name="outer_sum")
+    a.start(t[0])
+    (t,) = b.step([t], name="first_sum")
+    b.start(t[0])
     (back_sum,) = sum_pieces(
         d.place,
         [f.reshape(2, 1, rows, width) for f in (back_keep, back_got)],
-        [1], 1, False, name="back_y",
+        [1], 1, False, [t], name="back_y",
     )
     back_over = swap(back_sum, "seq", 2)
-    t = a.step([back_sum], name="outer_x")
-    t = d.step([t], name="project_z")
-    t = b.step([t], name="inner_y")
-    t = a.step([t], name="outer_z")
-    t = d.step([t], name="project_zz")
-    t = b.step([t], name="inner_x")
-    t = a.step([t], name="outer_zz")
-    project = d.step([t], splits=4, name="project_sum")
-    t = b.step([project[0]], name="inner_zz")
-    (outer_total,) = a.step([t], name="outer_sum")
-
-    def finish(total):
-        for bit in rest:
-            total = add(total, swap(total, "dp", bit))
-        return total
-
-    def spread(piece, back):
-        for bit in back[:-1]:
-            piece = jnp.concatenate([piece, swap(piece, "dp", bit)], 0)
-        return piece, swap(piece, "dp", back[-1])
-
-    outer_total = spread(finish(outer_total)[0], a.back)
-    project = [finish(p) for p in project]
-    project = [project[0]] + [swap(project[j], "seq", j) for j in (1, 2, 3)]
-    project_total = spread(jnp.concatenate(project, 0)[None], d.back)
-    (inner_total,) = b.step(name="inner_sum")
-    inner_total = spread(finish(inner_total)[0], b.back)
-
-    grad_query_key_value, summed = project_place(d.spots, d.place, *project_total, hw)
-    grad_outer_weight = outer_place(a.spots, a.place, *outer_total)
-    grad_inner_weight, grad_attn_weight = inner_place(b.spots, b.place, *inner_total, hw)
+    d.start(jnp.concatenate(parts, 0)[None])
+    (t,) = c.step([t], name="second_sum")
+    c.start(t[0])
+    t = b.grow([t])
+    t = a.grow([t])
+    t = d.grow([t])
+    t = c.grow([t])
+    t = b.grow([t])
+    t = d.grow([t])
+    t = a.grow([t])
+    t = c.grow([t])
+    grad_query_key_value, summed = project_place(d.spots, d.place, d.own, d.got, hw)
+    grad_outer_weight = outer_place(a.spots, a.place, a.own, a.got)
+    grad_inner_weight, grad_attn_weight = inner_place(
+        b.spots, c.spots, b.place, c.place, (b.own, b.got), (c.own, c.got), hw
+    )
     input_grad = (
         grad_one + back_keep[0].reshape(rows, width).astype(F32)
         + back_got[0].reshape(rows, width).astype(F32)

time: 213 us -> 197 us (0.925)
  waiting for transfers between devices: 111 us -> 67.2 us
  starting transfers between devices: 31 us -> 56.7 us
  Pallas kernels: 55.8 us -> 62.5 us
  local copies, waits for them, and re-layouts: 11.6 us -> 7.68 us
    ppermute x38 -> x45, waiting for transfers between devices: 111 us -> 67.2 us  [swap(): return lax.ppermute(field, axis, [(i, i ^ bit) for i in range(count)])]
    ppermute x38 -> x45, starting transfers between devices: 31 us -> 56.7 us  [swap(): return lax.ppermute(field, axis, [(i, i ^ bit) for i in range(count)])]
    pallas_call x6 -> x14, Pallas kernels: 17.7 us -> 23 us  [the longest x1 8.66 us: rows_pass(): pl.pallas_call(rows_kernel, in_specs=[SMEM, vmem(), HBM, HBM, HBM] + [vme...]
    unnamed x64 -> x62, local copies, waits for them, and re-layouts: 8.78 us -> 4.9 us
    pallas_call x12 -> x16, Pallas kernels: 7.85 us -> 10 us  [sum_pieces(): pl.pallas_call(lambda *refs: sum_kernel(spec, *refs), in_specs=[SMEM] + [...]
  transfers between devices with their start and end apart: 38 -> 45, of which waited for: 24 -> 18; matrix products, arithmetic and copies ran while one was open for 2% -> 2% of each run, Pallas kernels for 14% -> 20%
where the time goes in v3:
time: 197 us
  waiting for transfers between devices  67.2 us (34%)
  Pallas kernels  62.5 us (32%)
  starting transfers between devices  56.7 us (29%)
  local copies, waits for them, and re-layouts  7.68 us (4%)
    ppermute x45, waiting for transfers between devices, swap(): return lax.ppermute(field, axis, [(i, i ^ bit) for i in range(count)])  67.2 us
    ppermute x45, starting transfers between devices, swap(): return lax.ppermute(field, axis, [(i, i ^ bit) for i in range(count)])  56.7 us
    pallas_call x1, Pallas kernels, attend_back(): pl.pallas_call(attend_back_kernel, grid=(passages,), in_specs=[SMEM, SMEM...  12.4 us
    pallas_call x16, Pallas kernels, sum_pieces(): pl.pallas_call(lambda *refs: sum_kernel(spec, *refs), in_specs=[SMEM] + [...  10 us
    pallas_call x1, Pallas kernels, rows_pass(): pl.pallas_call(rows_kernel, in_specs=[SMEM, vmem(), HBM, HBM, HBM] + [vme...  8.66 us
    pallas_call x1, Pallas kernels, attend(): pl.pallas_call(attend_kernel, grid=(passages,), in_specs=[SMEM, SMEM] + [...  8.45 us
    pallas_call x1, Pallas kernels, inner_grad(): pl.pallas_call(inner_grad_kernel, grid=(half,), in_specs=[SMEM, whole(2,...  5.09 us
    unnamed x62, local copies, waits for them, and re-layouts  4.9 us
  transfers between devices with their start and end apart: 45, of which 18 were waited for; matrix products, arithmetic and copies ran while one was open for 2% of the time, Pallas kernels for 20%

profile of v3, /device:TPU:0, one launch (start us, length us, event | category | flops | bytes accessed | tf_op | source)
XLA Modules:
  0.0 196.7 jit_solution(8914413235920919454)
XLA Ops:
  0.6 3.0 %collective-permute-start.1 = (bf16[2,128,768]{2,1,0:T(8,128)(2,1)}, bf16[2,128,768]{2,1,0:T(8,128)(2,1)S(1)}, u32[]{:S(2)}, u32[]{:S(2)}) collective-permute-start(bf16[2,128,768]{2,1,0:T(8,128)(2,1)} %x0.3), channel_id=1, source_target_pairs={{0,2},{1,3},{2,0},{3,1},{4,6},{5,7},{6,4},{7,5},{8,10},{9,11},{10,... | collective-permute-start | bytes 1179656 | tf_op jit(solution)/shard_map/ppermute | solution.py:723
  3.7 9.3 %collective-permute-done.1.x2 = bf16[2,128,768]{2,1,0:T(8,128)(2,1)S(1)} collective-permute-done((bf16[2,128,768]{2,1,0:T(8,128)(2,1)}, bf16[2,128,768]{2,1,0:T(8,128)(2,1)S(1)}, u32[]{:S(2)}, u32[]{:S(2)}) %collective-permute-start.1) | collective-permute-done | bytes 393248 | tf_op jit(solution)/shard_map/ppermute | solution.py:723
  16.2 8.4 %attend.1 = (bf16[2,512,576]{2,1,0:T(8,128)(2,1)}, f32[2,3,512]{2,1,0:T(4,128)}, bf16[768,576]{1,0:T(8,128)(2,1)}, bf16[2,2,128,192]{3,2,1,0:T(8,128)(2,1)S(1)},...) custom-call(s32[1]{0:T(128)} %bitcast.where, s32[2]{0:T(128)S(1)} %copy-done.8, ...), custom_call_target="tpu_custom_call" | custom-call | flops 6325000192 | bytes 20295000 | tf_op jit(solution)/shard_map/attend/pallas_call | solution.py:113
  24.7 1.8 collective-permute-start.3
  26.5 6.8 %collective-permute-done.3.refs_1_ = bf16[2,2,128,192]{3,2,1,0:T(8,128)(2,1)S(1)} collective-permute-done((bf16[2,2,128,192]{3,2,1,0:T(8,128)(2,1)S(1)}, bf16[2,2,128,192]{3,2,1,0:T(8,128)(2,1)S(1)}, u32[]{:S(2)}, u32[]{:S(2)}) %collective-permute-start.3) | collective-permute-done | bytes 196640 | tf_op jit(solution)/shard_map/ppermute | solution.py:723
  34.0 1.3 collective-permute-done.4
  36.0 8.7 %rows_pass.1 = (bf16[256,768]{1,0:T(8,128)(2,1)}, bf16[2,192,256]{2,1,0:T(8,128)(2,1)}, bf16[2,192,256]{2,1,0:T(8,128)(2,1)S(1)}, bf16[256,1536]{1,0:T(8,128)(2,...) custom-call(s32[1]{0:T(128)} %bitcast.where, ...), custom_call_target="tpu_custom_call" | custom-call | flops 6899999744 | bytes 22140000 | tf_op jit(solution)/shard_map/rows_pass/pallas_call | solution.py:348
  45.3 4.5 %rows_back.1 = (f32[256,768]{1,0:T(8,128)}, bf16[256,3072]{1,0:T(8,128)(2,1)}, bf16[256,768]{1,0:T(8,128)(2,1)}, bf16[2,256,192]{2,1,0:T(8,128)(2,1)}, bf16[2,25...) custom-call(s32[1]{0:T(128)} %bitcast.where, f32[4,256,768]{2,1,0:T(8,128)S(1)} %get-tuple-element.63.slope, ...), custom_call_target="tpu_custom_call" | custom-call | flops 5750000128 | bytes 18450000 | tf_op jit(solution)/shard_map/rows_back/pallas_call | solution.py:424
  50.8 1.8 collective-permute-start.5
  52.6 2.4 %collective-permute-done.7.grad_got = bf16[256,768]{1,0:T(8,128)(2,1)S(1)} collective-permute-done((bf16[256,768]{1,0:T(8,128)(2,1)S(1)}, bf16[256,768]{1,0:T(8,128)(2,1)S(1)}, u32[]{:S(2)}, u32[]{:S(2)}) %collective-permute-start.7) | collective-permute-done | bytes 393248 | tf_op jit(solution)/shard_map/ppermute | solution.py:723
  56.0 3.3 %outer_grad.1 = (bf16[2,4,96,768]{3,2,1,0:T(8,128)(2,1)S(1)}, bf16[2,4,96,768]{3,2,1,0:T(8,128)(2,1)S(1)}) custom-call(s32[2]{0:T(128)S(1)} %pad_add_fusion.place.refs_0_, bf16[256,1536]{1,0:T(8,128)(2,1)} %get-tuple-element.77.active, bf16[256,1536]{1,0:T(8,128)(2,1)} %copy-done.20, bf16[256,768]{1,0:T(8,128)(2,1)} %copy-done.3, bf16[256,768]{1,0:T(8,128)(2,1)} %copy-done.24), custom_call_target="tpu_custom_call" | custom-call | flops 6899999744 | bytes 22140000 | tf_op jit(solution)/shard_map/outer_grad/pallas_call | solution.py:457
  60.2 1.8 collective-permute-start.15
  62.9 5.1 %inner_grad.1 = (bf16[2,4,128,384]{3,2,1,0:T(8,128)(2,1)S(1)}, bf16[2,4,128,384]{3,2,1,0:T(8,128)(2,1)S(1)}, bf16[1,8,112,384]{3,2,1,0:T(8,128)(2,1)S(1)}, bf16[1,8,112,384]{3,2,1,0:T(8,128)(2,1)S(1)}) custom-call(s32[2]{0:T(128)S(1)} %pad_add_fusion.1.place.refs_0_, bf16[2,192,256]{2,1,0:T(8,128)(2,1)} %get-tuple-element.82.hidden, ...), custom_call_target="tpu_custom_call" | custom-call | flops 4600000000 | bytes 14760000 | tf_op jit(solution)/shard_map/inner_grad/pallas_call | solution.py:521
  68.0 1.6 collective-permute-start.14
  69.5 1.5 collective-permute-start.19
  71.8 12.4 %attend_back.1 = (bf16[2,2,128,768]{3,2,1,0:T(8,128)(2,1)S(1)}, bf16[2,2,128,768]{3,2,1,0:T(8,128)(2,1)S(1)}, bf16[1,4,96,640]{3,2,1,0:T(8,128)(2,1)S(1)}, bf16[1,4,96,640]{3,2,1,0:T(8,128)(2,1)S(1)}) custom-call(s32[2]{0:T(128)S(1)} %pad_add_fusion.place.refs_0_, s32[2]{0:T(128)S(1)} %copy-done.9, bf16[2,128,768]{2,1,0:T(8,128)(2,1)} %x0.3, ...), custom_call_target="tpu_custom_call" | custom-call | flops 12650000384 | bytes 40590000 | tf_op jit(solution)/shard_map/attend_back/pallas_call | solution.py:217
  84.8 4.2 %collective-permute-done.15.refs_2_ = bf16[2,4,96,768]{3,2,1,0:T(8,128)(2,1)S(1)} collective-permute-done((bf16[2,4,96,768]{3,2,1,0:T(8,128)(2,1)S(1)}, bf16[2,4,96,768]{3,2,1,0:T(8,128)(2,1)S(1)}, u32[]{:S(2)}, u32[]{:S(2)}) %collective-permute-start.15) | collective-permute-done | bytes 1179680 | tf_op jit(solution)/shard_map/ppermute | solution.py:723
  89.7 1.8 collective-permute-start.17
  92.2 1.6 collective-permute-start.16
  94.5 2.6 %collective-permute-start.22 = (bf16[1,4,112,384]{3,2,1,0:T(8,128)(2,1)S(1)}, bf16[1,4,112,384]{3,2,1,0:T(8,128)(2,1)S(1)}, u32[]{:S(2)}, u32[]{:S(2)}) collective-permute-start(bf16[1,4,112,384]{3,2,1,0:T(8,128)(2,1)S(1)} %second_m.1.refs_3_), channel_id=1, source_target_pairs={{0,16},{4,20},{8,24},{12,28},{16,0},{20,4},{24,8},{28,12},{1,17},{... | collective-permute-start | bytes 1032200 | tf_op jit(solution)/shard_map/ppermute | solution.py:723
  97.1 9.8 %collective-permute-done.18.refs_2_ = bf16[1,4,96,640]{3,2,1,0:T(8,128)(2,1)S(1)} collective-permute-done((bf16[1,4,96,640]{3,2,1,0:T(8,128)(2,1)S(1)}, bf16[1,4,96,640]{3,2,1,0:T(8,128)(2,1)S(1)}, u32[]{:S(2)}, u32[]{:S(2)}) %collective-permute-start.18) | collective-permute-done | bytes 491552 | tf_op jit(solution)/shard_map/ppermute | solution.py:723
  107.6 1.8 collective-permute-start.23
  110.4 4.2 %collective-permute-done.16.refs_3_ = bf16[2,2,128,384]{3,2,1,0:T(8,128)(2,1)S(1)} collective-permute-done((bf16[2,2,128,384]{3,2,1,0:T(8,128)(2,1)S(1)}, bf16[2,2,128,384]{3,2,1,0:T(8,128)(2,1)S(1)}, u32[]{:S(2)}, u32[]{:S(2)}) %collective-permute-start.16) | collective-permute-done | bytes 393248 | tf_op jit(solution)/shard_map/ppermute | solution.py:723
  115.2 1.8 collective-permute-start.20
  117.6 1.7 collective-permute-start.27
  120.0 1.6 collective-permute-start.26
  122.2 1.3 collective-permute-start.25
  124.1 4.1 %collective-permute-done.27.refs_4_ = bf16[1,1,96,640]{3,2,1,0:T(8,128)(2,1)S(1)} collective-permute-done((bf16[1,1,96,640]{3,2,1,0:T(8,128)(2,1)S(1)}, bf16[1,1,96,640]{3,2,1,0:T(8,128)(2,1)S(1)}, u32[]{:S(2)}, u32[]{:S(2)}) %collective-permute-start.27) | collective-permute-done | bytes 122912 | tf_op jit(solution)/shard_map/ppermute | solution.py:723
  128.9 1.8 collective-permute-start.29
  132.8 3.7 %collective-permute-start.35 = (bf16[1,1,112,384]{3,2,1,0:T(8,128)(2,1)S(1)}, bf16[1,1,112,384]{3,2,1,0:T(8,128)(2,1)S(1)}, u32[]{:S(2)}, u32[]{:S(2)}) collective-permute-start(bf16[1,1,112,384]{3,2,1,0:T(8,128)(2,1)S(1)} %second_z.1.refs_6_), channel_id=1, source_target_pairs={{0,8},{4,12},{8,0},{12,4},{16,24},{20,28},{24,16},{28,20},{1,9},{5... | collective-permute-start | bytes 258056 | tf_op jit(solution)/shard_map/ppermute | solution.py:723
  138.1 2.1 %collective-permute-start.33 = (bf16[1,96,768]{2,1,0:T(8,128)(2,1)S(1)}, bf16[1,96,768]{2,1,0:T(8,128)(2,1)S(1)}, u32[]{:S(2)}, u32[]{:S(2)}) collective-permute-start(bf16[1,96,768]{2,1,0:T(8,128)(2,1)S(1)} %bitcast.52), channel_id=1, source_target_pairs={{0,16},{4,20},{8,24},{12,28},{16,0},{20,4},{24,8},{28,12},{1,17},{... | collective-permute-start | bytes 442376 | tf_op jit(solution)/shard_map/ppermute | solution.py:723
  141.5 1.1 collective-permute-start.28
  142.6 7.9 %collective-permute-start.34 = (bf16[1,128,384]{2,1,0:T(8,128)(2,1)S(1)}, bf16[1,128,384]{2,1,0:T(8,128)(2,1)S(1)}, u32[]{:S(2)}, u32[]{:S(2)}) collective-permute-start(bf16[1,128,384]{2,1,0:T(8,128)(2,1)S(1)} %bitcast.54), channel_id=1, source_target_pairs={{0,4},{4,0},{8,12},{12,8},{16,20},{20,16},{24,28},{28,24},{1,5},{5... | collective-permute-start | bytes 294920 | tf_op jit(solution)/shard_map/ppermute | solution.py:723
  151.3 1.9 collective-permute-done.34.refs_1_
  153.9 2.0 %collective-permute-start.42 = (bf16[2,96,768]{2,1,0:T(8,128)(2,1)S(1)}, bf16[2,96,768]{2,1,0:T(8,128)(2,1)S(1)}, u32[]{:S(2)}, u32[]{:S(2)}) collective-permute-start(bf16[2,96,768]{2,1,0:T(8,128)(2,1)S(1)} %join.9.refs_2_.refs_0_), channel_id=1, source_target_pairs={{0,8},{4,12},{8,0},{12,4},{16,24},{20,28},{24,16},{28,20},{1,9},{5... | collective-permute-start | bytes 884744 | tf_op jit(solution)/shard_map/ppermute | solution.py:723
  156.3 2.1 %collective-permute-start.36 = (bf16[2,96,640]{2,1,0:T(8,128)(2,1)S(1)}, bf16[2,96,640]{2,1,0:T(8,128)(2,1)S(1)}, u32[]{:S(2)}, u32[]{:S(2)}) collective-permute-start(bf16[2,96,640]{2,1,0:T(8,128)(2,1)S(1)} %join.10.refs_2_.refs_0_), channel_id=1, source_target_pairs={{0,4},{4,0},{8,12},{12,8},{16,20},{20,16},{24,28},{28,24},{1,5},{5... | collective-permute-start | bytes 737288 | tf_op jit(solution)/shard_map/ppermute | solution.py:723
  158.7 2.4 %collective-permute-done.37.refs_1_ = bf16[2,128,384]{2,1,0:T(8,128)(2,1)S(1)} collective-permute-done((bf16[2,128,384]{2,1,0:T(8,128)(2,1)S(1)}, bf16[2,128,384]{2,1,0:T(8,128)(2,1)S(1)}, u32[]{:S(2)}, u32[]{:S(2)}) %collective-permute-start.37) | collective-permute-done | bytes 196640 | tf_op jit(solution)/shard_map/ppermute | solution.py:723
  161.7 2.2 %collective-permute-done.36.refs_1_ = bf16[2,96,640]{2,1,0:T(8,128)(2,1)S(1)} collective-permute-done((bf16[2,96,640]{2,1,0:T(8,128)(2,1)S(1)}, bf16[2,96,640]{2,1,0:T(8,128)(2,1)S(1)}, u32[]{:S(2)}, u32[]{:S(2)}) %collective-permute-start.36) | collective-permute-done | bytes 245792 | tf_op jit(solution)/shard_map/ppermute | solution.py:723
  164.6 1.8 collective-permute-done.42.refs_1_
  167.0 1.0 collective-permute-start.43
  168.1 1.1 collective-permute-start.39
  169.2 3.9 %collective-permute-start.44 = (bf16[4,96,768]{2,1,0:T(8,128)(2,1)S(1)}, bf16[4,96,768]{2,1,0:T(8,128)(2,1)S(1)}, u32[]{:S(2)}, u32[]{:S(2)}) collective-permute-start(bf16[4,96,768]{2,1,0:T(8,128)(2,1)S(1)} %join.14.refs_2_.refs_1_), channel_id=1, source_target_pairs={{0,4},{4,0},{8,12},{12,8},{16,20},{20,16},{24,28},{28,24},{1,5},{5... | collective-permute-start | bytes 1769480 | tf_op jit(solution)/shard_map/ppermute | solution.py:723
  174.1 3.9 %collective-permute-done.40.refs_3_ = bf16[4,128,384]{2,1,0:T(8,128)(2,1)S(1)} collective-permute-done((bf16[4,128,384]{2,1,0:T(8,128)(2,1)S(1)}, bf16[4,128,384]{2,1,0:T(8,128)(2,1)S(1)}, u32[]{:S(2)}, u32[]{:S(2)}) %collective-permute-start.40) | collective-permute-done | bytes 393248 | tf_op jit(solution)/shard_map/ppermute | solution.py:723
  178.0 5.8 %collective-permute-done.43.refs_5_ = bf16[4,112,384]{2,1,0:T(8,128)(2,1)S(1)} collective-permute-done((bf16[4,112,384]{2,1,0:T(8,128)(2,1)S(1)}, bf16[4,112,384]{2,1,0:T(8,128)(2,1)S(1)}, u32[]{:S(2)}, u32[]{:S(2)}) %collective-permute-start.43) | collective-permute-done | bytes 344096 | tf_op jit(solution)/shard_map/ppermute | solution.py:723
  183.8 2.3 %inner_place.1 = (f32[192,3072]{1,0:T(8,128)}, f32[192,768]{1,0:T(8,128)}) custom-call(s32[2]{0:T(128)S(1)} %pad_add_fusion.1.place.refs_0_, s32[2]{0:T(128)S(1)} %pad_add_fusion.2.refs_0_.refs_1_, bf16[4,128,384]{2,1,0:T(8,128)(2,1)S(1)} %join.12.refs_2_, bf16[4,128,384]{2,1,0:T(8,128)(2,1)S(1)} %collective-permute-done.40.refs_3_, ...), custom_call_target="tpu_custom_call" | custom-call | flops 2300000000 | bytes 7380000 | tf_op jit(solution)/shard_map/inner_place/pallas_call | solution.py:620
  186.1 5.2 %collective-permute-done.39.refs_2_ = bf16[4,96,640]{2,1,0:T(8,128)(2,1)S(1)} collective-permute-done((bf16[4,96,640]{2,1,0:T(8,128)(2,1)S(1)}, bf16[4,96,640]{2,1,0:T(8,128)(2,1)S(1)}, u32[]{:S(2)}, u32[]{:S(2)}) %collective-permute-start.39) | collective-permute-done | bytes 491552 | tf_op jit(solution)/shard_map/ppermute | solution.py:723
  191.3 2.0 %project_place.1 = (f32[192,2304]{1,0:T(8,128)}, f32[16,192]{1,0:T(8,128)S(1)}) custom-call(s32[2]{0:T(128)S(1)} %pad_add_fusion.place.refs_0_, bf16[4,96,640]{2,1,0:T(8,128)(2,1)S(1)} %join.13.refs_1_.refs_2_, bf16[4,96,640]{2,1,0:T(8,128)(2,1)S(1)} %collective-permute-done.39.refs_2_), custom_call_target="tpu_custom_call" | custom-call | flops 2300000000 | bytes 7380000 | tf_op jit(solution)/shard_map/project_place/pallas_call | solution.py:658
  194.6 2.1 %outer_place.1 = f32[768,768]{1,0:T(8,128)} custom-call(s32[2]{0:T(128)S(1)} %pad_add_fusion.place.refs_0_, bf16[4,96,768]{2,1,0:T(8,128)(2,1)S(1)} %join.14.refs_2_.refs_1_, bf16[4,96,768]{2,1,0:T(8,128)(2,1)S(1)} %collective-permute-done.44.refs_2_), custom_call_target="tpu_custom_call" | custom-call | flops 2300000000 | bytes 7380000 | tf_op jit(solution)/shard_map/outer_place/pallas_call | solution.py:590
  (160 shorter events, 28.7 us)
Async XLA Ops:
  0.6 12.4 %collective-permute-start.1 = (bf16[2,128,768]{2,1,0:T(8,128)(2,1)}, bf16[2,128,768]{2,1,0:T(8,128)(2,1)S(1)}, u32[]{:S(2)}, u32[]{:S(2)}) collective-permute-start(bf16[2,128,768]{2,1,0:T(8,128)(2,1)} %x0.3), channel_id=1, source_target_pairs={{0,2},{1,3},{2,0},{3,1},{4,6},{5,7},{6,4},{7,5},{8,10},{9,11},{10,... | collective-permute-start | bytes 1179656 | tf_op jit(solution)/shard_map/ppermute | solution.py:723
  3.7 10.7 %collective-permute-start = (bf16[2,128,768]{2,1,0:T(8,128)(2,1)}, bf16[2,128,768]{2,1,0:T(8,128)(2,1)S(1)}, u32[]{:S(2)}, u32[]{:S(2)}) collective-permute-start(bf16[2,128,768]{2,1,0:T(8,128)(2,1)} %x0.3), channel_id=1, source_target_pairs={{0,1},{1,0},{2,3},{3,2},{4,5},{5,4},{6,7},{7,6},{8,9},{9,8},{10,11... | collective-permute-start | bytes 1179656 | tf_op jit(solution)/shard_map/ppermute | solution.py:723
  13.0 1.7 collective-permute-start.2
  24.7 11.3 %copy-start = (bf16[768,768]{1,0:T(8,128)(2,1)S(1)}, bf16[768,768]{1,0:T(8,128)(2,1)}, u32[]{:S(2)}) copy-start(bf16[768,768]{1,0:T(8,128)(2,1)} %param.21) | copy-start | bytes 3538948
  24.7 11.3 %copy-start.1 = (bf16[2,128,768]{2,1,0:T(8,128)(2,1)S(1)}, bf16[2,128,768]{2,1,0:T(8,128)(2,1)}, u32[]{:S(2)}) copy-start(bf16[2,128,768]{2,1,0:T(8,128)(2,1)} %param.31) | copy-start | bytes 1179652
  24.7 11.3 %copy-start.2 = (bf16[2,128,768]{2,1,0:T(8,128)(2,1)S(1)}, bf16[2,128,768]{2,1,0:T(8,128)(2,1)}, u32[]{:S(2)}) copy-start(bf16[2,128,768]{2,1,0:T(8,128)(2,1)} %x0.3) | copy-start | bytes 1179652
  24.7 8.6 %collective-permute-start.3 = (bf16[2,2,128,192]{3,2,1,0:T(8,128)(2,1)S(1)}, bf16[2,2,128,192]{3,2,1,0:T(8,128)(2,1)S(1)}, u32[]{:S(2)}, u32[]{:S(2)}) collective-permute-start(bf16[2,2,128,192]{3,2,1,0:T(8,128)(2,1)S(1)} %get-tuple-element.61), channel_id=1, source_target_pairs={{0,2},{1,3},{2,0},{3,1},{4,6},{5,7},{6,4},{7,5},{8,10},{9,11},{10,... | collective-permute-start | bytes 589832 | tf_op jit(solution)/shard_map/ppermute | solution.py:723
  33.7 1.6 collective-permute-start.4
  49.8 12.2 %collective-permute-start.10 = (bf16[256,3072]{1,0:T(8,128)(2,1)}, bf16[256,3072]{1,0:T(8,128)(2,1)}, u32[]{:S(2)}, u32[]{:S(2)}) collective-permute-start(bf16[256,3072]{1,0:T(8,128)(2,1)} %get-tuple-element.84.inner), channel_id=1, source_target_pairs={{0,1},{1,0},{2,3},{3,2},{4,5},{5,4},{6,7},{7,6},{8,9},{9,8},{10,11... | collective-permute-start | bytes 4718600 | tf_op jit(solution)/shard_map/ppermute | solution.py:723
  50.0 5.1 %collective-permute-start.6 = (bf16[256,1536]{1,0:T(8,128)(2,1)S(1)}, bf16[256,1536]{1,0:T(8,128)(2,1)S(1)}, u32[]{:S(2)}, u32[]{:S(2)}) collective-permute-start(bf16[256,1536]{1,0:T(8,128)(2,1)S(1)} %get-tuple-element.78), channel_id=1, source_target_pairs={{0,1},{1,0},{2,3},{3,2},{4,5},{5,4},{6,7},{7,6},{8,9},{9,8},{10,11... | collective-permute-start | bytes 2359304 | tf_op jit(solution)/shard_map/ppermute | solution.py:723
  50.4 4.6 %collective-permute-start.7 = (bf16[256,768]{1,0:T(8,128)(2,1)S(1)}, bf16[256,768]{1,0:T(8,128)(2,1)S(1)}, u32[]{:S(2)}, u32[]{:S(2)}) collective-permute-start(bf16[256,768]{1,0:T(8,128)(2,1)S(1)} %get-tuple-element.64.outer.grad), channel_id=1, source_target_pairs={{0,1},{1,0},{2,3},{3,2},{4,5},{5,4},{6,7},{7,6},{8,9},{9,8},{10,11... | collective-permute-start | bytes 1179656 | tf_op jit(solution)/shard_map/ppermute | solution.py:723
  50.8 8.6 %collective-permute-start.5 = (bf16[2,256,192]{2,1,0:T(8,128)(2,1)S(1)}, bf16[2,256,192]{2,1,0:T(8,128)(2,1)S(1)}, u32[]{:S(2)}, u32[]{:S(2)}) collective-permute-start(bf16[2,256,192]{2,1,0:T(8,128)(2,1)S(1)} %get-tuple-element.76), channel_id=1, source_target_pairs={{0,2},{1,3},{2,0},{3,1},{4,6},{5,7},{6,4},{7,5},{8,10},{9,11},{10,... | collective-permute-start | bytes 589832 | tf_op jit(solution)/shard_map/ppermute | solution.py:723
  52.5 7.7 %collective-permute-start.9 = (bf16[2,192,256]{2,1,0:T(8,128)(2,1)S(1)}, bf16[2,192,256]{2,1,0:T(8,128)(2,1)S(1)}, u32[]{:S(2)}, u32[]{:S(2)}) collective-permute-start(bf16[2,192,256]{2,1,0:T(8,128)(2,1)S(1)} %copy-done.7), channel_id=1, source_target_pairs={{0,1},{1,0},{2,3},{3,2},{4,5},{5,4},{6,7},{7,6},{8,9},{9,8},{10,11... | collective-permute-start | bytes 589832 | tf_op jit(solution)/shard_map/ppermute | solution.py:723
  55.0 7.0 %collective-permute-start.12 = (bf16[256,768]{1,0:T(8,128)(2,1)}, bf16[256,768]{1,0:T(8,128)(2,1)S(1)}, u32[]{:S(2)}, u32[]{:S(2)}) collective-permute-start(bf16[256,768]{1,0:T(8,128)(2,1)} %get-tuple-element.86.attn), channel_id=1, source_target_pairs={{0,1},{1,0},{2,3},{3,2},{4,5},{5,4},{6,7},{7,6},{8,9},{9,8},{10,11... | collective-permute-start | bytes 1179656 | tf_op jit(solution)/shard_map/ppermute | solution.py:723
  55.1 6.9 %collective-permute-start.11 = (bf16[2,2,128,192]{3,2,1,0:T(8,128)(2,1)S(1)}, bf16[2,2,128,192]{3,2,1,0:T(8,128)(2,1)S(1)}, u32[]{:S(2)}, u32[]{:S(2)}) collective-permute-start(bf16[2,2,128,192]{3,2,1,0:T(8,128)(2,1)S(1)} %copy-done.27), channel_id=1, source_target_pairs={{0,1},{1,0},{2,3},{3,2},{4,5},{5,4},{6,7},{7,6},{8,9},{9,8},{10,11... | collective-permute-start | bytes 589832 | tf_op jit(solution)/shard_map/ppermute | solution.py:723
  59.8 11.3 %collective-permute-start.8 = (bf16[2,256,192]{2,1,0:T(8,128)(2,1)S(1)}, bf16[2,256,192]{2,1,0:T(8,128)(2,1)S(1)}, u32[]{:S(2)}, u32[]{:S(2)}) collective-permute-start(bf16[2,256,192]{2,1,0:T(8,128)(2,1)S(1)} %get-tuple-element.80.refs_0_), channel_id=1, source_target_pairs={{0,1},{1,0},{2,3},{3,2},{4,5},{5,4},{6,7},{7,6},{8,9},{9,8},{10,11... | collective-permute-start | bytes 589832 | tf_op jit(solution)/shard_map/ppermute | solution.py:723
  60.2 28.8 %collective-permute-start.15 = (bf16[2,4,96,768]{3,2,1,0:T(8,128)(2,1)S(1)}, bf16[2,4,96,768]{3,2,1,0:T(8,128)(2,1)S(1)}, u32[]{:S(2)}, u32[]{:S(2)}) collective-permute-start(bf16[2,4,96,768]{3,2,1,0:T(8,128)(2,1)S(1)} %get-tuple-element.93), channel_id=1, source_target_pairs={{0,8},{4,12},{8,0},{12,4},{16,24},{20,28},{24,16},{28,20},{1,9},{5... | collective-permute-start | bytes 3538952 | tf_op jit(solution)/shard_map/ppermute | solution.py:723
  68.0 23.5 %collective-permute-start.14 = (bf16[2,4,128,384]{3,2,1,0:T(8,128)(2,1)S(1)}, bf16[2,4,128,384]{3,2,1,0:T(8,128)(2,1)S(1)}, u32[]{:S(2)}, u32[]{:S(2)}) collective-permute-start(bf16[2,4,128,384]{3,2,1,0:T(8,128)(2,1)S(1)} %get-tuple-element.91), channel_id=1, source_target_pairs={{0,4},{4,0},{8,12},{12,8},{16,20},{20,16},{24,28},{28,24},{1,5},{5... | collective-permute-start | bytes 2359304 | tf_op jit(solution)/shard_map/ppermute | solution.py:723
  69.5 24.3 %collective-permute-start.19 = (bf16[1,8,112,384]{3,2,1,0:T(8,128)(2,1)S(1)}, bf16[1,8,112,384]{3,2,1,0:T(8,128)(2,1)S(1)}, u32[]{:S(2)}, u32[]{:S(2)}) collective-permute-start(bf16[1,8,112,384]{3,2,1,0:T(8,128)(2,1)S(1)} %get-tuple-element.87.refs_0_), channel_id=1, source_target_pairs={{0,2},{1,3},{2,0},{3,1},{4,6},{5,7},{6,4},{7,5},{8,10},{9,11},{10,... | collective-permute-start | bytes 2064392 | tf_op jit(solution)/shard_map/ppermute | solution.py:723
  84.2 56.7 %collective-permute-start.13 = (bf16[2,2,128,768]{3,2,1,0:T(8,128)(2,1)S(1)}, bf16[2,2,128,768]{3,2,1,0:T(8,128)(2,1)S(1)}, u32[]{:S(2)}, u32[]{:S(2)}) collective-permute-start(bf16[2,2,128,768]{3,2,1,0:T(8,128)(2,1)S(1)} %get-tuple-element.89), channel_id=1, source_target_pairs={{0,1},{1,0},{2,3},{3,2},{4,5},{5,4},{6,7},{7,6},{8,9},{9,8},{10,11... | collective-permute-start | bytes 2359304 | tf_op jit(solution)/shard_map/ppermute | solution.py:723
  84.3 22.6 %collective-permute-start.18 = (bf16[1,4,96,640]{3,2,1,0:T(8,128)(2,1)S(1)}, bf16[1,4,96,640]{3,2,1,0:T(8,128)(2,1)S(1)}, u32[]{:S(2)}, u32[]{:S(2)}) collective-permute-start(bf16[1,4,96,640]{3,2,1,0:T(8,128)(2,1)S(1)} %get-tuple-element.95), channel_id=1, source_target_pairs={{0,8},{4,12},{8,0},{12,4},{16,24},{20,28},{24,16},{28,20},{1,9},{5... | collective-permute-start | bytes 1474568 | tf_op jit(solution)/shard_map/ppermute | solution.py:723
  89.7 19.6 %collective-permute-start.17 = (bf16[1,4,96,768]{3,2,1,0:T(8,128)(2,1)S(1)}, bf16[1,4,96,768]{3,2,1,0:T(8,128)(2,1)S(1)}, u32[]{:S(2)}, u32[]{:S(2)}) collective-permute-start(bf16[1,4,96,768]{3,2,1,0:T(8,128)(2,1)S(1)} %outer_y.1.refs_3_), channel_id=1, source_target_pairs={{0,2},{1,3},{2,0},{3,1},{4,6},{5,7},{6,4},{7,5},{8,10},{9,11},{10,... | collective-permute-start | bytes 1769480 | tf_op jit(solution)/shard_map/ppermute | solution.py:723
  92.2 22.4 %collective-permute-start.16 = (bf16[2,2,128,384]{3,2,1,0:T(8,128)(2,1)S(1)}, bf16[2,2,128,384]{3,2,1,0:T(8,128)(2,1)S(1)}, u32[]{:S(2)}, u32[]{:S(2)}) collective-permute-start(bf16[2,2,128,384]{3,2,1,0:T(8,128)(2,1)S(1)} %first_z.1.refs_3_), channel_id=1, source_target_pairs={{0,8},{4,12},{8,0},{12,4},{16,24},{20,28},{24,16},{28,20},{1,9},{5... | collective-permute-start | bytes 1179656 | tf_op jit(solution)/shard_map/ppermute | solution.py:723
  94.5 24.9 %collective-permute-start.22 = (bf16[1,4,112,384]{3,2,1,0:T(8,128)(2,1)S(1)}, bf16[1,4,112,384]{3,2,1,0:T(8,128)(2,1)S(1)}, u32[]{:S(2)}, u32[]{:S(2)}) collective-permute-start(bf16[1,4,112,384]{3,2,1,0:T(8,128)(2,1)S(1)} %second_m.1.refs_3_), channel_id=1, source_target_pairs={{0,16},{4,20},{8,24},{12,28},{16,0},{20,4},{24,8},{28,12},{1,17},{... | collective-permute-start | bytes 1032200 | tf_op jit(solution)/shard_map/ppermute | solution.py:723
  107.6 9.4 %collective-permute-start.23 = (bf16[1,2,96,640]{3,2,1,0:T(8,128)(2,1)S(1)}, bf16[1,2,96,640]{3,2,1,0:T(8,128)(2,1)S(1)}, u32[]{:S(2)}, u32[]{:S(2)}) collective-permute-start(bf16[1,2,96,640]{3,2,1,0:T(8,128)(2,1)S(1)} %project_x.1.refs_4_), channel_id=1, source_target_pairs={{0,4},{4,0},{8,12},{12,8},{16,20},{20,16},{24,28},{28,24},{1,5},{5... | collective-permute-start | bytes 737288 | tf_op jit(solution)/shard_map/ppermute | solution.py:723
  110.0 11.5 %collective-permute-start.21 = (bf16[1,2,96,768]{3,2,1,0:T(8,128)(2,1)S(1)}, bf16[1,2,96,768]{3,2,1,0:T(8,128)(2,1)S(1)}, u32[]{:S(2)}, u32[]{:S(2)}) collective-permute-start(bf16[1,2,96,768]{3,2,1,0:T(8,128)(2,1)S(1)} %outer_x.1.refs_4_), channel_id=1, source_target_pairs={{0,4},{4,0},{8,12},{12,8},{16,20},{20,16},{24,28},{28,24},{1,5},{5... | collective-permute-start | bytes 884744 | tf_op jit(solution)/shard_map/ppermute | solution.py:723
  115.2 8.2 %collective-permute-start.20 = (bf16[1,2,128,384]{3,2,1,0:T(8,128)(2,1)S(1)}, bf16[1,2,128,384]{3,2,1,0:T(8,128)(2,1)S(1)}, u32[]{:S(2)}, u32[]{:S(2)}) collective-permute-start(bf16[1,2,128,384]{3,2,1,0:T(8,128)(2,1)S(1)} %first_y.1.refs_4_), channel_id=1, source_target_pairs={{0,2},{1,3},{2,0},{3,1},{4,6},{5,7},{6,4},{7,5},{8,10},{9,11},{10,... | collective-permute-start | bytes 589832 | tf_op jit(solution)/shard_map/ppermute | solution.py:723
  117.6 10.6 %collective-permute-start.27 = (bf16[1,1,96,640]{3,2,1,0:T(8,128)(2,1)S(1)}, bf16[1,1,96,640]{3,2,1,0:T(8,128)(2,1)S(1)}, u32[]{:S(2)}, u32[]{:S(2)}) collective-permute-start(bf16[1,1,96,640]{3,2,1,0:T(8,128)(2,1)S(1)} %project_m.1.refs_4_), channel_id=1, source_target_pairs={{0,16},{4,20},{8,24},{12,28},{16,0},{20,4},{24,8},{28,12},{1,17},{... | collective-permute-start | bytes 368648 | tf_op jit(solution)/shard_map/ppermute | solution.py:723
  120.0 9.0 %collective-permute-start.26 = (bf16[1,2,112,384]{3,2,1,0:T(8,128)(2,1)S(1)}, bf16[1,2,112,384]{3,2,1,0:T(8,128)(2,1)S(1)}, u32[]{:S(2)}, u32[]{:S(2)}) collective-permute-start(bf16[1,2,112,384]{3,2,1,0:T(8,128)(2,1)S(1)} %second_x.1.refs_5_), channel_id=1, source_target_pairs={{0,4},{4,0},{8,12},{12,8},{16,20},{20,16},{24,28},{28,24},{1,5},{5... | collective-permute-start | bytes 516104 | tf_op jit(solution)/shard_map/ppermute | solution.py:723
  122.2 15.3 %collective-permute-start.25 = (bf16[1,1,96,768]{3,2,1,0:T(8,128)(2,1)S(1)}, bf16[1,1,96,768]{3,2,1,0:T(8,128)(2,1)S(1)}, u32[]{:S(2)}, u32[]{:S(2)}) collective-permute-start(bf16[1,1,96,768]{3,2,1,0:T(8,128)(2,1)S(1)} %outer_m.1.refs_5_), channel_id=1, source_target_pairs={{0,16},{4,20},{8,24},{12,28},{16,0},{20,4},{24,8},{28,12},{1,17},{... | collective-permute-start | bytes 442376 | tf_op jit(solution)/shard_map/ppermute | solution.py:723
  128.8 3.4 %collective-permute-start.31 = (bf16[24,640]{1,0:T(8,128)(2,1)S(1)}, bf16[24,640]{1,0:T(8,128)(2,1)S(1)}, u32[]{:S(2)}, u32[]{:S(2)}) collective-permute-start(bf16[24,640]{1,0:T(8,128)(2,1)S(1)} %get-tuple-element.100), channel_id=1, source_target_pairs={{0,3},{1,2},{2,1},{3,0},{4,7},{5,6},{6,5},{7,4},{8,11},{9,10},{10,... | collective-permute-start | bytes 92168 | tf_op jit(solution)/shard_map/ppermute | solution.py:723
  128.8 4.0 %collective-permute-start.30 = (bf16[24,640]{1,0:T(8,128)(2,1)S(1)}, bf16[24,640]{1,0:T(8,128)(2,1)S(1)}, u32[]{:S(2)}, u32[]{:S(2)}) collective-permute-start(bf16[24,640]{1,0:T(8,128)(2,1)S(1)} %get-tuple-element.99), channel_id=1, source_target_pairs={{0,2},{1,3},{2,0},{3,1},{4,6},{5,7},{6,4},{7,5},{8,10},{9,11},{10,... | collective-permute-start | bytes 92168 | tf_op jit(solution)/shard_map/ppermute | solution.py:723
  128.9 7.6 %collective-permute-start.29 = (bf16[24,640]{1,0:T(8,128)(2,1)S(1)}, bf16[24,640]{1,0:T(8,128)(2,1)S(1)}, u32[]{:S(2)}, u32[]{:S(2)}) collective-permute-start(bf16[24,640]{1,0:T(8,128)(2,1)S(1)} %get-tuple-element.98), channel_id=1, source_target_pairs={{0,1},{1,0},{2,3},{3,2},{4,5},{5,4},{6,7},{7,6},{8,9},{9,8},{10,11... | collective-permute-start | bytes 92168 | tf_op jit(solution)/shard_map/ppermute | solution.py:723
  132.2 8.1 %collective-permute-start.24 = (bf16[1,1,128,384]{3,2,1,0:T(8,128)(2,1)S(1)}, bf16[1,1,128,384]{3,2,1,0:T(8,128)(2,1)S(1)}, u32[]{:S(2)}, u32[]{:S(2)}) collective-permute-start(bf16[1,1,128,384]{3,2,1,0:T(8,128)(2,1)S(1)} %first_m.1.refs_5_), channel_id=1, source_target_pairs={{0,16},{4,20},{8,24},{12,28},{16,0},{20,4},{24,8},{28,12},{1,17},{... | collective-permute-start | bytes 294920 | tf_op jit(solution)/shard_map/ppermute | solution.py:723
  132.8 17.7 %collective-permute-start.35 = (bf16[1,1,112,384]{3,2,1,0:T(8,128)(2,1)S(1)}, bf16[1,1,112,384]{3,2,1,0:T(8,128)(2,1)S(1)}, u32[]{:S(2)}, u32[]{:S(2)}) collective-permute-start(bf16[1,1,112,384]{3,2,1,0:T(8,128)(2,1)S(1)} %second_z.1.refs_6_), channel_id=1, source_target_pairs={{0,8},{4,12},{8,0},{12,4},{16,24},{20,28},{24,16},{28,20},{1,9},{5... | collective-permute-start | bytes 258056 | tf_op jit(solution)/shard_map/ppermute | solution.py:723
  136.6 19.4 %collective-permute-start.32 = (bf16[1,96,640]{2,1,0:T(8,128)(2,1)S(1)}, bf16[1,96,640]{2,1,0:T(8,128)(2,1)S(1)}, u32[]{:S(2)}, u32[]{:S(2)}) collective-permute-start(bf16[1,96,640]{2,1,0:T(8,128)(2,1)S(1)} %maximum_bitcast_fusion.refs_0_), channel_id=1, source_target_pairs={{0,16},{4,20},{8,24},{12,28},{16,0},{20,4},{24,8},{28,12},{1,17},{... | collective-permute-start | bytes 368648 | tf_op jit(solution)/shard_map/ppermute | solution.py:723
  138.1 15.3 %collective-permute-start.33 = (bf16[1,96,768]{2,1,0:T(8,128)(2,1)S(1)}, bf16[1,96,768]{2,1,0:T(8,128)(2,1)S(1)}, u32[]{:S(2)}, u32[]{:S(2)}) collective-permute-start(bf16[1,96,768]{2,1,0:T(8,128)(2,1)S(1)} %bitcast.52), channel_id=1, source_target_pairs={{0,16},{4,20},{8,24},{12,28},{16,0},{20,4},{24,8},{28,12},{1,17},{... | collective-permute-start | bytes 442376 | tf_op jit(solution)/shard_map/ppermute | solution.py:723
  141.5 31.5 %collective-permute-start.28 = (bf16[1,1,256,768]{3,2,1,0:T(8,128)(2,1)S(1)}, bf16[1,1,256,768]{3,2,1,0:T(8,128)(2,1)S(1)}, u32[]{:S(2)}, u32[]{:S(2)}) collective-permute-start(bf16[1,1,256,768]{3,2,1,0:T(8,128)(2,1)S(1)} %back_y.1), channel_id=1, source_target_pairs={{0,2},{1,3},{2,0},{3,1},{4,6},{5,7},{6,4},{7,5},{8,10},{9,11},{10,... | collective-permute-start | bytes 1179656 | tf_op jit(solution)/shard_map/ppermute | solution.py:723
  142.6 10.5 %collective-permute-start.34 = (bf16[1,128,384]{2,1,0:T(8,128)(2,1)S(1)}, bf16[1,128,384]{2,1,0:T(8,128)(2,1)S(1)}, u32[]{:S(2)}, u32[]{:S(2)}) collective-permute-start(bf16[1,128,384]{2,1,0:T(8,128)(2,1)S(1)} %bitcast.54), channel_id=1, source_target_pairs={{0,4},{4,0},{8,12},{12,8},{16,20},{20,16},{24,28},{28,24},{1,5},{5... | collective-permute-start | bytes 294920 | tf_op jit(solution)/shard_map/ppermute | solution.py:723
  151.2 7.2 %collective-permute-start.38 = (bf16[1,112,384]{2,1,0:T(8,128)(2,1)S(1)}, bf16[1,112,384]{2,1,0:T(8,128)(2,1)S(1)}, u32[]{:S(2)}, u32[]{:S(2)}) collective-permute-start(bf16[1,112,384]{2,1,0:T(8,128)(2,1)S(1)} %bitcast.56), channel_id=1, source_target_pairs={{0,16},{4,20},{8,24},{12,28},{16,0},{20,4},{24,8},{28,12},{1,17},{... | collective-permute-start | bytes 258056 | tf_op jit(solution)/shard_map/ppermute | solution.py:723
  153.4 7.7 %collective-permute-start.37 = (bf16[2,128,384]{2,1,0:T(8,128)(2,1)S(1)}, bf16[2,128,384]{2,1,0:T(8,128)(2,1)S(1)}, u32[]{:S(2)}, u32[]{:S(2)}) collective-permute-start(bf16[2,128,384]{2,1,0:T(8,128)(2,1)S(1)} %join.8.refs_2_.refs_0_), channel_id=1, source_target_pairs={{0,8},{4,12},{8,0},{12,4},{16,24},{20,28},{24,16},{28,20},{1,9},{5... | collective-permute-start | bytes 589832 | tf_op jit(solution)/shard_map/ppermute | solution.py:723
  153.9 12.4 %collective-permute-start.42 = (bf16[2,96,768]{2,1,0:T(8,128)(2,1)S(1)}, bf16[2,96,768]{2,1,0:T(8,128)(2,1)S(1)}, u32[]{:S(2)}, u32[]{:S(2)}) collective-permute-start(bf16[2,96,768]{2,1,0:T(8,128)(2,1)S(1)} %join.9.refs_2_.refs_0_), channel_id=1, source_target_pairs={{0,8},{4,12},{8,0},{12,4},{16,24},{20,28},{24,16},{28,20},{1,9},{5... | collective-permute-start | bytes 884744 | tf_op jit(solution)/shard_map/ppermute | solution.py:723
  156.3 7.6 %collective-permute-start.36 = (bf16[2,96,640]{2,1,0:T(8,128)(2,1)S(1)}, bf16[2,96,640]{2,1,0:T(8,128)(2,1)S(1)}, u32[]{:S(2)}, u32[]{:S(2)}) collective-permute-start(bf16[2,96,640]{2,1,0:T(8,128)(2,1)S(1)} %join.10.refs_2_.refs_0_), channel_id=1, source_target_pairs={{0,4},{4,0},{8,12},{12,8},{16,20},{20,16},{24,28},{28,24},{1,5},{5... | collective-permute-start | bytes 737288 | tf_op jit(solution)/shard_map/ppermute | solution.py:723
  158.6 7.9 %collective-permute-start.41 = (bf16[2,112,384]{2,1,0:T(8,128)(2,1)S(1)}, bf16[2,112,384]{2,1,0:T(8,128)(2,1)S(1)}, u32[]{:S(2)}, u32[]{:S(2)}) collective-permute-start(bf16[2,112,384]{2,1,0:T(8,128)(2,1)S(1)} %join.11.refs_2_.refs_0_), channel_id=1, source_target_pairs={{0,4},{4,0},{8,12},{12,8},{16,20},{20,16},{24,28},{28,24},{1,5},{5... | collective-permute-start | bytes 516104 | tf_op jit(solution)/shard_map/ppermute | solution.py:723
  161.6 16.4 %collective-permute-start.40 = (bf16[4,128,384]{2,1,0:T(8,128)(2,1)S(1)}, bf16[4,128,384]{2,1,0:T(8,128)(2,1)S(1)}, u32[]{:S(2)}, u32[]{:S(2)}) collective-permute-start(bf16[4,128,384]{2,1,0:T(8,128)(2,1)S(1)} %join.12.refs_2_), channel_id=1, source_target_pairs={{0,16},{4,20},{8,24},{12,28},{16,0},{20,4},{24,8},{28,12},{1,17},{... | collective-permute-start | bytes 1179656 | tf_op jit(solution)/shard_map/ppermute | solution.py:723
  167.0 16.8 %collective-permute-start.43 = (bf16[4,112,384]{2,1,0:T(8,128)(2,1)S(1)}, bf16[4,112,384]{2,1,0:T(8,128)(2,1)S(1)}, u32[]{:S(2)}, u32[]{:S(2)}) collective-permute-start(bf16[4,112,384]{2,1,0:T(8,128)(2,1)S(1)} %join.15.refs_4_), channel_id=1, source_target_pairs={{0,8},{4,12},{8,0},{12,4},{16,24},{20,28},{24,16},{28,20},{1,9},{5... | collective-permute-start | bytes 1032200 | tf_op jit(solution)/shard_map/ppermute | solution.py:723
  168.1 23.2 %collective-permute-start.39 = (bf16[4,96,640]{2,1,0:T(8,128)(2,1)S(1)}, bf16[4,96,640]{2,1,0:T(8,128)(2,1)S(1)}, u32[]{:S(2)}, u32[]{:S(2)}) collective-permute-start(bf16[4,96,640]{2,1,0:T(8,128)(2,1)S(1)} %join.13.refs_1_.refs_2_), channel_id=1, source_target_pairs={{0,8},{4,12},{8,0},{12,4},{16,24},{20,28},{24,16},{28,20},{1,9},{5... | collective-permute-start | bytes 1474568 | tf_op jit(solution)/shard_map/ppermute | solution.py:723
  169.2 25.4 %collective-permute-start.44 = (bf16[4,96,768]{2,1,0:T(8,128)(2,1)S(1)}, bf16[4,96,768]{2,1,0:T(8,128)(2,1)S(1)}, u32[]{:S(2)}, u32[]{:S(2)}) collective-permute-start(bf16[4,96,768]{2,1,0:T(8,128)(2,1)S(1)} %join.14.refs_2_.refs_1_), channel_id=1, source_target_pairs={{0,4},{4,0},{8,12},{12,8},{16,20},{20,16},{24,28},{28,24},{1,5},{5... | collective-permute-start | bytes 1769480 | tf_op jit(solution)/shard_map/ppermute | solution.py:723
  (28 other events, 137.5 us)

commit v4 on v3

v4 whole, which is shorter than its diff:
```python
import jax
import jax.numpy as jnp
from jax import lax
from jax.experimental import pallas as pl
from jax.experimental.pallas import tpu as pltpu
from jax.sharding import PartitionSpec as P

H = 12
HD = 64
EPS = 1e-12
F32 = jnp.float32
LOW = jnp.bfloat16
MIB = 1 << 20
PIECES = 8
STEP = 1.0
BACK = 1.0
FORE = 0.1


def cost(us):
    return pl.CostEstimate(flops=int(us * 1.15e9), bytes_accessed=int(us * 3.69e6), transcendentals=0)


def dot(a, b):
    return lax.dot_general(a, b, (((1,), (0,)), ((), ())), preferred_element_type=F32)


def dot_nt(a, b):
    return lax.dot_general(a, b, (((1,), (1,)), ((), ())), preferred_element_type=F32)


def dot_tn(a, b):
    return lax.dot_general(a, b, (((0,), (0,)), ((), ())), preferred_element_type=F32)


def vmem(shape=None, index=None):
    if shape is None:
        return pl.BlockSpec(memory_space=pltpu.VMEM)
    return pl.BlockSpec(shape, index)


SMEM = pl.BlockSpec(memory_space=pltpu.SMEM)
HBM = pl.BlockSpec(memory_space=pltpu.HBM)


def far(array):
    return pltpu.with_memory_space_constraint(array, pltpu.HBM)


def key_mask(me, length, rows, quarter):
    slot = lax.broadcasted_iota(jnp.int32, (rows, 1), 0)
    block = slot // quarter
    return ((block ^ me) * quarter + (slot - block * quarter)) < length


BLOCK = 128


def choose_kernel(where, w_hbm, qb, vb, w_out, bias_out, wide, w_here, sem):
    me = where[0]
    hw = bias_out.shape[1]
    width = wide.shape[1]
    window = wide.shape[2]
    first = pl.multiple_of(me * hw - (me & 1) * HD, 128)
    choose = lambda f: jnp.where((me & 1) == 1, f[:, HD : HD + hw], f[:, :hw])
    copies = []
    for t in range(3):
        at = pl.ds(pl.multiple_of(t * width + first, 128), window)
        copies.append(pltpu.make_async_copy(w_hbm.at[:, at], wide.at[t], sem.at[t]))
        copies[t].start()
    for i, bias in enumerate((qb, vb)):
        bias_out[i : i + 1, :] = choose(bias[:, pl.ds(first, window)].astype(F32))
    for t in range(3):
        copies[t].wait()
        w_here[:, t * hw : (t + 1) * hw] = choose(wide[t])
    copy = pltpu.make_async_copy(w_here, w_out, sem.at[3])
    copy.start()
    copy.wait()


def choose_heads(where, w, qb, vb):
    width = w.shape[0]
    hw = width // 4
    return pl.pallas_call(
        choose_kernel,
        in_specs=[SMEM, HBM, vmem(), vmem()],
        out_specs=[HBM, vmem()],
        out_shape=[pltpu.HBM((width, 3 * hw), LOW), jax.ShapeDtypeStruct((2, hw), F32)],
        scratch_shapes=[
            pltpu.VMEM((3, width, hw + HD), LOW),
            pltpu.VMEM((width, 3 * hw), LOW),
            pltpu.SemaphoreType.DMA((4,)),
        ],
        compiler_params=pltpu.CompilerParams(vmem_limit_bytes=6 * MIB),
        cost_estimate=cost(1.5),
        name="choose_heads",
    )(where, far(w), qb, vb)


def attend_kernel(where, lengths, x0, x1, x2, x3, w_hbm, bias, *refs):
    qkv_out, chance_out, own_out, c1, c2, c3 = refs[:6]
    x, w, qkv_here, chance_here, own_here, load_sem, store_sem = refs[6:]
    me = where[0]
    passages, quarter, width = x0.shape
    rows = 4 * quarter
    hw = w.shape[1] // 3
    heads = hw // HD
    loads = [pltpu.make_async_copy(w_hbm, w, load_sem.at[4 * passages])]
    for p in range(passages):
        for j, shard in enumerate((x0, x1, x2, x3)):
            here = x.at[p, pl.ds(j * quarter, quarter)]
            loads.append(pltpu.make_async_copy(shard.at[p], here, load_sem.at[p * 4 + j]))
    for copy in loads:
        copy.start()
    loads[0].wait()
    stores = []

    def store(here, out):
        stores.append(pltpu.make_async_copy(here, out, store_sem.at[len(stores)]))
        stores[-1].start()

    for p in range(passages):
        for copy in loads[1 + 4 * p : 5 + 4 * p]:
            copy.wait()
        proj = dot(x[p], w[...])
        q = ((proj[:, :hw] + bias[0:1, :]).astype(LOW).astype(F32) * HD ** (-0.5)).astype(LOW)
        k = proj[:, hw : 2 * hw].astype(LOW)
        v = (proj[:, 2 * hw :] + bias[1:2, :]).astype(LOW)
        qkv_here[p] = jnp.concatenate([q, k, v], 1)
        store(qkv_here.at[p], qkv_out.at[p])
        usable = key_mask(me, lengths[p], rows, quarter)
        parts = []
        for h in range(heads):
            cols = slice(h * HD, (h + 1) * HD)
            some = []
            for b in range(rows // BLOCK):
                mine = slice(b * BLOCK, (b + 1) * BLOCK)
                logits = jnp.where(usable, dot_nt(k[:, cols], q[mine, cols]), -1e9)
                highest = jnp.max(logits, 0, keepdims=True)
                weight = jnp.exp(logits - highest)
                total = jnp.sum(weight, 0, keepdims=True)
                chance = (weight * (1.0 / total)).astype(LOW)
                chance_here[p, h, :, mine] = chance
                some.append(dot_tn(chance, v[:, cols]))
            store(chance_here.at[p, h], chance_out.at[p, h])
            parts.append(jnp.concatenate(some, 0))
        context = jnp.concatenate(parts, 1).astype(LOW)
        own_here[p] = context[:quarter]
        store(own_here.at[p], own_out.at[p])
        for j, out in enumerate((c1, c2, c3)):
            out[p] = context[(j + 1) * quarter : (j + 2) * quarter]
    for copy in stores:
        copy.wait()


def attend(where, lengths, shards, w, bias):
    passages, quarter, width = shards[0].shape
    rows = 4 * quarter
    hw = width // 4
    heads = hw // HD
    kinds = [((passages, rows, 3 * hw), LOW), ((passages, heads, rows, rows), LOW), ((passages, quarter, hw), LOW)]
    return pl.pallas_call(
        attend_kernel,
        in_specs=[SMEM, SMEM] + [HBM] * 5 + [vmem()],
        out_specs=[HBM] * 3 + [vmem()] * 3,
        out_shape=[pltpu.HBM(*kind) for kind in kinds] + [jax.ShapeDtypeStruct(*kinds[2])] * 3,
        scratch_shapes=[pltpu.VMEM((passages, rows, width), LOW), pltpu.VMEM((width, 3 * hw), LOW)]
        + [pltpu.VMEM(*kind) for kind in kinds]
        + [pltpu.SemaphoreType.DMA((4 * passages + 1,)), pltpu.SemaphoreType.DMA((passages * (heads + 2),))],
        compiler_params=pltpu.CompilerParams(vmem_limit_bytes=24 * MIB),
        cost_estimate=cost(FORE),
        name="attend",
    )(where, lengths, *map(far, shards), far(w), bias)


def attend_back_kernel(place, *refs):
    x0, x1, x2, x3, w_hbm, qkv_hbm, chance_hbm, near, near_got, far_got, vectors = refs[:11]
    keep_out, send_out, weight_send, weight_keep = refs[-16:-12]
    x, w, qkv, chance, g, extra_here, joined, back, keep_here, acc, load_sem, store_sem = refs[-12:]
    me = place[1]
    quarter, hw = near.shape[2:]
    rows = 4 * quarter
    heads = hw // HD
    wide = 3 * hw
    scale = HD ** (-0.5)
    made = []

    def load(source, here):
        made.append(pltpu.make_async_copy(source, here, load_sem.at[len(made)]))
        return made[-1]

    needs = []
    for p in range(2):
        mine = [load(qkv_hbm.at[p], qkv.at[p])]
        for j, source in enumerate((near.at[0, p], near_got.at[0, p], far_got.at[0, p], near_got.at[1, p])):
            mine.append(load(source, g.at[p, pl.ds(j * quarter, quarter)]))
        needs.append((mine, [load(chance_hbm.at[p, h], chance.at[p, h]) for h in range(heads)]))
    last = [load(w_hbm, w)]
    late = [load(vectors, extra_here)]
    for p in range(2):
        for j, shard in enumerate((x0, x1, x2, x3)):
            late.append(load(shard.at[p], x.at[pl.ds(p * rows + j * quarter, quarter)]))
    for copy in needs[0][0] + needs[0][1]:
        copy.start()
    stores = []
    sums = [0.0, 0.0]
    for p in range(2):
        for copy in needs[p][0]:
            copy.wait()
        for copy in last + needs[1][0] + needs[1][1] if p == 0 else late:
            copy.start()
        grad_q, grad_k, grad_v = [], [], []
        for h in range(heads):
            cols = slice(h * HD, (h + 1) * HD)
            qh, kh, vh = (qkv[p, :, t * hw + h * HD : t * hw + (h + 1) * HD] for t in range(3))
            gh = g[p, :, cols]
            grad_chance = dot_nt(vh, gh)
            needs[p][1][h].wait()
            low = chance[p, h]
            full = low.astype(F32)
            inner = jnp.sum(grad_chance * full, 0, keepdims=True)
            grad_logits = (full * (grad_chance - inner)).astype(LOW)
            grad_q.append(dot_tn(grad_logits, kh) * scale)
            grad_k.append(dot(grad_logits, qh))
            grad_v.append(dot(low, gh))
        some = jnp.concatenate([jnp.concatenate(f, 1).astype(LOW) for f in (grad_q, grad_k, grad_v)], 1)
        joined[p * rows : (p + 1) * rows, :] = some
        sums = [
            total + jnp.sum(some[:, at : at + hw].astype(F32), 0, keepdims=True)
            for total, at in zip(sums, (0, 2 * hw))
        ]
        if p == 0:
            last[0].wait()
        back[p] = dot_nt(some, w[...]).astype(LOW)
        for j in range(4):
            out = send_out if j % 2 else keep_out
            piece = back.at[p, pl.ds(j * quarter, quarter)]
            stores.append(pltpu.make_async_copy(piece, out.at[j // 2, p], store_sem.at[len(stores)]))
            stores[-1].start()
    for copy in late:
        copy.wait()
    acc[:, :wide] = dot_tn(x[...], joined[...])
    spread = []
    for total in sums:
        blank = jnp.zeros_like(total)
        spread.append(jnp.concatenate([jnp.where(me == i, total, blank) for i in range(4)], 1))
    extra = jnp.concatenate([extra_here[:10, :]] + spread + [jnp.zeros((52, extra_here.shape[1]), F32)], 0)
    acc[:, wide:] = extra.T
    half = PIECES // 2
    n = weight_send.shape[2] // 4
    spot = place[0] & half
    for out, first in ((weight_send, spot ^ half), (keep_here, spot)):
        for j in range(4):
            for e in range(half):
                start = pl.multiple_of((me ^ j) * (n * PIECES) + (first + e) * n, 8)
                out[0, e, j * n : (j + 1) * n, :] = acc[pl.ds(start, n), :].astype(LOW)
    stores.append(pltpu.make_async_copy(keep_here, weight_keep, store_sem.at[len(stores)]))
    stores[-1].start()
    for copy in stores:
        copy.wait()


def attend_back(place, shards, w, qkv, chance, grads, vectors, after=()):
    passages, quarter, width = shards[0].shape
    rows = 4 * quarter
    hw = width // 4
    heads = hw // HD
    n = width // (4 * PIECES)
    weight = ((1, PIECES // 2, 4 * n, 3 * hw + 64), LOW)
    back = ((2, passages, quarter, width), LOW)
    scratch = [
        ((passages * rows, width), LOW), ((width, 3 * hw), LOW), ((passages, rows, 3 * hw), LOW),
        ((passages, heads, rows, rows), LOW), ((passages, rows, hw), LOW), (vectors.shape, F32),
        ((passages * rows, 3 * hw), LOW), ((passages, rows, width), LOW), weight, ((width, 3 * hw + 64), F32),
    ]
    arrays = [*shards, w, qkv, chance, *grads, vectors]
    return pl.pallas_call(
        attend_back_kernel,
        in_specs=[SMEM] + [HBM] * len(arrays) + [ANYWHERE] * len(after),
        out_specs=[HBM, HBM, vmem(), HBM],
        out_shape=[pltpu.HBM(*back), pltpu.HBM(*back), jax.ShapeDtypeStruct(*weight), pltpu.HBM(*weight)],
        scratch_shapes=[pltpu.VMEM(*kind) for kind in scratch]
        + [pltpu.SemaphoreType.DMA((passages * (heads + 9) + 2,)), pltpu.SemaphoreType.DMA((4 * passages + 1,))],
        compiler_params=pltpu.CompilerParams(vmem_limit_bytes=32 * MIB),
        cost_estimate=cost(BACK),
        name="attend_back",
    )(place, *map(far, arrays), *after)


def normalise(field):
    centre = field - jnp.mean(field, -1, keepdims=True)
    scale = lax.rsqrt(jnp.mean(centre * centre, -1, keepdims=True) + EPS)
    return centre * scale, scale


def normalise_back(grad, normal, scale):
    return (
        grad
        - jnp.mean(grad, -1, keepdims=True)
        - normal * jnp.mean(grad * normal, -1, keepdims=True)
    ) * scale


def rows_kernel(
    where, x, c0, c1, c2, c3, cot, wa, vec, ib, wi_hbm, wo_hbm,
    layer_out, grad_one_out, active_out, first_out, second_out, left_out, left_send, near_out, sums_out, across_out,
    wi, wo, slope, parts, layer_here, grad_one_here, active_here, first_here, second_here, left_here, near_here,
    sums_here, flipped, load_sem, weight_sem, store_sem, inner_sem,
):
    me = where[0]
    rows, width = x.shape
    chunk = width
    hw = wa.shape[1]
    loads = [pltpu.make_async_copy(f, parts.at[j], load_sem.at[j]) for j, f in enumerate((c0, c1, c2, c3))]
    order = (0, 1, 2, 3)
    weights = []
    for k, c in enumerate(order):
        cols = pl.ds(pl.multiple_of((me ^ c) * chunk, 128), chunk)
        weights.append(pltpu.make_async_copy(wi_hbm.at[:, cols], wi.at[:, cols], weight_sem.at[2 * k]))
        weights.append(pltpu.make_async_copy(wo_hbm.at[cols, :], wo.at[cols, :], weight_sem.at[2 * k + 1]))
    for copy in loads + weights[:2]:
        copy.start()
    stores = [
        pltpu.make_async_copy(here, out, store_sem.at[i])
        for i, (here, out) in enumerate(
            (
                (left_here.at[0], left_out), (left_here.at[1], left_send), (active_here, active_out),
                (first_here, first_out), (layer_here, layer_out), (grad_one_here, grad_one_out),
                (near_here, near_out), (sums_here, sums_out),
            )
        )
    ]
    row = lambda r: vec[r : r + 1, :]
    attn_bias, attn_gain, attn_shift, outer_bias, ffn_gain, ffn_shift = (row(r) for r in range(6))
    sums_here[...] = jnp.zeros_like(sums_here)
    attended = attn_bias + x[...].astype(F32)
    for copy in loads:
        copy.wait()
    for copy in weights[2:4]:
        copy.start()
    for j in range(4):
        attended += dot(parts[j], wa[me ^ j])
    for j in range(4):
        left_here[j & 1, 2 + (j >> 1)] = parts[j].astype(F32).T.astype(LOW)
    normal_one, scale_one = normalise(attended)
    hidden = normal_one * attn_gain + attn_shift
    hidden_low = hidden.astype(LOW)
    flipped[...] = hidden.T
    for j in range(4):
        start = pl.multiple_of((me ^ j) * hw, 64)
        left_here[j & 1, j >> 1] = flipped[pl.ds(start, hw), :].astype(LOW)
    stores[0].start()
    stores[1].start()
    pre_two = hidden + outer_bias
    for k, c in enumerate(order):
        cols = pl.ds(pl.multiple_of((me ^ c) * chunk, 128), chunk)
        for copy in weights[2 * k + 4 : 2 * k + 6]:
            copy.start()
        weights[2 * k].wait()
        u = dot(hidden_low, wi[:, cols]) + ib[:, cols]
        below = 0.5 * (1.0 + lax.erf(u * (0.5**0.5)))
        density = jnp.exp(-0.5 * u * u) * 0.3989422804014327
        active = (u * below).astype(LOW)
        slope[c] = below + u * density
        here = first_here if c & 1 else active_here
        here[:, (c >> 1) * chunk : ((c >> 1) + 1) * chunk] = active
        weights[2 * k + 1].wait()
        pre_two += dot(active, wo[cols, :])
    stores[2].start()
    normal_two, scale_two = normalise(pre_two)
    layer_here[...] = (normal_two * ffn_gain + ffn_shift).astype(LOW)
    stores[4].start()
    dy = cot[...].astype(F32)
    sums_here[4:5, :] = jnp.sum(dy * normal_two, 0, keepdims=True)
    sums_here[5:6, :] = jnp.sum(dy, 0, keepdims=True)
    grad_two = normalise_back(dy * ffn_gain, normal_two, scale_two)
    grad_outer = grad_two.astype(LOW)
    first_here[:, 2 * chunk :] = grad_outer
    stores[3].start()
    sums_here[3:4, :] = jnp.sum(grad_outer.astype(F32), 0, keepdims=True)
    grad_hidden = grad_two
    moved = []
    for c in range(5):
        some = pl.ds(c * chunk, chunk)
        moved.append(pltpu.make_async_copy(second_here.at[:, some], second_out.at[:, some], inner_sem.at[c]))
    for c in range(4):
        cols = slice(c * chunk, (c + 1) * chunk)
        grad_inner = (dot_nt(grad_outer, wo[cols, :]) * slope[me ^ c]).astype(LOW)
        second_here[:, cols] = grad_inner
        moved[c].start()
        column = jnp.sum(grad_inner.astype(F32), 0, keepdims=True)
        for i in range(4):
            sums_here[6 + i : 7 + i, c * hw : (c + 1) * hw] = column[:, i * hw : (i + 1) * hw]
        grad_hidden += dot_nt(grad_inner, wi[:, cols])
    sums_here[1:2, :] = jnp.sum(grad_hidden * normal_one, 0, keepdims=True)
    sums_here[2:3, :] = jnp.sum(grad_hidden, 0, keepdims=True)
    grad_one = normalise_back(grad_hidden * attn_gain, normal_one, scale_one)
    grad_one_here[...] = grad_one
    stores[5].start()
    grad_attn = grad_one.astype(LOW)
    second_here[:, 4 * chunk :] = grad_attn
    moved[4].start()
    sums_here[0:1, :] = jnp.sum(grad_attn.astype(F32), 0, keepdims=True)
    stores[7].start()
    for j in range(2):
        near_here[j] = dot_nt(grad_attn, wa[me ^ j]).astype(LOW)
    stores[6].start()
    for j in range(2):
        across_out[j] = dot_nt(grad_attn, wa[me ^ (j + 2)]).astype(LOW)
    for copy in moved + stores:
        copy.wait()


def rows_pass(where, x, context, cot, wa, vec, ib, wi, wo):
    rows, width = x.shape
    ff = ib.shape[1]
    hw = wa.shape[1]
    kinds = [
        ((rows, width), LOW), ((rows, width), F32), ((rows, 2 * width), LOW), ((rows, 3 * width), LOW),
        ((rows, ff + width), LOW), ((4, hw, rows), LOW), ((4, hw, rows), LOW), ((2, rows, hw), LOW), ((16, width), F32),
    ]
    here = kinds[:5] + [((2, 4, hw, rows), LOW)] + kinds[7:]
    return pl.pallas_call(
        rows_kernel,
        in_specs=[SMEM, vmem()] + [HBM] * 4 + [vmem()] * 4 + [HBM, HBM],
        out_specs=[HBM] * 9 + [vmem()],
        out_shape=[pltpu.HBM(*kind) for kind in kinds] + [jax.ShapeDtypeStruct((2, rows, hw), LOW)],
        scratch_shapes=[
            pltpu.VMEM(wi.shape, LOW),
            pltpu.VMEM(wo.shape, LOW),
            pltpu.VMEM((4, rows, width), F32),
            pltpu.VMEM((4, rows, hw), LOW),
        ]
        + [pltpu.VMEM(*kind) for kind in here]
        + [pltpu.VMEM((width, rows), F32)]
        + [pltpu.SemaphoreType.DMA((n,)) for n in (4, 8, 8, 5)],
        compiler_params=pltpu.CompilerParams(vmem_limit_bytes=36 * MIB),
        cost_estimate=cost(11),
        name="rows_pass",
    )(where, x, *map(far, context), cot, wa, vec, ib, far(wi), far(wo))


def outer_grad_kernel(place, active, active_got, grad, grad_got, send_out, keep_out):
    half = PIECES // 2
    n = grad.shape[1] // PIECES
    right = jnp.concatenate([grad[...], grad_got[...]], 0)
    product = dot_tn(jnp.concatenate([active[...], active_got[...]], 0), right)

    def store(low_out, high_out):
        for e in range(PIECES):
            out = high_out if e >= half else low_out
            out[0, e % half] = product[e * n : (e + 1) * n].astype(LOW)

    high = (place[0] & half) > 0
    pl.when(high)(lambda: store(send_out, keep_out))
    pl.when(jnp.logical_not(high))(lambda: store(keep_out, send_out))


def outer_grad(place, active, first, first_got):
    rows, width = first.shape
    width //= 3
    block = (1, PIECES // 2, width // PIECES, width)
    side = vmem((rows, width), lambda y: (0, y))
    last = vmem((rows, width), lambda y: (0, 2))
    return pl.pallas_call(
        outer_grad_kernel,
        grid=(2,),
        in_specs=[SMEM, side, side, last, last],
        out_specs=[vmem(block, lambda y: (y, 0, 0, 0))] * 2,
        out_shape=[jax.ShapeDtypeStruct((2,) + block[1:], LOW)] * 2,
        compiler_params=pltpu.CompilerParams(vmem_limit_bytes=16 * MIB),
        cost_estimate=cost(30),
        name="outer_grad",
    )(place, far(active), *map(far, (first_got, first, first_got)))


SPLIT = 128
ORDERS = {
    "a": ([2, 1, "y"], 4, [2, 1]),
    "b": ([4, "y", 2], 1, [2, 4]),
    "c": ([1, "y", 2], 4, [2, 1]),
    "d": ([1, 2], 4, [1, 2]),
}
SEQUENCE = "cacdbcadbcabdcbdabda"


def inner_grad_kernel(
    mine, mine_got, inner, inner_got, attn, attn_got, *refs
):
    first_send, first_keep, second_send, second_keep, left, rest = refs[-6:]
    step = pl.program_id(0)
    hw = mine.shape[1]
    rows, width = attn.shape
    half = PIECES // 2
    n = hw // PIECES
    cols = inner.shape[1] // 2

    @pl.when(step == 0)
    def _():
        grads = jnp.concatenate([attn[...], attn_got[...]], 0)
        for y in range(2):
            left[y * hw : (y + 1) * hw, :rows] = mine[y]
            left[y * hw : (y + 1) * hw, rows:] = mine_got[y]
            rest[y] = dot(jnp.concatenate([mine[2 + y], mine_got[2 + y]], 1), grads)

    product = dot(left[...], jnp.concatenate([inner[...], inner_got[...]], 0))

    bits = refs[:2]

    def store(part, send_out, keep_out, which):
        def put(out, y, at, k):
            some = product[y * hw : (y + 1) * hw, k * cols : (k + 1) * cols]
            if part == 0:
                some = some[:SPLIT]
            else:
                more = rest[y, pl.ds(pl.multiple_of((2 * step + k) * n, 8), n), :]
                some = jnp.concatenate([some[SPLIT:], more[:, : width // 2], more[:, width // 2 :]], 0)
            out[at[0], at[1]] = some.astype(LOW)

        if ORDERS[which][0][0] == "y":
            for k in range(2):
                for y, out in enumerate((keep_out, send_out)):
                    put(out, y, (0, 2 * step + k), k)
        else:
            kept = (bits[part][0] & half) == (step >> 1) * half
            for here, out in ((kept, keep_out), (jnp.logical_not(kept), send_out)):

                @pl.when(here)
                def _(out=out):
                    for k in range(2):
                        for y in range(2):
                            put(out, y, (y, 2 * (step & 1) + k), k)

    store(0, first_send, first_keep, "b")
    store(1, second_send, second_keep, "c")


def inner_grad(places, mine, mine_got, second, second_got, after):
    hw = mine.shape[1]
    rows = second.shape[0]
    width = 4 * hw
    half = PIECES // 2
    cols = 4 * width // PIECES
    counts = [(1, PIECES) if ORDERS[which][0][0] == "y" else (2, half) for which in "bc"]
    first = counts[0] + (SPLIT, cols)
    rest = counts[1] + (hw - SPLIT + 2 * hw // PIECES, cols)
    whole = lambda *s: vmem(s, lambda t: (0,) * len(s))
    side = vmem((rows, 2 * cols), lambda t: (0, t))
    last = vmem((rows, width), lambda t: (0, 4))
    return pl.pallas_call(
        inner_grad_kernel,
        grid=(half,),
        in_specs=[whole(4, hw, rows), whole(4, hw, rows), side, side, last, last, SMEM, SMEM]
        + [ANYWHERE] * len(after),
        out_specs=[whole(*first)] * 2 + [whole(*rest)] * 2,
        out_shape=[jax.ShapeDtypeStruct(s, LOW) for s in (first, first, rest, rest)],
        scratch_shapes=[pltpu.VMEM((2 * hw, 2 * rows), LOW), pltpu.VMEM((2, hw, width), F32)],
        compiler_params=pltpu.CompilerParams(vmem_limit_bytes=20 * MIB),
        cost_estimate=cost(4),
        name="inner_grad",
    )(*map(far, (mine, mine_got, second, second_got, second, second_got)), *places, *after)


ANYWHERE = pl.BlockSpec(memory_space=pl.ANY)


def sum_kernel(spec, place, *refs):
    leads, count, flip, inputs, splits = spec
    ins = refs[: len(inputs)]
    outs = refs[-splits:]
    first = (place[0] // count) * count
    if flip:
        first = first ^ count
    for y, lead in enumerate(leads):
        for r in range(count):
            total = None
            for ref in ins:
                pieces = ref.shape[1]
                base = first & (pieces - 1) if count < pieces else 0
                term = ref[lead if ref.shape[0] > 1 else 0, base + r].astype(F32)
                total = term if total is None else total + term
            if splits == 1:
                outs[0][y, r] = total.astype(LOW)
            else:
                n = total.shape[0] // splits
                for j in range(splits):
                    outs[j][r] = total[j * n : (j + 1) * n].astype(LOW)


def sum_pieces(place, inputs, leads, count, flip, after=(), splits=1, name="sum_pieces"):
    tall, wide = inputs[0].shape[2:]
    spec = (tuple(leads), count, flip, tuple(range(len(inputs))), splits)
    if splits == 1:
        out_shape = [jax.ShapeDtypeStruct((len(leads), count, tall, wide), LOW)]
    else:
        out_shape = [jax.ShapeDtypeStruct((count, tall // splits, wide), LOW)] * splits
    return pl.pallas_call(
        lambda *refs: sum_kernel(spec, *refs),
        in_specs=[SMEM] + [vmem()] * len(inputs) + [ANYWHERE] * len(after),
        out_specs=[vmem()] * splits,
        out_shape=out_shape,
        compiler_params=pltpu.CompilerParams(vmem_limit_bytes=4 * MIB),
        cost_estimate=cost(STEP),
        name=name,
    )(place, *inputs, *after)


def outer_place_kernel(spots, place, own, got, *refs):
    out = refs[-1]
    n = own.shape[1]
    for i, spot in enumerate(spots):
        piece = own[i] if i < 4 else got[i - 4]
        out[pl.ds(pl.multiple_of((place[0] ^ spot) * n, 8), n), :] = piece.astype(F32)


def outer_place(spots, place, own, got, after=()):
    n, width = own.shape[1:]
    return pl.pallas_call(
        lambda *refs: outer_place_kernel(spots, *refs),
        in_specs=[SMEM, vmem(), vmem()] + [ANYWHERE] * len(after),
        out_specs=vmem(),
        out_shape=jax.ShapeDtypeStruct((PIECES * n, width), F32),
        compiler_params=pltpu.CompilerParams(vmem_limit_bytes=4 * MIB),
        cost_estimate=cost(2),
        name="outer_place",
    )(place, own, got, *after)


def inner_place_kernel(spots_one, spots_two, one, two, own, got, own_two, got_two, *refs):
    inner, attn = refs[-2:]
    hw, cols = inner.shape[0], own.shape[2]
    n = attn.shape[0] // PIECES
    for i in range(PIECES):
        piece = (own[i] if i < 4 else got[i - 4]).astype(F32)
        here = one[0] ^ spots_one[i]
        inner[:SPLIT, pl.ds(pl.multiple_of(here * cols, 128), cols)] = piece
        piece = (own_two[i] if i < 4 else got_two[i - 4]).astype(F32)
        here = two[0] ^ spots_two[i]
        some = hw - SPLIT
        inner[SPLIT:, pl.ds(pl.multiple_of(here * cols, 128), cols)] = piece[:some]
        more = jnp.concatenate([piece[some : some + n], piece[some + n :]], 1)
        attn[pl.ds(pl.multiple_of(here * n, 8), n), :] = more


def inner_place(spots_one, spots_two, one, two, parts_one, parts_two, hw, after=()):
    cols = parts_one[0].shape[2]
    n = hw // PIECES
    return pl.pallas_call(
        lambda *refs: inner_place_kernel(spots_one, spots_two, *refs),
        in_specs=[SMEM, SMEM] + [vmem()] * 4 + [ANYWHERE] * len(after),
        out_specs=[vmem(), vmem()],
        out_shape=[
            jax.ShapeDtypeStruct((hw, PIECES * cols), F32),
            jax.ShapeDtypeStruct((PIECES * n, 2 * cols), F32),
        ],
        compiler_params=pltpu.CompilerParams(vmem_limit_bytes=4 * MIB),
        cost_estimate=cost(2),
        name="inner_place",
    )(one, two, *parts_one, *parts_two, *after)


def project_place_kernel(spots, place, own, got, *refs):
    out, vectors, tall = refs[-3:]
    n = own.shape[1] // 4
    hw = out.shape[1] // 12
    wide = 3 * hw
    for i, spot in enumerate(spots):
        ref, k = (own, i) if i < 4 else (got, i - 4)
        rows = pl.ds(pl.multiple_of((place[0] ^ spot) * n, 8), n)
        total = None
        for owner in range(4):
            start = pl.multiple_of((owner ^ place[1]) * n, 8)
            block = ref[k, pl.ds(start, n), :].astype(F32)
            for t in range(3):
                at = t * 4 * hw + owner * hw
                out[rows, at : at + hw] = block[:, t * hw : (t + 1) * hw]
            extra = block[:, wide:]
            total = extra if total is None else total + extra
        tall[rows, : total.shape[1]] = total
    vectors[...] = tall[...].T[: vectors.shape[0]]


def project_place(spots, place, own, got, hw, after=()):
    _, tall, wide = own.shape
    n = tall // 4
    return pl.pallas_call(
        lambda *refs: project_place_kernel(spots, *refs),
        in_specs=[SMEM, vmem(), vmem()] + [ANYWHERE] * len(after),
        out_specs=[vmem(), vmem()],
        out_shape=[
            jax.ShapeDtypeStruct((PIECES * n, 12 * hw), F32),
            jax.ShapeDtypeStruct((16, PIECES * n), F32),
        ],
        scratch_shapes=[pltpu.VMEM((PIECES * n, 128), F32)],
        compiler_params=pltpu.CompilerParams(vmem_limit_bytes=4 * MIB),
        cost_estimate=cost(2),
        name="project_place",
    )(place, own, got, *after)


def join_kernel(*refs):
    out, sem = refs[-2:]
    own, got = refs[:2]
    n = own.shape[0]
    copies = [pltpu.make_async_copy(f, out.at[pl.ds(i * n, n)], sem.at[i]) for i, f in enumerate((own, got))]
    for copy in copies:
        copy.start()
    for copy in copies:
        copy.wait()


def join(own, got, after):
    shape = (2 * own.shape[0],) + own.shape[1:]
    return pl.pallas_call(
        join_kernel,
        in_specs=[ANYWHERE] * (2 + len(after)),
        out_specs=ANYWHERE,
        out_shape=jax.ShapeDtypeStruct(shape, own.dtype),
        scratch_shapes=[pltpu.SemaphoreType.DMA((2,))],
        compiler_params=pltpu.CompilerParams(vmem_limit_bytes=2 * MIB),
        cost_estimate=cost(STEP),
        name="join",
    )(own, got, *after)


def pair_kernel(gates, near, far, *refs):
    out, sem = refs[-1 - gates - 1], refs[-1]
    copies = [pltpu.make_async_copy(f.at[1], out.at[i], sem.at[i]) for i, f in enumerate((near, far))]
    for copy in copies:
        copy.start()
    for copy in copies:
        copy.wait()


def pair(near, far, gated, after=()):
    return pl.pallas_call(
        lambda *refs: pair_kernel(len(gated), *refs),
        in_specs=[ANYWHERE] * (2 + len(gated) + len(after)),
        out_specs=[ANYWHERE] * (1 + len(gated)),
        out_shape=[jax.ShapeDtypeStruct(f.shape, f.dtype) for f in (near, *gated)],
        input_output_aliases={2 + i: 1 + i for i in range(len(gated))},
        scratch_shapes=[pltpu.SemaphoreType.DMA((2,))],
        compiler_params=pltpu.CompilerParams(vmem_limit_bytes=2 * MIB),
        cost_estimate=cost(0.5),
        name="pair",
    )(near, far, *gated, *after)


def swap(field, axis, bit):
    count = lax.axis_size(axis)
    return lax.ppermute(field, axis, [(i, i ^ bit) for i in range(count)])


def add(left, right):
    return (left.astype(F32) + right.astype(F32)).astype(LOW)


class Reduction:
    def __init__(self, order, last, back, lane, me, rest):
        self.order = list(order)
        self.last = last
        self.back = list(back)
        self.rest = rest
        bits = [o for o in order if o != "y"]
        weight = {bit: PIECES >> (k + 1) for k, bit in enumerate(bits)}
        spot = sum(jnp.where(lane & bit, w, 0) for bit, w in weight.items())
        weight[last] = 0
        self.spots = [
            i % 2 + sum(weight[bit] for t, bit in enumerate(back) if i >> (t + 1) & 1) for i in range(PIECES)
        ]
        self.own = None
        self.place = jnp.stack([spot.astype(jnp.int32), me.astype(jnp.int32)])

    def begin(self, keep, send):
        axis = self.order.pop(0)
        got = swap(send, "seq", 2) if axis == "y" else swap(send, "dp", axis)
        self.arrays = [keep, got]
        self.left = keep.shape[1]
        self.folded = keep.shape[0] == 1

    def step(self, after=(), splits=1, name="sum"):
        if not self.order and self.last is None:
            return sum_pieces(self.place, self.arrays, [0], self.left, False, after, splits, name)
        leads = [0] if self.folded else [0, 1]
        if not self.order:
            (sent,) = sum_pieces(self.place, self.arrays, [0], self.left, False, after, name=name)
            self.arrays = [sent, swap(sent, "dp", self.last)]
            self.last = None
            return sent
        axis = self.order.pop(0)
        if axis == "y":
            (sent,) = sum_pieces(self.place, self.arrays, [1], self.left, False, after, name=name)
            self.folded = True
            got = swap(sent, "seq", 2)
        else:
            self.left //= 2
            (sent,) = sum_pieces(self.place, self.arrays, leads, self.left, True, after, name=name)
            got = swap(sent, "dp", axis)
        self.arrays = self.arrays + [got]
        return sent

    def start(self, piece):
        for bit in self.rest:
            piece = add(piece, swap(piece, "dp", bit))
        self.own = piece
        self.got = swap(piece, "dp", self.back[0])
        self.done = 1

    def grow(self, after):
        self.own = join(self.own, self.got, after)
        self.got = swap(self.own, "dp", self.back[self.done])
        self.done += 1
        return self.own


def local(
    tokens, lengths, query_key_value, query_bias, value_bias, attn_weight, attn_bias, attn_gain,
    attn_shift, inner_weight, inner_bias, outer_weight, outer_bias, ffn_gain, ffn_shift, cotangent,
):
    groups = lax.axis_size("seq")
    lanes = lax.axis_size("dp")
    me = lax.axis_index("seq")
    lane = lax.axis_index("dp")
    passages, quarter, width = tokens.shape
    hw = H // groups * HD
    rows = passages * quarter
    ff = inner_bias.shape[0]
    rest = [1 << i for i in range(3, lanes.bit_length() - 1)]
    where = me.astype(jnp.int32).reshape(1)

    across = swap(tokens, "seq", 2)
    beside = swap(tokens, "seq", 1)
    corner = swap(across, "seq", 1)
    shards = (tokens, beside, across, corner)
    vec = jnp.stack([attn_bias, attn_gain, attn_shift, outer_bias, ffn_gain, ffn_shift, ffn_shift, ffn_shift])
    vec = vec.astype(F32)
    ib = inner_bias.astype(F32).reshape(1, ff)

    w, bias = choose_heads(where, query_key_value, query_bias.reshape(1, width), value_bias.reshape(1, width))
    qkv, chance, own, *context_h = attend(where, lengths, shards, w, bias)
    context = [own] + [swap(part, "seq", j) for j, part in zip((1, 2, 3), context_h)]
    context = [part.reshape(rows, hw) for part in context]

    wa = attn_weight.reshape(groups, hw, width)
    layer_out, grad_one, active, first, second, mine, mine_send, near, vectors, across_heads = rows_pass(
        where, tokens.reshape(rows, width), context, cotangent.reshape(rows, width), wa, vec, ib, inner_weight,
        outer_weight,
    )
    first_got = swap(first, "seq", 1)
    second_got = swap(second, "seq", 1)
    mine_got = swap(mine_send, "seq", 1)
    a, b, c, d = (Reduction(*ORDERS[which], lane, me, rest) for which in "abcd")
    far_got = swap(across_heads, "seq", 2)
    outer_send, outer_keep = outer_grad(a.place, active, first, first_got)
    (near_send,) = pair(near, far_got, [], [outer_send])
    near_got = swap(near_send, "seq", 1)
    a.begin(outer_keep, outer_send)
    first_send, first_keep, second_send, second_keep = inner_grad(
        [b.place, c.place], mine, mine_got, second, second_got, [near_send]
    )
    b.begin(first_keep, first_send)
    c.begin(second_keep, second_send)
    grads_h = [f.reshape(2, passages, quarter, hw) for f in (near, near_got, far_got)]
    back_keep, back_send, project_send, project_keep = attend_back(
        d.place, shards, w, qkv, chance, grads_h, vectors, [second_send]
    )
    d.begin(project_keep, project_send)
    back_got = swap(back_send, "seq", 1)
    (back_sum,) = sum_pieces(
        d.place,
        [f.reshape(2, 1, rows, width) for f in (back_keep, back_got)],
        [1], 1, False, name="back_y",
    )
    back_over = swap(back_sum, "seq", 2)
    token = back_keep
    parts = None
    for letter in SEQUENCE:
        chunk = {"a": a, "b": b, "c": c, "d": d}[letter]
        if chunk.order or chunk.last is not None:
            token = chunk.step([token], name="sum_" + letter)
        elif chunk.own is not None:
            token = chunk.grow([token])
        elif chunk is d and parts is None:
            parts = d.step([token], splits=4, name="total_d")
            token = parts[0]
            parts = [parts[0]] + [swap(parts[j], "seq", j) for j in (1, 2, 3)]
        elif chunk is d:
            d.start(jnp.concatenate(parts, 1))
        else:
            (token,) = chunk.step([token], name="total_" + letter)
            chunk.start(token[0])
    grad_query_key_value, summed = project_place(d.spots, d.place, d.own, d.got, hw)
    grad_outer_weight = outer_place(a.spots, a.place, a.own, a.got)
    grad_inner_weight, grad_attn_weight = inner_place(
        b.spots, c.spots, b.place, c.place, (b.own, b.got), (c.own, c.got), hw
    )
    input_grad = (
        grad_one + back_keep[0].reshape(rows, width).astype(F32)
        + back_got[0].reshape(rows, width).astype(F32)
        + back_over[0, 0].astype(F32)
    ).astype(LOW)
    return (
        layer_out.reshape(passages, quarter, width),
        input_grad.reshape(passages, quarter, width),
        grad_query_key_value,
        summed[10],
        summed[11],
        grad_attn_weight,
        summed[0],
        summed[1],
        summed[2],
        grad_inner_weight,
        summed[6:10].reshape(-1),
        grad_outer_weight,
        summed[3],
        summed[4],
        summed[5],
    )


def solution(mesh):
    rows = P("dp", "seq", None)
    return jax.shard_map(
        local,
        mesh=mesh,
        in_specs=(rows, P("dp")) + (P(),) * 13 + (rows,),
        out_specs=(
            rows,
            rows,
            P("seq", None),
            P("seq"),
            P("seq"),
            P("seq", None),
            P("seq"),
            P("seq"),
            P("seq"),
            P("seq", None),
            P("seq"),
            P("seq", None),
            P("seq"),
            P("seq"),
            P("seq"),
        ),
        check_vma=False,
    )
```

time: 197 us -> 181 us (0.919)
  starting transfers between devices: 56.7 us -> 38.6 us
    ppermute x45 -> x39, starting transfers between devices: 56.7 us -> 38.6 us  [swap(): return lax.ppermute(field, axis, [(i, i ^ bit) for i in range(count)])]
    ppermute x45 -> x39, waiting for transfers between devices: 67.2 us -> 68.8 us  [swap(): return lax.ppermute(field, axis, [(i, i ^ bit) for i in range(count)])]
    unnamed x62 -> x57, local copies, waits for them, and re-layouts: 4.9 us -> 5.87 us
  transfers between devices with their start and end apart: 45 -> 39, of which waited for: 18 -> 15; matrix products, arithmetic and copies ran while one was open for 2% -> 2% of each run, Pallas kernels for 20% -> 22%
where the time goes in v4:
time: 181 us
  waiting for transfers between devices  68.8 us (38%)
  Pallas kernels  62.5 us (35%)
  starting transfers between devices  38.6 us (21%)
  local copies, waits for them, and re-layouts  8.66 us (5%)
    ppermute x39, waiting for transfers between devices, swap(): return lax.ppermute(field, axis, [(i, i ^ bit) for i in range(count)])  68.8 us
    ppermute x39, starting transfers between devices, swap(): return lax.ppermute(field, axis, [(i, i ^ bit) for i in range(count)])  38.6 us
    pallas_call x1, Pallas kernels, rows_pass(): pl.pallas_call(rows_kernel, in_specs=[SMEM, vmem()] + [HBM] * 4 + [vmem()...  13 us
    pallas_call x1, Pallas kernels, attend_back(): pl.pallas_call(attend_back_kernel, in_specs=[SMEM] + [HBM] * len(arrays)...  12.1 us
    pallas_call x16, Pallas kernels, sum_pieces(): pl.pallas_call(lambda *refs: sum_kernel(spec, *refs), in_specs=[SMEM] + [...  10.1 us
    pallas_call x1, Pallas kernels, attend(): pl.pallas_call(attend_kernel, in_specs=[SMEM, SMEM] + [HBM] * 5 + [vmem()...  7.57 us
    unnamed x57, local copies, waits for them, and re-layouts  5.87 us
    pallas_call x1, Pallas kernels, inner_grad(): pl.pallas_call(inner_grad_kernel, grid=(half,), in_specs=[whole(4, hw, ro...  5.06 us
  transfers between devices with their start and end apart: 39, of which 15 were waited for; matrix products, arithmetic and copies ran while one was open for 2% of the time, Pallas kernels for 22%

profile of v4, /device:TPU:0, one launch (start us, length us, event | category | flops | bytes accessed | tf_op | source)
XLA Modules:
  0.0 181.1 jit_solution(7931495049824360970)
XLA Ops:
  0.6 3.0 %collective-permute-start.1 = (bf16[2,128,768]{2,1,0:T(8,128)(2,1)}, bf16[2,128,768]{2,1,0:T(8,128)(2,1)S(1)}, u32[]{:S(2)}, u32[]{:S(2)}) collective-permute-start(bf16[2,128,768]{2,1,0:T(8,128)(2,1)} %refs_0_.1), channel_id=1, source_target_pairs={{0,2},{1,3},{2,0},{3,1},{4,6},{5,7},{6,4},{7,5},{8,10},{9,11},{10,... | collective-permute-start | bytes 1179656 | tf_op jit(solution)/shard_map/ppermute | solution.py:751
  3.7 9.3 %collective-permute-done.1.x2.refs_2_ = bf16[2,128,768]{2,1,0:T(8,128)(2,1)S(1)} collective-permute-done((bf16[2,128,768]{2,1,0:T(8,128)(2,1)}, bf16[2,128,768]{2,1,0:T(8,128)(2,1)S(1)}, u32[]{:S(2)}, u32[]{:S(2)}) %collective-permute-start.1) | collective-permute-done | bytes 393248 | tf_op jit(solution)/shard_map/ppermute | solution.py:751
  14.4 2.7 %choose_heads.1 = (bf16[768,576]{1,0:T(8,128)(2,1)}, f32[2,192]{1,0:T(2,128)S(1)}) custom-call(s32[1]{0:T(128)} %bitcast.where, bf16[768,2304]{1,0:T(8,128)(2,1)} %w_hbm.1, bf16[1,768]{1,0:T(2,128)(2,1)S(1)} %reshape.97.qb, bf16[1,768]{1,0:T(2,128)(2,1)S(1)} %reshape.98.vb), custom_call_target="tpu_custom_call" | custom-call | flops 1724999936 | bytes 5535000 | tf_op jit(solution)/shard_map/choose_heads/pallas_call | solution.py:84
  17.3 0.7 copy-done.10
  18.2 7.6 %attend.1 = (bf16[2,512,576]{2,1,0:T(8,128)(2,1)}, bf16[2,3,512,512]{3,2,1,0:T(8,128)(2,1)}, bf16[2,128,192]{2,1,0:T(8,128)(2,1)}, bf16[2,128,192]{2,1,0:T(8,128...) custom-call(s32[1]{0:T(128)} %bitcast.where, s32[2]{0:T(128)S(1)} %copy-done.5, ...), custom_call_target="tpu_custom_call" | custom-call | flops 115000000 | bytes 369000 | tf_op jit(solution)/shard_map/attend/pallas_call | solution.py:162
  26.3 1.7 collective-permute-start.4
  28.3 4.2 %collective-permute-done.4 = bf16[2,128,192]{2,1,0:T(8,128)(2,1)S(1)} collective-permute-done((bf16[2,128,192]{2,1,0:T(8,128)(2,1)S(1)}, bf16[2,128,192]{2,1,0:T(8,128)(2,1)S(1)}, u32[]{:S(2)}, u32[]{:S(2)}) %collective-permute-start.4) | collective-permute-done | bytes 98336 | tf_op jit(solution)/shard_map/ppermute | solution.py:751
  32.5 1.3 collective-permute-done.5
  34.5 13.0 %rows_pass.1 = (bf16[256,768]{1,0:T(8,128)(2,1)}, f32[256,768]{1,0:T(8,128)}, bf16[256,1536]{1,0:T(8,128)(2,1)}, bf16[256,2304]{1,0:T(8,128)(2,1)}, bf16[256,384...) custom-call(s32[1]{0:T(128)} %bitcast.where, ...), custom_call_target="tpu_custom_call" | custom-call | flops 12650000384 | bytes 40590000 | tf_op jit(solution)/shard_map/rows_pass/pallas_call | solution.py:423
  48.4 1.7 collective-permute-start.6
  50.9 1.0 copy-done.22
  51.9 3.3 %outer_grad.1 = (bf16[2,4,96,768]{3,2,1,0:T(8,128)(2,1)S(1)}, bf16[2,4,96,768]{3,2,1,0:T(8,128)(2,1)S(1)}) custom-call(s32[2]{0:T(128)S(1)} %pad_add_fusion.1.place.refs_0_, bf16[256,1536]{1,0:T(8,128)(2,1)} %get-tuple-element.63.active, bf16[256,2304]{1,0:T(8,128)(2,1)} %copy-done.22, bf16[256,2304]{1,0:T(8,128)(2,1)} %get-tuple-element.64.grad, ...), custom_call_target="tpu_custom_call" | custom-call | flops 34500001792 | bytes 110700000 | tf_op jit(solution)/shard_map/outer_grad/pallas_call | solution.py:465
  55.2 1.9 %collective-permute-start.16 = (bf16[2,4,96,768]{3,2,1,0:T(8,128)(2,1)S(1)}, bf16[2,4,96,768]{3,2,1,0:T(8,128)(2,1)S(1)}, u32[]{:S(2)}, u32[]{:S(2)}) collective-permute-start(bf16[2,4,96,768]{3,2,1,0:T(8,128)(2,1)S(1)} %get-tuple-element.65.refs_2_), channel_id=1, source_target_pairs={{0,8},{4,12},{8,0},{12,4},{16,24},{20,28},{24,16},{28,20},{1,9},{5... | collective-permute-start | bytes 3538952 | tf_op jit(solution)/shard_map/ppermute | solution.py:751
  57.5 0.7 copy-done.23
  58.9 5.1 %inner_grad.1 = (bf16[2,4,128,384]{3,2,1,0:T(8,128)(2,1)S(1)}, bf16[2,4,128,384]{3,2,1,0:T(8,128)(2,1)S(1)}, bf16[2,4,112,384]{3,2,1,0:T(8,128)(2,1)S(1)}, bf16[2,4,112,384]{3,2,1,0:T(8,128)(2,1)S(1)}) custom-call(bf16[4,192,256]{2,1,0:T(8,128)(2,1)} %get-tuple-element.67.mine, bf16[4,192,256]{2,1,0:T(8,128)(2,1)} %copy-done.23, ...), custom_call_target="tpu_custom_call" | custom-call | flops 4600000000 | bytes 14760000 | tf_op jit(solution)/shard_map/inner_grad/pallas_call | solution.py:550
  64.0 1.6 collective-permute-start.14
  65.5 2.6 %collective-permute-start.20 = (bf16[2,4,128,384]{3,2,1,0:T(8,128)(2,1)S(1)}, bf16[2,4,128,384]{3,2,1,0:T(8,128)(2,1)S(1)}, u32[]{:S(2)}, u32[]{:S(2)}) collective-permute-start(bf16[2,4,128,384]{3,2,1,0:T(8,128)(2,1)S(1)} %get-tuple-element.78), channel_id=1, source_target_pairs={{0,16},{4,20},{8,24},{12,28},{16,0},{20,4},{24,8},{28,12},{1,17},{... | collective-permute-start | bytes 2359304 | tf_op jit(solution)/shard_map/ppermute | solution.py:751
  68.1 0.7 copy-done.13
  68.8 12.1 %attend_back.1 = (bf16[2,2,128,768]{3,2,1,0:T(8,128)(2,1)}, bf16[2,2,128,768]{3,2,1,0:T(8,128)(2,1)}, bf16[1,4,96,640]{3,2,1,0:T(8,128)(2,1)S(1)}, bf16[1,4,96,640]{3,2,1,0:T(8,128)(2,1)}) custom-call(s32[2]{0:T(128)S(1)} %pad_add_fusion.refs_1_.place.refs_0_, bf16[2,128,768]{2,1,0:T(8,128)(2,1)} %refs_0_.1, bf16[2,128,768]{2,1,0:T(8,128)(2,1)} %copy-done.10, ...), custom_call_target="tpu_custom_call" | custom-call | flops 1150000000 | bytes 3690000 | tf_op jit(solution)/shard_map/attend_back/pallas_call | solution.py:277
  81.8 1.1 copy-done.3
  83.6 1.6 collective-permute-start.15
  85.1 14.8 %collective-permute-done.16.refs_2_ = bf16[2,4,96,768]{3,2,1,0:T(8,128)(2,1)S(1)} collective-permute-done((bf16[2,4,96,768]{3,2,1,0:T(8,128)(2,1)S(1)}, bf16[2,4,96,768]{3,2,1,0:T(8,128)(2,1)S(1)}, u32[]{:S(2)}, u32[]{:S(2)}) %collective-permute-start.16) | collective-permute-done | bytes 1179680 | tf_op jit(solution)/shard_map/ppermute | solution.py:751
  100.6 2.2 %collective-permute-start.18 = (bf16[2,2,96,768]{3,2,1,0:T(8,128)(2,1)S(1)}, bf16[2,2,96,768]{3,2,1,0:T(8,128)(2,1)S(1)}, u32[]{:S(2)}, u32[]{:S(2)}) collective-permute-start(bf16[2,2,96,768]{3,2,1,0:T(8,128)(2,1)S(1)} %sum_a.3.refs_4_), channel_id=1, source_target_pairs={{0,4},{4,0},{8,12},{12,8},{16,20},{20,16},{24,28},{28,24},{1,5},{5... | collective-permute-start | bytes 1769480 | tf_op jit(solution)/shard_map/ppermute | solution.py:751
  104.2 2.1 %collective-permute-start.17 = (bf16[1,2,96,640]{3,2,1,0:T(8,128)(2,1)S(1)}, bf16[1,2,96,640]{3,2,1,0:T(8,128)(2,1)S(1)}, u32[]{:S(2)}, u32[]{:S(2)}) collective-permute-start(bf16[1,2,96,640]{3,2,1,0:T(8,128)(2,1)S(1)} %sum_d.2.refs_3_), channel_id=1, source_target_pairs={{0,8},{4,12},{8,0},{12,4},{16,24},{20,28},{24,16},{28,20},{1,9},{5... | collective-permute-start | bytes 737288 | tf_op jit(solution)/shard_map/ppermute | solution.py:751
  106.9 1.6 collective-permute-start.22
  109.7 1.1 collective-permute-done.19.refs_4_
  112.1 3.8 %collective-permute-done.18.refs_3_ = bf16[2,2,96,768]{3,2,1,0:T(8,128)(2,1)S(1)} collective-permute-done((bf16[2,2,96,768]{3,2,1,0:T(8,128)(2,1)S(1)}, bf16[2,2,96,768]{3,2,1,0:T(8,128)(2,1)S(1)}, u32[]{:S(2)}, u32[]{:S(2)}) %collective-permute-start.18) | collective-permute-done | bytes 589856 | tf_op jit(solution)/shard_map/ppermute | solution.py:751
  116.6 1.6 collective-permute-start.24
  119.7 2.5 %collective-permute-start.23 = (bf16[1,2,128,384]{3,2,1,0:T(8,128)(2,1)S(1)}, bf16[1,2,128,384]{3,2,1,0:T(8,128)(2,1)S(1)}, u32[]{:S(2)}, u32[]{:S(2)}) collective-permute-start(bf16[1,2,128,384]{3,2,1,0:T(8,128)(2,1)S(1)} %sum_b.4.refs_3_), channel_id=1, source_target_pairs={{0,8},{4,12},{8,0},{12,4},{16,24},{20,28},{24,16},{28,20},{1,9},{5... | collective-permute-start | bytes 589832 | tf_op jit(solution)/shard_map/ppermute | solution.py:751
  122.8 8.6 %collective-permute-done.24.refs_4_ = bf16[1,2,96,768]{3,2,1,0:T(8,128)(2,1)S(1)} collective-permute-done((bf16[1,2,96,768]{3,2,1,0:T(8,128)(2,1)S(1)}, bf16[1,2,96,768]{3,2,1,0:T(8,128)(2,1)S(1)}, u32[]{:S(2)}, u32[]{:S(2)}) %collective-permute-start.24) | collective-permute-done | bytes 294944 | tf_op jit(solution)/shard_map/ppermute | solution.py:751
  131.5 0.7 sum_a.5.refs_5_.refs_1_
  132.2 0.9 collective-permute-start.33
  133.8 1.1 collective-permute-start.30
  135.6 1.1 collective-permute-start.27
  137.1 0.9 collective-permute-start.28
  138.0 2.0 %collective-permute-done.27 = bf16[2,24,640]{2,1,0:T(8,128)(2,1)S(1)} collective-permute-done((bf16[2,24,640]{2,1,0:T(8,128)(2,1)S(1)}, bf16[2,24,640]{2,1,0:T(8,128)(2,1)S(1)}, u32[]{:S(2)}, u32[]{:S(2)}) %collective-permute-start.27) | collective-permute-done | bytes 61472 | tf_op jit(solution)/shard_map/ppermute | solution.py:751
  140.7 1.2 collective-permute-start.32
  141.9 1.6 collective-permute-start.29
  144.1 2.1 %collective-permute-done.33.refs_2_ = bf16[1,2,96,768]{3,2,1,0:T(8,128)(2,1)S(1)} collective-permute-done((bf16[1,2,96,768]{3,2,1,0:T(8,128)(2,1)S(1)}, bf16[1,2,96,768]{3,2,1,0:T(8,128)(2,1)S(1)}, u32[]{:S(2)}, u32[]{:S(2)}) %collective-permute-start.33) | collective-permute-done | bytes 294944 | tf_op jit(solution)/shard_map/ppermute | solution.py:751
  147.0 3.5 %collective-permute-done.32.refs_1_ = bf16[2,128,384]{2,1,0:T(8,128)(2,1)S(1)} collective-permute-done((bf16[2,128,384]{2,1,0:T(8,128)(2,1)S(1)}, bf16[2,128,384]{2,1,0:T(8,128)(2,1)S(1)}, u32[]{:S(2)}, u32[]{:S(2)}) %collective-permute-start.32) | collective-permute-done | bytes 196640 | tf_op jit(solution)/shard_map/ppermute | solution.py:751
  151.8 2.6 %collective-permute-start.34 = (bf16[4,96,640]{2,1,0:T(8,128)(2,1)S(1)}, bf16[4,96,640]{2,1,0:T(8,128)(2,1)S(1)}, u32[]{:S(2)}, u32[]{:S(2)}) collective-permute-start(bf16[4,96,640]{2,1,0:T(8,128)(2,1)S(1)} %join.6.refs_1_.refs_2_), channel_id=1, source_target_pairs={{0,8},{4,12},{8,0},{12,4},{16,24},{20,28},{24,16},{28,20},{1,9},{5... | collective-permute-start | bytes 1474568 | tf_op jit(solution)/shard_map/ppermute | solution.py:751
  154.3 1.0 fusion
  155.4 3.2 %collective-permute-done.37.refs_1_ = bf16[2,96,768]{2,1,0:T(8,128)(2,1)S(1)} collective-permute-done((bf16[2,96,768]{2,1,0:T(8,128)(2,1)S(1)}, bf16[2,96,768]{2,1,0:T(8,128)(2,1)S(1)}, u32[]{:S(2)}, u32[]{:S(2)}) %collective-permute-start.37) | collective-permute-done | bytes 294944 | tf_op jit(solution)/shard_map/ppermute | solution.py:751
  159.0 12.4 %collective-permute-done.35.refs_3_ = bf16[4,128,384]{2,1,0:T(8,128)(2,1)S(1)} collective-permute-done((bf16[4,128,384]{2,1,0:T(8,128)(2,1)S(1)}, bf16[4,128,384]{2,1,0:T(8,128)(2,1)S(1)}, u32[]{:S(2)}, u32[]{:S(2)}) %collective-permute-start.35) | collective-permute-done | bytes 393248 | tf_op jit(solution)/shard_map/ppermute | solution.py:751
  171.4 2.3 %inner_place.1 = (f32[192,3072]{1,0:T(8,128)}, f32[192,768]{1,0:T(8,128)}) custom-call(s32[2]{0:T(128)S(1)} %pad_add_fusion.2.refs_0_, s32[2]{0:T(128)S(1)} %pad_add_fusion.refs_1_.place.refs_0_, bf16[4,128,384]{2,1,0:T(8,128)(2,1)S(1)} %join.5.refs_2_, bf16[4,128,384]{2,1,0:T(8,128)(2,1)S(1)} %collective-permute-done.35.refs_3_, ...), custom_call_target="tpu_custom_call" | custom-call | flops 2300000000 | bytes 7380000 | tf_op jit(solution)/shard_map/inner_place/pallas_call | solution.py:648
  173.8 1.9 %collective-permute-done.34.refs_2_ = bf16[4,96,640]{2,1,0:T(8,128)(2,1)S(1)} collective-permute-done((bf16[4,96,640]{2,1,0:T(8,128)(2,1)S(1)}, bf16[4,96,640]{2,1,0:T(8,128)(2,1)S(1)}, u32[]{:S(2)}, u32[]{:S(2)}) %collective-permute-start.34) | collective-permute-done | bytes 491552 | tf_op jit(solution)/shard_map/ppermute | solution.py:751
  175.7 2.0 %project_place.1 = (f32[192,2304]{1,0:T(8,128)}, f32[16,192]{1,0:T(8,128)S(1)}) custom-call(s32[2]{0:T(128)S(1)} %pad_add_fusion.refs_1_.place.refs_0_, bf16[4,96,640]{2,1,0:T(8,128)(2,1)S(1)} %join.6.refs_1_.refs_2_, bf16[4,96,640]{2,1,0:T(8,128)(2,1)S(1)} %collective-permute-done.34.refs_2_), custom_call_target="tpu_custom_call" | custom-call | flops 2300000000 | bytes 7380000 | tf_op jit(solution)/shard_map/project_place/pallas_call | solution.py:686
  179.0 2.1 %outer_place.1 = f32[768,768]{1,0:T(8,128)} custom-call(s32[2]{0:T(128)S(1)} %pad_add_fusion.1.place.refs_0_, bf16[4,96,768]{2,1,0:T(8,128)(2,1)S(1)} %join.7.refs_1_, bf16[4,96,768]{2,1,0:T(8,128)(2,1)S(1)} %collective-permute-done.38.refs_2_), custom_call_target="tpu_custom_call" | custom-call | flops 2300000000 | bytes 7380000 | tf_op jit(solution)/shard_map/outer_place/pallas_call | solution.py:618
  (138 shorter events, 21.7 us)
Async XLA Ops:
  0.6 12.4 %collective-permute-start.1 = (bf16[2,128,768]{2,1,0:T(8,128)(2,1)}, bf16[2,128,768]{2,1,0:T(8,128)(2,1)S(1)}, u32[]{:S(2)}, u32[]{:S(2)}) collective-permute-start(bf16[2,128,768]{2,1,0:T(8,128)(2,1)} %refs_0_.1), channel_id=1, source_target_pairs={{0,2},{1,3},{2,0},{3,1},{4,6},{5,7},{6,4},{7,5},{8,10},{9,11},{10,... | collective-permute-start | bytes 1179656 | tf_op jit(solution)/shard_map/ppermute | solution.py:751
  3.7 13.6 %collective-permute-start = (bf16[2,128,768]{2,1,0:T(8,128)(2,1)}, bf16[2,128,768]{2,1,0:T(8,128)(2,1)S(1)}, u32[]{:S(2)}, u32[]{:S(2)}) collective-permute-start(bf16[2,128,768]{2,1,0:T(8,128)(2,1)} %refs_0_.1), channel_id=1, source_target_pairs={{0,1},{1,0},{2,3},{3,2},{4,5},{5,4},{6,7},{7,6},{8,9},{9,8},{10,11... | collective-permute-start | bytes 1179656 | tf_op jit(solution)/shard_map/ppermute | solution.py:751
  13.0 4.3 %collective-permute-start.2 = (bf16[2,128,768]{2,1,0:T(8,128)(2,1)S(1)}, bf16[2,128,768]{2,1,0:T(8,128)(2,1)S(1)}, u32[]{:S(2)}, u32[]{:S(2)}) collective-permute-start(bf16[2,128,768]{2,1,0:T(8,128)(2,1)S(1)} %collective-permute-done.1.x2.refs_2_), channel_id=1, source_target_pairs={{0,1},{1,0},{2,3},{3,2},{4,5},{5,4},{6,7},{7,6},{8,9},{9,8},{10,11... | collective-permute-start | bytes 1179656 | tf_op jit(solution)/shard_map/ppermute | solution.py:751
  17.1 10.9 %copy-start.15 = (bf16[768]{0:T(1024)(128)(2,1)S(1)}, bf16[768]{0:T(1024)(128)(2,1)}, u32[]{:S(2)}) copy-start(bf16[768]{0:T(1024)(128)(2,1)} %param.22) | copy-start | bytes 4612
  17.2 10.9 %copy-start.17 = (bf16[768]{0:T(1024)(128)(2,1)S(1)}, bf16[768]{0:T(1024)(128)(2,1)}, u32[]{:S(2)}) copy-start(bf16[768]{0:T(1024)(128)(2,1)} %param.24) | copy-start | bytes 4612
  17.2 11.0 %copy-start.18 = (bf16[768]{0:T(1024)(128)(2,1)S(1)}, bf16[768]{0:T(1024)(128)(2,1)}, u32[]{:S(2)}) copy-start(bf16[768]{0:T(1024)(128)(2,1)} %param.28) | copy-start | bytes 4612
  17.2 11.0 %copy-start.19 = (bf16[768]{0:T(1024)(128)(2,1)S(1)}, bf16[768]{0:T(1024)(128)(2,1)}, u32[]{:S(2)}) copy-start(bf16[768]{0:T(1024)(128)(2,1)} %param.29) | copy-start | bytes 4612
  17.2 11.0 %copy-start.20 = (bf16[768]{0:T(1024)(128)(2,1)S(1)}, bf16[768]{0:T(1024)(128)(2,1)}, u32[]{:S(2)}) copy-start(bf16[768]{0:T(1024)(128)(2,1)} %param.30) | copy-start | bytes 4612
  17.2 11.1 %copy-start.14 = (bf16[3072]{0:T(1024)(128)(2,1)S(1)}, bf16[3072]{0:T(1024)(128)(2,1)}, u32[]{:S(2)}) copy-start(bf16[3072]{0:T(1024)(128)(2,1)} %param.26) | copy-start | bytes 18436
  17.2 17.3 %copy-start = (bf16[2,128,768]{2,1,0:T(8,128)(2,1)S(1)}, bf16[2,128,768]{2,1,0:T(8,128)(2,1)}, u32[]{:S(2)}) copy-start(bf16[2,128,768]{2,1,0:T(8,128)(2,1)} %refs_0_.1) | copy-start | bytes 1179652
  17.2 17.3 %copy-start.6 = (bf16[768,768]{1,0:T(8,128)(2,1)S(1)}, bf16[768,768]{1,0:T(8,128)(2,1)}, u32[]{:S(2)}) copy-start(bf16[768,768]{1,0:T(8,128)(2,1)} %param.21) | copy-start | bytes 3538948
  17.2 17.3 %copy-start.8 = (bf16[2,128,768]{2,1,0:T(8,128)(2,1)S(1)}, bf16[2,128,768]{2,1,0:T(8,128)(2,1)}, u32[]{:S(2)}) copy-start(bf16[2,128,768]{2,1,0:T(8,128)(2,1)} %param.31) | copy-start | bytes 1179652
  25.8 2.5 %collective-permute-start.3 = (bf16[2,128,192]{2,1,0:T(8,128)(2,1)S(1)}, bf16[2,128,192]{2,1,0:T(8,128)(2,1)S(1)}, u32[]{:S(2)}, u32[]{:S(2)}) collective-permute-start(bf16[2,128,192]{2,1,0:T(8,128)(2,1)S(1)} %get-tuple-element.54), channel_id=1, source_target_pairs={{0,1},{1,0},{2,3},{3,2},{4,5},{5,4},{6,7},{7,6},{8,9},{9,8},{10,11... | collective-permute-start | bytes 294920 | tf_op jit(solution)/shard_map/ppermute | solution.py:751
  26.3 6.2 %collective-permute-start.4 = (bf16[2,128,192]{2,1,0:T(8,128)(2,1)S(1)}, bf16[2,128,192]{2,1,0:T(8,128)(2,1)S(1)}, u32[]{:S(2)}, u32[]{:S(2)}) collective-permute-start(bf16[2,128,192]{2,1,0:T(8,128)(2,1)S(1)} %get-tuple-element.55), channel_id=1, source_target_pairs={{0,2},{1,3},{2,0},{3,1},{4,6},{5,7},{6,4},{7,5},{8,10},{9,11},{10,... | collective-permute-start | bytes 294920 | tf_op jit(solution)/shard_map/ppermute | solution.py:751
  28.1 5.8 %collective-permute-start.5 = (bf16[2,128,192]{2,1,0:T(8,128)(2,1)S(1)}, bf16[2,128,192]{2,1,0:T(8,128)(2,1)S(1)}, u32[]{:S(2)}, u32[]{:S(2)}) collective-permute-start(bf16[2,128,192]{2,1,0:T(8,128)(2,1)S(1)} %get-tuple-element.56), channel_id=1, source_target_pairs={{0,3},{1,2},{2,1},{3,0},{4,7},{5,6},{6,5},{7,4},{8,11},{9,10},{10,... | collective-permute-start | bytes 294920 | tf_op jit(solution)/shard_map/ppermute | solution.py:751
  47.6 3.3 %collective-permute-start.7 = (bf16[256,2304]{1,0:T(8,128)(2,1)}, bf16[256,2304]{1,0:T(8,128)(2,1)S(1)}, u32[]{:S(2)}, u32[]{:S(2)}) collective-permute-start(bf16[256,2304]{1,0:T(8,128)(2,1)} %get-tuple-element.64.grad), channel_id=1, source_target_pairs={{0,1},{1,0},{2,3},{3,2},{4,5},{5,4},{6,7},{7,6},{8,9},{9,8},{10,11... | collective-permute-start | bytes 3538952 | tf_op jit(solution)/shard_map/ppermute | solution.py:751
  48.4 8.7 %collective-permute-start.6 = (bf16[2,256,192]{2,1,0:T(8,128)(2,1)S(1)}, bf16[2,256,192]{2,1,0:T(8,128)(2,1)S(1)}, u32[]{:S(2)}, u32[]{:S(2)}) collective-permute-start(bf16[2,256,192]{2,1,0:T(8,128)(2,1)S(1)} %get-tuple-element.62), channel_id=1, source_target_pairs={{0,2},{1,3},{2,0},{3,1},{4,6},{5,7},{6,4},{7,5},{8,10},{9,11},{10,... | collective-permute-start | bytes 589832 | tf_op jit(solution)/shard_map/ppermute | solution.py:751
  50.1 7.4 %collective-permute-start.10 = (bf16[256,3840]{1,0:T(8,128)(2,1)}, bf16[256,3840]{1,0:T(8,128)(2,1)S(1)}, u32[]{:S(2)}, u32[]{:S(2)}) collective-permute-start(bf16[256,3840]{1,0:T(8,128)(2,1)} %get-tuple-element.69.inner.attn), channel_id=1, source_target_pairs={{0,1},{1,0},{2,3},{3,2},{4,5},{5,4},{6,7},{7,6},{8,9},{9,8},{10,11... | collective-permute-start | bytes 5898248 | tf_op jit(solution)/shard_map/ppermute | solution.py:751
  50.1 7.3 %collective-permute-start.9 = (bf16[4,192,256]{2,1,0:T(8,128)(2,1)}, bf16[4,192,256]{2,1,0:T(8,128)(2,1)S(1)}, u32[]{:S(2)}, u32[]{:S(2)}) collective-permute-start(bf16[4,192,256]{2,1,0:T(8,128)(2,1)} %get-tuple-element.68), channel_id=1, source_target_pairs={{0,1},{1,0},{2,3},{3,2},{4,5},{5,4},{6,7},{7,6},{8,9},{9,8},{10,11... | collective-permute-start | bytes 1179656 | tf_op jit(solution)/shard_map/ppermute | solution.py:751
  55.2 44.7 %collective-permute-start.16 = (bf16[2,4,96,768]{3,2,1,0:T(8,128)(2,1)S(1)}, bf16[2,4,96,768]{3,2,1,0:T(8,128)(2,1)S(1)}, u32[]{:S(2)}, u32[]{:S(2)}) collective-permute-start(bf16[2,4,96,768]{3,2,1,0:T(8,128)(2,1)S(1)} %get-tuple-element.65.refs_2_), channel_id=1, source_target_pairs={{0,8},{4,12},{8,0},{12,4},{16,24},{20,28},{24,16},{28,20},{1,9},{5... | collective-permute-start | bytes 3538952 | tf_op jit(solution)/shard_map/ppermute | solution.py:751
  64.0 17.8 %collective-permute-start.14 = (bf16[2,4,112,384]{3,2,1,0:T(8,128)(2,1)S(1)}, bf16[2,4,112,384]{3,2,1,0:T(8,128)(2,1)S(1)}, u32[]{:S(2)}, u32[]{:S(2)}) collective-permute-start(bf16[2,4,112,384]{3,2,1,0:T(8,128)(2,1)S(1)} %get-tuple-element.70.refs_11_), channel_id=1, source_target_pairs={{0,4},{4,0},{8,12},{12,8},{16,20},{20,16},{24,28},{28,24},{1,5},{5... | collective-permute-start | bytes 2064392 | tf_op jit(solution)/shard_map/ppermute | solution.py:751
  65.5 2.6 %collective-permute-start.8 = (bf16[2,256,192]{2,1,0:T(8,128)(2,1)S(1)}, bf16[2,256,192]{2,1,0:T(8,128)(2,1)S(1)}, u32[]{:S(2)}, u32[]{:S(2)}) collective-permute-start(bf16[2,256,192]{2,1,0:T(8,128)(2,1)S(1)} %pair.1.refs_2_), channel_id=1, source_target_pairs={{0,1},{1,0},{2,3},{3,2},{4,5},{5,4},{6,7},{7,6},{8,9},{9,8},{10,11... | collective-permute-start | bytes 589832 | tf_op jit(solution)/shard_map/ppermute | solution.py:751
  65.5 40.8 %collective-permute-start.20 = (bf16[2,4,128,384]{3,2,1,0:T(8,128)(2,1)S(1)}, bf16[2,4,128,384]{3,2,1,0:T(8,128)(2,1)S(1)}, u32[]{:S(2)}, u32[]{:S(2)}) collective-permute-start(bf16[2,4,128,384]{3,2,1,0:T(8,128)(2,1)S(1)} %get-tuple-element.78), channel_id=1, source_target_pairs={{0,16},{4,20},{8,24},{12,28},{16,0},{20,4},{24,8},{28,12},{1,17},{... | collective-permute-start | bytes 2359304 | tf_op jit(solution)/shard_map/ppermute | solution.py:751
  81.0 27.5 %collective-permute-start.11 = (bf16[2,2,128,768]{3,2,1,0:T(8,128)(2,1)}, bf16[2,2,128,768]{3,2,1,0:T(8,128)(2,1)S(1)}, u32[]{:S(2)}, u32[]{:S(2)}) collective-permute-start(bf16[2,2,128,768]{3,2,1,0:T(8,128)(2,1)} %get-tuple-element.72), channel_id=1, source_target_pairs={{0,1},{1,0},{2,3},{3,2},{4,5},{5,4},{6,7},{7,6},{8,9},{9,8},{10,11... | collective-permute-start | bytes 2359304 | tf_op jit(solution)/shard_map/ppermute | solution.py:751
  81.2 22.3 %collective-permute-start.13 = (bf16[1,4,96,640]{3,2,1,0:T(8,128)(2,1)S(1)}, bf16[1,4,96,640]{3,2,1,0:T(8,128)(2,1)S(1)}, u32[]{:S(2)}, u32[]{:S(2)}) collective-permute-start(bf16[1,4,96,640]{3,2,1,0:T(8,128)(2,1)S(1)} %get-tuple-element.74), channel_id=1, source_target_pairs={{0,4},{4,0},{8,12},{12,8},{16,20},{20,16},{24,28},{28,24},{1,5},{5... | collective-permute-start | bytes 1474568 | tf_op jit(solution)/shard_map/ppermute | solution.py:751
  83.6 19.3 %collective-permute-start.15 = (bf16[1,4,112,384]{3,2,1,0:T(8,128)(2,1)S(1)}, bf16[1,4,112,384]{3,2,1,0:T(8,128)(2,1)S(1)}, u32[]{:S(2)}, u32[]{:S(2)}) collective-permute-start(bf16[1,4,112,384]{3,2,1,0:T(8,128)(2,1)S(1)} %sum_c.3.refs_3_), channel_id=1, source_target_pairs={{0,2},{1,3},{2,0},{3,1},{4,6},{5,7},{6,4},{7,5},{8,10},{9,11},{10,... | collective-permute-start | bytes 1032200 | tf_op jit(solution)/shard_map/ppermute | solution.py:751
  100.6 15.3 %collective-permute-start.18 = (bf16[2,2,96,768]{3,2,1,0:T(8,128)(2,1)S(1)}, bf16[2,2,96,768]{3,2,1,0:T(8,128)(2,1)S(1)}, u32[]{:S(2)}, u32[]{:S(2)}) collective-permute-start(bf16[2,2,96,768]{3,2,1,0:T(8,128)(2,1)S(1)} %sum_a.3.refs_4_), channel_id=1, source_target_pairs={{0,4},{4,0},{8,12},{12,8},{16,20},{20,16},{24,28},{28,24},{1,5},{5... | collective-permute-start | bytes 1769480 | tf_op jit(solution)/shard_map/ppermute | solution.py:751
  103.5 7.4 %collective-permute-start.19 = (bf16[1,2,112,384]{3,2,1,0:T(8,128)(2,1)S(1)}, bf16[1,2,112,384]{3,2,1,0:T(8,128)(2,1)S(1)}, u32[]{:S(2)}, u32[]{:S(2)}) collective-permute-start(bf16[1,2,112,384]{3,2,1,0:T(8,128)(2,1)S(1)} %sum_c.4.refs_3_), channel_id=1, source_target_pairs={{0,8},{4,12},{8,0},{12,4},{16,24},{20,28},{24,16},{28,20},{1,9},{5... | collective-permute-start | bytes 516104 | tf_op jit(solution)/shard_map/ppermute | solution.py:751
  104.2 13.9 %collective-permute-start.17 = (bf16[1,2,96,640]{3,2,1,0:T(8,128)(2,1)S(1)}, bf16[1,2,96,640]{3,2,1,0:T(8,128)(2,1)S(1)}, u32[]{:S(2)}, u32[]{:S(2)}) collective-permute-start(bf16[1,2,96,640]{3,2,1,0:T(8,128)(2,1)S(1)} %sum_d.2.refs_3_), channel_id=1, source_target_pairs={{0,8},{4,12},{8,0},{12,4},{16,24},{20,28},{24,16},{28,20},{1,9},{5... | collective-permute-start | bytes 737288 | tf_op jit(solution)/shard_map/ppermute | solution.py:751
  106.9 12.1 %collective-permute-start.22 = (bf16[1,4,128,384]{3,2,1,0:T(8,128)(2,1)S(1)}, bf16[1,4,128,384]{3,2,1,0:T(8,128)(2,1)S(1)}, u32[]{:S(2)}, u32[]{:S(2)}) collective-permute-start(bf16[1,4,128,384]{3,2,1,0:T(8,128)(2,1)S(1)} %sum_b.3.refs_5_), channel_id=1, source_target_pairs={{0,2},{1,3},{2,0},{3,1},{4,6},{5,7},{6,4},{7,5},{8,10},{9,11},{10,... | collective-permute-start | bytes 1179656 | tf_op jit(solution)/shard_map/ppermute | solution.py:751
  109.1 45.2 %collective-permute-start.12 = (bf16[1,1,256,768]{3,2,1,0:T(8,128)(2,1)S(1)}, bf16[1,1,256,768]{3,2,1,0:T(8,128)(2,1)S(1)}, u32[]{:S(2)}, u32[]{:S(2)}) collective-permute-start(bf16[1,1,256,768]{3,2,1,0:T(8,128)(2,1)S(1)} %back_y.1), channel_id=1, source_target_pairs={{0,2},{1,3},{2,0},{3,1},{4,6},{5,7},{6,4},{7,5},{8,10},{9,11},{10,... | collective-permute-start | bytes 1179656 | tf_op jit(solution)/shard_map/ppermute | solution.py:751
  111.5 10.6 %collective-permute-start.25 = (bf16[1,2,112,384]{3,2,1,0:T(8,128)(2,1)S(1)}, bf16[1,2,112,384]{3,2,1,0:T(8,128)(2,1)S(1)}, u32[]{:S(2)}, u32[]{:S(2)}) collective-permute-start(bf16[1,2,112,384]{3,2,1,0:T(8,128)(2,1)S(1)} %sum_c.5.refs_4_.refs_1_), channel_id=1, source_target_pairs={{0,16},{4,20},{8,24},{12,28},{16,0},{20,4},{24,8},{28,12},{1,17},{... | collective-permute-start | bytes 516104 | tf_op jit(solution)/shard_map/ppermute | solution.py:751
  116.6 14.9 %collective-permute-start.24 = (bf16[1,2,96,768]{3,2,1,0:T(8,128)(2,1)S(1)}, bf16[1,2,96,768]{3,2,1,0:T(8,128)(2,1)S(1)}, u32[]{:S(2)}, u32[]{:S(2)}) collective-permute-start(bf16[1,2,96,768]{3,2,1,0:T(8,128)(2,1)S(1)} %sum_a.4.refs_4_), channel_id=1, source_target_pairs={{0,2},{1,3},{2,0},{3,1},{4,6},{5,7},{6,4},{7,5},{8,10},{9,11},{10,... | collective-permute-start | bytes 884744 | tf_op jit(solution)/shard_map/ppermute | solution.py:751
  118.8 16.1 %collective-permute-start.21 = (bf16[1,2,96,640]{3,2,1,0:T(8,128)(2,1)S(1)}, bf16[1,2,96,640]{3,2,1,0:T(8,128)(2,1)S(1)}, u32[]{:S(2)}, u32[]{:S(2)}) collective-permute-start(bf16[1,2,96,640]{3,2,1,0:T(8,128)(2,1)S(1)} %sum_d.3.refs_4_.refs_1_), channel_id=1, source_target_pairs={{0,16},{4,20},{8,24},{12,28},{16,0},{20,4},{24,8},{28,12},{1,17},{... | collective-permute-start | bytes 737288 | tf_op jit(solution)/shard_map/ppermute | solution.py:751
  119.7 13.4 %collective-permute-start.23 = (bf16[1,2,128,384]{3,2,1,0:T(8,128)(2,1)S(1)}, bf16[1,2,128,384]{3,2,1,0:T(8,128)(2,1)S(1)}, u32[]{:S(2)}, u32[]{:S(2)}) collective-permute-start(bf16[1,2,128,384]{3,2,1,0:T(8,128)(2,1)S(1)} %sum_b.4.refs_3_), channel_id=1, source_target_pairs={{0,8},{4,12},{8,0},{12,4},{16,24},{20,28},{24,16},{28,20},{1,9},{5... | collective-permute-start | bytes 589832 | tf_op jit(solution)/shard_map/ppermute | solution.py:751
  122.7 12.8 %collective-permute-start.31 = (bf16[2,112,384]{2,1,0:T(8,128)(2,1)S(1)}, bf16[2,112,384]{2,1,0:T(8,128)(2,1)S(1)}, u32[]{:S(2)}, u32[]{:S(2)}) collective-permute-start(bf16[2,112,384]{2,1,0:T(8,128)(2,1)S(1)} %bitcast.51), channel_id=1, source_target_pairs={{0,8},{4,12},{8,0},{12,4},{16,24},{20,28},{24,16},{28,20},{1,9},{5... | collective-permute-start | bytes 516104 | tf_op jit(solution)/shard_map/ppermute | solution.py:751
  132.2 14.1 %collective-permute-start.33 = (bf16[1,2,96,768]{3,2,1,0:T(8,128)(2,1)S(1)}, bf16[1,2,96,768]{3,2,1,0:T(8,128)(2,1)S(1)}, u32[]{:S(2)}, u32[]{:S(2)}) collective-permute-start(bf16[1,2,96,768]{3,2,1,0:T(8,128)(2,1)S(1)} %sum_a.5.refs_5_.refs_1_), channel_id=1, source_target_pairs={{0,16},{4,20},{8,24},{12,28},{16,0},{20,4},{24,8},{28,12},{1,17},{... | collective-permute-start | bytes 884744 | tf_op jit(solution)/shard_map/ppermute | solution.py:751
  133.8 6.3 %collective-permute-start.30 = (bf16[1,2,128,384]{3,2,1,0:T(8,128)(2,1)S(1)}, bf16[1,2,128,384]{3,2,1,0:T(8,128)(2,1)S(1)}, u32[]{:S(2)}, u32[]{:S(2)}) collective-permute-start(bf16[1,2,128,384]{3,2,1,0:T(8,128)(2,1)S(1)} %sum_b.5.refs_3_.refs_1_), channel_id=1, source_target_pairs={{0,4},{4,0},{8,12},{12,8},{16,20},{20,16},{24,28},{28,24},{1,5},{5... | collective-permute-start | bytes 589832 | tf_op jit(solution)/shard_map/ppermute | solution.py:751
  135.5 1.6 collective-permute-start.26
  135.6 4.5 %collective-permute-start.27 = (bf16[2,24,640]{2,1,0:T(8,128)(2,1)S(1)}, bf16[2,24,640]{2,1,0:T(8,128)(2,1)S(1)}, u32[]{:S(2)}, u32[]{:S(2)}) collective-permute-start(bf16[2,24,640]{2,1,0:T(8,128)(2,1)S(1)} %get-tuple-element.81), channel_id=1, source_target_pairs={{0,2},{1,3},{2,0},{3,1},{4,6},{5,7},{6,4},{7,5},{8,10},{9,11},{10,... | collective-permute-start | bytes 184328 | tf_op jit(solution)/shard_map/ppermute | solution.py:751
  137.1 4.8 %collective-permute-start.28 = (bf16[2,24,640]{2,1,0:T(8,128)(2,1)S(1)}, bf16[2,24,640]{2,1,0:T(8,128)(2,1)S(1)}, u32[]{:S(2)}, u32[]{:S(2)}) collective-permute-start(bf16[2,24,640]{2,1,0:T(8,128)(2,1)S(1)} %get-tuple-element.82), channel_id=1, source_target_pairs={{0,3},{1,2},{2,1},{3,0},{4,7},{5,6},{6,5},{7,4},{8,11},{9,10},{10,... | collective-permute-start | bytes 184328 | tf_op jit(solution)/shard_map/ppermute | solution.py:751
  140.7 9.8 %collective-permute-start.32 = (bf16[2,128,384]{2,1,0:T(8,128)(2,1)S(1)}, bf16[2,128,384]{2,1,0:T(8,128)(2,1)S(1)}, u32[]{:S(2)}, u32[]{:S(2)}) collective-permute-start(bf16[2,128,384]{2,1,0:T(8,128)(2,1)S(1)} %bitcast.49), channel_id=1, source_target_pairs={{0,8},{4,12},{8,0},{12,4},{16,24},{20,28},{24,16},{28,20},{1,9},{5... | collective-permute-start | bytes 589832 | tf_op jit(solution)/shard_map/ppermute | solution.py:751
  141.9 9.3 %collective-permute-start.29 = (bf16[2,96,640]{2,1,0:T(8,128)(2,1)S(1)}, bf16[2,96,640]{2,1,0:T(8,128)(2,1)S(1)}, u32[]{:S(2)}, u32[]{:S(2)}) collective-permute-start(bf16[2,96,640]{2,1,0:T(8,128)(2,1)S(1)} %constant_dynamic-update-slice_fusion.refs_0_), channel_id=1, source_target_pairs={{0,4},{4,0},{8,12},{12,8},{16,20},{20,16},{24,28},{28,24},{1,5},{5... | collective-permute-start | bytes 737288 | tf_op jit(solution)/shard_map/ppermute | solution.py:751
  143.6 15.4 %collective-permute-start.36 = (bf16[4,112,384]{2,1,0:T(8,128)(2,1)S(1)}, bf16[4,112,384]{2,1,0:T(8,128)(2,1)S(1)}, u32[]{:S(2)}, u32[]{:S(2)}) collective-permute-start(bf16[4,112,384]{2,1,0:T(8,128)(2,1)S(1)} %join.4.refs_3_.refs_4_), channel_id=1, source_target_pairs={{0,4},{4,0},{8,12},{12,8},{16,20},{20,16},{24,28},{28,24},{1,5},{5... | collective-permute-start | bytes 1032200 | tf_op jit(solution)/shard_map/ppermute | solution.py:751
  146.9 11.7 %collective-permute-start.37 = (bf16[2,96,768]{2,1,0:T(8,128)(2,1)S(1)}, bf16[2,96,768]{2,1,0:T(8,128)(2,1)S(1)}, u32[]{:S(2)}, u32[]{:S(2)}) collective-permute-start(bf16[2,96,768]{2,1,0:T(8,128)(2,1)S(1)} %bitcast.47), channel_id=1, source_target_pairs={{0,8},{4,12},{8,0},{12,4},{16,24},{20,28},{24,16},{28,20},{1,9},{5... | collective-permute-start | bytes 884744 | tf_op jit(solution)/shard_map/ppermute | solution.py:751
  151.0 20.4 %collective-permute-start.35 = (bf16[4,128,384]{2,1,0:T(8,128)(2,1)S(1)}, bf16[4,128,384]{2,1,0:T(8,128)(2,1)S(1)}, u32[]{:S(2)}, u32[]{:S(2)}) collective-permute-start(bf16[4,128,384]{2,1,0:T(8,128)(2,1)S(1)} %join.5.refs_2_), channel_id=1, source_target_pairs={{0,16},{4,20},{8,24},{12,28},{16,0},{20,4},{24,8},{28,12},{1,17},{... | collective-permute-start | bytes 1179656 | tf_op jit(solution)/shard_map/ppermute | solution.py:751
  151.8 23.9 %collective-permute-start.34 = (bf16[4,96,640]{2,1,0:T(8,128)(2,1)S(1)}, bf16[4,96,640]{2,1,0:T(8,128)(2,1)S(1)}, u32[]{:S(2)}, u32[]{:S(2)}) collective-permute-start(bf16[4,96,640]{2,1,0:T(8,128)(2,1)S(1)} %join.6.refs_1_.refs_2_), channel_id=1, source_target_pairs={{0,8},{4,12},{8,0},{12,4},{16,24},{20,28},{24,16},{28,20},{1,9},{5... | collective-permute-start | bytes 1474568 | tf_op jit(solution)/shard_map/ppermute | solution.py:751
  158.7 20.2 %collective-permute-start.38 = (bf16[4,96,768]{2,1,0:T(8,128)(2,1)S(1)}, bf16[4,96,768]{2,1,0:T(8,128)(2,1)S(1)}, u32[]{:S(2)}, u32[]{:S(2)}) collective-permute-start(bf16[4,96,768]{2,1,0:T(8,128)(2,1)S(1)} %join.7.refs_1_), channel_id=1, source_target_pairs={{0,4},{4,0},{8,12},{12,8},{16,20},{20,16},{24,28},{28,24},{1,5},{5... | collective-permute-start | bytes 1769480 | tf_op jit(solution)/shard_map/ppermute | solution.py:751
  (18 other events, 53.7 us)

commit v5 on v4

--- a/solution.py
+++ b/solution.py
@@ -43,6 +43,9 @@
 HBM = pl.BlockSpec(memory_space=pltpu.HBM)
 
 
+TOKEN = pltpu.HBM((8, 128), jnp.float32)
+
+
 def far(array):
     return pltpu.with_memory_space_constraint(array, pltpu.HBM)
 
@@ -56,7 +59,7 @@
 BLOCK = 128
 
 
-def choose_kernel(where, w_hbm, qb, vb, w_out, bias_out, wide, w_here, sem):
+def choose_kernel(where, w_hbm, qb, vb, w_out, bias_out, token, wide, w_here, sem):
     me = where[0]
     hw = bias_out.shape[1]
     width = wide.shape[1]
@@ -84,8 +87,8 @@
     return pl.pallas_call(
         choose_kernel,
         in_specs=[SMEM, HBM, vmem(), vmem()],
-        out_specs=[HBM, vmem()],
-        out_shape=[pltpu.HBM((width, 3 * hw), LOW), jax.ShapeDtypeStruct((2, hw), F32)],
+        out_specs=[HBM, vmem(), HBM],
+        out_shape=[pltpu.HBM((width, 3 * hw), LOW), jax.ShapeDtypeStruct((2, hw), F32), TOKEN],
         scratch_shapes=[
             pltpu.VMEM((3, width, hw + HD), LOW),
             pltpu.VMEM((width, 3 * hw), LOW),
@@ -98,8 +101,8 @@
 
 
 def attend_kernel(where, lengths, x0, x1, x2, x3, w_hbm, bias, *refs):
-    qkv_out, chance_out, own_out, c1, c2, c3 = refs[:6]
-    x, w, qkv_here, chance_here, own_here, load_sem, store_sem = refs[6:]
+    qkv_out, chance_out, own_out, x_out, c1, c2, c3 = refs[:7]
+    x, w, qkv_here, chance_here, own_here, load_sem, store_sem = refs[7:]
     me = where[0]
     passages, quarter, width = x0.shape
     rows = 4 * quarter
@@ -122,6 +125,7 @@
     for p in range(passages):
         for copy in loads[1 + 4 * p : 5 + 4 * p]:
             copy.wait()
+        store(x.at[p], x_out.at[p])
         proj = dot(x[p], w[...])
         q = ((proj[:, :hw] + bias[0:1, :]).astype(LOW).astype(F32) * HD ** (-0.5)).astype(LOW)
         k = proj[:, hw : 2 * hw].astype(LOW)
@@ -159,23 +163,24 @@
     hw = width // 4
     heads = hw // HD
     kinds = [((passages, rows, 3 * hw), LOW), ((passages, heads, rows, rows), LOW), ((passages, quarter, hw), LOW)]
+    whole = ((passages, rows, width), LOW)
     return pl.pallas_call(
         attend_kernel,
-        in_specs=[SMEM, SMEM] + [HBM] * 5 + [vmem()],
-        out_specs=[HBM] * 3 + [vmem()] * 3,
-        out_shape=[pltpu.HBM(*kind) for kind in kinds] + [jax.ShapeDtypeStruct(*kinds[2])] * 3,
-        scratch_shapes=[pltpu.VMEM((passages, rows, width), LOW), pltpu.VMEM((width, 3 * hw), LOW)]
+        in_specs=[SMEM, SMEM] + [HBM] * 3 + [vmem(), HBM, vmem()],
+        out_specs=[HBM] * 4 + [vmem()] * 3,
+        out_shape=[pltpu.HBM(*kind) for kind in kinds + [whole]] + [jax.ShapeDtypeStruct(*kinds[2])] * 3,
+        scratch_shapes=[pltpu.VMEM(*whole), pltpu.VMEM((width, 3 * hw), LOW)]
         + [pltpu.VMEM(*kind) for kind in kinds]
-        + [pltpu.SemaphoreType.DMA((4 * passages + 1,)), pltpu.SemaphoreType.DMA((passages * (heads + 2),))],
+        + [pltpu.SemaphoreType.DMA((4 * passages + 1,)), pltpu.SemaphoreType.DMA((passages * (heads + 3),))],
         compiler_params=pltpu.CompilerParams(vmem_limit_bytes=24 * MIB),
         cost_estimate=cost(FORE),
         name="attend",
-    )(where, lengths, *map(far, shards), far(w), bias)
+    )(where, lengths, *map(far, shards[:3]), shards[3], far(w), bias)
 
 
 def attend_back_kernel(place, *refs):
-    x0, x1, x2, x3, w_hbm, qkv_hbm, chance_hbm, near, near_got, far_got, vectors = refs[:11]
-    keep_out, send_out, weight_send, weight_keep = refs[-16:-12]
+    x_hbm, w_hbm, qkv_hbm, chance_hbm, near, near_got, far_got, vectors = refs[:8]
+    keep_out, send_out, weight_send, weight_keep, _ = refs[-17:-12]
     x, w, qkv, chance, g, extra_here, joined, back, keep_here, acc, load_sem, store_sem = refs[-12:]
     me = place[1]
     quarter, hw = near.shape[2:]
@@ -198,8 +203,7 @@
     last = [load(w_hbm, w)]
     late = [load(vectors, extra_here)]
     for p in range(2):
-        for j, shard in enumerate((x0, x1, x2, x3)):
-            late.append(load(shard.at[p], x.at[pl.ds(p * rows + j * quarter, quarter)]))
+        late.append(load(x_hbm.at[p], x.at[pl.ds(p * rows, rows)]))
     for copy in needs[0][0] + needs[0][1]:
         copy.start()
     stores = []
@@ -249,20 +253,21 @@
     half = PIECES // 2
     n = weight_send.shape[2] // 4
     spot = place[0] & half
-    for out, first in ((weight_send, spot ^ half), (keep_here, spot)):
+    for out, first in ((keep_here, spot), (weight_send, spot ^ half)):
         for j in range(4):
             for e in range(half):
                 start = pl.multiple_of((me ^ j) * (n * PIECES) + (first + e) * n, 8)
                 out[0, e, j * n : (j + 1) * n, :] = acc[pl.ds(start, n), :].astype(LOW)
-    stores.append(pltpu.make_async_copy(keep_here, weight_keep, store_sem.at[len(stores)]))
-    stores[-1].start()
+        if out is keep_here:
+            stores.append(pltpu.make_async_copy(keep_here, weight_keep, store_sem.at[len(stores)]))
+            stores[-1].start()
     for copy in stores:
         copy.wait()
 
 
-def attend_back(place, shards, w, qkv, chance, grads, vectors, after=()):
-    passages, quarter, width = shards[0].shape
-    rows = 4 * quarter
+def attend_back(place, x, w, qkv, chance, grads, vectors, after=()):
+    passages, rows, width = x.shape
+    quarter = rows // 4
     hw = width // 4
     heads = hw // HD
     n = width // (4 * PIECES)
@@ -273,18 +278,18 @@
         ((passages, heads, rows, rows), LOW), ((passages, rows, hw), LOW), (vectors.shape, F32),
         ((passages * rows, 3 * hw), LOW), ((passages, rows, width), LOW), weight, ((width, 3 * hw + 64), F32),
     ]
-    arrays = [*shards, w, qkv, chance, *grads, vectors]
+    arrays = [x, w, qkv, chance, *grads, vectors]
     return pl.pallas_call(
         attend_back_kernel,
-        in_specs=[SMEM] + [HBM] * len(arrays) + [ANYWHERE] * len(after),
-        out_specs=[HBM, HBM, vmem(), HBM],
-        out_shape=[pltpu.HBM(*back), pltpu.HBM(*back), jax.ShapeDtypeStruct(*weight), pltpu.HBM(*weight)],
+        in_specs=[SMEM] + [HBM] * 5 + [vmem()] + [HBM] * 2 + [HBM] * len(after),
+        out_specs=[HBM, HBM, vmem(), HBM, HBM],
+        out_shape=[pltpu.HBM(*back), pltpu.HBM(*back), jax.ShapeDtypeStruct(*weight), pltpu.HBM(*weight), TOKEN],
         scratch_shapes=[pltpu.VMEM(*kind) for kind in scratch]
         + [pltpu.SemaphoreType.DMA((passages * (heads + 9) + 2,)), pltpu.SemaphoreType.DMA((4 * passages + 1,))],
         compiler_params=pltpu.CompilerParams(vmem_limit_bytes=32 * MIB),
         cost_estimate=cost(BACK),
         name="attend_back",
-    )(place, *map(far, arrays), *after)
+    )(place, *map(far, arrays[:5]), arrays[5], *map(far, arrays[6:]), *map(far, after))
 
 
 def normalise(field):
@@ -400,11 +405,11 @@
     grad_attn = grad_one.astype(LOW)
     second_here[:, 4 * chunk :] = grad_attn
     moved[4].start()
-    sums_here[0:1, :] = jnp.sum(grad_attn.astype(F32), 0, keepdims=True)
-    stores[7].start()
     for j in range(2):
         near_here[j] = dot_nt(grad_attn, wa[me ^ j]).astype(LOW)
     stores[6].start()
+    sums_here[0:1, :] = jnp.sum(grad_attn.astype(F32), 0, keepdims=True)
+    stores[7].start()
     for j in range(2):
         across_out[j] = dot_nt(grad_attn, wa[me ^ (j + 2)]).astype(LOW)
     for copy in moved + stores:
@@ -422,7 +427,7 @@
     here = kinds[:5] + [((2, 4, hw, rows), LOW)] + kinds[7:]
     return pl.pallas_call(
         rows_kernel,
-        in_specs=[SMEM, vmem()] + [HBM] * 4 + [vmem()] * 4 + [HBM, HBM],
+        in_specs=[SMEM, vmem()] + [HBM] * 3 + [vmem()] * 5 + [HBM, HBM],
         out_specs=[HBM] * 9 + [vmem()],
         out_shape=[pltpu.HBM(*kind) for kind in kinds] + [jax.ShapeDtypeStruct((2, rows, hw), LOW)],
         scratch_shapes=[
@@ -437,10 +442,10 @@
         compiler_params=pltpu.CompilerParams(vmem_limit_bytes=36 * MIB),
         cost_estimate=cost(11),
         name="rows_pass",
-    )(where, x, *map(far, context), cot, wa, vec, ib, far(wi), far(wo))
-
-
-def outer_grad_kernel(place, active, active_got, grad, grad_got, send_out, keep_out):
+    )(where, x, *map(far, context[:3]), context[3], cot, wa, vec, ib, far(wi), far(wo))
+
+
+def outer_grad_kernel(place, active, active_got, grad, grad_got, send_out, keep_out, token):
     half = PIECES // 2
     n = grad.shape[1] // PIECES
     right = jnp.concatenate([grad[...], grad_got[...]], 0)
@@ -466,99 +471,112 @@
         outer_grad_kernel,
         grid=(2,),
         in_specs=[SMEM, side, side, last, last],
-        out_specs=[vmem(block, lambda y: (y, 0, 0, 0))] * 2,
-        out_shape=[jax.ShapeDtypeStruct((2,) + block[1:], LOW)] * 2,
+        out_specs=[vmem(block, lambda y: (y, 0, 0, 0))] * 2 + [HBM],
+        out_shape=[jax.ShapeDtypeStruct((2,) + block[1:], LOW)] * 2 + [TOKEN],
         compiler_params=pltpu.CompilerParams(vmem_limit_bytes=16 * MIB),
         cost_estimate=cost(30),
         name="outer_grad",
-    )(place, far(active), *map(far, (first_got, first, first_got)))
+    )(place, far(active), first_got, far(first), first_got)
 
 
 SPLIT = 128
 ORDERS = {
-    "a": ([2, 1, "y"], 4, [2, 1]),
-    "b": ([4, "y", 2], 1, [2, 4]),
-    "c": ([1, "y", 2], 4, [2, 1]),
-    "d": ([1, 2], 4, [1, 2]),
+    "a": ([1, "y", 2], 4, [2, 1]),
+    "b": (["y", 2, 1], 4, [2, 1]),
+    "c": ([2, 1, "y"], 4, [2, 1]),
+    "d": ([1, 4], 2, [1, 4]),
 }
-SEQUENCE = "cacdbcadbcabdcbdabda"
-
-
-def inner_grad_kernel(
-    mine, mine_got, inner, inner_got, attn, attn_got, *refs
-):
-    first_send, first_keep, second_send, second_keep, left, rest = refs[-6:]
-    step = pl.program_id(0)
-    hw = mine.shape[1]
-    rows, width = attn.shape
+SEQUENCE = "abcdbacbdacbddbcadca"
+
+
+def inner_grad_kernel(bit_b, bit_c, mine_hbm, second_hbm, mine_got, second_got, *refs):
+    outs, (mine, second, left, rest, *heres, load_sem, store_sem) = refs[-13:-9], refs[-8:]
+    hw, rows = mine.shape[1:]
+    width = 4 * hw
     half = PIECES // 2
     n = hw // PIECES
-    cols = inner.shape[1] // 2
-
-    @pl.when(step == 0)
-    def _():
-        grads = jnp.concatenate([attn[...], attn_got[...]], 0)
-        for y in range(2):
-            left[y * hw : (y + 1) * hw, :rows] = mine[y]
-            left[y * hw : (y + 1) * hw, rows:] = mine_got[y]
-            rest[y] = dot(jnp.concatenate([mine[2 + y], mine_got[2 + y]], 1), grads)
-
-    product = dot(left[...], jnp.concatenate([inner[...], inner_got[...]], 0))
-
-    bits = refs[:2]
-
-    def store(part, send_out, keep_out, which):
-        def put(out, y, at, k):
-            some = product[y * hw : (y + 1) * hw, k * cols : (k + 1) * cols]
-            if part == 0:
-                some = some[:SPLIT]
+    cols = width // 2
+    loads = [pltpu.make_async_copy(mine_hbm, mine, load_sem.at[5])]
+    for c in (4, 0, 1, 2, 3):
+        some = pl.ds(c * width, width)
+        loads.append(pltpu.make_async_copy(second_hbm.at[:, some], second.at[:, some], load_sem.at[c]))
+    for copy in loads:
+        copy.start()
+    for copy in loads[:2]:
+        copy.wait()
+    grads = jnp.concatenate([second[:, 4 * width :], second_got[:, 4 * width :]], 0)
+    for y in range(2):
+        left[y * hw : (y + 1) * hw, :rows] = mine[y]
+        left[y * hw : (y + 1) * hw, rows:] = mine_got[y]
+        rest[y] = dot(jnp.concatenate([mine[2 + y], mine_got[2 + y]], 1), grads)
+    waits = []
+
+    def send(part, piece, y, at, keep):
+        here = heres[part]
+        out = outs[2 * part + 1] if keep else outs[2 * part]
+        spot = (part * PIECES + piece) * 2 + y
+        copy = pltpu.make_async_copy(here.at[y, piece], out.at[at[0], at[1]], store_sem.at[spot])
+        copy.start()
+        return copy
+
+    for c in range(4):
+        loads[2 + c].wait()
+        here = slice(c * width, (c + 1) * width)
+        product = dot(left[...], jnp.concatenate([second[:, here], second_got[:, here]], 0))
+        for k in range(2):
+            piece = 2 * c + k
+            for y in range(2):
+                some = product[y * hw : (y + 1) * hw, k * cols : (k + 1) * cols]
+                heres[0][y, piece] = some[:SPLIT].astype(LOW)
+                more = rest[y, piece * n : (piece + 1) * n, :]
+                more = jnp.concatenate([some[SPLIT:], more[:, :cols], more[:, cols:]], 0)
+                heres[1][y, piece] = more.astype(LOW)
+        for part, (which, bit) in enumerate((("b", bit_b), ("c", bit_c))):
+            both = [(2 * c + k, y) for k in range(2) for y in range(2)]
+            if ORDERS[which][0][0] == "y":
+                for piece, y in both:
+                    waits.append(send(part, piece, y, (0, piece), y == 0))
             else:
-                more = rest[y, pl.ds(pl.multiple_of((2 * step + k) * n, 8), n), :]
-                some = jnp.concatenate([some[SPLIT:], more[:, : width // 2], more[:, width // 2 :]], 0)
-            out[at[0], at[1]] = some.astype(LOW)
-
-        if ORDERS[which][0][0] == "y":
-            for k in range(2):
-                for y, out in enumerate((keep_out, send_out)):
-                    put(out, y, (0, 2 * step + k), k)
-        else:
-            kept = (bits[part][0] & half) == (step >> 1) * half
-            for here, out in ((kept, keep_out), (jnp.logical_not(kept), send_out)):
-
-                @pl.when(here)
-                def _(out=out):
-                    for k in range(2):
-                        for y in range(2):
-                            put(out, y, (y, 2 * (step & 1) + k), k)
-
-    store(0, first_send, first_keep, "b")
-    store(1, second_send, second_keep, "c")
+                kept = (bit[0] & half) == (c >> 1) * half
+                for here, keep in ((kept, True), (jnp.logical_not(kept), False)):
+
+                    @pl.when(here)
+                    def _(part=part, both=both, keep=keep):
+                        for piece, y in both:
+                            send(part, piece, y, (y, piece % half), keep)
+
+                for piece, y in both:
+                    spot = (part * PIECES + piece) * 2 + y
+                    out = outs[2 * part].at[y, piece % half]
+                    waits.append(pltpu.make_async_copy(heres[part].at[y, piece], out, store_sem.at[spot]))
+    for copy in waits:
+        copy.wait()
 
 
 def inner_grad(places, mine, mine_got, second, second_got, after):
     hw = mine.shape[1]
-    rows = second.shape[0]
     width = 4 * hw
     half = PIECES // 2
-    cols = 4 * width // PIECES
     counts = [(1, PIECES) if ORDERS[which][0][0] == "y" else (2, half) for which in "bc"]
-    first = counts[0] + (SPLIT, cols)
-    rest = counts[1] + (hw - SPLIT + 2 * hw // PIECES, cols)
-    whole = lambda *s: vmem(s, lambda t: (0,) * len(s))
-    side = vmem((rows, 2 * cols), lambda t: (0, t))
-    last = vmem((rows, width), lambda t: (0, 4))
+    talls = [SPLIT, hw - SPLIT + 2 * hw // PIECES]
+    shapes = [count + (tall, width // 2) for count, tall in zip(counts, talls)]
     return pl.pallas_call(
         inner_grad_kernel,
-        grid=(half,),
-        in_specs=[whole(4, hw, rows), whole(4, hw, rows), side, side, last, last, SMEM, SMEM]
-        + [ANYWHERE] * len(after),
-        out_specs=[whole(*first)] * 2 + [whole(*rest)] * 2,
-        out_shape=[jax.ShapeDtypeStruct(s, LOW) for s in (first, first, rest, rest)],
-        scratch_shapes=[pltpu.VMEM((2 * hw, 2 * rows), LOW), pltpu.VMEM((2, hw, width), F32)],
+        in_specs=[SMEM, SMEM, HBM, HBM, vmem(), vmem()] + [HBM] * len(after),
+        out_specs=[HBM] * 5,
+        out_shape=[pltpu.HBM(shape, LOW) for shape in shapes for _ in range(2)] + [TOKEN],
+        scratch_shapes=[
+            pltpu.VMEM(mine.shape, LOW),
+            pltpu.VMEM(second.shape, LOW),
+            pltpu.VMEM((2 * hw, 2 * mine.shape[2]), LOW),
+            pltpu.VMEM((2, hw, width), F32),
+        ]
+        + [pltpu.VMEM((2, PIECES, tall, width // 2), LOW) for tall in talls]
+        + [pltpu.SemaphoreType.DMA((6,)), pltpu.SemaphoreType.DMA((4 * PIECES,))],
         compiler_params=pltpu.CompilerParams(vmem_limit_bytes=20 * MIB),
         cost_estimate=cost(4),
         name="inner_grad",
-    )(*map(far, (mine, mine_got, second, second_got, second, second_got)), *places, *after)
+    )(*places, far(mine), far(second), mine_got, second_got, *map(far, after))
 
 
 ANYWHERE = pl.BlockSpec(memory_space=pl.ANY)
@@ -567,7 +585,7 @@
 def sum_kernel(spec, place, *refs):
     leads, count, flip, inputs, splits = spec
     ins = refs[: len(inputs)]
-    outs = refs[-splits:]
+    outs = refs[-1 - splits : -1]
     first = (place[0] // count) * count
     if flip:
         first = first ^ count
@@ -596,13 +614,13 @@
         out_shape = [jax.ShapeDtypeStruct((count, tall // splits, wide), LOW)] * splits
     return pl.pallas_call(
         lambda *refs: sum_kernel(spec, *refs),
-        in_specs=[SMEM] + [vmem()] * len(inputs) + [ANYWHERE] * len(after),
-        out_specs=[vmem()] * splits,
-        out_shape=out_shape,
+        in_specs=[SMEM] + [vmem()] * len(inputs) + [HBM] * len(after),
+        out_specs=[vmem()] * splits + [HBM],
+        out_shape=out_shape + [TOKEN],
         compiler_params=pltpu.CompilerParams(vmem_limit_bytes=4 * MIB),
         cost_estimate=cost(STEP),
         name=name,
-    )(place, *inputs, *after)
+    )(place, *inputs, *map(far, after))
 
 
 def outer_place_kernel(spots, place, own, got, *refs):
@@ -617,13 +635,13 @@
     n, width = own.shape[1:]
     return pl.pallas_call(
         lambda *refs: outer_place_kernel(spots, *refs),
-        in_specs=[SMEM, vmem(), vmem()] + [ANYWHERE] * len(after),
+        in_specs=[SMEM, vmem(), vmem()] + [HBM] * len(after),
         out_specs=vmem(),
         out_shape=jax.ShapeDtypeStruct((PIECES * n, width), F32),
         compiler_params=pltpu.CompilerParams(vmem_limit_bytes=4 * MIB),
         cost_estimate=cost(2),
         name="outer_place",
-    )(place, own, got, *after)
+    )(place, own, got, *map(far, after))
 
 
 def inner_place_kernel(spots_one, spots_two, one, two, own, got, own_two, got_two, *refs):
@@ -647,7 +665,7 @@
     n = hw // PIECES
     return pl.pallas_call(
         lambda *refs: inner_place_kernel(spots_one, spots_two, *refs),
-        in_specs=[SMEM, SMEM] + [vmem()] * 4 + [ANYWHERE] * len(after),
+        in_specs=[SMEM, SMEM] + [vmem()] * 4 + [HBM] * len(after),
         out_specs=[vmem(), vmem()],
         out_shape=[
             jax.ShapeDtypeStruct((hw, PIECES * cols), F32),
@@ -656,7 +674,7 @@
         compiler_params=pltpu.CompilerParams(vmem_limit_bytes=4 * MIB),
         cost_estimate=cost(2),
         name="inner_place",
-    )(one, two, *parts_one, *parts_two, *after)
+    )(one, two, *parts_one, *parts_two, *map(far, after))
 
 
 def project_place_kernel(spots, place, own, got, *refs):
@@ -685,7 +703,7 @@
     n = tall // 4
     return pl.pallas_call(
         lambda *refs: project_place_kernel(spots, *refs),
-        in_specs=[SMEM, vmem(), vmem()] + [ANYWHERE] * len(after),
+        in_specs=[SMEM, vmem(), vmem()] + [HBM] * len(after),
         out_specs=[vmem(), vmem()],
         out_shape=[
             jax.ShapeDtypeStruct((PIECES * n, 12 * hw), F32),
@@ -695,11 +713,11 @@
         compiler_params=pltpu.CompilerParams(vmem_limit_bytes=4 * MIB),
         cost_estimate=cost(2),
         name="project_place",
-    )(place, own, got, *after)
+    )(place, own, got, *map(far, after))
 
 
 def join_kernel(*refs):
-    out, sem = refs[-2:]
+    out, token, sem = refs[-3:]
     own, got = refs[:2]
     n = own.shape[0]
     copies = [pltpu.make_async_copy(f, out.at[pl.ds(i * n, n)], sem.at[i]) for i, f in enumerate((own, got))]
@@ -713,18 +731,40 @@
     shape = (2 * own.shape[0],) + own.shape[1:]
     return pl.pallas_call(
         join_kernel,
-        in_specs=[ANYWHERE] * (2 + len(after)),
-        out_specs=ANYWHERE,
-        out_shape=jax.ShapeDtypeStruct(shape, own.dtype),
+        in_specs=[ANYWHERE] * 2 + [HBM] * len(after),
+        out_specs=[ANYWHERE, HBM],
+        out_shape=[jax.ShapeDtypeStruct(shape, own.dtype), TOKEN],
         scratch_shapes=[pltpu.SemaphoreType.DMA((2,))],
         compiler_params=pltpu.CompilerParams(vmem_limit_bytes=2 * MIB),
         cost_estimate=cost(STEP),
         name="join",
-    )(own, got, *after)
-
-
-def pair_kernel(gates, near, far, *refs):
-    out, sem = refs[-1 - gates - 1], refs[-1]
+    )(own, got, *map(far, after))
+
+
+def pass_on_kernel(source, *refs):
+    outs, sem = refs[-3:-1], refs[-1]
+    copies = [pltpu.make_async_copy(source, out, sem.at[i]) for i, out in enumerate(outs)]
+    for copy in copies:
+        copy.start()
+    for copy in copies:
+        copy.wait()
+
+
+def pass_on(source, after):
+    return pl.pallas_call(
+        pass_on_kernel,
+        in_specs=[vmem()] + [HBM] * len(after),
+        out_specs=[vmem(), HBM],
+        out_shape=[jax.ShapeDtypeStruct(source.shape, source.dtype), pltpu.HBM(source.shape, source.dtype)],
+        scratch_shapes=[pltpu.SemaphoreType.DMA((2,))],
+        compiler_params=pltpu.CompilerParams(vmem_limit_bytes=2 * MIB),
+        cost_estimate=cost(0.5),
+        name="pass_on",
+    )(source, *map(far, after))
+
+
+def pair_kernel(near, far, *refs):
+    out, token, sem = refs[-3:]
     copies = [pltpu.make_async_copy(f.at[1], out.at[i], sem.at[i]) for i, f in enumerate((near, far))]
     for copy in copies:
         copy.start()
@@ -732,18 +772,17 @@
         copy.wait()
 
 
-def pair(near, far, gated, after=()):
-    return pl.pallas_call(
-        lambda *refs: pair_kernel(len(gated), *refs),
-        in_specs=[ANYWHERE] * (2 + len(gated) + len(after)),
-        out_specs=[ANYWHERE] * (1 + len(gated)),
-        out_shape=[jax.ShapeDtypeStruct(f.shape, f.dtype) for f in (near, *gated)],
-        input_output_aliases={2 + i: 1 + i for i in range(len(gated))},
+def pair(near, far_got, after):
+    return pl.pallas_call(
+        pair_kernel,
+        in_specs=[ANYWHERE] * 2 + [HBM] * len(after),
+        out_specs=[ANYWHERE, HBM],
+        out_shape=[jax.ShapeDtypeStruct(near.shape, near.dtype), TOKEN],
         scratch_shapes=[pltpu.SemaphoreType.DMA((2,))],
         compiler_params=pltpu.CompilerParams(vmem_limit_bytes=2 * MIB),
         cost_estimate=cost(0.5),
         name="pair",
-    )(near, far, *gated, *after)
+    )(near, far_got, *map(far, after))
 
 
 def swap(field, axis, bit):
@@ -783,21 +822,21 @@
             return sum_pieces(self.place, self.arrays, [0], self.left, False, after, splits, name)
         leads = [0] if self.folded else [0, 1]
         if not self.order:
-            (sent,) = sum_pieces(self.place, self.arrays, [0], self.left, False, after, name=name)
+            sent, token = sum_pieces(self.place, self.arrays, [0], self.left, False, after, name=name)
             self.arrays = [sent, swap(sent, "dp", self.last)]
             self.last = None
-            return sent
+            return token
         axis = self.order.pop(0)
         if axis == "y":
-            (sent,) = sum_pieces(self.place, self.arrays, [1], self.left, False, after, name=name)
+            sent, token = sum_pieces(self.place, self.arrays, [1], self.left, False, after, name=name)
             self.folded = True
             got = swap(sent, "seq", 2)
         else:
             self.left //= 2
-            (sent,) = sum_pieces(self.place, self.arrays, leads, self.left, True, after, name=name)
+            sent, token = sum_pieces(self.place, self.arrays, leads, self.left, True, after, name=name)
             got = swap(sent, "dp", axis)
         self.arrays = self.arrays + [got]
-        return sent
+        return token
 
     def start(self, piece):
         for bit in self.rest:
@@ -807,10 +846,10 @@
         self.done = 1
 
     def grow(self, after):
-        self.own = join(self.own, self.got, after)
+        self.own, token = join(self.own, self.got, after)
         self.got = swap(self.own, "dp", self.back[self.done])
         self.done += 1
-        return self.own
+        return token
 
 
 def local(
@@ -830,14 +869,16 @@
 
     across = swap(tokens, "seq", 2)
     beside = swap(tokens, "seq", 1)
-    corner = swap(across, "seq", 1)
+    biases = (query_bias.reshape(1, width), value_bias.reshape(1, width))
+    w, bias, token = choose_heads(where, query_key_value, *biases)
+    passed, across = pass_on(across, [token])
+    corner = swap(passed, "seq", 1)
     shards = (tokens, beside, across, corner)
     vec = jnp.stack([attn_bias, attn_gain, attn_shift, outer_bias, ffn_gain, ffn_shift, ffn_shift, ffn_shift])
     vec = vec.astype(F32)
     ib = inner_bias.astype(F32).reshape(1, ff)
 
-    w, bias = choose_heads(where, query_key_value, query_bias.reshape(1, width), value_bias.reshape(1, width))
-    qkv, chance, own, *context_h = attend(where, lengths, shards, w, bias)
+    qkv, chance, own, x_all, *context_h = attend(where, lengths, shards, w, bias)
     context = [own] + [swap(part, "seq", j) for j, part in zip((1, 2, 3), context_h)]
     context = [part.reshape(rows, hw) for part in context]
 
@@ -851,28 +892,27 @@
     mine_got = swap(mine_send, "seq", 1)
     a, b, c, d = (Reduction(*ORDERS[which], lane, me, rest) for which in "abcd")
     far_got = swap(across_heads, "seq", 2)
-    outer_send, outer_keep = outer_grad(a.place, active, first, first_got)
-    (near_send,) = pair(near, far_got, [], [outer_send])
+    outer_send, outer_keep, token = outer_grad(a.place, active, first, first_got)
+    near_send, paired = pair(near, far_got, [token])
     near_got = swap(near_send, "seq", 1)
     a.begin(outer_keep, outer_send)
-    first_send, first_keep, second_send, second_keep = inner_grad(
-        [b.place, c.place], mine, mine_got, second, second_got, [near_send]
+    first_send, first_keep, second_send, second_keep, token = inner_grad(
+        [b.place, c.place], mine, mine_got, second, second_got, [paired]
     )
     b.begin(first_keep, first_send)
     c.begin(second_keep, second_send)
     grads_h = [f.reshape(2, passages, quarter, hw) for f in (near, near_got, far_got)]
-    back_keep, back_send, project_send, project_keep = attend_back(
-        d.place, shards, w, qkv, chance, grads_h, vectors, [second_send]
+    back_keep, back_send, project_send, project_keep, token = attend_back(
+        d.place, x_all, w, qkv, chance, grads_h, vectors, [token]
     )
     d.begin(project_keep, project_send)
     back_got = swap(back_send, "seq", 1)
-    (back_sum,) = sum_pieces(
+    back_sum, _ = sum_pieces(
         d.place,
         [f.reshape(2, 1, rows, width) for f in (back_keep, back_got)],
         [1], 1, False, name="back_y",
     )
     back_over = swap(back_sum, "seq", 2)
-    token = back_keep
     parts = None
     for letter in SEQUENCE:
         chunk = {"a": a, "b": b, "c": c, "d": d}[letter]
@@ -881,14 +921,13 @@
         elif chunk.own is not None:
             token = chunk.grow([token])
         elif chunk is d and parts is None:
-            parts = d.step([token], splits=4, name="total_d")
-            token = parts[0]
+            *parts, token = d.step([token], splits=4, name="total_d")
             parts = [parts[0]] + [swap(parts[j], "seq", j) for j in (1, 2, 3)]
         elif chunk is d:
             d.start(jnp.concatenate(parts, 1))
         else:
-            (token,) = chunk.step([token], name="total_" + letter)
-            chunk.start(token[0])
+            total, token = chunk.step([token], name="total_" + letter)
+            chunk.start(total[0])
     grad_query_key_value, summed = project_place(d.spots, d.place, d.own, d.got, hw)
     grad_outer_weight = outer_place(a.spots, a.place, a.own, a.got)
     grad_inner_weight, grad_attn_weight = inner_place(

time: 181 us -> 171 us (0.945)
  waiting for transfers between devices: 68.8 us -> 56.3 us
  local copies, waits for them, and re-layouts: 8.66 us -> 2.94 us
  starting transfers between devices: 38.6 us -> 44.2 us
  Pallas kernels: 62.5 us -> 65 us
    ppermute x39, waiting for transfers between devices: 68.8 us -> 56.3 us  [swap(): return lax.ppermute(field, axis, [(i, i ^ bit) for i in range(count)])]
    unnamed x57 -> x49, local copies, waits for them, and re-layouts: 5.87 us -> 0.15 us
    ppermute x39, starting transfers between devices: 38.6 us -> 44.2 us  [swap(): return lax.ppermute(field, axis, [(i, i ^ bit) for i in range(count)])]
    pallas_call x16, Pallas kernels: 10.1 us -> 12.1 us  [sum_pieces(): pl.pallas_call(lambda *refs: sum_kernel(spec, *refs), in_specs=[SMEM] + [...]
    pallas_call x9 -> x10, Pallas kernels: 39.8 us -> 40.6 us  [the longest x1 12.4 us: attend_back(): pl.pallas_call(attend_back_kernel, in_specs=[SMEM] + [HBM] * 5 + [vmem()]...]
  transfers between devices with their start and end apart: 39 -> 39, of which waited for: 15 -> 18; matrix products, arithmetic and copies ran while one was open for 2% -> 2% of each run, Pallas kernels for 22% -> 25%
where the time goes in v5:
time: 171 us
  Pallas kernels  65 us (38%)
  waiting for transfers between devices  56.3 us (33%)
  starting transfers between devices  44.2 us (26%)
  local copies, waits for them, and re-layouts  2.94 us (2%)
    ppermute x39, waiting for transfers between devices, swap(): return lax.ppermute(field, axis, [(i, i ^ bit) for i in range(count)])  56.3 us
    ppermute x39, starting transfers between devices, swap(): return lax.ppermute(field, axis, [(i, i ^ bit) for i in range(count)])  44.2 us
    pallas_call x1, Pallas kernels, attend_back(): pl.pallas_call(attend_back_kernel, in_specs=[SMEM] + [HBM] * 5 + [vmem()]...  12.4 us
    pallas_call x16, Pallas kernels, sum_pieces(): pl.pallas_call(lambda *refs: sum_kernel(spec, *refs), in_specs=[SMEM] + [...  12.1 us
    pallas_call x1, Pallas kernels, rows_pass(): pl.pallas_call(rows_kernel, in_specs=[SMEM, vmem()] + [HBM] * 3 + [vmem()...  11.9 us
    pallas_call x1, Pallas kernels, attend(): pl.pallas_call(attend_kernel, in_specs=[SMEM, SMEM] + [HBM] * 3 + [vmem()...  7.52 us
    pallas_call x1, Pallas kernels, inner_grad(): pl.pallas_call(inner_grad_kernel, in_specs=[SMEM, SMEM, HBM, HBM, vmem(),...  5.69 us
  transfers between devices with their start and end apart: 39, of which 18 were waited for; matrix products, arithmetic and copies ran while one was open for 2% of the time, Pallas kernels for 25%

profile of v5, /device:TPU:0, one launch (start us, length us, event | category | flops | bytes accessed | tf_op | source)
XLA Modules:
  0.0 170.9 jit_solution(12120128748614613571)
XLA Ops:
  0.6 3.0 %collective-permute-start.1 = (bf16[2,128,768]{2,1,0:T(8,128)(2,1)}, bf16[2,128,768]{2,1,0:T(8,128)(2,1)S(1)}, u32[]{:S(2)}, u32[]{:S(2)}) collective-permute-start(bf16[2,128,768]{2,1,0:T(8,128)(2,1)} %x0.1), channel_id=1, source_target_pairs={{0,2},{1,3},{2,0},{3,1},{4,6},{5,7},{6,4},{7,5},{8,10},{9,11},{10,... | collective-permute-start | bytes 1179656 | tf_op jit(solution)/shard_map/ppermute | solution.py:790
  5.1 2.7 %choose_heads.1 = (bf16[768,576]{1,0:T(8,128)(2,1)}, f32[2,192]{1,0:T(2,128)S(1)}, f32[8,128]{1,0:T(8,128)}) custom-call(s32[1]{0:T(128)} %bitcast.where, bf16[768,2304]{1,0:T(8,128)(2,1)} %w_hbm.1, bf16[1,768]{1,0:T(2,128)(2,1)S(1)} %reshape.97.qb, bf16[1,768]{1,0:T(2,128)(2,1)S(1)} %reshape.98.vb), custom_call_target="tpu_custom_call" | custom-call | flops 1724999936 | bytes 5535000 | tf_op jit(solution)/shard_map/choose_heads/pallas_call | solution.py:87
  7.8 5.2 %collective-permute-done.1.source = bf16[2,128,768]{2,1,0:T(8,128)(2,1)S(1)} collective-permute-done((bf16[2,128,768]{2,1,0:T(8,128)(2,1)}, bf16[2,128,768]{2,1,0:T(8,128)(2,1)S(1)}, u32[]{:S(2)}, u32[]{:S(2)}) %collective-permute-start.1) | collective-permute-done | bytes 393248 | tf_op jit(solution)/shard_map/ppermute | solution.py:790
  14.2 1.7 collective-permute-done.2.x3
  15.9 7.5 %attend.1 = (bf16[2,512,576]{2,1,0:T(8,128)(2,1)}, bf16[2,3,512,512]{3,2,1,0:T(8,128)(2,1)}, bf16[2,128,192]{2,1,0:T(8,128)(2,1)}, bf16[2,512,768]{2,1,0:T(8,128...) custom-call(s32[1]{0:T(128)} %bitcast.where, ...), custom_call_target="tpu_custom_call" | custom-call | flops 115000000 | bytes 369000 | tf_op jit(solution)/shard_map/attend/pallas_call | solution.py:167
  23.6 1.8 %collective-permute-start.4 = (bf16[2,128,192]{2,1,0:T(8,128)(2,1)S(1)}, bf16[2,128,192]{2,1,0:T(8,128)(2,1)S(1)}, u32[]{:S(2)}, u32[]{:S(2)}) collective-permute-start(bf16[2,128,192]{2,1,0:T(8,128)(2,1)S(1)} %get-tuple-element.104), channel_id=1, source_target_pairs={{0,2},{1,3},{2,0},{3,1},{4,6},{5,7},{6,4},{7,5},{8,10},{9,11},{10,... | collective-permute-start | bytes 294920 | tf_op jit(solution)/shard_map/ppermute | solution.py:790
  25.6 4.3 %collective-permute-done.4 = bf16[2,128,192]{2,1,0:T(8,128)(2,1)S(1)} collective-permute-done((bf16[2,128,192]{2,1,0:T(8,128)(2,1)S(1)}, bf16[2,128,192]{2,1,0:T(8,128)(2,1)S(1)}, u32[]{:S(2)}, u32[]{:S(2)}) %collective-permute-start.4) | collective-permute-done | bytes 98336 | tf_op jit(solution)/shard_map/ppermute | solution.py:790
  29.9 1.7 collective-permute-done.5
  31.7 11.9 %rows_pass.1 = (bf16[256,768]{1,0:T(8,128)(2,1)}, f32[256,768]{1,0:T(8,128)}, bf16[256,1536]{1,0:T(8,128)(2,1)}, bf16[256,2304]{1,0:T(8,128)(2,1)}, bf16[256,384...) custom-call(s32[1]{0:T(128)} %bitcast.where, ...), custom_call_target="tpu_custom_call" | custom-call | flops 12650000384 | bytes 40590000 | tf_op jit(solution)/shard_map/rows_pass/pallas_call | solution.py:428
  44.1 1.7 %collective-permute-start.6 = (bf16[2,256,192]{2,1,0:T(8,128)(2,1)S(1)}, bf16[2,256,192]{2,1,0:T(8,128)(2,1)S(1)}, u32[]{:S(2)}, u32[]{:S(2)}) collective-permute-start(bf16[2,256,192]{2,1,0:T(8,128)(2,1)S(1)} %get-tuple-element.112), channel_id=1, source_target_pairs={{0,2},{1,3},{2,0},{3,1},{4,6},{5,7},{6,4},{7,5},{8,10},{9,11},{10,... | collective-permute-start | bytes 589832 | tf_op jit(solution)/shard_map/ppermute | solution.py:790
  46.7 3.1 %outer_grad.1 = (bf16[2,4,96,768]{3,2,1,0:T(8,128)(2,1)S(1)}, bf16[2,4,96,768]{3,2,1,0:T(8,128)(2,1)S(1)}, f32[8,128]{1,0:T(8,128)}) custom-call(s32[2]{0:T(128)S(1)} %pad_add_fusion.1.place.refs_0_, bf16[256,1536]{1,0:T(8,128)(2,1)} %get-tuple-element.113.active, bf16[256,2304]{1,0:T(8,128)(2,1)S(1)} %collective-permute-done.7.active_got.grad_got, ...), custom_call_target="tpu_custom_call" | custom-call | flops 34500001792 | bytes 110700000 | tf_op jit(solution)/shard_map/outer_grad/pallas_call | solution.py:470
  49.8 1.8 %collective-permute-start.16 = (bf16[2,4,96,768]{3,2,1,0:T(8,128)(2,1)S(1)}, bf16[2,4,96,768]{3,2,1,0:T(8,128)(2,1)S(1)}, u32[]{:S(2)}, u32[]{:S(2)}) collective-permute-start(bf16[2,4,96,768]{3,2,1,0:T(8,128)(2,1)S(1)} %get-tuple-element.133), channel_id=1, source_target_pairs={{0,4},{4,0},{8,12},{12,8},{16,20},{20,16},{24,28},{28,24},{1,5},{5... | collective-permute-start | bytes 3538952 | tf_op jit(solution)/shard_map/ppermute | solution.py:790
  52.9 5.7 %inner_grad.1 = (bf16[1,8,128,384]{3,2,1,0:T(8,128)(2,1)}, bf16[1,8,128,384]{3,2,1,0:T(8,128)(2,1)}, bf16[2,4,112,384]{3,2,1,0:T(8,128)(2,1)}, bf16[2,4,112,384]{3,2,1,0:T(8,128)(2,1)}, f32[8,128]{1,0:T(8,128)}) custom-call(s32[2]{0:T(128)S(1)} %pad_add_fusion.2.bit_b.bit_c.refs_0_.refs_1_, s32[2]{0:T(128)S(1)} %pad_add_fusion.2.bit_b.bit_c.refs_0_.refs_1_, ...), custom_call_target="tpu_custom_call" | custom-call | flops 4600000000 | bytes 14760000 | tf_op jit(solution)/shard_map/inner_grad/pallas_call | solution.py:563
  58.6 1.8 %collective-permute-start.15 = (bf16[1,8,128,384]{3,2,1,0:T(8,128)(2,1)}, bf16[1,8,128,384]{3,2,1,0:T(8,128)(2,1)}, u32[]{:S(2)}, u32[]{:S(2)}) collective-permute-start(bf16[1,8,128,384]{3,2,1,0:T(8,128)(2,1)} %get-tuple-element.131), channel_id=1, source_target_pairs={{0,2},{1,3},{2,0},{3,1},{4,6},{5,7},{6,4},{7,5},{8,10},{9,11},{10,... | collective-permute-start | bytes 2359304 | tf_op jit(solution)/shard_map/ppermute | solution.py:790
  60.5 1.6 collective-permute-start.14
  62.0 12.4 %attend_back.1 = (bf16[2,2,128,768]{3,2,1,0:T(8,128)(2,1)}, bf16[2,2,128,768]{3,2,1,0:T(8,128)(2,1)}, bf16[1,4,96,640]{3,2,1,0:T(8,128)(2,1)S(1)}, bf16[1,4,96,640]{3,2,1,0:T(8,128)(2,1)}, f32[8,128]{1,0:T(8,128)}) custom-call(s32[2]{0:T(128)S(1)} %pad_add_fusion.place.refs_0_, bf16[2,512,768]{2,1,0:T(8,128)(2,1)} %get-tuple-element.108.refs_0_, ...), custom_call_target="tpu_custom_call" | custom-call | flops 1150000000 | bytes 3690000 | tf_op jit(solution)/shard_map/attend_back/pallas_call | solution.py:282
  74.6 1.6 collective-permute-start.13
  76.1 2.3 %collective-permute-done.16.refs_2_ = bf16[2,4,96,768]{3,2,1,0:T(8,128)(2,1)S(1)} collective-permute-done((bf16[2,4,96,768]{3,2,1,0:T(8,128)(2,1)S(1)}, bf16[2,4,96,768]{3,2,1,0:T(8,128)(2,1)S(1)}, u32[]{:S(2)}, u32[]{:S(2)}) %collective-permute-start.16) | collective-permute-done | bytes 1179680 | tf_op jit(solution)/shard_map/ppermute | solution.py:790
  79.2 2.0 %collective-permute-start.21 = (bf16[1,4,96,768]{3,2,1,0:T(8,128)(2,1)S(1)}, bf16[1,4,96,768]{3,2,1,0:T(8,128)(2,1)S(1)}, u32[]{:S(2)}, u32[]{:S(2)}) collective-permute-start(bf16[1,4,96,768]{3,2,1,0:T(8,128)(2,1)S(1)} %get-tuple-element.143), channel_id=1, source_target_pairs={{0,2},{1,3},{2,0},{3,1},{4,6},{5,7},{6,4},{7,5},{8,10},{9,11},{10,... | collective-permute-start | bytes 1769480 | tf_op jit(solution)/shard_map/ppermute | solution.py:790
  81.2 1.4 sum_b.3
  82.6 1.6 collective-permute-start.18
  84.9 1.6 collective-permute-start.20
  87.7 1.3 collective-permute-done.13.refs_2_
  89.6 3.1 %collective-permute-start.17 = (bf16[1,2,96,640]{3,2,1,0:T(8,128)(2,1)S(1)}, bf16[1,2,96,640]{3,2,1,0:T(8,128)(2,1)S(1)}, u32[]{:S(2)}, u32[]{:S(2)}) collective-permute-start(bf16[1,2,96,640]{3,2,1,0:T(8,128)(2,1)S(1)} %get-tuple-element.138), channel_id=1, source_target_pairs={{0,16},{4,20},{8,24},{12,28},{16,0},{20,4},{24,8},{28,12},{1,17},{... | collective-permute-start | bytes 737288 | tf_op jit(solution)/shard_map/ppermute | solution.py:790
  92.7 1.2 sum_b.4
  94.0 1.6 collective-permute-start.19
  96.2 2.0 %collective-permute-start.25 = (bf16[1,2,96,768]{3,2,1,0:T(8,128)(2,1)S(1)}, bf16[1,2,96,768]{3,2,1,0:T(8,128)(2,1)S(1)}, u32[]{:S(2)}, u32[]{:S(2)}) collective-permute-start(bf16[1,2,96,768]{3,2,1,0:T(8,128)(2,1)S(1)} %get-tuple-element.151), channel_id=1, source_target_pairs={{0,8},{4,12},{8,0},{12,4},{16,24},{20,28},{24,16},{28,20},{1,9},{5... | collective-permute-start | bytes 884744 | tf_op jit(solution)/shard_map/ppermute | solution.py:790
  98.9 1.6 collective-permute-start.24
  100.4 1.3 sum_b.5
  101.7 2.7 %collective-permute-start.23 = (bf16[1,2,128,384]{3,2,1,0:T(8,128)(2,1)S(1)}, bf16[1,2,128,384]{3,2,1,0:T(8,128)(2,1)S(1)}, u32[]{:S(2)}, u32[]{:S(2)}) collective-permute-start(bf16[1,2,128,384]{3,2,1,0:T(8,128)(2,1)S(1)} %get-tuple-element.149.refs_1_), channel_id=1, source_target_pairs={{0,16},{4,20},{8,24},{12,28},{16,0},{20,4},{24,8},{28,12},{1,17},{... | collective-permute-start | bytes 589832 | tf_op jit(solution)/shard_map/ppermute | solution.py:790
  105.0 1.7 collective-permute-start.22
  106.7 9.1 %collective-permute-done.25.refs_4_ = bf16[1,2,96,768]{3,2,1,0:T(8,128)(2,1)S(1)} collective-permute-done((bf16[1,2,96,768]{3,2,1,0:T(8,128)(2,1)S(1)}, bf16[1,2,96,768]{3,2,1,0:T(8,128)(2,1)S(1)}, u32[]{:S(2)}, u32[]{:S(2)}) %collective-permute-start.25) | collective-permute-done | bytes 294944 | tf_op jit(solution)/shard_map/ppermute | solution.py:790
  117.3 2.9 %collective-permute-start.30 = (bf16[1,2,96,768]{3,2,1,0:T(8,128)(2,1)S(1)}, bf16[1,2,96,768]{3,2,1,0:T(8,128)(2,1)S(1)}, u32[]{:S(2)}, u32[]{:S(2)}) collective-permute-start(bf16[1,2,96,768]{3,2,1,0:T(8,128)(2,1)S(1)} %get-tuple-element.160.refs_1_), channel_id=1, source_target_pairs={{0,16},{4,20},{8,24},{12,28},{16,0},{20,4},{24,8},{28,12},{1,17},{... | collective-permute-start | bytes 884744 | tf_op jit(solution)/shard_map/ppermute | solution.py:790
  120.9 1.9 %collective-permute-done.22.refs_2_ = bf16[1,2,96,640]{3,2,1,0:T(8,128)(2,1)S(1)} collective-permute-done((bf16[1,2,96,640]{3,2,1,0:T(8,128)(2,1)S(1)}, bf16[1,2,96,640]{3,2,1,0:T(8,128)(2,1)S(1)}, u32[]{:S(2)}, u32[]{:S(2)}) %collective-permute-start.22) | collective-permute-done | bytes 245792 | tf_op jit(solution)/shard_map/ppermute | solution.py:790
  123.5 1.2 collective-permute-done.26
  124.7 4.2 %collective-permute-done.27 = bf16[2,24,640]{2,1,0:T(8,128)(2,1)S(1)} collective-permute-done((bf16[2,24,640]{2,1,0:T(8,128)(2,1)S(1)}, bf16[2,24,640]{2,1,0:T(8,128)(2,1)S(1)}, u32[]{:S(2)}, u32[]{:S(2)}) %collective-permute-start.27) | collective-permute-done | bytes 61472 | tf_op jit(solution)/shard_map/ppermute | solution.py:790
  129.0 3.8 %collective-permute-done.28 = bf16[2,24,640]{2,1,0:T(8,128)(2,1)S(1)} collective-permute-done((bf16[2,24,640]{2,1,0:T(8,128)(2,1)S(1)}, bf16[2,24,640]{2,1,0:T(8,128)(2,1)S(1)}, u32[]{:S(2)}, u32[]{:S(2)}) %collective-permute-start.28) | collective-permute-done | bytes 61472 | tf_op jit(solution)/shard_map/ppermute | solution.py:790
  134.7 2.0 %collective-permute-start.37 = (bf16[2,96,768]{2,1,0:T(8,128)(2,1)S(1)}, bf16[2,96,768]{2,1,0:T(8,128)(2,1)S(1)}, u32[]{:S(2)}, u32[]{:S(2)}) collective-permute-start(bf16[2,96,768]{2,1,0:T(8,128)(2,1)S(1)} %bitcast.48), channel_id=1, source_target_pairs={{0,8},{4,12},{8,0},{12,4},{16,24},{20,28},{24,16},{28,20},{1,9},{5... | collective-permute-start | bytes 884744 | tf_op jit(solution)/shard_map/ppermute | solution.py:790
  136.8 2.0 %collective-permute-start.34 = (bf16[4,128,384]{2,1,0:T(8,128)(2,1)S(1)}, bf16[4,128,384]{2,1,0:T(8,128)(2,1)S(1)}, u32[]{:S(2)}, u32[]{:S(2)}) collective-permute-start(bf16[4,128,384]{2,1,0:T(8,128)(2,1)S(1)} %get-tuple-element.170.refs_2_), channel_id=1, source_target_pairs={{0,4},{4,0},{8,12},{12,8},{16,20},{20,16},{24,28},{28,24},{1,5},{5... | collective-permute-start | bytes 1179656 | tf_op jit(solution)/shard_map/ppermute | solution.py:790
  138.7 2.9 %collective-permute-done.29.refs_1_ = bf16[2,96,640]{2,1,0:T(8,128)(2,1)S(1)} collective-permute-done((bf16[2,96,640]{2,1,0:T(8,128)(2,1)S(1)}, bf16[2,96,640]{2,1,0:T(8,128)(2,1)S(1)}, u32[]{:S(2)}, u32[]{:S(2)}) %collective-permute-start.29) | collective-permute-done | bytes 245792 | tf_op jit(solution)/shard_map/ppermute | solution.py:790
  144.8 5.9 %collective-permute-done.37.refs_1_ = bf16[2,96,768]{2,1,0:T(8,128)(2,1)S(1)} collective-permute-done((bf16[2,96,768]{2,1,0:T(8,128)(2,1)S(1)}, bf16[2,96,768]{2,1,0:T(8,128)(2,1)S(1)}, u32[]{:S(2)}, u32[]{:S(2)}) %collective-permute-start.37) | collective-permute-done | bytes 294944 | tf_op jit(solution)/shard_map/ppermute | solution.py:790
  150.8 2.9 %collective-permute-start.38 = (bf16[4,96,768]{2,1,0:T(8,128)(2,1)S(1)}, bf16[4,96,768]{2,1,0:T(8,128)(2,1)S(1)}, u32[]{:S(2)}, u32[]{:S(2)}) collective-permute-start(bf16[4,96,768]{2,1,0:T(8,128)(2,1)S(1)} %get-tuple-element.178.refs_1_), channel_id=1, source_target_pairs={{0,4},{4,0},{8,12},{12,8},{16,20},{20,16},{24,28},{28,24},{1,5},{5... | collective-permute-start | bytes 1769480 | tf_op jit(solution)/shard_map/ppermute | solution.py:790
  153.7 3.8 %collective-permute-done.36.refs_5_ = bf16[4,112,384]{2,1,0:T(8,128)(2,1)S(1)} collective-permute-done((bf16[4,112,384]{2,1,0:T(8,128)(2,1)S(1)}, bf16[4,112,384]{2,1,0:T(8,128)(2,1)S(1)}, u32[]{:S(2)}, u32[]{:S(2)}) %collective-permute-start.36) | collective-permute-done | bytes 344096 | tf_op jit(solution)/shard_map/ppermute | solution.py:790
  157.5 2.3 %inner_place.1 = (f32[192,3072]{1,0:T(8,128)}, f32[192,768]{1,0:T(8,128)}) custom-call(s32[2]{0:T(128)S(1)} %pad_add_fusion.2.bit_b.bit_c.refs_0_.refs_1_, s32[2]{0:T(128)S(1)} %pad_add_fusion.2.bit_b.bit_c.refs_0_.refs_1_, bf16[4,128,384]{2,1,0:T(8,128)(2,1)S(1)} %get-tuple-element.170.refs_2_, bf16[4,128,384]{2,1,0:T(8,128)(2,1)S(1)} %collective-permute-done.34.refs_3_, ...), custom_call_target="tpu_custom_call" | custom-call | flops 2300000000 | bytes 7380000 | tf_op jit(solution)/shard_map/inner_place/pallas_call | solution.py:666
  159.8 4.6 %collective-permute-done.33.refs_2_ = bf16[4,96,640]{2,1,0:T(8,128)(2,1)S(1)} collective-permute-done((bf16[4,96,640]{2,1,0:T(8,128)(2,1)S(1)}, bf16[4,96,640]{2,1,0:T(8,128)(2,1)S(1)}, u32[]{:S(2)}, u32[]{:S(2)}) %collective-permute-start.33) | collective-permute-done | bytes 491552 | tf_op jit(solution)/shard_map/ppermute | solution.py:790
  164.4 2.0 %project_place.1 = (f32[192,2304]{1,0:T(8,128)}, f32[16,192]{1,0:T(8,128)S(1)}) custom-call(s32[2]{0:T(128)S(1)} %pad_add_fusion.place.refs_0_, bf16[4,96,640]{2,1,0:T(8,128)(2,1)S(1)} %get-tuple-element.167.refs_1_, bf16[4,96,640]{2,1,0:T(8,128)(2,1)S(1)} %collective-permute-done.33.refs_2_), custom_call_target="tpu_custom_call" | custom-call | flops 2300000000 | bytes 7380000 | tf_op jit(solution)/shard_map/project_place/pallas_call | solution.py:704
  167.7 1.1 collective-permute-done.38.refs_2_
  168.8 2.1 %outer_place.1 = f32[768,768]{1,0:T(8,128)} custom-call(s32[2]{0:T(128)S(1)} %pad_add_fusion.1.place.refs_0_, bf16[4,96,768]{2,1,0:T(8,128)(2,1)S(1)} %get-tuple-element.178.refs_1_, bf16[4,96,768]{2,1,0:T(8,128)(2,1)S(1)} %collective-permute-done.38.refs_2_), custom_call_target="tpu_custom_call" | custom-call | flops 2300000000 | bytes 7380000 | tf_op jit(solution)/shard_map/outer_place/pallas_call | solution.py:636
  (131 shorter events, 20.0 us)
Async XLA Ops:
  0.6 12.4 %collective-permute-start.1 = (bf16[2,128,768]{2,1,0:T(8,128)(2,1)}, bf16[2,128,768]{2,1,0:T(8,128)(2,1)S(1)}, u32[]{:S(2)}, u32[]{:S(2)}) collective-permute-start(bf16[2,128,768]{2,1,0:T(8,128)(2,1)} %x0.1), channel_id=1, source_target_pairs={{0,2},{1,3},{2,0},{3,1},{4,6},{5,7},{6,4},{7,5},{8,10},{9,11},{10,... | collective-permute-start | bytes 1179656 | tf_op jit(solution)/shard_map/ppermute | solution.py:790
  3.7 10.5 %collective-permute-start = (bf16[2,128,768]{2,1,0:T(8,128)(2,1)}, bf16[2,128,768]{2,1,0:T(8,128)(2,1)S(1)}, u32[]{:S(2)}, u32[]{:S(2)}) collective-permute-start(bf16[2,128,768]{2,1,0:T(8,128)(2,1)} %x0.1), channel_id=1, source_target_pairs={{0,1},{1,0},{2,3},{3,2},{4,5},{5,4},{6,7},{7,6},{8,9},{9,8},{10,11... | collective-permute-start | bytes 1179656 | tf_op jit(solution)/shard_map/ppermute | solution.py:790
  14.0 11.4 %copy-start.17 = (bf16[768]{0:T(1024)(128)(2,1)S(1)}, bf16[768]{0:T(1024)(128)(2,1)}, u32[]{:S(2)}) copy-start(bf16[768]{0:T(1024)(128)(2,1)} %param.24) | copy-start | bytes 4612
  14.0 11.4 %copy-start.18 = (bf16[768]{0:T(1024)(128)(2,1)S(1)}, bf16[768]{0:T(1024)(128)(2,1)}, u32[]{:S(2)}) copy-start(bf16[768]{0:T(1024)(128)(2,1)} %param.28) | copy-start | bytes 4612
  14.0 11.5 %copy-start.19 = (bf16[768]{0:T(1024)(128)(2,1)S(1)}, bf16[768]{0:T(1024)(128)(2,1)}, u32[]{:S(2)}) copy-start(bf16[768]{0:T(1024)(128)(2,1)} %param.29) | copy-start | bytes 4612
  14.0 11.5 %copy-start.20 = (bf16[768]{0:T(1024)(128)(2,1)S(1)}, bf16[768]{0:T(1024)(128)(2,1)}, u32[]{:S(2)}) copy-start(bf16[768]{0:T(1024)(128)(2,1)} %param.30) | copy-start | bytes 4612
  14.0 11.5 %copy-start.14 = (bf16[3072]{0:T(1024)(128)(2,1)S(1)}, bf16[3072]{0:T(1024)(128)(2,1)}, u32[]{:S(2)}) copy-start(bf16[3072]{0:T(1024)(128)(2,1)} %param.26) | copy-start | bytes 18436
  14.0 17.6 %copy-start = (bf16[2,128,768]{2,1,0:T(8,128)(2,1)S(1)}, bf16[2,128,768]{2,1,0:T(8,128)(2,1)}, u32[]{:S(2)}) copy-start(bf16[2,128,768]{2,1,0:T(8,128)(2,1)} %x0.1) | copy-start | bytes 1179652
  14.1 17.6 %copy-start.5 = (bf16[768,768]{1,0:T(8,128)(2,1)S(1)}, bf16[768,768]{1,0:T(8,128)(2,1)}, u32[]{:S(2)}) copy-start(bf16[768,768]{1,0:T(8,128)(2,1)} %param.21) | copy-start | bytes 3538948
  14.1 17.6 %copy-start.7 = (bf16[2,128,768]{2,1,0:T(8,128)(2,1)S(1)}, bf16[2,128,768]{2,1,0:T(8,128)(2,1)}, u32[]{:S(2)}) copy-start(bf16[2,128,768]{2,1,0:T(8,128)(2,1)} %param.31) | copy-start | bytes 1179652
  14.1 1.8 %collective-permute-start.2 = (bf16[2,128,768]{2,1,0:T(8,128)(2,1)S(1)}, bf16[2,128,768]{2,1,0:T(8,128)(2,1)S(1)}, u32[]{:S(2)}, u32[]{:S(2)}) collective-permute-start(bf16[2,128,768]{2,1,0:T(8,128)(2,1)S(1)} %get-tuple-element.99), channel_id=1, source_target_pairs={{0,1},{1,0},{2,3},{3,2},{4,5},{5,4},{6,7},{7,6},{8,9},{9,8},{10,11... | collective-permute-start | bytes 1179656 | tf_op jit(solution)/shard_map/ppermute | solution.py:790
  23.4 2.2 %collective-permute-start.3 = (bf16[2,128,192]{2,1,0:T(8,128)(2,1)S(1)}, bf16[2,128,192]{2,1,0:T(8,128)(2,1)S(1)}, u32[]{:S(2)}, u32[]{:S(2)}) collective-permute-start(bf16[2,128,192]{2,1,0:T(8,128)(2,1)S(1)} %get-tuple-element.103), channel_id=1, source_target_pairs={{0,1},{1,0},{2,3},{3,2},{4,5},{5,4},{6,7},{7,6},{8,9},{9,8},{10,11... | collective-permute-start | bytes 294920 | tf_op jit(solution)/shard_map/ppermute | solution.py:790
  23.6 6.3 %collective-permute-start.4 = (bf16[2,128,192]{2,1,0:T(8,128)(2,1)S(1)}, bf16[2,128,192]{2,1,0:T(8,128)(2,1)S(1)}, u32[]{:S(2)}, u32[]{:S(2)}) collective-permute-start(bf16[2,128,192]{2,1,0:T(8,128)(2,1)S(1)} %get-tuple-element.104), channel_id=1, source_target_pairs={{0,2},{1,3},{2,0},{3,1},{4,6},{5,7},{6,4},{7,5},{8,10},{9,11},{10,... | collective-permute-start | bytes 294920 | tf_op jit(solution)/shard_map/ppermute | solution.py:790
  25.4 6.3 %collective-permute-start.5 = (bf16[2,128,192]{2,1,0:T(8,128)(2,1)S(1)}, bf16[2,128,192]{2,1,0:T(8,128)(2,1)S(1)}, u32[]{:S(2)}, u32[]{:S(2)}) collective-permute-start(bf16[2,128,192]{2,1,0:T(8,128)(2,1)S(1)} %get-tuple-element.105), channel_id=1, source_target_pairs={{0,3},{1,2},{2,1},{3,0},{4,7},{5,6},{6,5},{7,4},{8,11},{9,10},{10,... | collective-permute-start | bytes 294920 | tf_op jit(solution)/shard_map/ppermute | solution.py:790
  43.6 3.1 %collective-permute-start.7 = (bf16[256,2304]{1,0:T(8,128)(2,1)}, bf16[256,2304]{1,0:T(8,128)(2,1)S(1)}, u32[]{:S(2)}, u32[]{:S(2)}) collective-permute-start(bf16[256,2304]{1,0:T(8,128)(2,1)} %get-tuple-element.114.grad), channel_id=1, source_target_pairs={{0,1},{1,0},{2,3},{3,2},{4,5},{5,4},{6,7},{7,6},{8,9},{9,8},{10,11... | collective-permute-start | bytes 3538952 | tf_op jit(solution)/shard_map/ppermute | solution.py:790
  44.1 8.3 %collective-permute-start.6 = (bf16[2,256,192]{2,1,0:T(8,128)(2,1)S(1)}, bf16[2,256,192]{2,1,0:T(8,128)(2,1)S(1)}, u32[]{:S(2)}, u32[]{:S(2)}) collective-permute-start(bf16[2,256,192]{2,1,0:T(8,128)(2,1)S(1)} %get-tuple-element.112), channel_id=1, source_target_pairs={{0,2},{1,3},{2,0},{3,1},{4,6},{5,7},{6,4},{7,5},{8,10},{9,11},{10,... | collective-permute-start | bytes 589832 | tf_op jit(solution)/shard_map/ppermute | solution.py:790
  45.8 7.0 %collective-permute-start.9 = (bf16[4,192,256]{2,1,0:T(8,128)(2,1)}, bf16[4,192,256]{2,1,0:T(8,128)(2,1)S(1)}, u32[]{:S(2)}, u32[]{:S(2)}) collective-permute-start(bf16[4,192,256]{2,1,0:T(8,128)(2,1)} %get-tuple-element.120), channel_id=1, source_target_pairs={{0,1},{1,0},{2,3},{3,2},{4,5},{5,4},{6,7},{7,6},{8,9},{9,8},{10,11... | collective-permute-start | bytes 1179656 | tf_op jit(solution)/shard_map/ppermute | solution.py:790
  45.8 7.0 %collective-permute-start.10 = (bf16[256,3840]{1,0:T(8,128)(2,1)}, bf16[256,3840]{1,0:T(8,128)(2,1)S(1)}, u32[]{:S(2)}, u32[]{:S(2)}) collective-permute-start(bf16[256,3840]{1,0:T(8,128)(2,1)} %get-tuple-element.119.second_hbm), channel_id=1, source_target_pairs={{0,1},{1,0},{2,3},{3,2},{4,5},{5,4},{6,7},{7,6},{8,9},{9,8},{10,11... | collective-permute-start | bytes 5898248 | tf_op jit(solution)/shard_map/ppermute | solution.py:790
  49.8 28.7 %collective-permute-start.16 = (bf16[2,4,96,768]{3,2,1,0:T(8,128)(2,1)S(1)}, bf16[2,4,96,768]{3,2,1,0:T(8,128)(2,1)S(1)}, u32[]{:S(2)}, u32[]{:S(2)}) collective-permute-start(bf16[2,4,96,768]{3,2,1,0:T(8,128)(2,1)S(1)} %get-tuple-element.133), channel_id=1, source_target_pairs={{0,4},{4,0},{8,12},{12,8},{16,20},{20,16},{24,28},{28,24},{1,5},{5... | collective-permute-start | bytes 3538952 | tf_op jit(solution)/shard_map/ppermute | solution.py:790
  52.8 9.3 %collective-permute-start.8 = (bf16[2,256,192]{2,1,0:T(8,128)(2,1)S(1)}, bf16[2,256,192]{2,1,0:T(8,128)(2,1)S(1)}, u32[]{:S(2)}, u32[]{:S(2)}) collective-permute-start(bf16[2,256,192]{2,1,0:T(8,128)(2,1)S(1)} %get-tuple-element.116), channel_id=1, source_target_pairs={{0,1},{1,0},{2,3},{3,2},{4,5},{5,4},{6,7},{7,6},{8,9},{9,8},{10,11... | collective-permute-start | bytes 589832 | tf_op jit(solution)/shard_map/ppermute | solution.py:790
  58.6 22.6 %collective-permute-start.15 = (bf16[1,8,128,384]{3,2,1,0:T(8,128)(2,1)}, bf16[1,8,128,384]{3,2,1,0:T(8,128)(2,1)}, u32[]{:S(2)}, u32[]{:S(2)}) collective-permute-start(bf16[1,8,128,384]{3,2,1,0:T(8,128)(2,1)} %get-tuple-element.131), channel_id=1, source_target_pairs={{0,2},{1,3},{2,0},{3,1},{4,6},{5,7},{6,4},{7,5},{8,10},{9,11},{10,... | collective-permute-start | bytes 2359304 | tf_op jit(solution)/shard_map/ppermute | solution.py:790
  60.5 23.8 %collective-permute-start.14 = (bf16[2,4,112,384]{3,2,1,0:T(8,128)(2,1)}, bf16[2,4,112,384]{3,2,1,0:T(8,128)(2,1)S(1)}, u32[]{:S(2)}, u32[]{:S(2)}) collective-permute-start(bf16[2,4,112,384]{3,2,1,0:T(8,128)(2,1)} %get-tuple-element.129), channel_id=1, source_target_pairs={{0,8},{4,12},{8,0},{12,4},{16,24},{20,28},{24,16},{28,20},{1,9},{5... | collective-permute-start | bytes 2064392 | tf_op jit(solution)/shard_map/ppermute | solution.py:790
  62.0 16.4 %copy-start.9 = (bf16[2,4,96,768]{3,2,1,0:T(8,128)(2,1)S(1)}, bf16[2,4,96,768]{3,2,1,0:T(8,128)(2,1)}, u32[]{:S(2)}) copy-start(bf16[2,4,96,768]{3,2,1,0:T(8,128)(2,1)} %copy-done.8) | copy-start | bytes 3538948
  74.5 12.0 %collective-permute-start.11 = (bf16[2,2,128,768]{3,2,1,0:T(8,128)(2,1)}, bf16[2,2,128,768]{3,2,1,0:T(8,128)(2,1)S(1)}, u32[]{:S(2)}, u32[]{:S(2)}) collective-permute-start(bf16[2,2,128,768]{3,2,1,0:T(8,128)(2,1)} %get-tuple-element.124), channel_id=1, source_target_pairs={{0,1},{1,0},{2,3},{3,2},{4,5},{5,4},{6,7},{7,6},{8,9},{9,8},{10,11... | collective-permute-start | bytes 2359304 | tf_op jit(solution)/shard_map/ppermute | solution.py:790
  74.6 14.4 %collective-permute-start.13 = (bf16[1,4,96,640]{3,2,1,0:T(8,128)(2,1)S(1)}, bf16[1,4,96,640]{3,2,1,0:T(8,128)(2,1)S(1)}, u32[]{:S(2)}, u32[]{:S(2)}) collective-permute-start(bf16[1,4,96,640]{3,2,1,0:T(8,128)(2,1)S(1)} %get-tuple-element.127), channel_id=1, source_target_pairs={{0,4},{4,0},{8,12},{12,8},{16,20},{20,16},{24,28},{28,24},{1,5},{5... | collective-permute-start | bytes 1474568 | tf_op jit(solution)/shard_map/ppermute | solution.py:790
  79.2 16.4 %collective-permute-start.21 = (bf16[1,4,96,768]{3,2,1,0:T(8,128)(2,1)S(1)}, bf16[1,4,96,768]{3,2,1,0:T(8,128)(2,1)S(1)}, u32[]{:S(2)}, u32[]{:S(2)}) collective-permute-start(bf16[1,4,96,768]{3,2,1,0:T(8,128)(2,1)S(1)} %get-tuple-element.143), channel_id=1, source_target_pairs={{0,2},{1,3},{2,0},{3,1},{4,6},{5,7},{6,4},{7,5},{8,10},{9,11},{10,... | collective-permute-start | bytes 1769480 | tf_op jit(solution)/shard_map/ppermute | solution.py:790
  82.6 10.2 %collective-permute-start.18 = (bf16[1,4,128,384]{3,2,1,0:T(8,128)(2,1)S(1)}, bf16[1,4,128,384]{3,2,1,0:T(8,128)(2,1)S(1)}, u32[]{:S(2)}, u32[]{:S(2)}) collective-permute-start(bf16[1,4,128,384]{3,2,1,0:T(8,128)(2,1)S(1)} %get-tuple-element.139), channel_id=1, source_target_pairs={{0,8},{4,12},{8,0},{12,4},{16,24},{20,28},{24,16},{28,20},{1,9},{5... | collective-permute-start | bytes 1179656 | tf_op jit(solution)/shard_map/ppermute | solution.py:790
  84.9 13.3 %collective-permute-start.20 = (bf16[2,2,112,384]{3,2,1,0:T(8,128)(2,1)S(1)}, bf16[2,2,112,384]{3,2,1,0:T(8,128)(2,1)S(1)}, u32[]{:S(2)}, u32[]{:S(2)}) collective-permute-start(bf16[2,2,112,384]{3,2,1,0:T(8,128)(2,1)S(1)} %get-tuple-element.142), channel_id=1, source_target_pairs={{0,4},{4,0},{8,12},{12,8},{16,20},{20,16},{24,28},{28,24},{1,5},{5... | collective-permute-start | bytes 1032200 | tf_op jit(solution)/shard_map/ppermute | solution.py:790
  87.1 56.7 %collective-permute-start.12 = (bf16[1,1,256,768]{3,2,1,0:T(8,128)(2,1)S(1)}, bf16[1,1,256,768]{3,2,1,0:T(8,128)(2,1)S(1)}, u32[]{:S(2)}, u32[]{:S(2)}) collective-permute-start(bf16[1,1,256,768]{3,2,1,0:T(8,128)(2,1)S(1)} %get-tuple-element.125), channel_id=1, source_target_pairs={{0,2},{1,3},{2,0},{3,1},{4,6},{5,7},{6,4},{7,5},{8,10},{9,11},{10,... | collective-permute-start | bytes 1179656 | tf_op jit(solution)/shard_map/ppermute | solution.py:790
  89.6 14.7 %collective-permute-start.17 = (bf16[1,2,96,640]{3,2,1,0:T(8,128)(2,1)S(1)}, bf16[1,2,96,640]{3,2,1,0:T(8,128)(2,1)S(1)}, u32[]{:S(2)}, u32[]{:S(2)}) collective-permute-start(bf16[1,2,96,640]{3,2,1,0:T(8,128)(2,1)S(1)} %get-tuple-element.138), channel_id=1, source_target_pairs={{0,16},{4,20},{8,24},{12,28},{16,0},{20,4},{24,8},{28,12},{1,17},{... | collective-permute-start | bytes 737288 | tf_op jit(solution)/shard_map/ppermute | solution.py:790
  94.0 6.5 %collective-permute-start.19 = (bf16[1,2,128,384]{3,2,1,0:T(8,128)(2,1)S(1)}, bf16[1,2,128,384]{3,2,1,0:T(8,128)(2,1)S(1)}, u32[]{:S(2)}, u32[]{:S(2)}) collective-permute-start(bf16[1,2,128,384]{3,2,1,0:T(8,128)(2,1)S(1)} %get-tuple-element.141), channel_id=1, source_target_pairs={{0,4},{4,0},{8,12},{12,8},{16,20},{20,16},{24,28},{28,24},{1,5},{5... | collective-permute-start | bytes 589832 | tf_op jit(solution)/shard_map/ppermute | solution.py:790
  96.2 19.6 %collective-permute-start.25 = (bf16[1,2,96,768]{3,2,1,0:T(8,128)(2,1)S(1)}, bf16[1,2,96,768]{3,2,1,0:T(8,128)(2,1)S(1)}, u32[]{:S(2)}, u32[]{:S(2)}) collective-permute-start(bf16[1,2,96,768]{3,2,1,0:T(8,128)(2,1)S(1)} %get-tuple-element.151), channel_id=1, source_target_pairs={{0,8},{4,12},{8,0},{12,4},{16,24},{20,28},{24,16},{28,20},{1,9},{5... | collective-permute-start | bytes 884744 | tf_op jit(solution)/shard_map/ppermute | solution.py:790
  98.9 17.7 %collective-permute-start.24 = (bf16[1,2,112,384]{3,2,1,0:T(8,128)(2,1)S(1)}, bf16[1,2,112,384]{3,2,1,0:T(8,128)(2,1)S(1)}, u32[]{:S(2)}, u32[]{:S(2)}) collective-permute-start(bf16[1,2,112,384]{3,2,1,0:T(8,128)(2,1)S(1)} %get-tuple-element.150), channel_id=1, source_target_pairs={{0,2},{1,3},{2,0},{3,1},{4,6},{5,7},{6,4},{7,5},{8,10},{9,11},{10,... | collective-permute-start | bytes 516104 | tf_op jit(solution)/shard_map/ppermute | solution.py:790
  101.7 18.5 %collective-permute-start.23 = (bf16[1,2,128,384]{3,2,1,0:T(8,128)(2,1)S(1)}, bf16[1,2,128,384]{3,2,1,0:T(8,128)(2,1)S(1)}, u32[]{:S(2)}, u32[]{:S(2)}) collective-permute-start(bf16[1,2,128,384]{3,2,1,0:T(8,128)(2,1)S(1)} %get-tuple-element.149.refs_1_), channel_id=1, source_target_pairs={{0,16},{4,20},{8,24},{12,28},{16,0},{20,4},{24,8},{28,12},{1,17},{... | collective-permute-start | bytes 589832 | tf_op jit(solution)/shard_map/ppermute | solution.py:790
  105.0 17.8 %collective-permute-start.22 = (bf16[1,2,96,640]{3,2,1,0:T(8,128)(2,1)S(1)}, bf16[1,2,96,640]{3,2,1,0:T(8,128)(2,1)S(1)}, u32[]{:S(2)}, u32[]{:S(2)}) collective-permute-start(bf16[1,2,96,640]{3,2,1,0:T(8,128)(2,1)S(1)} %get-tuple-element.148.refs_1_), channel_id=1, source_target_pairs={{0,8},{4,12},{8,0},{12,4},{16,24},{20,28},{24,16},{28,20},{1,9},{5... | collective-permute-start | bytes 737288 | tf_op jit(solution)/shard_map/ppermute | solution.py:790
  117.2 16.2 %collective-permute-start.31 = (bf16[1,2,112,384]{3,2,1,0:T(8,128)(2,1)S(1)}, bf16[1,2,112,384]{3,2,1,0:T(8,128)(2,1)S(1)}, u32[]{:S(2)}, u32[]{:S(2)}) collective-permute-start(bf16[1,2,112,384]{3,2,1,0:T(8,128)(2,1)S(1)} %get-tuple-element.161.refs_1_), channel_id=1, source_target_pairs={{0,16},{4,20},{8,24},{12,28},{16,0},{20,4},{24,8},{28,12},{1,17},{... | collective-permute-start | bytes 516104 | tf_op jit(solution)/shard_map/ppermute | solution.py:790
  117.3 16.9 %collective-permute-start.30 = (bf16[1,2,96,768]{3,2,1,0:T(8,128)(2,1)S(1)}, bf16[1,2,96,768]{3,2,1,0:T(8,128)(2,1)S(1)}, u32[]{:S(2)}, u32[]{:S(2)}) collective-permute-start(bf16[1,2,96,768]{3,2,1,0:T(8,128)(2,1)S(1)} %get-tuple-element.160.refs_1_), channel_id=1, source_target_pairs={{0,16},{4,20},{8,24},{12,28},{16,0},{20,4},{24,8},{28,12},{1,17},{... | collective-permute-start | bytes 884744 | tf_op jit(solution)/shard_map/ppermute | solution.py:790
  120.8 12.0 %collective-permute-start.32 = (bf16[2,128,384]{2,1,0:T(8,128)(2,1)S(1)}, bf16[2,128,384]{2,1,0:T(8,128)(2,1)S(1)}, u32[]{:S(2)}, u32[]{:S(2)}) collective-permute-start(bf16[2,128,384]{2,1,0:T(8,128)(2,1)S(1)} %bitcast.50), channel_id=1, source_target_pairs={{0,8},{4,12},{8,0},{12,4},{16,24},{20,28},{24,16},{28,20},{1,9},{5... | collective-permute-start | bytes 589832 | tf_op jit(solution)/shard_map/ppermute | solution.py:790
  123.4 1.3 collective-permute-start.26
  124.7 4.2 %collective-permute-start.27 = (bf16[2,24,640]{2,1,0:T(8,128)(2,1)S(1)}, bf16[2,24,640]{2,1,0:T(8,128)(2,1)S(1)}, u32[]{:S(2)}, u32[]{:S(2)}) collective-permute-start(bf16[2,24,640]{2,1,0:T(8,128)(2,1)S(1)} %get-tuple-element.158), channel_id=1, source_target_pairs={{0,2},{1,3},{2,0},{3,1},{4,6},{5,7},{6,4},{7,5},{8,10},{9,11},{10,... | collective-permute-start | bytes 184328 | tf_op jit(solution)/shard_map/ppermute | solution.py:790
  128.9 3.8 %collective-permute-start.28 = (bf16[2,24,640]{2,1,0:T(8,128)(2,1)S(1)}, bf16[2,24,640]{2,1,0:T(8,128)(2,1)S(1)}, u32[]{:S(2)}, u32[]{:S(2)}) collective-permute-start(bf16[2,24,640]{2,1,0:T(8,128)(2,1)S(1)} %get-tuple-element.159), channel_id=1, source_target_pairs={{0,3},{1,2},{2,1},{3,0},{4,7},{5,6},{6,5},{7,4},{8,11},{9,10},{10,... | collective-permute-start | bytes 184328 | tf_op jit(solution)/shard_map/ppermute | solution.py:790
  132.7 8.9 %collective-permute-start.29 = (bf16[2,96,640]{2,1,0:T(8,128)(2,1)S(1)}, bf16[2,96,640]{2,1,0:T(8,128)(2,1)S(1)}, u32[]{:S(2)}, u32[]{:S(2)}) collective-permute-start(bf16[2,96,640]{2,1,0:T(8,128)(2,1)S(1)} %constant_dynamic-update-slice_fusion.refs_0_), channel_id=1, source_target_pairs={{0,4},{4,0},{8,12},{12,8},{16,20},{20,16},{24,28},{28,24},{1,5},{5... | collective-permute-start | bytes 737288 | tf_op jit(solution)/shard_map/ppermute | solution.py:790
  134.0 8.4 %collective-permute-start.35 = (bf16[2,112,384]{2,1,0:T(8,128)(2,1)S(1)}, bf16[2,112,384]{2,1,0:T(8,128)(2,1)S(1)}, u32[]{:S(2)}, u32[]{:S(2)}) collective-permute-start(bf16[2,112,384]{2,1,0:T(8,128)(2,1)S(1)} %bitcast.52), channel_id=1, source_target_pairs={{0,8},{4,12},{8,0},{12,4},{16,24},{20,28},{24,16},{28,20},{1,9},{5... | collective-permute-start | bytes 516104 | tf_op jit(solution)/shard_map/ppermute | solution.py:790
  134.7 16.0 %collective-permute-start.37 = (bf16[2,96,768]{2,1,0:T(8,128)(2,1)S(1)}, bf16[2,96,768]{2,1,0:T(8,128)(2,1)S(1)}, u32[]{:S(2)}, u32[]{:S(2)}) collective-permute-start(bf16[2,96,768]{2,1,0:T(8,128)(2,1)S(1)} %bitcast.48), channel_id=1, source_target_pairs={{0,8},{4,12},{8,0},{12,4},{16,24},{20,28},{24,16},{28,20},{1,9},{5... | collective-permute-start | bytes 884744 | tf_op jit(solution)/shard_map/ppermute | solution.py:790
  136.8 16.9 %collective-permute-start.34 = (bf16[4,128,384]{2,1,0:T(8,128)(2,1)S(1)}, bf16[4,128,384]{2,1,0:T(8,128)(2,1)S(1)}, u32[]{:S(2)}, u32[]{:S(2)}) collective-permute-start(bf16[4,128,384]{2,1,0:T(8,128)(2,1)S(1)} %get-tuple-element.170.refs_2_), channel_id=1, source_target_pairs={{0,4},{4,0},{8,12},{12,8},{16,20},{20,16},{24,28},{28,24},{1,5},{5... | collective-permute-start | bytes 1179656 | tf_op jit(solution)/shard_map/ppermute | solution.py:790
  142.3 22.1 %collective-permute-start.33 = (bf16[4,96,640]{2,1,0:T(8,128)(2,1)S(1)}, bf16[4,96,640]{2,1,0:T(8,128)(2,1)S(1)}, u32[]{:S(2)}, u32[]{:S(2)}) collective-permute-start(bf16[4,96,640]{2,1,0:T(8,128)(2,1)S(1)} %get-tuple-element.167.refs_1_), channel_id=1, source_target_pairs={{0,16},{4,20},{8,24},{12,28},{16,0},{20,4},{24,8},{28,12},{1,17},{... | collective-permute-start | bytes 1474568 | tf_op jit(solution)/shard_map/ppermute | solution.py:790
  142.9 14.6 %collective-permute-start.36 = (bf16[4,112,384]{2,1,0:T(8,128)(2,1)S(1)}, bf16[4,112,384]{2,1,0:T(8,128)(2,1)S(1)}, u32[]{:S(2)}, u32[]{:S(2)}) collective-permute-start(bf16[4,112,384]{2,1,0:T(8,128)(2,1)S(1)} %get-tuple-element.173.refs_4_), channel_id=1, source_target_pairs={{0,4},{4,0},{8,12},{12,8},{16,20},{20,16},{24,28},{28,24},{1,5},{5... | collective-permute-start | bytes 1032200 | tf_op jit(solution)/shard_map/ppermute | solution.py:790
  150.8 17.9 %collective-permute-start.38 = (bf16[4,96,768]{2,1,0:T(8,128)(2,1)S(1)}, bf16[4,96,768]{2,1,0:T(8,128)(2,1)S(1)}, u32[]{:S(2)}, u32[]{:S(2)}) collective-permute-start(bf16[4,96,768]{2,1,0:T(8,128)(2,1)S(1)} %get-tuple-element.178.refs_1_), channel_id=1, source_target_pairs={{0,4},{4,0},{8,12},{12,8},{16,20},{20,16},{24,28},{28,24},{1,5},{5... | collective-permute-start | bytes 1769480 | tf_op jit(solution)/shard_map/ppermute | solution.py:790
  (14 other events, 73.8 us)

commit v6 on v5

--- a/solution.py
+++ b/solution.py
@@ -12,7 +12,8 @@
 LOW = jnp.bfloat16
 MIB = 1 << 20
 PIECES = 8
-STEP = 1.0
+STEP = 0.85
+JOIN = 1.3
 BACK = 1.0
 FORE = 0.1
 
@@ -166,7 +167,7 @@
     whole = ((passages, rows, width), LOW)
     return pl.pallas_call(
         attend_kernel,
-        in_specs=[SMEM, SMEM] + [HBM] * 3 + [vmem(), HBM, vmem()],
+        in_specs=[SMEM, SMEM, vmem(), HBM, vmem(), vmem(), HBM, vmem()],
         out_specs=[HBM] * 4 + [vmem()] * 3,
         out_shape=[pltpu.HBM(*kind) for kind in kinds + [whole]] + [jax.ShapeDtypeStruct(*kinds[2])] * 3,
         scratch_shapes=[pltpu.VMEM(*whole), pltpu.VMEM((width, 3 * hw), LOW)]
@@ -175,7 +176,7 @@
         compiler_params=pltpu.CompilerParams(vmem_limit_bytes=24 * MIB),
         cost_estimate=cost(FORE),
         name="attend",
-    )(where, lengths, *map(far, shards[:3]), shards[3], far(w), bias)
+    )(where, lengths, shards[0], far(shards[1]), shards[2], shards[3], far(w), bias)
 
 
 def attend_back_kernel(place, *refs):
@@ -483,10 +484,10 @@
 ORDERS = {
     "a": ([1, "y", 2], 4, [2, 1]),
     "b": (["y", 2, 1], 4, [2, 1]),
-    "c": ([2, 1, "y"], 4, [2, 1]),
+    "c": ([2, 1, "y"], 4, [1, 2]),
     "d": ([1, 4], 2, [1, 4]),
 }
-SEQUENCE = "abcdbacbdacbddbcadca"
+SEQUENCE = "abcdbacbdacbdedbcadca"
 
 
 def inner_grad_kernel(bit_b, bit_c, mine_hbm, second_hbm, mine_got, second_got, *refs):
@@ -736,27 +737,25 @@
         out_shape=[jax.ShapeDtypeStruct(shape, own.dtype), TOKEN],
         scratch_shapes=[pltpu.SemaphoreType.DMA((2,))],
         compiler_params=pltpu.CompilerParams(vmem_limit_bytes=2 * MIB),
-        cost_estimate=cost(STEP),
+        cost_estimate=cost(JOIN),
         name="join",
     )(own, got, *map(far, after))
 
 
 def pass_on_kernel(source, *refs):
-    outs, sem = refs[-3:-1], refs[-1]
-    copies = [pltpu.make_async_copy(source, out, sem.at[i]) for i, out in enumerate(outs)]
-    for copy in copies:
-        copy.start()
-    for copy in copies:
-        copy.wait()
+    out, sem = refs[-2:]
+    copy = pltpu.make_async_copy(source, out, sem.at[0])
+    copy.start()
+    copy.wait()
 
 
 def pass_on(source, after):
     return pl.pallas_call(
         pass_on_kernel,
         in_specs=[vmem()] + [HBM] * len(after),
-        out_specs=[vmem(), HBM],
-        out_shape=[jax.ShapeDtypeStruct(source.shape, source.dtype), pltpu.HBM(source.shape, source.dtype)],
-        scratch_shapes=[pltpu.SemaphoreType.DMA((2,))],
+        out_specs=vmem(),
+        out_shape=jax.ShapeDtypeStruct(source.shape, source.dtype),
+        scratch_shapes=[pltpu.SemaphoreType.DMA((1,))],
         compiler_params=pltpu.CompilerParams(vmem_limit_bytes=2 * MIB),
         cost_estimate=cost(0.5),
         name="pass_on",
@@ -871,8 +870,8 @@
     beside = swap(tokens, "seq", 1)
     biases = (query_bias.reshape(1, width), value_bias.reshape(1, width))
     w, bias, token = choose_heads(where, query_key_value, *biases)
-    passed, across = pass_on(across, [token])
-    corner = swap(passed, "seq", 1)
+    across = pass_on(across, [token])
+    corner = swap(across, "seq", 1)
     shards = (tokens, beside, across, corner)
     vec = jnp.stack([attn_bias, attn_gain, attn_shift, outer_bias, ffn_gain, ffn_shift, ffn_shift, ffn_shift])
     vec = vec.astype(F32)
@@ -907,14 +906,22 @@
     )
     d.begin(project_keep, project_send)
     back_got = swap(back_send, "seq", 1)
-    back_sum, _ = sum_pieces(
-        d.place,
-        [f.reshape(2, 1, rows, width) for f in (back_keep, back_got)],
-        [1], 1, False, name="back_y",
-    )
-    back_over = swap(back_sum, "seq", 2)
+
+    def begin_back(after):
+        total, token = sum_pieces(
+            d.place,
+            [f.reshape(2, 1, rows, width) for f in (back_keep, back_got)],
+            [1], 1, False, after, name="back_y",
+        )
+        return swap(total, "seq", 2), token
+
+    if "e" not in SEQUENCE:
+        back_over, _ = begin_back([])
     parts = None
     for letter in SEQUENCE:
+        if letter == "e":
+            back_over, token = begin_back([token])
+            continue
         chunk = {"a": a, "b": b, "c": c, "d": d}[letter]
         if chunk.order or chunk.last is not None:
             token = chunk.step([token], name="sum_" + letter)

time: 171 us -> 168 us (0.982)
  waiting for transfers between devices: 56.3 us -> 53.4 us
  starting transfers between devices: 44.2 us -> 42.2 us
    ppermute x39, waiting for transfers between devices: 56.3 us -> 53.4 us  [swap(): return lax.ppermute(field, axis, [(i, i ^ bit) for i in range(count)])]
    ppermute x39, starting transfers between devices: 44.2 us -> 42.2 us  [swap(): return lax.ppermute(field, axis, [(i, i ^ bit) for i in range(count)])]
  transfers between devices with their start and end apart: 39 -> 39, of which waited for: 18 -> 21; matrix products, arithmetic and copies ran while one was open for 2% -> 2% of each run, Pallas kernels for 25% -> 27%
where the time goes in v6:
time: 168 us; the launch traced here: 167 us
  Pallas kernels  66.1 us (39%)
  waiting for transfers between devices  53.4 us (32%)
  starting transfers between devices  42.2 us (25%)
  local copies, waits for them, and re-layouts  2.96 us (2%)
    ppermute x39, waiting for transfers between devices, swap(): return lax.ppermute(field, axis, [(i, i ^ bit) for i in range(count)])  53.4 us
    ppermute x39, starting transfers between devices, swap(): return lax.ppermute(field, axis, [(i, i ^ bit) for i in range(count)])  42.2 us
    pallas_call x16, Pallas kernels, sum_pieces(): pl.pallas_call(lambda *refs: sum_kernel(spec, *refs), in_specs=[SMEM] + [...  13.8 us
    pallas_call x1, Pallas kernels, attend_back(): pl.pallas_call(attend_back_kernel, in_specs=[SMEM] + [HBM] * 5 + [vmem()]...  12.4 us
    pallas_call x1, Pallas kernels, rows_pass(): pl.pallas_call(rows_kernel, in_specs=[SMEM, vmem()] + [HBM] * 3 + [vmem()...  11.9 us
    pallas_call x1, Pallas kernels, attend(): pl.pallas_call(attend_kernel, in_specs=[SMEM, SMEM, vmem(), HBM, vmem(),...  7.71 us
    pallas_call x1, Pallas kernels, inner_grad(): pl.pallas_call(inner_grad_kernel, in_specs=[SMEM, SMEM, HBM, HBM, vmem(),...  5.69 us
  transfers between devices with their start and end apart: 39, of which 21 were waited for; matrix products, arithmetic and copies ran while one was open for 2% of the time, Pallas kernels for 27%

profile of v6, /device:TPU:0, one launch (start us, length us, event | category | flops | bytes accessed | tf_op | source)
XLA Modules:
  0.0 167.1 jit_solution(10850098859503982134)
XLA Ops:
  0.6 3.0 %collective-permute-start.1 = (bf16[2,128,768]{2,1,0:T(8,128)(2,1)}, bf16[2,128,768]{2,1,0:T(8,128)(2,1)S(1)}, u32[]{:S(2)}, u32[]{:S(2)}) collective-permute-start(bf16[2,128,768]{2,1,0:T(8,128)(2,1)} %x0.1), channel_id=1, source_target_pairs={{0,2},{1,3},{2,0},{3,1},{4,6},{5,7},{6,4},{7,5},{8,10},{9,11},{10,... | collective-permute-start | bytes 1179656 | tf_op jit(solution)/shard_map/ppermute | solution.py:789
  5.1 2.7 %choose_heads.1 = (bf16[768,576]{1,0:T(8,128)(2,1)}, f32[2,192]{1,0:T(2,128)S(1)}, f32[8,128]{1,0:T(8,128)}) custom-call(s32[1]{0:T(128)} %bitcast.where, bf16[768,2304]{1,0:T(8,128)(2,1)} %w_hbm.1, bf16[1,768]{1,0:T(2,128)(2,1)S(1)} %reshape.97.qb, bf16[1,768]{1,0:T(2,128)(2,1)S(1)} %reshape.98.vb), custom_call_target="tpu_custom_call" | custom-call | flops 1724999936 | bytes 5535000 | tf_op jit(solution)/shard_map/choose_heads/pallas_call | solution.py:88
  7.8 5.2 %collective-permute-done.1.source = bf16[2,128,768]{2,1,0:T(8,128)(2,1)S(1)} collective-permute-done((bf16[2,128,768]{2,1,0:T(8,128)(2,1)}, bf16[2,128,768]{2,1,0:T(8,128)(2,1)S(1)}, u32[]{:S(2)}, u32[]{:S(2)}) %collective-permute-start.1) | collective-permute-done | bytes 393248 | tf_op jit(solution)/shard_map/ppermute | solution.py:789
  13.4 1.7 %collective-permute-done.2.x3 = bf16[2,128,768]{2,1,0:T(8,128)(2,1)S(1)} collective-permute-done((bf16[2,128,768]{2,1,0:T(8,128)(2,1)S(1)}, bf16[2,128,768]{2,1,0:T(8,128)(2,1)S(1)}, u32[]{:S(2)}, u32[]{:S(2)}) %collective-permute-start.2) | collective-permute-done | bytes 393248 | tf_op jit(solution)/shard_map/ppermute | solution.py:789
  15.1 7.7 %attend.1 = (bf16[2,512,576]{2,1,0:T(8,128)(2,1)}, bf16[2,3,512,512]{3,2,1,0:T(8,128)(2,1)}, bf16[2,128,192]{2,1,0:T(8,128)(2,1)}, bf16[2,512,768]{2,1,0:T(8,128...) custom-call(s32[1]{0:T(128)} %bitcast.where, ...), custom_call_target="tpu_custom_call" | custom-call | flops 115000000 | bytes 369000 | tf_op jit(solution)/shard_map/attend/pallas_call | solution.py:168
  23.0 1.8 %collective-permute-start.4 = (bf16[2,128,192]{2,1,0:T(8,128)(2,1)S(1)}, bf16[2,128,192]{2,1,0:T(8,128)(2,1)S(1)}, u32[]{:S(2)}, u32[]{:S(2)}) collective-permute-start(bf16[2,128,192]{2,1,0:T(8,128)(2,1)S(1)} %get-tuple-element.101), channel_id=1, source_target_pairs={{0,2},{1,3},{2,0},{3,1},{4,6},{5,7},{6,4},{7,5},{8,10},{9,11},{10,... | collective-permute-start | bytes 294920 | tf_op jit(solution)/shard_map/ppermute | solution.py:789
  25.0 4.3 %collective-permute-done.4 = bf16[2,128,192]{2,1,0:T(8,128)(2,1)S(1)} collective-permute-done((bf16[2,128,192]{2,1,0:T(8,128)(2,1)S(1)}, bf16[2,128,192]{2,1,0:T(8,128)(2,1)S(1)}, u32[]{:S(2)}, u32[]{:S(2)}) %collective-permute-start.4) | collective-permute-done | bytes 98336 | tf_op jit(solution)/shard_map/ppermute | solution.py:789
  29.4 1.7 %collective-permute-done.5 = bf16[2,128,192]{2,1,0:T(8,128)(2,1)S(1)} collective-permute-done((bf16[2,128,192]{2,1,0:T(8,128)(2,1)S(1)}, bf16[2,128,192]{2,1,0:T(8,128)(2,1)S(1)}, u32[]{:S(2)}, u32[]{:S(2)}) %collective-permute-start.5) | collective-permute-done | bytes 98336 | tf_op jit(solution)/shard_map/ppermute | solution.py:789
  31.1 11.9 %rows_pass.1 = (bf16[256,768]{1,0:T(8,128)(2,1)}, f32[256,768]{1,0:T(8,128)}, bf16[256,1536]{1,0:T(8,128)(2,1)}, bf16[256,2304]{1,0:T(8,128)(2,1)}, bf16[256,384...) custom-call(s32[1]{0:T(128)} %bitcast.where, ...), custom_call_target="tpu_custom_call" | custom-call | flops 12650000384 | bytes 40590000 | tf_op jit(solution)/shard_map/rows_pass/pallas_call | solution.py:429
  43.5 1.7 %collective-permute-start.6 = (bf16[2,256,192]{2,1,0:T(8,128)(2,1)S(1)}, bf16[2,256,192]{2,1,0:T(8,128)(2,1)S(1)}, u32[]{:S(2)}, u32[]{:S(2)}) collective-permute-start(bf16[2,256,192]{2,1,0:T(8,128)(2,1)S(1)} %get-tuple-element.109), channel_id=1, source_target_pairs={{0,2},{1,3},{2,0},{3,1},{4,6},{5,7},{6,4},{7,5},{8,10},{9,11},{10,... | collective-permute-start | bytes 589832 | tf_op jit(solution)/shard_map/ppermute | solution.py:789
  46.1 3.1 %outer_grad.1 = (bf16[2,4,96,768]{3,2,1,0:T(8,128)(2,1)S(1)}, bf16[2,4,96,768]{3,2,1,0:T(8,128)(2,1)S(1)}, f32[8,128]{1,0:T(8,128)}) custom-call(s32[2]{0:T(128)S(1)} %pad_add_fusion.1.place.refs_0_, bf16[256,1536]{1,0:T(8,128)(2,1)} %get-tuple-element.110.active, bf16[256,2304]{1,0:T(8,128)(2,1)S(1)} %collective-permute-done.7.active_got.grad_got, ...), custom_call_target="tpu_custom_call" | custom-call | flops 34500001792 | bytes 110700000 | tf_op jit(solution)/shard_map/outer_grad/pallas_call | solution.py:471
  49.2 1.8 %collective-permute-start.15 = (bf16[2,4,96,768]{3,2,1,0:T(8,128)(2,1)S(1)}, bf16[2,4,96,768]{3,2,1,0:T(8,128)(2,1)S(1)}, u32[]{:S(2)}, u32[]{:S(2)}) collective-permute-start(bf16[2,4,96,768]{3,2,1,0:T(8,128)(2,1)S(1)} %get-tuple-element.129), channel_id=1, source_target_pairs={{0,4},{4,0},{8,12},{12,8},{16,20},{20,16},{24,28},{28,24},{1,5},{5... | collective-permute-start | bytes 3538952 | tf_op jit(solution)/shard_map/ppermute | solution.py:789
  52.2 5.7 %inner_grad.1 = (bf16[1,8,128,384]{3,2,1,0:T(8,128)(2,1)}, bf16[1,8,128,384]{3,2,1,0:T(8,128)(2,1)}, bf16[2,4,112,384]{3,2,1,0:T(8,128)(2,1)}, bf16[2,4,112,384]{3,2,1,0:T(8,128)(2,1)}, f32[8,128]{1,0:T(8,128)}) custom-call(s32[2]{0:T(128)S(1)} %pad_add_fusion.2.bit_b.bit_c.refs_0_.refs_1_, s32[2]{0:T(128)S(1)} %pad_add_fusion.2.bit_b.bit_c.refs_0_.refs_1_, ...), custom_call_target="tpu_custom_call" | custom-call | flops 4600000000 | bytes 14760000 | tf_op jit(solution)/shard_map/inner_grad/pallas_call | solution.py:564
  57.9 1.8 %collective-permute-start.14 = (bf16[1,8,128,384]{3,2,1,0:T(8,128)(2,1)}, bf16[1,8,128,384]{3,2,1,0:T(8,128)(2,1)}, u32[]{:S(2)}, u32[]{:S(2)}) collective-permute-start(bf16[1,8,128,384]{3,2,1,0:T(8,128)(2,1)} %get-tuple-element.127), channel_id=1, source_target_pairs={{0,2},{1,3},{2,0},{3,1},{4,6},{5,7},{6,4},{7,5},{8,10},{9,11},{10,... | collective-permute-start | bytes 2359304 | tf_op jit(solution)/shard_map/ppermute | solution.py:789
  59.7 1.6 collective-permute-start.13
  61.4 1.5 collective-permute-done.8
  62.9 12.4 %attend_back.1 = (bf16[2,2,128,768]{3,2,1,0:T(8,128)(2,1)}, bf16[2,2,128,768]{3,2,1,0:T(8,128)(2,1)}, bf16[1,4,96,640]{3,2,1,0:T(8,128)(2,1)S(1)}, bf16[1,4,96,640]{3,2,1,0:T(8,128)(2,1)}, f32[8,128]{1,0:T(8,128)}) custom-call(s32[2]{0:T(128)S(1)} %pad_add_fusion.place.refs_0_, bf16[2,512,768]{2,1,0:T(8,128)(2,1)} %get-tuple-element.105.refs_0_, ...), custom_call_target="tpu_custom_call" | custom-call | flops 1150000000 | bytes 3690000 | tf_op jit(solution)/shard_map/attend_back/pallas_call | solution.py:283
  75.3 1.6 collective-permute-start.12
  78.3 2.4 %collective-permute-start.20 = (bf16[1,4,96,768]{3,2,1,0:T(8,128)(2,1)S(1)}, bf16[1,4,96,768]{3,2,1,0:T(8,128)(2,1)S(1)}, u32[]{:S(2)}, u32[]{:S(2)}) collective-permute-start(bf16[1,4,96,768]{3,2,1,0:T(8,128)(2,1)S(1)} %get-tuple-element.139), channel_id=1, source_target_pairs={{0,2},{1,3},{2,0},{3,1},{4,6},{5,7},{6,4},{7,5},{8,10},{9,11},{10,... | collective-permute-start | bytes 1769480 | tf_op jit(solution)/shard_map/ppermute | solution.py:789
  80.6 1.3 sum_b.3
  81.9 1.6 collective-permute-start.17
  83.6 1.3 sum_c.3
  84.9 1.5 collective-permute-start.19
  86.4 3.0 %collective-permute-done.12.refs_2_ = bf16[1,4,96,640]{3,2,1,0:T(8,128)(2,1)S(1)} collective-permute-done((bf16[1,4,96,640]{3,2,1,0:T(8,128)(2,1)S(1)}, bf16[1,4,96,640]{3,2,1,0:T(8,128)(2,1)S(1)}, u32[]{:S(2)}, u32[]{:S(2)}) %collective-permute-start.12) | collective-permute-done | bytes 491552 | tf_op jit(solution)/shard_map/ppermute | solution.py:789
  90.1 2.6 %collective-permute-start.16 = (bf16[1,2,96,640]{3,2,1,0:T(8,128)(2,1)S(1)}, bf16[1,2,96,640]{3,2,1,0:T(8,128)(2,1)S(1)}, u32[]{:S(2)}, u32[]{:S(2)}) collective-permute-start(bf16[1,2,96,640]{3,2,1,0:T(8,128)(2,1)S(1)} %get-tuple-element.134), channel_id=1, source_target_pairs={{0,16},{4,20},{8,24},{12,28},{16,0},{20,4},{24,8},{28,12},{1,17},{... | collective-permute-start | bytes 737288 | tf_op jit(solution)/shard_map/ppermute | solution.py:789
  92.7 1.2 sum_b.4
  94.0 1.6 collective-permute-start.18
  97.3 1.2 sum_c.4
  98.5 1.6 collective-permute-start.23
  100.2 1.3 sum_b.5
  101.5 2.6 %collective-permute-start.22 = (bf16[1,2,128,384]{3,2,1,0:T(8,128)(2,1)S(1)}, bf16[1,2,128,384]{3,2,1,0:T(8,128)(2,1)S(1)}, u32[]{:S(2)}, u32[]{:S(2)}) collective-permute-start(bf16[1,2,128,384]{3,2,1,0:T(8,128)(2,1)S(1)} %get-tuple-element.145.refs_1_), channel_id=1, source_target_pairs={{0,16},{4,20},{8,24},{12,28},{16,0},{20,4},{24,8},{28,12},{1,17},{... | collective-permute-start | bytes 589832 | tf_op jit(solution)/shard_map/ppermute | solution.py:789
  104.8 1.3 collective-permute-start.21
  106.1 9.3 %collective-permute-done.24.refs_4_ = bf16[1,2,96,768]{3,2,1,0:T(8,128)(2,1)S(1)} collective-permute-done((bf16[1,2,96,768]{3,2,1,0:T(8,128)(2,1)S(1)}, bf16[1,2,96,768]{3,2,1,0:T(8,128)(2,1)S(1)}, u32[]{:S(2)}, u32[]{:S(2)}) %collective-permute-start.24) | collective-permute-done | bytes 294944 | tf_op jit(solution)/shard_map/ppermute | solution.py:789
  116.2 1.2 sum_c.5
  117.5 2.9 %collective-permute-start.30 = (bf16[1,2,96,768]{3,2,1,0:T(8,128)(2,1)S(1)}, bf16[1,2,96,768]{3,2,1,0:T(8,128)(2,1)S(1)}, u32[]{:S(2)}, u32[]{:S(2)}) collective-permute-start(bf16[1,2,96,768]{3,2,1,0:T(8,128)(2,1)S(1)} %get-tuple-element.158.refs_1_), channel_id=1, source_target_pairs={{0,16},{4,20},{8,24},{12,28},{16,0},{20,4},{24,8},{28,12},{1,17},{... | collective-permute-start | bytes 884744 | tf_op jit(solution)/shard_map/ppermute | solution.py:789
  121.0 1.4 collective-permute-done.21.refs_2_
  124.4 1.3 collective-permute-start.28
  125.8 2.1 %collective-permute-done.27 = bf16[2,24,640]{2,1,0:T(8,128)(2,1)S(1)} collective-permute-done((bf16[2,24,640]{2,1,0:T(8,128)(2,1)S(1)}, bf16[2,24,640]{2,1,0:T(8,128)(2,1)S(1)}, u32[]{:S(2)}, u32[]{:S(2)}) %collective-permute-start.27) | collective-permute-done | bytes 61472 | tf_op jit(solution)/shard_map/ppermute | solution.py:789
  129.9 2.1 %collective-permute-start.35 = (bf16[2,112,384]{2,1,0:T(8,128)(2,1)S(1)}, bf16[2,112,384]{2,1,0:T(8,128)(2,1)S(1)}, u32[]{:S(2)}, u32[]{:S(2)}) collective-permute-start(bf16[2,112,384]{2,1,0:T(8,128)(2,1)S(1)} %bitcast.52), channel_id=1, source_target_pairs={{0,4},{4,0},{8,12},{12,8},{16,20},{20,16},{24,28},{28,24},{1,5},{5... | collective-permute-start | bytes 516104 | tf_op jit(solution)/shard_map/ppermute | solution.py:789
  133.6 1.5 collective-permute-start.34
  135.1 2.5 %collective-permute-done.29.refs_1_ = bf16[2,96,640]{2,1,0:T(8,128)(2,1)S(1)} collective-permute-done((bf16[2,96,640]{2,1,0:T(8,128)(2,1)S(1)}, bf16[2,96,640]{2,1,0:T(8,128)(2,1)S(1)}, u32[]{:S(2)}, u32[]{:S(2)}) %collective-permute-start.29) | collective-permute-done | bytes 245792 | tf_op jit(solution)/shard_map/ppermute | solution.py:789
  139.1 2.1 %collective-permute-done.35.refs_1_ = bf16[2,112,384]{2,1,0:T(8,128)(2,1)S(1)} collective-permute-done((bf16[2,112,384]{2,1,0:T(8,128)(2,1)S(1)}, bf16[2,112,384]{2,1,0:T(8,128)(2,1)S(1)}, u32[]{:S(2)}, u32[]{:S(2)}) %collective-permute-start.35) | collective-permute-done | bytes 172064 | tf_op jit(solution)/shard_map/ppermute | solution.py:789
  144.1 5.5 %collective-permute-done.34.refs_3_ = bf16[4,128,384]{2,1,0:T(8,128)(2,1)S(1)} collective-permute-done((bf16[4,128,384]{2,1,0:T(8,128)(2,1)S(1)}, bf16[4,128,384]{2,1,0:T(8,128)(2,1)S(1)}, u32[]{:S(2)}, u32[]{:S(2)}) %collective-permute-start.34) | collective-permute-done | bytes 393248 | tf_op jit(solution)/shard_map/ppermute | solution.py:789
  149.6 7.5 %collective-permute-done.36.refs_5_ = bf16[4,112,384]{2,1,0:T(8,128)(2,1)S(1)} collective-permute-done((bf16[4,112,384]{2,1,0:T(8,128)(2,1)S(1)}, bf16[4,112,384]{2,1,0:T(8,128)(2,1)S(1)}, u32[]{:S(2)}, u32[]{:S(2)}) %collective-permute-start.36) | collective-permute-done | bytes 344096 | tf_op jit(solution)/shard_map/ppermute | solution.py:789
  157.2 2.3 %inner_place.1 = (f32[192,3072]{1,0:T(8,128)}, f32[192,768]{1,0:T(8,128)}) custom-call(s32[2]{0:T(128)S(1)} %pad_add_fusion.2.bit_b.bit_c.refs_0_.refs_1_, s32[2]{0:T(128)S(1)} %pad_add_fusion.2.bit_b.bit_c.refs_0_.refs_1_, bf16[4,128,384]{2,1,0:T(8,128)(2,1)S(1)} %get-tuple-element.168.refs_2_, bf16[4,128,384]{2,1,0:T(8,128)(2,1)S(1)} %collective-permute-done.34.refs_3_, ...), custom_call_target="tpu_custom_call" | custom-call | flops 2300000000 | bytes 7380000 | tf_op jit(solution)/shard_map/inner_place/pallas_call | solution.py:667
  159.5 2.2 %collective-permute-done.33.refs_2_ = bf16[4,96,640]{2,1,0:T(8,128)(2,1)S(1)} collective-permute-done((bf16[4,96,640]{2,1,0:T(8,128)(2,1)S(1)}, bf16[4,96,640]{2,1,0:T(8,128)(2,1)S(1)}, u32[]{:S(2)}, u32[]{:S(2)}) %collective-permute-start.33) | collective-permute-done | bytes 491552 | tf_op jit(solution)/shard_map/ppermute | solution.py:789
  161.7 2.0 %project_place.1 = (f32[192,2304]{1,0:T(8,128)}, f32[16,192]{1,0:T(8,128)S(1)}) custom-call(s32[2]{0:T(128)S(1)} %pad_add_fusion.place.refs_0_, bf16[4,96,640]{2,1,0:T(8,128)(2,1)S(1)} %get-tuple-element.165.refs_1_, bf16[4,96,640]{2,1,0:T(8,128)(2,1)S(1)} %collective-permute-done.33.refs_2_), custom_call_target="tpu_custom_call" | custom-call | flops 2300000000 | bytes 7380000 | tf_op jit(solution)/shard_map/project_place/pallas_call | solution.py:705
  165.0 2.1 %outer_place.1 = f32[768,768]{1,0:T(8,128)} custom-call(s32[2]{0:T(128)S(1)} %pad_add_fusion.1.place.refs_0_, bf16[4,96,768]{2,1,0:T(8,128)(2,1)S(1)} %get-tuple-element.176.refs_1_, bf16[4,96,768]{2,1,0:T(8,128)(2,1)S(1)} %collective-permute-done.38.refs_2_), custom_call_target="tpu_custom_call" | custom-call | flops 2300000000 | bytes 7380000 | tf_op jit(solution)/shard_map/outer_place/pallas_call | solution.py:637
  (131 shorter events, 22.0 us)
Async XLA Ops:
  0.6 12.4 %collective-permute-start.1 = (bf16[2,128,768]{2,1,0:T(8,128)(2,1)}, bf16[2,128,768]{2,1,0:T(8,128)(2,1)S(1)}, u32[]{:S(2)}, u32[]{:S(2)}) collective-permute-start(bf16[2,128,768]{2,1,0:T(8,128)(2,1)} %x0.1), channel_id=1, source_target_pairs={{0,2},{1,3},{2,0},{3,1},{4,6},{5,7},{6,4},{7,5},{8,10},{9,11},{10,... | collective-permute-start | bytes 1179656 | tf_op jit(solution)/shard_map/ppermute | solution.py:789
  3.7 9.7 %collective-permute-start = (bf16[2,128,768]{2,1,0:T(8,128)(2,1)}, bf16[2,128,768]{2,1,0:T(8,128)(2,1)S(1)}, u32[]{:S(2)}, u32[]{:S(2)}) collective-permute-start(bf16[2,128,768]{2,1,0:T(8,128)(2,1)} %x0.1), channel_id=1, source_target_pairs={{0,1},{1,0},{2,3},{3,2},{4,5},{5,4},{6,7},{7,6},{8,9},{9,8},{10,11... | collective-permute-start | bytes 1179656 | tf_op jit(solution)/shard_map/ppermute | solution.py:789
  13.2 11.6 %copy-start.15 = (bf16[768]{0:T(1024)(128)(2,1)S(1)}, bf16[768]{0:T(1024)(128)(2,1)}, u32[]{:S(2)}) copy-start(bf16[768]{0:T(1024)(128)(2,1)} %param.22) | copy-start | bytes 4612
  13.2 11.6 %copy-start.17 = (bf16[768]{0:T(1024)(128)(2,1)S(1)}, bf16[768]{0:T(1024)(128)(2,1)}, u32[]{:S(2)}) copy-start(bf16[768]{0:T(1024)(128)(2,1)} %param.24) | copy-start | bytes 4612
  13.2 11.6 %copy-start.18 = (bf16[768]{0:T(1024)(128)(2,1)S(1)}, bf16[768]{0:T(1024)(128)(2,1)}, u32[]{:S(2)}) copy-start(bf16[768]{0:T(1024)(128)(2,1)} %param.28) | copy-start | bytes 4612
  13.3 11.6 %copy-start.19 = (bf16[768]{0:T(1024)(128)(2,1)S(1)}, bf16[768]{0:T(1024)(128)(2,1)}, u32[]{:S(2)}) copy-start(bf16[768]{0:T(1024)(128)(2,1)} %param.29) | copy-start | bytes 4612
  13.3 11.6 %copy-start.20 = (bf16[768]{0:T(1024)(128)(2,1)S(1)}, bf16[768]{0:T(1024)(128)(2,1)}, u32[]{:S(2)}) copy-start(bf16[768]{0:T(1024)(128)(2,1)} %param.30) | copy-start | bytes 4612
  13.3 11.7 %copy-start.14 = (bf16[3072]{0:T(1024)(128)(2,1)S(1)}, bf16[3072]{0:T(1024)(128)(2,1)}, u32[]{:S(2)}) copy-start(bf16[3072]{0:T(1024)(128)(2,1)} %param.26) | copy-start | bytes 18436
  13.3 17.8 %copy-start.5 = (bf16[768,768]{1,0:T(8,128)(2,1)S(1)}, bf16[768,768]{1,0:T(8,128)(2,1)}, u32[]{:S(2)}) copy-start(bf16[768,768]{1,0:T(8,128)(2,1)} %param.21) | copy-start | bytes 3538948
  13.3 17.8 %copy-start.7 = (bf16[2,128,768]{2,1,0:T(8,128)(2,1)S(1)}, bf16[2,128,768]{2,1,0:T(8,128)(2,1)}, u32[]{:S(2)}) copy-start(bf16[2,128,768]{2,1,0:T(8,128)(2,1)} %param.31) | copy-start | bytes 1179652
  13.3 1.8 %collective-permute-start.2 = (bf16[2,128,768]{2,1,0:T(8,128)(2,1)S(1)}, bf16[2,128,768]{2,1,0:T(8,128)(2,1)S(1)}, u32[]{:S(2)}, u32[]{:S(2)}) collective-permute-start(bf16[2,128,768]{2,1,0:T(8,128)(2,1)S(1)} %pass_on.1.x2), channel_id=1, source_target_pairs={{0,1},{1,0},{2,3},{3,2},{4,5},{5,4},{6,7},{7,6},{8,9},{9,8},{10,11... | collective-permute-start | bytes 1179656 | tf_op jit(solution)/shard_map/ppermute | solution.py:789
  22.8 2.2 %collective-permute-start.3 = (bf16[2,128,192]{2,1,0:T(8,128)(2,1)S(1)}, bf16[2,128,192]{2,1,0:T(8,128)(2,1)S(1)}, u32[]{:S(2)}, u32[]{:S(2)}) collective-permute-start(bf16[2,128,192]{2,1,0:T(8,128)(2,1)S(1)} %get-tuple-element.100), channel_id=1, source_target_pairs={{0,1},{1,0},{2,3},{3,2},{4,5},{5,4},{6,7},{7,6},{8,9},{9,8},{10,11... | collective-permute-start | bytes 294920 | tf_op jit(solution)/shard_map/ppermute | solution.py:789
  23.0 6.3 %collective-permute-start.4 = (bf16[2,128,192]{2,1,0:T(8,128)(2,1)S(1)}, bf16[2,128,192]{2,1,0:T(8,128)(2,1)S(1)}, u32[]{:S(2)}, u32[]{:S(2)}) collective-permute-start(bf16[2,128,192]{2,1,0:T(8,128)(2,1)S(1)} %get-tuple-element.101), channel_id=1, source_target_pairs={{0,2},{1,3},{2,0},{3,1},{4,6},{5,7},{6,4},{7,5},{8,10},{9,11},{10,... | collective-permute-start | bytes 294920 | tf_op jit(solution)/shard_map/ppermute | solution.py:789
  24.8 6.3 %collective-permute-start.5 = (bf16[2,128,192]{2,1,0:T(8,128)(2,1)S(1)}, bf16[2,128,192]{2,1,0:T(8,128)(2,1)S(1)}, u32[]{:S(2)}, u32[]{:S(2)}) collective-permute-start(bf16[2,128,192]{2,1,0:T(8,128)(2,1)S(1)} %get-tuple-element.102), channel_id=1, source_target_pairs={{0,3},{1,2},{2,1},{3,0},{4,7},{5,6},{6,5},{7,4},{8,11},{9,10},{10,... | collective-permute-start | bytes 294920 | tf_op jit(solution)/shard_map/ppermute | solution.py:789
  43.0 3.1 %collective-permute-start.7 = (bf16[256,2304]{1,0:T(8,128)(2,1)}, bf16[256,2304]{1,0:T(8,128)(2,1)S(1)}, u32[]{:S(2)}, u32[]{:S(2)}) collective-permute-start(bf16[256,2304]{1,0:T(8,128)(2,1)} %get-tuple-element.111.grad), channel_id=1, source_target_pairs={{0,1},{1,0},{2,3},{3,2},{4,5},{5,4},{6,7},{7,6},{8,9},{9,8},{10,11... | collective-permute-start | bytes 3538952 | tf_op jit(solution)/shard_map/ppermute | solution.py:789
  43.5 8.3 %collective-permute-start.6 = (bf16[2,256,192]{2,1,0:T(8,128)(2,1)S(1)}, bf16[2,256,192]{2,1,0:T(8,128)(2,1)S(1)}, u32[]{:S(2)}, u32[]{:S(2)}) collective-permute-start(bf16[2,256,192]{2,1,0:T(8,128)(2,1)S(1)} %get-tuple-element.109), channel_id=1, source_target_pairs={{0,2},{1,3},{2,0},{3,1},{4,6},{5,7},{6,4},{7,5},{8,10},{9,11},{10,... | collective-permute-start | bytes 589832 | tf_op jit(solution)/shard_map/ppermute | solution.py:789
  45.3 7.0 %collective-permute-start.9 = (bf16[4,192,256]{2,1,0:T(8,128)(2,1)}, bf16[4,192,256]{2,1,0:T(8,128)(2,1)S(1)}, u32[]{:S(2)}, u32[]{:S(2)}) collective-permute-start(bf16[4,192,256]{2,1,0:T(8,128)(2,1)} %get-tuple-element.117), channel_id=1, source_target_pairs={{0,1},{1,0},{2,3},{3,2},{4,5},{5,4},{6,7},{7,6},{8,9},{9,8},{10,11... | collective-permute-start | bytes 1179656 | tf_op jit(solution)/shard_map/ppermute | solution.py:789
  45.3 7.0 %collective-permute-start.10 = (bf16[256,3840]{1,0:T(8,128)(2,1)}, bf16[256,3840]{1,0:T(8,128)(2,1)S(1)}, u32[]{:S(2)}, u32[]{:S(2)}) collective-permute-start(bf16[256,3840]{1,0:T(8,128)(2,1)} %get-tuple-element.116.second_hbm), channel_id=1, source_target_pairs={{0,1},{1,0},{2,3},{3,2},{4,5},{5,4},{6,7},{7,6},{8,9},{9,8},{10,11... | collective-permute-start | bytes 5898248 | tf_op jit(solution)/shard_map/ppermute | solution.py:789
  49.2 28.3 %collective-permute-start.15 = (bf16[2,4,96,768]{3,2,1,0:T(8,128)(2,1)S(1)}, bf16[2,4,96,768]{3,2,1,0:T(8,128)(2,1)S(1)}, u32[]{:S(2)}, u32[]{:S(2)}) collective-permute-start(bf16[2,4,96,768]{3,2,1,0:T(8,128)(2,1)S(1)} %get-tuple-element.129), channel_id=1, source_target_pairs={{0,4},{4,0},{8,12},{12,8},{16,20},{20,16},{24,28},{28,24},{1,5},{5... | collective-permute-start | bytes 3538952 | tf_op jit(solution)/shard_map/ppermute | solution.py:789
  57.9 22.7 %collective-permute-start.14 = (bf16[1,8,128,384]{3,2,1,0:T(8,128)(2,1)}, bf16[1,8,128,384]{3,2,1,0:T(8,128)(2,1)}, u32[]{:S(2)}, u32[]{:S(2)}) collective-permute-start(bf16[1,8,128,384]{3,2,1,0:T(8,128)(2,1)} %get-tuple-element.127), channel_id=1, source_target_pairs={{0,2},{1,3},{2,0},{3,1},{4,6},{5,7},{6,4},{7,5},{8,10},{9,11},{10,... | collective-permute-start | bytes 2359304 | tf_op jit(solution)/shard_map/ppermute | solution.py:789
  59.7 23.8 %collective-permute-start.13 = (bf16[2,4,112,384]{3,2,1,0:T(8,128)(2,1)}, bf16[2,4,112,384]{3,2,1,0:T(8,128)(2,1)}, u32[]{:S(2)}, u32[]{:S(2)}) collective-permute-start(bf16[2,4,112,384]{3,2,1,0:T(8,128)(2,1)} %get-tuple-element.125), channel_id=1, source_target_pairs={{0,8},{4,12},{8,0},{12,4},{16,24},{20,28},{24,16},{28,20},{1,9},{5... | collective-permute-start | bytes 2064392 | tf_op jit(solution)/shard_map/ppermute | solution.py:789
  61.3 1.5 collective-permute-start.8
  62.9 14.7 %copy-start.9 = (bf16[2,4,96,768]{3,2,1,0:T(8,128)(2,1)S(1)}, bf16[2,4,96,768]{3,2,1,0:T(8,128)(2,1)}, u32[]{:S(2)}) copy-start(bf16[2,4,96,768]{3,2,1,0:T(8,128)(2,1)} %copy-done.8) | copy-start | bytes 3538948
  75.3 14.1 %collective-permute-start.12 = (bf16[1,4,96,640]{3,2,1,0:T(8,128)(2,1)S(1)}, bf16[1,4,96,640]{3,2,1,0:T(8,128)(2,1)S(1)}, u32[]{:S(2)}, u32[]{:S(2)}) collective-permute-start(bf16[1,4,96,640]{3,2,1,0:T(8,128)(2,1)S(1)} %get-tuple-element.123), channel_id=1, source_target_pairs={{0,4},{4,0},{8,12},{12,8},{16,20},{20,16},{24,28},{28,24},{1,5},{5... | collective-permute-start | bytes 1474568 | tf_op jit(solution)/shard_map/ppermute | solution.py:789
  76.9 20.4 %collective-permute-start.11 = (bf16[2,2,128,768]{3,2,1,0:T(8,128)(2,1)}, bf16[2,2,128,768]{3,2,1,0:T(8,128)(2,1)S(1)}, u32[]{:S(2)}, u32[]{:S(2)}) collective-permute-start(bf16[2,2,128,768]{3,2,1,0:T(8,128)(2,1)} %get-tuple-element.121), channel_id=1, source_target_pairs={{0,1},{1,0},{2,3},{3,2},{4,5},{5,4},{6,7},{7,6},{8,9},{9,8},{10,11... | collective-permute-start | bytes 2359304 | tf_op jit(solution)/shard_map/ppermute | solution.py:789
  78.3 17.3 %collective-permute-start.20 = (bf16[1,4,96,768]{3,2,1,0:T(8,128)(2,1)S(1)}, bf16[1,4,96,768]{3,2,1,0:T(8,128)(2,1)S(1)}, u32[]{:S(2)}, u32[]{:S(2)}) collective-permute-start(bf16[1,4,96,768]{3,2,1,0:T(8,128)(2,1)S(1)} %get-tuple-element.139), channel_id=1, source_target_pairs={{0,2},{1,3},{2,0},{3,1},{4,6},{5,7},{6,4},{7,5},{8,10},{9,11},{10,... | collective-permute-start | bytes 1769480 | tf_op jit(solution)/shard_map/ppermute | solution.py:789
  81.9 10.8 %collective-permute-start.17 = (bf16[1,4,128,384]{3,2,1,0:T(8,128)(2,1)S(1)}, bf16[1,4,128,384]{3,2,1,0:T(8,128)(2,1)S(1)}, u32[]{:S(2)}, u32[]{:S(2)}) collective-permute-start(bf16[1,4,128,384]{3,2,1,0:T(8,128)(2,1)S(1)} %get-tuple-element.135), channel_id=1, source_target_pairs={{0,8},{4,12},{8,0},{12,4},{16,24},{20,28},{24,16},{28,20},{1,9},{5... | collective-permute-start | bytes 1179656 | tf_op jit(solution)/shard_map/ppermute | solution.py:789
  84.9 12.5 %collective-permute-start.19 = (bf16[2,2,112,384]{3,2,1,0:T(8,128)(2,1)S(1)}, bf16[2,2,112,384]{3,2,1,0:T(8,128)(2,1)S(1)}, u32[]{:S(2)}, u32[]{:S(2)}) collective-permute-start(bf16[2,2,112,384]{3,2,1,0:T(8,128)(2,1)S(1)} %get-tuple-element.138), channel_id=1, source_target_pairs={{0,4},{4,0},{8,12},{12,8},{16,20},{20,16},{24,28},{28,24},{1,5},{5... | collective-permute-start | bytes 1032200 | tf_op jit(solution)/shard_map/ppermute | solution.py:789
  90.1 14.1 %collective-permute-start.16 = (bf16[1,2,96,640]{3,2,1,0:T(8,128)(2,1)S(1)}, bf16[1,2,96,640]{3,2,1,0:T(8,128)(2,1)S(1)}, u32[]{:S(2)}, u32[]{:S(2)}) collective-permute-start(bf16[1,2,96,640]{3,2,1,0:T(8,128)(2,1)S(1)} %get-tuple-element.134), channel_id=1, source_target_pairs={{0,16},{4,20},{8,24},{12,28},{16,0},{20,4},{24,8},{28,12},{1,17},{... | collective-permute-start | bytes 737288 | tf_op jit(solution)/shard_map/ppermute | solution.py:789
  94.0 6.3 %collective-permute-start.18 = (bf16[1,2,128,384]{3,2,1,0:T(8,128)(2,1)S(1)}, bf16[1,2,128,384]{3,2,1,0:T(8,128)(2,1)S(1)}, u32[]{:S(2)}, u32[]{:S(2)}) collective-permute-start(bf16[1,2,128,384]{3,2,1,0:T(8,128)(2,1)S(1)} %get-tuple-element.137), channel_id=1, source_target_pairs={{0,4},{4,0},{8,12},{12,8},{16,20},{20,16},{24,28},{28,24},{1,5},{5... | collective-permute-start | bytes 589832 | tf_op jit(solution)/shard_map/ppermute | solution.py:789
  96.2 19.2 %collective-permute-start.24 = (bf16[1,2,96,768]{3,2,1,0:T(8,128)(2,1)S(1)}, bf16[1,2,96,768]{3,2,1,0:T(8,128)(2,1)S(1)}, u32[]{:S(2)}, u32[]{:S(2)}) collective-permute-start(bf16[1,2,96,768]{3,2,1,0:T(8,128)(2,1)S(1)} %get-tuple-element.147), channel_id=1, source_target_pairs={{0,8},{4,12},{8,0},{12,4},{16,24},{20,28},{24,16},{28,20},{1,9},{5... | collective-permute-start | bytes 884744 | tf_op jit(solution)/shard_map/ppermute | solution.py:789
  98.5 17.6 %collective-permute-start.23 = (bf16[1,2,112,384]{3,2,1,0:T(8,128)(2,1)S(1)}, bf16[1,2,112,384]{3,2,1,0:T(8,128)(2,1)S(1)}, u32[]{:S(2)}, u32[]{:S(2)}) collective-permute-start(bf16[1,2,112,384]{3,2,1,0:T(8,128)(2,1)S(1)} %get-tuple-element.146), channel_id=1, source_target_pairs={{0,2},{1,3},{2,0},{3,1},{4,6},{5,7},{6,4},{7,5},{8,10},{9,11},{10,... | collective-permute-start | bytes 516104 | tf_op jit(solution)/shard_map/ppermute | solution.py:789
  101.5 18.9 %collective-permute-start.22 = (bf16[1,2,128,384]{3,2,1,0:T(8,128)(2,1)S(1)}, bf16[1,2,128,384]{3,2,1,0:T(8,128)(2,1)S(1)}, u32[]{:S(2)}, u32[]{:S(2)}) collective-permute-start(bf16[1,2,128,384]{3,2,1,0:T(8,128)(2,1)S(1)} %get-tuple-element.145.refs_1_), channel_id=1, source_target_pairs={{0,16},{4,20},{8,24},{12,28},{16,0},{20,4},{24,8},{28,12},{1,17},{... | collective-permute-start | bytes 589832 | tf_op jit(solution)/shard_map/ppermute | solution.py:789
  104.8 17.7 %collective-permute-start.21 = (bf16[1,2,96,640]{3,2,1,0:T(8,128)(2,1)S(1)}, bf16[1,2,96,640]{3,2,1,0:T(8,128)(2,1)S(1)}, u32[]{:S(2)}, u32[]{:S(2)}) collective-permute-start(bf16[1,2,96,640]{3,2,1,0:T(8,128)(2,1)S(1)} %get-tuple-element.144.refs_1_), channel_id=1, source_target_pairs={{0,8},{4,12},{8,0},{12,4},{16,24},{20,28},{24,16},{28,20},{1,9},{5... | collective-permute-start | bytes 737288 | tf_op jit(solution)/shard_map/ppermute | solution.py:789
  117.4 11.9 %collective-permute-start.31 = (bf16[1,2,112,384]{3,2,1,0:T(8,128)(2,1)S(1)}, bf16[1,2,112,384]{3,2,1,0:T(8,128)(2,1)S(1)}, u32[]{:S(2)}, u32[]{:S(2)}) collective-permute-start(bf16[1,2,112,384]{3,2,1,0:T(8,128)(2,1)S(1)} %get-tuple-element.159.refs_1_), channel_id=1, source_target_pairs={{0,16},{4,20},{8,24},{12,28},{16,0},{20,4},{24,8},{28,12},{1,17},{... | collective-permute-start | bytes 516104 | tf_op jit(solution)/shard_map/ppermute | solution.py:789
  117.5 14.7 %collective-permute-start.30 = (bf16[1,2,96,768]{3,2,1,0:T(8,128)(2,1)S(1)}, bf16[1,2,96,768]{3,2,1,0:T(8,128)(2,1)S(1)}, u32[]{:S(2)}, u32[]{:S(2)}) collective-permute-start(bf16[1,2,96,768]{3,2,1,0:T(8,128)(2,1)S(1)} %get-tuple-element.158.refs_1_), channel_id=1, source_target_pairs={{0,16},{4,20},{8,24},{12,28},{16,0},{20,4},{24,8},{28,12},{1,17},{... | collective-permute-start | bytes 884744 | tf_op jit(solution)/shard_map/ppermute | solution.py:789
  121.0 7.8 %collective-permute-start.32 = (bf16[2,128,384]{2,1,0:T(8,128)(2,1)S(1)}, bf16[2,128,384]{2,1,0:T(8,128)(2,1)S(1)}, u32[]{:S(2)}, u32[]{:S(2)}) collective-permute-start(bf16[2,128,384]{2,1,0:T(8,128)(2,1)S(1)} %bitcast.50), channel_id=1, source_target_pairs={{0,8},{4,12},{8,0},{12,4},{16,24},{20,28},{24,16},{28,20},{1,9},{5... | collective-permute-start | bytes 589832 | tf_op jit(solution)/shard_map/ppermute | solution.py:789
  123.1 1.3 collective-permute-start.26
  123.2 4.7 %collective-permute-start.27 = (bf16[2,24,640]{2,1,0:T(8,128)(2,1)S(1)}, bf16[2,24,640]{2,1,0:T(8,128)(2,1)S(1)}, u32[]{:S(2)}, u32[]{:S(2)}) collective-permute-start(bf16[2,24,640]{2,1,0:T(8,128)(2,1)S(1)} %get-tuple-element.156), channel_id=1, source_target_pairs={{0,2},{1,3},{2,0},{3,1},{4,6},{5,7},{6,4},{7,5},{8,10},{9,11},{10,... | collective-permute-start | bytes 184328 | tf_op jit(solution)/shard_map/ppermute | solution.py:789
  124.4 4.2 %collective-permute-start.28 = (bf16[2,24,640]{2,1,0:T(8,128)(2,1)S(1)}, bf16[2,24,640]{2,1,0:T(8,128)(2,1)S(1)}, u32[]{:S(2)}, u32[]{:S(2)}) collective-permute-start(bf16[2,24,640]{2,1,0:T(8,128)(2,1)S(1)} %get-tuple-element.157), channel_id=1, source_target_pairs={{0,3},{1,2},{2,1},{3,0},{4,7},{5,6},{6,5},{7,4},{8,11},{9,10},{10,... | collective-permute-start | bytes 184328 | tf_op jit(solution)/shard_map/ppermute | solution.py:789
  127.8 14.5 %collective-permute-start.25 = (bf16[1,1,256,768]{3,2,1,0:T(8,128)(2,1)S(1)}, bf16[1,1,256,768]{3,2,1,0:T(8,128)(2,1)S(1)}, u32[]{:S(2)}, u32[]{:S(2)}) collective-permute-start(bf16[1,1,256,768]{3,2,1,0:T(8,128)(2,1)S(1)} %get-tuple-element.153), channel_id=1, source_target_pairs={{0,2},{1,3},{2,0},{3,1},{4,6},{5,7},{6,4},{7,5},{8,10},{9,11},{10,... | collective-permute-start | bytes 1179656 | tf_op jit(solution)/shard_map/ppermute | solution.py:789
  128.7 8.9 %collective-permute-start.29 = (bf16[2,96,640]{2,1,0:T(8,128)(2,1)S(1)}, bf16[2,96,640]{2,1,0:T(8,128)(2,1)S(1)}, u32[]{:S(2)}, u32[]{:S(2)}) collective-permute-start(bf16[2,96,640]{2,1,0:T(8,128)(2,1)S(1)} %constant_dynamic-update-slice_fusion.refs_0_), channel_id=1, source_target_pairs={{0,4},{4,0},{8,12},{12,8},{16,20},{20,16},{24,28},{28,24},{1,5},{5... | collective-permute-start | bytes 737288 | tf_op jit(solution)/shard_map/ppermute | solution.py:789
  129.9 11.3 %collective-permute-start.35 = (bf16[2,112,384]{2,1,0:T(8,128)(2,1)S(1)}, bf16[2,112,384]{2,1,0:T(8,128)(2,1)S(1)}, u32[]{:S(2)}, u32[]{:S(2)}) collective-permute-start(bf16[2,112,384]{2,1,0:T(8,128)(2,1)S(1)} %bitcast.52), channel_id=1, source_target_pairs={{0,4},{4,0},{8,12},{12,8},{16,20},{20,16},{24,28},{28,24},{1,5},{5... | collective-permute-start | bytes 516104 | tf_op jit(solution)/shard_map/ppermute | solution.py:789
  132.8 10.5 %collective-permute-start.37 = (bf16[2,96,768]{2,1,0:T(8,128)(2,1)S(1)}, bf16[2,96,768]{2,1,0:T(8,128)(2,1)S(1)}, u32[]{:S(2)}, u32[]{:S(2)}) collective-permute-start(bf16[2,96,768]{2,1,0:T(8,128)(2,1)S(1)} %bitcast.48), channel_id=1, source_target_pairs={{0,8},{4,12},{8,0},{12,4},{16,24},{20,28},{24,16},{28,20},{1,9},{5... | collective-permute-start | bytes 884744 | tf_op jit(solution)/shard_map/ppermute | solution.py:789
  133.6 16.0 %collective-permute-start.34 = (bf16[4,128,384]{2,1,0:T(8,128)(2,1)S(1)}, bf16[4,128,384]{2,1,0:T(8,128)(2,1)S(1)}, u32[]{:S(2)}, u32[]{:S(2)}) collective-permute-start(bf16[4,128,384]{2,1,0:T(8,128)(2,1)S(1)} %get-tuple-element.168.refs_2_), channel_id=1, source_target_pairs={{0,4},{4,0},{8,12},{12,8},{16,20},{20,16},{24,28},{28,24},{1,5},{5... | collective-permute-start | bytes 1179656 | tf_op jit(solution)/shard_map/ppermute | solution.py:789
  138.1 23.5 %collective-permute-start.33 = (bf16[4,96,640]{2,1,0:T(8,128)(2,1)S(1)}, bf16[4,96,640]{2,1,0:T(8,128)(2,1)S(1)}, u32[]{:S(2)}, u32[]{:S(2)}) collective-permute-start(bf16[4,96,640]{2,1,0:T(8,128)(2,1)S(1)} %get-tuple-element.165.refs_1_), channel_id=1, source_target_pairs={{0,16},{4,20},{8,24},{12,28},{16,0},{20,4},{24,8},{28,12},{1,17},{... | collective-permute-start | bytes 1474568 | tf_op jit(solution)/shard_map/ppermute | solution.py:789
  141.7 15.5 %collective-permute-start.36 = (bf16[4,112,384]{2,1,0:T(8,128)(2,1)S(1)}, bf16[4,112,384]{2,1,0:T(8,128)(2,1)S(1)}, u32[]{:S(2)}, u32[]{:S(2)}) collective-permute-start(bf16[4,112,384]{2,1,0:T(8,128)(2,1)S(1)} %get-tuple-element.171.refs_4_), channel_id=1, source_target_pairs={{0,8},{4,12},{8,0},{12,4},{16,24},{20,28},{24,16},{28,20},{1,9},{5... | collective-permute-start | bytes 1032200 | tf_op jit(solution)/shard_map/ppermute | solution.py:789
  143.5 21.5 %collective-permute-start.38 = (bf16[4,96,768]{2,1,0:T(8,128)(2,1)S(1)}, bf16[4,96,768]{2,1,0:T(8,128)(2,1)S(1)}, u32[]{:S(2)}, u32[]{:S(2)}) collective-permute-start(bf16[4,96,768]{2,1,0:T(8,128)(2,1)S(1)} %get-tuple-element.176.refs_1_), channel_id=1, source_target_pairs={{0,4},{4,0},{8,12},{12,8},{16,20},{20,16},{24,28},{28,24},{1,5},{5... | collective-permute-start | bytes 1769480 | tf_op jit(solution)/shard_map/ppermute | solution.py:789
  (14 other events, 71.0 us)

commit v7 on v6

--- a/solution.py
+++ b/solution.py
@@ -205,15 +205,16 @@
     late = [load(vectors, extra_here)]
     for p in range(2):
         late.append(load(x_hbm.at[p], x.at[pl.ds(p * rows, rows)]))
-    for copy in needs[0][0] + needs[0][1]:
+    for copy in needs[0][0] + needs[0][1] + last + needs[1][0] + needs[1][1]:
         copy.start()
     stores = []
     sums = [0.0, 0.0]
     for p in range(2):
         for copy in needs[p][0]:
             copy.wait()
-        for copy in last + needs[1][0] + needs[1][1] if p == 0 else late:
-            copy.start()
+        if p == 0:
+            for copy in late:
+                copy.start()
         grad_q, grad_k, grad_v = [], [], []
         for h in range(heads):
             cols = slice(h * HD, (h + 1) * HD)

time: 168 us -> 167 us (level)
  transfers between devices with their start and end apart: 39 -> 39, of which waited for: 21 -> 20; matrix products, arithmetic and copies ran while one was open for 2% -> 2% of each run, Pallas kernels for 27% -> 26%
where the time goes in v7:
time: 167 us
  Pallas kernels  65.7 us (39%)
  waiting for transfers between devices  52.5 us (31%)
  starting transfers between devices  42.9 us (26%)
  local copies, waits for them, and re-layouts  2.94 us (2%)
    ppermute x39, waiting for transfers between devices, swap(): return lax.ppermute(field, axis, [(i, i ^ bit) for i in range(count)])  52.5 us
    ppermute x39, starting transfers between devices, swap(): return lax.ppermute(field, axis, [(i, i ^ bit) for i in range(count)])  42.9 us
    pallas_call x16, Pallas kernels, sum_pieces(): pl.pallas_call(lambda *refs: sum_kernel(spec, *refs), in_specs=[SMEM] + [...  13.8 us
    pallas_call x1, Pallas kernels, attend_back(): pl.pallas_call(attend_back_kernel, in_specs=[SMEM] + [HBM] * 5 + [vmem()]...  12.1 us
    pallas_call x1, Pallas kernels, rows_pass(): pl.pallas_call(rows_kernel, in_specs=[SMEM, vmem()] + [HBM] * 3 + [vmem()...  11.9 us
    pallas_call x1, Pallas kernels, attend(): pl.pallas_call(attend_kernel, in_specs=[SMEM, SMEM, vmem(), HBM, vmem(),...  7.71 us
    pallas_call x1, Pallas kernels, inner_grad(): pl.pallas_call(inner_grad_kernel, in_specs=[SMEM, SMEM, HBM, HBM, vmem(),...  5.69 us
  transfers between devices with their start and end apart: 39, of which 20 were waited for; matrix products, arithmetic and copies ran while one was open for 2% of the time, Pallas kernels for 26%

profile of v7, /device:TPU:0, one launch (start us, length us, event | category | flops | bytes accessed | tf_op | source)
XLA Modules:
  0.0 166.5 jit_solution(14040164542968467406)
XLA Ops:
  0.6 3.0 %collective-permute-start.1 = (bf16[2,128,768]{2,1,0:T(8,128)(2,1)}, bf16[2,128,768]{2,1,0:T(8,128)(2,1)S(1)}, u32[]{:S(2)}, u32[]{:S(2)}) collective-permute-start(bf16[2,128,768]{2,1,0:T(8,128)(2,1)} %x0.1), channel_id=1, source_target_pairs={{0,2},{1,3},{2,0},{3,1},{4,6},{5,7},{6,4},{7,5},{8,10},{9,11},{10,... | collective-permute-start | bytes 1179656 | tf_op jit(solution)/shard_map/ppermute | solution.py:790
  5.1 2.7 %choose_heads.1 = (bf16[768,576]{1,0:T(8,128)(2,1)}, f32[2,192]{1,0:T(2,128)S(1)}, f32[8,128]{1,0:T(8,128)}) custom-call(s32[1]{0:T(128)} %bitcast.where, bf16[768,2304]{1,0:T(8,128)(2,1)} %w_hbm.1, bf16[1,768]{1,0:T(2,128)(2,1)S(1)} %reshape.97.qb, bf16[1,768]{1,0:T(2,128)(2,1)S(1)} %reshape.98.vb), custom_call_target="tpu_custom_call" | custom-call | flops 1724999936 | bytes 5535000 | tf_op jit(solution)/shard_map/choose_heads/pallas_call | solution.py:88
  7.8 5.2 %collective-permute-done.1.source = bf16[2,128,768]{2,1,0:T(8,128)(2,1)S(1)} collective-permute-done((bf16[2,128,768]{2,1,0:T(8,128)(2,1)}, bf16[2,128,768]{2,1,0:T(8,128)(2,1)S(1)}, u32[]{:S(2)}, u32[]{:S(2)}) %collective-permute-start.1) | collective-permute-done | bytes 393248 | tf_op jit(solution)/shard_map/ppermute | solution.py:790
  13.4 1.7 %collective-permute-done.2.x3 = bf16[2,128,768]{2,1,0:T(8,128)(2,1)S(1)} collective-permute-done((bf16[2,128,768]{2,1,0:T(8,128)(2,1)S(1)}, bf16[2,128,768]{2,1,0:T(8,128)(2,1)S(1)}, u32[]{:S(2)}, u32[]{:S(2)}) %collective-permute-start.2) | collective-permute-done | bytes 393248 | tf_op jit(solution)/shard_map/ppermute | solution.py:790
  15.1 7.7 %attend.1 = (bf16[2,512,576]{2,1,0:T(8,128)(2,1)}, bf16[2,3,512,512]{3,2,1,0:T(8,128)(2,1)}, bf16[2,128,192]{2,1,0:T(8,128)(2,1)}, bf16[2,512,768]{2,1,0:T(8,128...) custom-call(s32[1]{0:T(128)} %bitcast.where, ...), custom_call_target="tpu_custom_call" | custom-call | flops 115000000 | bytes 369000 | tf_op jit(solution)/shard_map/attend/pallas_call | solution.py:168
  23.0 1.8 %collective-permute-start.4 = (bf16[2,128,192]{2,1,0:T(8,128)(2,1)S(1)}, bf16[2,128,192]{2,1,0:T(8,128)(2,1)S(1)}, u32[]{:S(2)}, u32[]{:S(2)}) collective-permute-start(bf16[2,128,192]{2,1,0:T(8,128)(2,1)S(1)} %get-tuple-element.101), channel_id=1, source_target_pairs={{0,2},{1,3},{2,0},{3,1},{4,6},{5,7},{6,4},{7,5},{8,10},{9,11},{10,... | collective-permute-start | bytes 294920 | tf_op jit(solution)/shard_map/ppermute | solution.py:790
  25.0 4.3 %collective-permute-done.4 = bf16[2,128,192]{2,1,0:T(8,128)(2,1)S(1)} collective-permute-done((bf16[2,128,192]{2,1,0:T(8,128)(2,1)S(1)}, bf16[2,128,192]{2,1,0:T(8,128)(2,1)S(1)}, u32[]{:S(2)}, u32[]{:S(2)}) %collective-permute-start.4) | collective-permute-done | bytes 98336 | tf_op jit(solution)/shard_map/ppermute | solution.py:790
  29.4 1.7 %collective-permute-done.5 = bf16[2,128,192]{2,1,0:T(8,128)(2,1)S(1)} collective-permute-done((bf16[2,128,192]{2,1,0:T(8,128)(2,1)S(1)}, bf16[2,128,192]{2,1,0:T(8,128)(2,1)S(1)}, u32[]{:S(2)}, u32[]{:S(2)}) %collective-permute-start.5) | collective-permute-done | bytes 98336 | tf_op jit(solution)/shard_map/ppermute | solution.py:790
  31.1 11.9 %rows_pass.1 = (bf16[256,768]{1,0:T(8,128)(2,1)}, f32[256,768]{1,0:T(8,128)}, bf16[256,1536]{1,0:T(8,128)(2,1)}, bf16[256,2304]{1,0:T(8,128)(2,1)}, bf16[256,384...) custom-call(s32[1]{0:T(128)} %bitcast.where, ...), custom_call_target="tpu_custom_call" | custom-call | flops 12650000384 | bytes 40590000 | tf_op jit(solution)/shard_map/rows_pass/pallas_call | solution.py:430
  43.5 1.7 %collective-permute-start.6 = (bf16[2,256,192]{2,1,0:T(8,128)(2,1)S(1)}, bf16[2,256,192]{2,1,0:T(8,128)(2,1)S(1)}, u32[]{:S(2)}, u32[]{:S(2)}) collective-permute-start(bf16[2,256,192]{2,1,0:T(8,128)(2,1)S(1)} %get-tuple-element.109), channel_id=1, source_target_pairs={{0,2},{1,3},{2,0},{3,1},{4,6},{5,7},{6,4},{7,5},{8,10},{9,11},{10,... | collective-permute-start | bytes 589832 | tf_op jit(solution)/shard_map/ppermute | solution.py:790
  46.1 3.1 %outer_grad.1 = (bf16[2,4,96,768]{3,2,1,0:T(8,128)(2,1)S(1)}, bf16[2,4,96,768]{3,2,1,0:T(8,128)(2,1)S(1)}, f32[8,128]{1,0:T(8,128)}) custom-call(s32[2]{0:T(128)S(1)} %pad_add_fusion.1.place.refs_0_, bf16[256,1536]{1,0:T(8,128)(2,1)} %get-tuple-element.110.active, bf16[256,2304]{1,0:T(8,128)(2,1)S(1)} %collective-permute-done.7.active_got.grad_got, ...), custom_call_target="tpu_custom_call" | custom-call | flops 34500001792 | bytes 110700000 | tf_op jit(solution)/shard_map/outer_grad/pallas_call | solution.py:472
  49.2 1.8 %collective-permute-start.15 = (bf16[2,4,96,768]{3,2,1,0:T(8,128)(2,1)S(1)}, bf16[2,4,96,768]{3,2,1,0:T(8,128)(2,1)S(1)}, u32[]{:S(2)}, u32[]{:S(2)}) collective-permute-start(bf16[2,4,96,768]{3,2,1,0:T(8,128)(2,1)S(1)} %get-tuple-element.129), channel_id=1, source_target_pairs={{0,4},{4,0},{8,12},{12,8},{16,20},{20,16},{24,28},{28,24},{1,5},{5... | collective-permute-start | bytes 3538952 | tf_op jit(solution)/shard_map/ppermute | solution.py:790
  52.2 5.7 %inner_grad.1 = (bf16[1,8,128,384]{3,2,1,0:T(8,128)(2,1)}, bf16[1,8,128,384]{3,2,1,0:T(8,128)(2,1)}, bf16[2,4,112,384]{3,2,1,0:T(8,128)(2,1)}, bf16[2,4,112,384]{3,2,1,0:T(8,128)(2,1)}, f32[8,128]{1,0:T(8,128)}) custom-call(s32[2]{0:T(128)S(1)} %pad_add_fusion.2.bit_b.bit_c.refs_0_.refs_1_, s32[2]{0:T(128)S(1)} %pad_add_fusion.2.bit_b.bit_c.refs_0_.refs_1_, ...), custom_call_target="tpu_custom_call" | custom-call | flops 4600000000 | bytes 14760000 | tf_op jit(solution)/shard_map/inner_grad/pallas_call | solution.py:565
  57.9 1.8 %collective-permute-start.14 = (bf16[1,8,128,384]{3,2,1,0:T(8,128)(2,1)}, bf16[1,8,128,384]{3,2,1,0:T(8,128)(2,1)}, u32[]{:S(2)}, u32[]{:S(2)}) collective-permute-start(bf16[1,8,128,384]{3,2,1,0:T(8,128)(2,1)} %get-tuple-element.127), channel_id=1, source_target_pairs={{0,2},{1,3},{2,0},{3,1},{4,6},{5,7},{6,4},{7,5},{8,10},{9,11},{10,... | collective-permute-start | bytes 2359304 | tf_op jit(solution)/shard_map/ppermute | solution.py:790
  59.7 1.6 collective-permute-start.13
  61.4 1.5 collective-permute-done.8
  62.9 12.1 %attend_back.1 = (bf16[2,2,128,768]{3,2,1,0:T(8,128)(2,1)}, bf16[2,2,128,768]{3,2,1,0:T(8,128)(2,1)}, bf16[1,4,96,640]{3,2,1,0:T(8,128)(2,1)S(1)}, bf16[1,4,96,640]{3,2,1,0:T(8,128)(2,1)}, f32[8,128]{1,0:T(8,128)}) custom-call(s32[2]{0:T(128)S(1)} %pad_add_fusion.place.refs_0_, bf16[2,512,768]{2,1,0:T(8,128)(2,1)} %get-tuple-element.105.refs_0_, ...), custom_call_target="tpu_custom_call" | custom-call | flops 1150000000 | bytes 3690000 | tf_op jit(solution)/shard_map/attend_back/pallas_call | solution.py:284
  75.0 1.6 collective-permute-start.12
  78.3 2.4 %collective-permute-start.20 = (bf16[1,4,96,768]{3,2,1,0:T(8,128)(2,1)S(1)}, bf16[1,4,96,768]{3,2,1,0:T(8,128)(2,1)S(1)}, u32[]{:S(2)}, u32[]{:S(2)}) collective-permute-start(bf16[1,4,96,768]{3,2,1,0:T(8,128)(2,1)S(1)} %get-tuple-element.139), channel_id=1, source_target_pairs={{0,2},{1,3},{2,0},{3,1},{4,6},{5,7},{6,4},{7,5},{8,10},{9,11},{10,... | collective-permute-start | bytes 1769480 | tf_op jit(solution)/shard_map/ppermute | solution.py:790
  80.6 1.3 sum_b.3
  81.9 1.6 collective-permute-start.17
  83.6 1.3 sum_c.3
  84.9 1.5 collective-permute-start.19
  86.4 2.7 %collective-permute-done.12.refs_2_ = bf16[1,4,96,640]{3,2,1,0:T(8,128)(2,1)S(1)} collective-permute-done((bf16[1,4,96,640]{3,2,1,0:T(8,128)(2,1)S(1)}, bf16[1,4,96,640]{3,2,1,0:T(8,128)(2,1)S(1)}, u32[]{:S(2)}, u32[]{:S(2)}) %collective-permute-start.12) | collective-permute-done | bytes 491552 | tf_op jit(solution)/shard_map/ppermute | solution.py:790
  89.7 2.6 %collective-permute-start.16 = (bf16[1,2,96,640]{3,2,1,0:T(8,128)(2,1)S(1)}, bf16[1,2,96,640]{3,2,1,0:T(8,128)(2,1)S(1)}, u32[]{:S(2)}, u32[]{:S(2)}) collective-permute-start(bf16[1,2,96,640]{3,2,1,0:T(8,128)(2,1)S(1)} %get-tuple-element.134), channel_id=1, source_target_pairs={{0,16},{4,20},{8,24},{12,28},{16,0},{20,4},{24,8},{28,12},{1,17},{... | collective-permute-start | bytes 737288 | tf_op jit(solution)/shard_map/ppermute | solution.py:790
  92.4 1.2 sum_b.4
  93.6 1.6 collective-permute-start.18
  95.9 1.4 collective-permute-start.24
  98.5 1.6 collective-permute-start.23
  100.1 1.3 sum_b.5
  101.4 2.4 %collective-permute-start.22 = (bf16[1,2,128,384]{3,2,1,0:T(8,128)(2,1)S(1)}, bf16[1,2,128,384]{3,2,1,0:T(8,128)(2,1)S(1)}, u32[]{:S(2)}, u32[]{:S(2)}) collective-permute-start(bf16[1,2,128,384]{3,2,1,0:T(8,128)(2,1)S(1)} %get-tuple-element.145.refs_1_), channel_id=1, source_target_pairs={{0,16},{4,20},{8,24},{12,28},{16,0},{20,4},{24,8},{28,12},{1,17},{... | collective-permute-start | bytes 589832 | tf_op jit(solution)/shard_map/ppermute | solution.py:790
  104.5 1.6 collective-permute-start.21
  106.1 9.1 %collective-permute-done.24.refs_4_ = bf16[1,2,96,768]{3,2,1,0:T(8,128)(2,1)S(1)} collective-permute-done((bf16[1,2,96,768]{3,2,1,0:T(8,128)(2,1)S(1)}, bf16[1,2,96,768]{3,2,1,0:T(8,128)(2,1)S(1)}, u32[]{:S(2)}, u32[]{:S(2)}) %collective-permute-start.24) | collective-permute-done | bytes 294944 | tf_op jit(solution)/shard_map/ppermute | solution.py:790
  115.9 1.2 sum_c.5
  117.2 2.9 %collective-permute-start.30 = (bf16[1,2,96,768]{3,2,1,0:T(8,128)(2,1)S(1)}, bf16[1,2,96,768]{3,2,1,0:T(8,128)(2,1)S(1)}, u32[]{:S(2)}, u32[]{:S(2)}) collective-permute-start(bf16[1,2,96,768]{3,2,1,0:T(8,128)(2,1)S(1)} %get-tuple-element.158.refs_1_), channel_id=1, source_target_pairs={{0,16},{4,20},{8,24},{12,28},{16,0},{20,4},{24,8},{28,12},{1,17},{... | collective-permute-start | bytes 884744 | tf_op jit(solution)/shard_map/ppermute | solution.py:790
  123.7 1.3 collective-permute-start.28
  125.1 2.1 %collective-permute-done.27 = bf16[2,24,640]{2,1,0:T(8,128)(2,1)S(1)} collective-permute-done((bf16[2,24,640]{2,1,0:T(8,128)(2,1)S(1)}, bf16[2,24,640]{2,1,0:T(8,128)(2,1)S(1)}, u32[]{:S(2)}, u32[]{:S(2)}) %collective-permute-start.27) | collective-permute-done | bytes 61472 | tf_op jit(solution)/shard_map/ppermute | solution.py:790
  129.2 2.1 %collective-permute-start.35 = (bf16[2,112,384]{2,1,0:T(8,128)(2,1)S(1)}, bf16[2,112,384]{2,1,0:T(8,128)(2,1)S(1)}, u32[]{:S(2)}, u32[]{:S(2)}) collective-permute-start(bf16[2,112,384]{2,1,0:T(8,128)(2,1)S(1)} %bitcast.52), channel_id=1, source_target_pairs={{0,4},{4,0},{8,12},{12,8},{16,20},{20,16},{24,28},{28,24},{1,5},{5... | collective-permute-start | bytes 516104 | tf_op jit(solution)/shard_map/ppermute | solution.py:790
  133.3 1.5 collective-permute-start.34
  134.7 2.1 %collective-permute-done.29.refs_1_ = bf16[2,96,640]{2,1,0:T(8,128)(2,1)S(1)} collective-permute-done((bf16[2,96,640]{2,1,0:T(8,128)(2,1)S(1)}, bf16[2,96,640]{2,1,0:T(8,128)(2,1)S(1)}, u32[]{:S(2)}, u32[]{:S(2)}) %collective-permute-start.29) | collective-permute-done | bytes 245792 | tf_op jit(solution)/shard_map/ppermute | solution.py:790
  137.5 1.4 collective-permute-start.33
  138.8 1.7 %collective-permute-done.35.refs_1_ = bf16[2,112,384]{2,1,0:T(8,128)(2,1)S(1)} collective-permute-done((bf16[2,112,384]{2,1,0:T(8,128)(2,1)S(1)}, bf16[2,112,384]{2,1,0:T(8,128)(2,1)S(1)}, u32[]{:S(2)}, u32[]{:S(2)}) %collective-permute-start.35) | collective-permute-done | bytes 172064 | tf_op jit(solution)/shard_map/ppermute | solution.py:790
  143.3 5.7 %collective-permute-done.34.refs_3_ = bf16[4,128,384]{2,1,0:T(8,128)(2,1)S(1)} collective-permute-done((bf16[4,128,384]{2,1,0:T(8,128)(2,1)S(1)}, bf16[4,128,384]{2,1,0:T(8,128)(2,1)S(1)}, u32[]{:S(2)}, u32[]{:S(2)}) %collective-permute-start.34) | collective-permute-done | bytes 393248 | tf_op jit(solution)/shard_map/ppermute | solution.py:790
  149.0 8.0 %collective-permute-done.36.refs_5_ = bf16[4,112,384]{2,1,0:T(8,128)(2,1)S(1)} collective-permute-done((bf16[4,112,384]{2,1,0:T(8,128)(2,1)S(1)}, bf16[4,112,384]{2,1,0:T(8,128)(2,1)S(1)}, u32[]{:S(2)}, u32[]{:S(2)}) %collective-permute-start.36) | collective-permute-done | bytes 344096 | tf_op jit(solution)/shard_map/ppermute | solution.py:790
  156.9 2.3 %inner_place.1 = (f32[192,3072]{1,0:T(8,128)}, f32[192,768]{1,0:T(8,128)}) custom-call(s32[2]{0:T(128)S(1)} %pad_add_fusion.2.bit_b.bit_c.refs_0_.refs_1_, s32[2]{0:T(128)S(1)} %pad_add_fusion.2.bit_b.bit_c.refs_0_.refs_1_, bf16[4,128,384]{2,1,0:T(8,128)(2,1)S(1)} %get-tuple-element.168.refs_2_, bf16[4,128,384]{2,1,0:T(8,128)(2,1)S(1)} %collective-permute-done.34.refs_3_, ...), custom_call_target="tpu_custom_call" | custom-call | flops 2300000000 | bytes 7380000 | tf_op jit(solution)/shard_map/inner_place/pallas_call | solution.py:668
  159.2 1.9 %collective-permute-done.33.refs_2_ = bf16[4,96,640]{2,1,0:T(8,128)(2,1)S(1)} collective-permute-done((bf16[4,96,640]{2,1,0:T(8,128)(2,1)S(1)}, bf16[4,96,640]{2,1,0:T(8,128)(2,1)S(1)}, u32[]{:S(2)}, u32[]{:S(2)}) %collective-permute-start.33) | collective-permute-done | bytes 491552 | tf_op jit(solution)/shard_map/ppermute | solution.py:790
  161.1 2.0 %project_place.1 = (f32[192,2304]{1,0:T(8,128)}, f32[16,192]{1,0:T(8,128)S(1)}) custom-call(s32[2]{0:T(128)S(1)} %pad_add_fusion.place.refs_0_, bf16[4,96,640]{2,1,0:T(8,128)(2,1)S(1)} %get-tuple-element.165.refs_1_, bf16[4,96,640]{2,1,0:T(8,128)(2,1)S(1)} %collective-permute-done.33.refs_2_), custom_call_target="tpu_custom_call" | custom-call | flops 2300000000 | bytes 7380000 | tf_op jit(solution)/shard_map/project_place/pallas_call | solution.py:706
  164.4 2.1 %outer_place.1 = f32[768,768]{1,0:T(8,128)} custom-call(s32[2]{0:T(128)S(1)} %pad_add_fusion.1.place.refs_0_, bf16[4,96,768]{2,1,0:T(8,128)(2,1)S(1)} %get-tuple-element.176.refs_1_, bf16[4,96,768]{2,1,0:T(8,128)(2,1)S(1)} %collective-permute-done.38.refs_2_), custom_call_target="tpu_custom_call" | custom-call | flops 2300000000 | bytes 7380000 | tf_op jit(solution)/shard_map/outer_place/pallas_call | solution.py:638
  (131 shorter events, 22.6 us)
Async XLA Ops:
  0.6 12.4 %collective-permute-start.1 = (bf16[2,128,768]{2,1,0:T(8,128)(2,1)}, bf16[2,128,768]{2,1,0:T(8,128)(2,1)S(1)}, u32[]{:S(2)}, u32[]{:S(2)}) collective-permute-start(bf16[2,128,768]{2,1,0:T(8,128)(2,1)} %x0.1), channel_id=1, source_target_pairs={{0,2},{1,3},{2,0},{3,1},{4,6},{5,7},{6,4},{7,5},{8,10},{9,11},{10,... | collective-permute-start | bytes 1179656 | tf_op jit(solution)/shard_map/ppermute | solution.py:790
  3.7 9.7 %collective-permute-start = (bf16[2,128,768]{2,1,0:T(8,128)(2,1)}, bf16[2,128,768]{2,1,0:T(8,128)(2,1)S(1)}, u32[]{:S(2)}, u32[]{:S(2)}) collective-permute-start(bf16[2,128,768]{2,1,0:T(8,128)(2,1)} %x0.1), channel_id=1, source_target_pairs={{0,1},{1,0},{2,3},{3,2},{4,5},{5,4},{6,7},{7,6},{8,9},{9,8},{10,11... | collective-permute-start | bytes 1179656 | tf_op jit(solution)/shard_map/ppermute | solution.py:790
  13.2 11.6 %copy-start.15 = (bf16[768]{0:T(1024)(128)(2,1)S(1)}, bf16[768]{0:T(1024)(128)(2,1)}, u32[]{:S(2)}) copy-start(bf16[768]{0:T(1024)(128)(2,1)} %param.22) | copy-start | bytes 4612
  13.2 11.6 %copy-start.17 = (bf16[768]{0:T(1024)(128)(2,1)S(1)}, bf16[768]{0:T(1024)(128)(2,1)}, u32[]{:S(2)}) copy-start(bf16[768]{0:T(1024)(128)(2,1)} %param.24) | copy-start | bytes 4612
  13.2 11.6 %copy-start.18 = (bf16[768]{0:T(1024)(128)(2,1)S(1)}, bf16[768]{0:T(1024)(128)(2,1)}, u32[]{:S(2)}) copy-start(bf16[768]{0:T(1024)(128)(2,1)} %param.28) | copy-start | bytes 4612
  13.3 11.6 %copy-start.19 = (bf16[768]{0:T(1024)(128)(2,1)S(1)}, bf16[768]{0:T(1024)(128)(2,1)}, u32[]{:S(2)}) copy-start(bf16[768]{0:T(1024)(128)(2,1)} %param.29) | copy-start | bytes 4612
  13.3 11.6 %copy-start.20 = (bf16[768]{0:T(1024)(128)(2,1)S(1)}, bf16[768]{0:T(1024)(128)(2,1)}, u32[]{:S(2)}) copy-start(bf16[768]{0:T(1024)(128)(2,1)} %param.30) | copy-start | bytes 4612
  13.3 11.7 %copy-start.14 = (bf16[3072]{0:T(1024)(128)(2,1)S(1)}, bf16[3072]{0:T(1024)(128)(2,1)}, u32[]{:S(2)}) copy-start(bf16[3072]{0:T(1024)(128)(2,1)} %param.26) | copy-start | bytes 18436
  13.3 17.8 %copy-start.5 = (bf16[768,768]{1,0:T(8,128)(2,1)S(1)}, bf16[768,768]{1,0:T(8,128)(2,1)}, u32[]{:S(2)}) copy-start(bf16[768,768]{1,0:T(8,128)(2,1)} %param.21) | copy-start | bytes 3538948
  13.3 17.8 %copy-start.7 = (bf16[2,128,768]{2,1,0:T(8,128)(2,1)S(1)}, bf16[2,128,768]{2,1,0:T(8,128)(2,1)}, u32[]{:S(2)}) copy-start(bf16[2,128,768]{2,1,0:T(8,128)(2,1)} %param.31) | copy-start | bytes 1179652
  13.3 1.8 %collective-permute-start.2 = (bf16[2,128,768]{2,1,0:T(8,128)(2,1)S(1)}, bf16[2,128,768]{2,1,0:T(8,128)(2,1)S(1)}, u32[]{:S(2)}, u32[]{:S(2)}) collective-permute-start(bf16[2,128,768]{2,1,0:T(8,128)(2,1)S(1)} %pass_on.1.x2), channel_id=1, source_target_pairs={{0,1},{1,0},{2,3},{3,2},{4,5},{5,4},{6,7},{7,6},{8,9},{9,8},{10,11... | collective-permute-start | bytes 1179656 | tf_op jit(solution)/shard_map/ppermute | solution.py:790
  22.8 2.2 %collective-permute-start.3 = (bf16[2,128,192]{2,1,0:T(8,128)(2,1)S(1)}, bf16[2,128,192]{2,1,0:T(8,128)(2,1)S(1)}, u32[]{:S(2)}, u32[]{:S(2)}) collective-permute-start(bf16[2,128,192]{2,1,0:T(8,128)(2,1)S(1)} %get-tuple-element.100), channel_id=1, source_target_pairs={{0,1},{1,0},{2,3},{3,2},{4,5},{5,4},{6,7},{7,6},{8,9},{9,8},{10,11... | collective-permute-start | bytes 294920 | tf_op jit(solution)/shard_map/ppermute | solution.py:790
  23.0 6.3 %collective-permute-start.4 = (bf16[2,128,192]{2,1,0:T(8,128)(2,1)S(1)}, bf16[2,128,192]{2,1,0:T(8,128)(2,1)S(1)}, u32[]{:S(2)}, u32[]{:S(2)}) collective-permute-start(bf16[2,128,192]{2,1,0:T(8,128)(2,1)S(1)} %get-tuple-element.101), channel_id=1, source_target_pairs={{0,2},{1,3},{2,0},{3,1},{4,6},{5,7},{6,4},{7,5},{8,10},{9,11},{10,... | collective-permute-start | bytes 294920 | tf_op jit(solution)/shard_map/ppermute | solution.py:790
  24.8 6.3 %collective-permute-start.5 = (bf16[2,128,192]{2,1,0:T(8,128)(2,1)S(1)}, bf16[2,128,192]{2,1,0:T(8,128)(2,1)S(1)}, u32[]{:S(2)}, u32[]{:S(2)}) collective-permute-start(bf16[2,128,192]{2,1,0:T(8,128)(2,1)S(1)} %get-tuple-element.102), channel_id=1, source_target_pairs={{0,3},{1,2},{2,1},{3,0},{4,7},{5,6},{6,5},{7,4},{8,11},{9,10},{10,... | collective-permute-start | bytes 294920 | tf_op jit(solution)/shard_map/ppermute | solution.py:790
  43.0 3.1 %collective-permute-start.7 = (bf16[256,2304]{1,0:T(8,128)(2,1)}, bf16[256,2304]{1,0:T(8,128)(2,1)S(1)}, u32[]{:S(2)}, u32[]{:S(2)}) collective-permute-start(bf16[256,2304]{1,0:T(8,128)(2,1)} %get-tuple-element.111.grad), channel_id=1, source_target_pairs={{0,1},{1,0},{2,3},{3,2},{4,5},{5,4},{6,7},{7,6},{8,9},{9,8},{10,11... | collective-permute-start | bytes 3538952 | tf_op jit(solution)/shard_map/ppermute | solution.py:790
  43.5 8.3 %collective-permute-start.6 = (bf16[2,256,192]{2,1,0:T(8,128)(2,1)S(1)}, bf16[2,256,192]{2,1,0:T(8,128)(2,1)S(1)}, u32[]{:S(2)}, u32[]{:S(2)}) collective-permute-start(bf16[2,256,192]{2,1,0:T(8,128)(2,1)S(1)} %get-tuple-element.109), channel_id=1, source_target_pairs={{0,2},{1,3},{2,0},{3,1},{4,6},{5,7},{6,4},{7,5},{8,10},{9,11},{10,... | collective-permute-start | bytes 589832 | tf_op jit(solution)/shard_map/ppermute | solution.py:790
  45.3 7.0 %collective-permute-start.9 = (bf16[4,192,256]{2,1,0:T(8,128)(2,1)}, bf16[4,192,256]{2,1,0:T(8,128)(2,1)S(1)}, u32[]{:S(2)}, u32[]{:S(2)}) collective-permute-start(bf16[4,192,256]{2,1,0:T(8,128)(2,1)} %get-tuple-element.117), channel_id=1, source_target_pairs={{0,1},{1,0},{2,3},{3,2},{4,5},{5,4},{6,7},{7,6},{8,9},{9,8},{10,11... | collective-permute-start | bytes 1179656 | tf_op jit(solution)/shard_map/ppermute | solution.py:790
  45.3 7.0 %collective-permute-start.10 = (bf16[256,3840]{1,0:T(8,128)(2,1)}, bf16[256,3840]{1,0:T(8,128)(2,1)S(1)}, u32[]{:S(2)}, u32[]{:S(2)}) collective-permute-start(bf16[256,3840]{1,0:T(8,128)(2,1)} %get-tuple-element.116.second_hbm), channel_id=1, source_target_pairs={{0,1},{1,0},{2,3},{3,2},{4,5},{5,4},{6,7},{7,6},{8,9},{9,8},{10,11... | collective-permute-start | bytes 5898248 | tf_op jit(solution)/shard_map/ppermute | solution.py:790
  49.2 28.3 %collective-permute-start.15 = (bf16[2,4,96,768]{3,2,1,0:T(8,128)(2,1)S(1)}, bf16[2,4,96,768]{3,2,1,0:T(8,128)(2,1)S(1)}, u32[]{:S(2)}, u32[]{:S(2)}) collective-permute-start(bf16[2,4,96,768]{3,2,1,0:T(8,128)(2,1)S(1)} %get-tuple-element.129), channel_id=1, source_target_pairs={{0,4},{4,0},{8,12},{12,8},{16,20},{20,16},{24,28},{28,24},{1,5},{5... | collective-permute-start | bytes 3538952 | tf_op jit(solution)/shard_map/ppermute | solution.py:790
  57.9 22.7 %collective-permute-start.14 = (bf16[1,8,128,384]{3,2,1,0:T(8,128)(2,1)}, bf16[1,8,128,384]{3,2,1,0:T(8,128)(2,1)}, u32[]{:S(2)}, u32[]{:S(2)}) collective-permute-start(bf16[1,8,128,384]{3,2,1,0:T(8,128)(2,1)} %get-tuple-element.127), channel_id=1, source_target_pairs={{0,2},{1,3},{2,0},{3,1},{4,6},{5,7},{6,4},{7,5},{8,10},{9,11},{10,... | collective-permute-start | bytes 2359304 | tf_op jit(solution)/shard_map/ppermute | solution.py:790
  59.7 23.8 %collective-permute-start.13 = (bf16[2,4,112,384]{3,2,1,0:T(8,128)(2,1)}, bf16[2,4,112,384]{3,2,1,0:T(8,128)(2,1)}, u32[]{:S(2)}, u32[]{:S(2)}) collective-permute-start(bf16[2,4,112,384]{3,2,1,0:T(8,128)(2,1)} %get-tuple-element.125), channel_id=1, source_target_pairs={{0,8},{4,12},{8,0},{12,4},{16,24},{20,28},{24,16},{28,20},{1,9},{5... | collective-permute-start | bytes 2064392 | tf_op jit(solution)/shard_map/ppermute | solution.py:790
  61.3 1.5 collective-permute-start.8
  62.9 14.7 %copy-start.9 = (bf16[2,4,96,768]{3,2,1,0:T(8,128)(2,1)S(1)}, bf16[2,4,96,768]{3,2,1,0:T(8,128)(2,1)}, u32[]{:S(2)}) copy-start(bf16[2,4,96,768]{3,2,1,0:T(8,128)(2,1)} %copy-done.8) | copy-start | bytes 3538948
  75.0 14.1 %collective-permute-start.12 = (bf16[1,4,96,640]{3,2,1,0:T(8,128)(2,1)S(1)}, bf16[1,4,96,640]{3,2,1,0:T(8,128)(2,1)S(1)}, u32[]{:S(2)}, u32[]{:S(2)}) collective-permute-start(bf16[1,4,96,640]{3,2,1,0:T(8,128)(2,1)S(1)} %get-tuple-element.123), channel_id=1, source_target_pairs={{0,4},{4,0},{8,12},{12,8},{16,20},{20,16},{24,28},{28,24},{1,5},{5... | collective-permute-start | bytes 1474568 | tf_op jit(solution)/shard_map/ppermute | solution.py:790
  76.5 20.8 %collective-permute-start.11 = (bf16[2,2,128,768]{3,2,1,0:T(8,128)(2,1)}, bf16[2,2,128,768]{3,2,1,0:T(8,128)(2,1)S(1)}, u32[]{:S(2)}, u32[]{:S(2)}) collective-permute-start(bf16[2,2,128,768]{3,2,1,0:T(8,128)(2,1)} %get-tuple-element.121), channel_id=1, source_target_pairs={{0,1},{1,0},{2,3},{3,2},{4,5},{5,4},{6,7},{7,6},{8,9},{9,8},{10,11... | collective-permute-start | bytes 2359304 | tf_op jit(solution)/shard_map/ppermute | solution.py:790
  78.3 16.9 %collective-permute-start.20 = (bf16[1,4,96,768]{3,2,1,0:T(8,128)(2,1)S(1)}, bf16[1,4,96,768]{3,2,1,0:T(8,128)(2,1)S(1)}, u32[]{:S(2)}, u32[]{:S(2)}) collective-permute-start(bf16[1,4,96,768]{3,2,1,0:T(8,128)(2,1)S(1)} %get-tuple-element.139), channel_id=1, source_target_pairs={{0,2},{1,3},{2,0},{3,1},{4,6},{5,7},{6,4},{7,5},{8,10},{9,11},{10,... | collective-permute-start | bytes 1769480 | tf_op jit(solution)/shard_map/ppermute | solution.py:790
  81.9 10.4 %collective-permute-start.17 = (bf16[1,4,128,384]{3,2,1,0:T(8,128)(2,1)S(1)}, bf16[1,4,128,384]{3,2,1,0:T(8,128)(2,1)S(1)}, u32[]{:S(2)}, u32[]{:S(2)}) collective-permute-start(bf16[1,4,128,384]{3,2,1,0:T(8,128)(2,1)S(1)} %get-tuple-element.135), channel_id=1, source_target_pairs={{0,8},{4,12},{8,0},{12,4},{16,24},{20,28},{24,16},{28,20},{1,9},{5... | collective-permute-start | bytes 1179656 | tf_op jit(solution)/shard_map/ppermute | solution.py:790
  84.9 12.5 %collective-permute-start.19 = (bf16[2,2,112,384]{3,2,1,0:T(8,128)(2,1)S(1)}, bf16[2,2,112,384]{3,2,1,0:T(8,128)(2,1)S(1)}, u32[]{:S(2)}, u32[]{:S(2)}) collective-permute-start(bf16[2,2,112,384]{3,2,1,0:T(8,128)(2,1)S(1)} %get-tuple-element.138), channel_id=1, source_target_pairs={{0,4},{4,0},{8,12},{12,8},{16,20},{20,16},{24,28},{28,24},{1,5},{5... | collective-permute-start | bytes 1032200 | tf_op jit(solution)/shard_map/ppermute | solution.py:790
  89.7 14.1 %collective-permute-start.16 = (bf16[1,2,96,640]{3,2,1,0:T(8,128)(2,1)S(1)}, bf16[1,2,96,640]{3,2,1,0:T(8,128)(2,1)S(1)}, u32[]{:S(2)}, u32[]{:S(2)}) collective-permute-start(bf16[1,2,96,640]{3,2,1,0:T(8,128)(2,1)S(1)} %get-tuple-element.134), channel_id=1, source_target_pairs={{0,16},{4,20},{8,24},{12,28},{16,0},{20,4},{24,8},{28,12},{1,17},{... | collective-permute-start | bytes 737288 | tf_op jit(solution)/shard_map/ppermute | solution.py:790
  93.6 6.5 %collective-permute-start.18 = (bf16[1,2,128,384]{3,2,1,0:T(8,128)(2,1)S(1)}, bf16[1,2,128,384]{3,2,1,0:T(8,128)(2,1)S(1)}, u32[]{:S(2)}, u32[]{:S(2)}) collective-permute-start(bf16[1,2,128,384]{3,2,1,0:T(8,128)(2,1)S(1)} %get-tuple-element.137), channel_id=1, source_target_pairs={{0,4},{4,0},{8,12},{12,8},{16,20},{20,16},{24,28},{28,24},{1,5},{5... | collective-permute-start | bytes 589832 | tf_op jit(solution)/shard_map/ppermute | solution.py:790
  95.9 19.3 %collective-permute-start.24 = (bf16[1,2,96,768]{3,2,1,0:T(8,128)(2,1)S(1)}, bf16[1,2,96,768]{3,2,1,0:T(8,128)(2,1)S(1)}, u32[]{:S(2)}, u32[]{:S(2)}) collective-permute-start(bf16[1,2,96,768]{3,2,1,0:T(8,128)(2,1)S(1)} %get-tuple-element.147), channel_id=1, source_target_pairs={{0,8},{4,12},{8,0},{12,4},{16,24},{20,28},{24,16},{28,20},{1,9},{5... | collective-permute-start | bytes 884744 | tf_op jit(solution)/shard_map/ppermute | solution.py:790
  98.5 17.4 %collective-permute-start.23 = (bf16[1,2,112,384]{3,2,1,0:T(8,128)(2,1)S(1)}, bf16[1,2,112,384]{3,2,1,0:T(8,128)(2,1)S(1)}, u32[]{:S(2)}, u32[]{:S(2)}) collective-permute-start(bf16[1,2,112,384]{3,2,1,0:T(8,128)(2,1)S(1)} %get-tuple-element.146), channel_id=1, source_target_pairs={{0,2},{1,3},{2,0},{3,1},{4,6},{5,7},{6,4},{7,5},{8,10},{9,11},{10,... | collective-permute-start | bytes 516104 | tf_op jit(solution)/shard_map/ppermute | solution.py:790
  101.4 18.7 %collective-permute-start.22 = (bf16[1,2,128,384]{3,2,1,0:T(8,128)(2,1)S(1)}, bf16[1,2,128,384]{3,2,1,0:T(8,128)(2,1)S(1)}, u32[]{:S(2)}, u32[]{:S(2)}) collective-permute-start(bf16[1,2,128,384]{3,2,1,0:T(8,128)(2,1)S(1)} %get-tuple-element.145.refs_1_), channel_id=1, source_target_pairs={{0,16},{4,20},{8,24},{12,28},{16,0},{20,4},{24,8},{28,12},{1,17},{... | collective-permute-start | bytes 589832 | tf_op jit(solution)/shard_map/ppermute | solution.py:790
  104.5 17.4 %collective-permute-start.21 = (bf16[1,2,96,640]{3,2,1,0:T(8,128)(2,1)S(1)}, bf16[1,2,96,640]{3,2,1,0:T(8,128)(2,1)S(1)}, u32[]{:S(2)}, u32[]{:S(2)}) collective-permute-start(bf16[1,2,96,640]{3,2,1,0:T(8,128)(2,1)S(1)} %get-tuple-element.144.refs_1_), channel_id=1, source_target_pairs={{0,8},{4,12},{8,0},{12,4},{16,24},{20,28},{24,16},{28,20},{1,9},{5... | collective-permute-start | bytes 737288 | tf_op jit(solution)/shard_map/ppermute | solution.py:790
  117.1 11.5 %collective-permute-start.31 = (bf16[1,2,112,384]{3,2,1,0:T(8,128)(2,1)S(1)}, bf16[1,2,112,384]{3,2,1,0:T(8,128)(2,1)S(1)}, u32[]{:S(2)}, u32[]{:S(2)}) collective-permute-start(bf16[1,2,112,384]{3,2,1,0:T(8,128)(2,1)S(1)} %get-tuple-element.159.refs_1_), channel_id=1, source_target_pairs={{0,16},{4,20},{8,24},{12,28},{16,0},{20,4},{24,8},{28,12},{1,17},{... | collective-permute-start | bytes 516104 | tf_op jit(solution)/shard_map/ppermute | solution.py:790
  117.2 14.5 %collective-permute-start.30 = (bf16[1,2,96,768]{3,2,1,0:T(8,128)(2,1)S(1)}, bf16[1,2,96,768]{3,2,1,0:T(8,128)(2,1)S(1)}, u32[]{:S(2)}, u32[]{:S(2)}) collective-permute-start(bf16[1,2,96,768]{3,2,1,0:T(8,128)(2,1)S(1)} %get-tuple-element.158.refs_1_), channel_id=1, source_target_pairs={{0,16},{4,20},{8,24},{12,28},{16,0},{20,4},{24,8},{28,12},{1,17},{... | collective-permute-start | bytes 884744 | tf_op jit(solution)/shard_map/ppermute | solution.py:790
  120.7 7.4 %collective-permute-start.32 = (bf16[2,128,384]{2,1,0:T(8,128)(2,1)S(1)}, bf16[2,128,384]{2,1,0:T(8,128)(2,1)S(1)}, u32[]{:S(2)}, u32[]{:S(2)}) collective-permute-start(bf16[2,128,384]{2,1,0:T(8,128)(2,1)S(1)} %bitcast.50), channel_id=1, source_target_pairs={{0,8},{4,12},{8,0},{12,4},{16,24},{20,28},{24,16},{28,20},{1,9},{5... | collective-permute-start | bytes 589832 | tf_op jit(solution)/shard_map/ppermute | solution.py:790
  122.4 1.3 collective-permute-start.26
  122.5 4.7 %collective-permute-start.27 = (bf16[2,24,640]{2,1,0:T(8,128)(2,1)S(1)}, bf16[2,24,640]{2,1,0:T(8,128)(2,1)S(1)}, u32[]{:S(2)}, u32[]{:S(2)}) collective-permute-start(bf16[2,24,640]{2,1,0:T(8,128)(2,1)S(1)} %get-tuple-element.156), channel_id=1, source_target_pairs={{0,2},{1,3},{2,0},{3,1},{4,6},{5,7},{6,4},{7,5},{8,10},{9,11},{10,... | collective-permute-start | bytes 184328 | tf_op jit(solution)/shard_map/ppermute | solution.py:790
  123.7 4.2 %collective-permute-start.28 = (bf16[2,24,640]{2,1,0:T(8,128)(2,1)S(1)}, bf16[2,24,640]{2,1,0:T(8,128)(2,1)S(1)}, u32[]{:S(2)}, u32[]{:S(2)}) collective-permute-start(bf16[2,24,640]{2,1,0:T(8,128)(2,1)S(1)} %get-tuple-element.157), channel_id=1, source_target_pairs={{0,3},{1,2},{2,1},{3,0},{4,7},{5,6},{6,5},{7,4},{8,11},{9,10},{10,... | collective-permute-start | bytes 184328 | tf_op jit(solution)/shard_map/ppermute | solution.py:790
  127.2 14.9 %collective-permute-start.25 = (bf16[1,1,256,768]{3,2,1,0:T(8,128)(2,1)S(1)}, bf16[1,1,256,768]{3,2,1,0:T(8,128)(2,1)S(1)}, u32[]{:S(2)}, u32[]{:S(2)}) collective-permute-start(bf16[1,1,256,768]{3,2,1,0:T(8,128)(2,1)S(1)} %get-tuple-element.153), channel_id=1, source_target_pairs={{0,2},{1,3},{2,0},{3,1},{4,6},{5,7},{6,4},{7,5},{8,10},{9,11},{10,... | collective-permute-start | bytes 1179656 | tf_op jit(solution)/shard_map/ppermute | solution.py:790
  128.0 8.9 %collective-permute-start.29 = (bf16[2,96,640]{2,1,0:T(8,128)(2,1)S(1)}, bf16[2,96,640]{2,1,0:T(8,128)(2,1)S(1)}, u32[]{:S(2)}, u32[]{:S(2)}) collective-permute-start(bf16[2,96,640]{2,1,0:T(8,128)(2,1)S(1)} %constant_dynamic-update-slice_fusion.refs_0_), channel_id=1, source_target_pairs={{0,4},{4,0},{8,12},{12,8},{16,20},{20,16},{24,28},{28,24},{1,5},{5... | collective-permute-start | bytes 737288 | tf_op jit(solution)/shard_map/ppermute | solution.py:790
  129.2 11.3 %collective-permute-start.35 = (bf16[2,112,384]{2,1,0:T(8,128)(2,1)S(1)}, bf16[2,112,384]{2,1,0:T(8,128)(2,1)S(1)}, u32[]{:S(2)}, u32[]{:S(2)}) collective-permute-start(bf16[2,112,384]{2,1,0:T(8,128)(2,1)S(1)} %bitcast.52), channel_id=1, source_target_pairs={{0,4},{4,0},{8,12},{12,8},{16,20},{20,16},{24,28},{28,24},{1,5},{5... | collective-permute-start | bytes 516104 | tf_op jit(solution)/shard_map/ppermute | solution.py:790
  132.3 10.7 %collective-permute-start.37 = (bf16[2,96,768]{2,1,0:T(8,128)(2,1)S(1)}, bf16[2,96,768]{2,1,0:T(8,128)(2,1)S(1)}, u32[]{:S(2)}, u32[]{:S(2)}) collective-permute-start(bf16[2,96,768]{2,1,0:T(8,128)(2,1)S(1)} %bitcast.48), channel_id=1, source_target_pairs={{0,8},{4,12},{8,0},{12,4},{16,24},{20,28},{24,16},{28,20},{1,9},{5... | collective-permute-start | bytes 884744 | tf_op jit(solution)/shard_map/ppermute | solution.py:790
  133.3 15.7 %collective-permute-start.34 = (bf16[4,128,384]{2,1,0:T(8,128)(2,1)S(1)}, bf16[4,128,384]{2,1,0:T(8,128)(2,1)S(1)}, u32[]{:S(2)}, u32[]{:S(2)}) collective-permute-start(bf16[4,128,384]{2,1,0:T(8,128)(2,1)S(1)} %get-tuple-element.168.refs_2_), channel_id=1, source_target_pairs={{0,4},{4,0},{8,12},{12,8},{16,20},{20,16},{24,28},{28,24},{1,5},{5... | collective-permute-start | bytes 1179656 | tf_op jit(solution)/shard_map/ppermute | solution.py:790
  137.5 23.6 %collective-permute-start.33 = (bf16[4,96,640]{2,1,0:T(8,128)(2,1)S(1)}, bf16[4,96,640]{2,1,0:T(8,128)(2,1)S(1)}, u32[]{:S(2)}, u32[]{:S(2)}) collective-permute-start(bf16[4,96,640]{2,1,0:T(8,128)(2,1)S(1)} %get-tuple-element.165.refs_1_), channel_id=1, source_target_pairs={{0,16},{4,20},{8,24},{12,28},{16,0},{20,4},{24,8},{28,12},{1,17},{... | collective-permute-start | bytes 1474568 | tf_op jit(solution)/shard_map/ppermute | solution.py:790
  141.0 15.9 %collective-permute-start.36 = (bf16[4,112,384]{2,1,0:T(8,128)(2,1)S(1)}, bf16[4,112,384]{2,1,0:T(8,128)(2,1)S(1)}, u32[]{:S(2)}, u32[]{:S(2)}) collective-permute-start(bf16[4,112,384]{2,1,0:T(8,128)(2,1)S(1)} %get-tuple-element.171.refs_4_), channel_id=1, source_target_pairs={{0,8},{4,12},{8,0},{12,4},{16,24},{20,28},{24,16},{28,20},{1,9},{5... | collective-permute-start | bytes 1032200 | tf_op jit(solution)/shard_map/ppermute | solution.py:790
  143.2 21.2 %collective-permute-start.38 = (bf16[4,96,768]{2,1,0:T(8,128)(2,1)S(1)}, bf16[4,96,768]{2,1,0:T(8,128)(2,1)S(1)}, u32[]{:S(2)}, u32[]{:S(2)}) collective-permute-start(bf16[4,96,768]{2,1,0:T(8,128)(2,1)S(1)} %get-tuple-element.176.refs_1_), channel_id=1, source_target_pairs={{0,4},{4,0},{8,12},{12,8},{16,20},{20,16},{24,28},{28,24},{1,5},{5... | collective-permute-start | bytes 1769480 | tf_op jit(solution)/shard_map/ppermute | solution.py:790
  (14 other events, 71.4 us)

commit v8 on v7

--- a/solution.py
+++ b/solution.py
@@ -625,25 +625,30 @@
     )(place, *inputs, *map(far, after))
 
 
-def outer_place_kernel(spots, place, own, got, *refs):
-    out = refs[-1]
+def outer_place_kernel(spots, place, own, got, out, here, sem):
     n = own.shape[1]
+    copies = []
     for i, spot in enumerate(spots):
-        piece = own[i] if i < 4 else got[i - 4]
-        out[pl.ds(pl.multiple_of((place[0] ^ spot) * n, 8), n), :] = piece.astype(F32)
-
-
-def outer_place(spots, place, own, got, after=()):
+        here[i] = (own[i] if i < 4 else got[i - 4]).astype(F32)
+        rows = pl.ds(pl.multiple_of((place[0] ^ spot) * n, 8), n)
+        copies.append(pltpu.make_async_copy(here.at[i], out.at[rows], sem.at[i]))
+        copies[i].start()
+    for copy in copies:
+        copy.wait()
+
+
+def outer_place(spots, place, own, got):
     n, width = own.shape[1:]
     return pl.pallas_call(
         lambda *refs: outer_place_kernel(spots, *refs),
-        in_specs=[SMEM, vmem(), vmem()] + [HBM] * len(after),
-        out_specs=vmem(),
-        out_shape=jax.ShapeDtypeStruct((PIECES * n, width), F32),
-        compiler_params=pltpu.CompilerParams(vmem_limit_bytes=4 * MIB),
+        in_specs=[SMEM, vmem(), vmem()],
+        out_specs=HBM,
+        out_shape=pltpu.HBM((PIECES * n, width), F32),
+        scratch_shapes=[pltpu.VMEM((PIECES, n, width), F32), pltpu.SemaphoreType.DMA((PIECES,))],
+        compiler_params=pltpu.CompilerParams(vmem_limit_bytes=6 * MIB),
         cost_estimate=cost(2),
         name="outer_place",
-    )(place, own, got, *map(far, after))
+    )(place, own, got)
 
 
 def inner_place_kernel(spots_one, spots_two, one, two, own, got, own_two, got_two, *refs):
@@ -679,11 +684,11 @@
     )(one, two, *parts_one, *parts_two, *map(far, after))
 
 
-def project_place_kernel(spots, place, own, got, *refs):
-    out, vectors, tall = refs[-3:]
+def project_place_kernel(spots, place, own, got, out, vectors, here, tall, sem):
     n = own.shape[1] // 4
     hw = out.shape[1] // 12
     wide = 3 * hw
+    copies = []
     for i, spot in enumerate(spots):
         ref, k = (own, i) if i < 4 else (got, i - 4)
         rows = pl.ds(pl.multiple_of((place[0] ^ spot) * n, 8), n)
@@ -693,29 +698,34 @@
             block = ref[k, pl.ds(start, n), :].astype(F32)
             for t in range(3):
                 at = t * 4 * hw + owner * hw
-                out[rows, at : at + hw] = block[:, t * hw : (t + 1) * hw]
+                here[i, :, at : at + hw] = block[:, t * hw : (t + 1) * hw]
             extra = block[:, wide:]
             total = extra if total is None else total + extra
+        copies.append(pltpu.make_async_copy(here.at[i], out.at[rows], sem.at[i]))
+        copies[i].start()
         tall[rows, : total.shape[1]] = total
     vectors[...] = tall[...].T[: vectors.shape[0]]
-
-
-def project_place(spots, place, own, got, hw, after=()):
+    for copy in copies:
+        copy.wait()
+
+
+def project_place(spots, place, own, got, hw):
     _, tall, wide = own.shape
     n = tall // 4
     return pl.pallas_call(
         lambda *refs: project_place_kernel(spots, *refs),
-        in_specs=[SMEM, vmem(), vmem()] + [HBM] * len(after),
-        out_specs=[vmem(), vmem()],
-        out_shape=[
-            jax.ShapeDtypeStruct((PIECES * n, 12 * hw), F32),
-            jax.ShapeDtypeStruct((16, PIECES * n), F32),
+        in_specs=[SMEM, vmem(), vmem()],
+        out_specs=[HBM, vmem()],
+        out_shape=[pltpu.HBM((PIECES * n, 12 * hw), F32), jax.ShapeDtypeStruct((16, PIECES * n), F32)],
+        scratch_shapes=[
+            pltpu.VMEM((PIECES, n, 12 * hw), F32),
+            pltpu.VMEM((PIECES * n, 128), F32),
+            pltpu.SemaphoreType.DMA((PIECES,)),
         ],
-        scratch_shapes=[pltpu.VMEM((PIECES * n, 128), F32)],
-        compiler_params=pltpu.CompilerParams(vmem_limit_bytes=4 * MIB),
+        compiler_params=pltpu.CompilerParams(vmem_limit_bytes=6 * MIB),
         cost_estimate=cost(2),
         name="project_place",
-    )(place, own, got, *map(far, after))
+    )(place, own, got)
 
 
 def join_kernel(*refs):

time: 167 us -> 167 us (level)
  no operation moved by 1% of the time
where the time goes in v8:
time: 167 us; the launch traced here: 166 us
  Pallas kernels  65.5 us (39%)
  waiting for transfers between devices  52.5 us (31%)
  starting transfers between devices  42.9 us (26%)
  local copies, waits for them, and re-layouts  2.93 us (2%)
    ppermute x39, waiting for transfers between devices, swap(): return lax.ppermute(field, axis, [(i, i ^ bit) for i in range(count)])  52.5 us
    ppermute x39, starting transfers between devices, swap(): return lax.ppermute(field, axis, [(i, i ^ bit) for i in range(count)])  42.9 us
    pallas_call x16, Pallas kernels, sum_pieces(): pl.pallas_call(lambda *refs: sum_kernel(spec, *refs), in_specs=[SMEM] + [...  13.8 us
    pallas_call x1, Pallas kernels, attend_back(): pl.pallas_call(attend_back_kernel, in_specs=[SMEM] + [HBM] * 5 + [vmem()]...  12.1 us
    pallas_call x1, Pallas kernels, rows_pass(): pl.pallas_call(rows_kernel, in_specs=[SMEM, vmem()] + [HBM] * 3 + [vmem()...  11.9 us
    pallas_call x1, Pallas kernels, attend(): pl.pallas_call(attend_kernel, in_specs=[SMEM, SMEM, vmem(), HBM, vmem(),...  7.71 us
    pallas_call x1, Pallas kernels, inner_grad(): pl.pallas_call(inner_grad_kernel, in_specs=[SMEM, SMEM, HBM, HBM, vmem(),...  5.69 us
  transfers between devices with their start and end apart: 39, of which 20 were waited for; matrix products, arithmetic and copies ran while one was open for 2% of the time, Pallas kernels for 26%

profile of v8, /device:TPU:0, one launch (start us, length us, event | category | flops | bytes accessed | tf_op | source)
XLA Modules:
  0.0 166.5 jit_solution(3039076126178614126)
XLA Ops:
  0.6 3.0 %collective-permute-start.1 = (bf16[2,128,768]{2,1,0:T(8,128)(2,1)}, bf16[2,128,768]{2,1,0:T(8,128)(2,1)S(1)}, u32[]{:S(2)}, u32[]{:S(2)}) collective-permute-start(bf16[2,128,768]{2,1,0:T(8,128)(2,1)} %x0.1), channel_id=1, source_target_pairs={{0,2},{1,3},{2,0},{3,1},{4,6},{5,7},{6,4},{7,5},{8,10},{9,11},{10,... | collective-permute-start | bytes 1179656 | tf_op jit(solution)/shard_map/ppermute | solution.py:800
  5.1 2.7 %choose_heads.1 = (bf16[768,576]{1,0:T(8,128)(2,1)}, f32[2,192]{1,0:T(2,128)S(1)}, f32[8,128]{1,0:T(8,128)}) custom-call(s32[1]{0:T(128)} %bitcast.where, bf16[768,2304]{1,0:T(8,128)(2,1)} %w_hbm.1, bf16[1,768]{1,0:T(2,128)(2,1)S(1)} %reshape.97.qb, bf16[1,768]{1,0:T(2,128)(2,1)S(1)} %reshape.98.vb), custom_call_target="tpu_custom_call" | custom-call | flops 1724999936 | bytes 5535000 | tf_op jit(solution)/shard_map/choose_heads/pallas_call | solution.py:88
  7.8 5.2 %collective-permute-done.1.source = bf16[2,128,768]{2,1,0:T(8,128)(2,1)S(1)} collective-permute-done((bf16[2,128,768]{2,1,0:T(8,128)(2,1)}, bf16[2,128,768]{2,1,0:T(8,128)(2,1)S(1)}, u32[]{:S(2)}, u32[]{:S(2)}) %collective-permute-start.1) | collective-permute-done | bytes 393248 | tf_op jit(solution)/shard_map/ppermute | solution.py:800
  13.4 1.7 %collective-permute-done.2.x3 = bf16[2,128,768]{2,1,0:T(8,128)(2,1)S(1)} collective-permute-done((bf16[2,128,768]{2,1,0:T(8,128)(2,1)S(1)}, bf16[2,128,768]{2,1,0:T(8,128)(2,1)S(1)}, u32[]{:S(2)}, u32[]{:S(2)}) %collective-permute-start.2) | collective-permute-done | bytes 393248 | tf_op jit(solution)/shard_map/ppermute | solution.py:800
  15.1 7.7 %attend.1 = (bf16[2,512,576]{2,1,0:T(8,128)(2,1)}, bf16[2,3,512,512]{3,2,1,0:T(8,128)(2,1)}, bf16[2,128,192]{2,1,0:T(8,128)(2,1)}, bf16[2,512,768]{2,1,0:T(8,128...) custom-call(s32[1]{0:T(128)} %bitcast.where, ...), custom_call_target="tpu_custom_call" | custom-call | flops 115000000 | bytes 369000 | tf_op jit(solution)/shard_map/attend/pallas_call | solution.py:168
  23.0 1.8 %collective-permute-start.4 = (bf16[2,128,192]{2,1,0:T(8,128)(2,1)S(1)}, bf16[2,128,192]{2,1,0:T(8,128)(2,1)S(1)}, u32[]{:S(2)}, u32[]{:S(2)}) collective-permute-start(bf16[2,128,192]{2,1,0:T(8,128)(2,1)S(1)} %get-tuple-element.101), channel_id=1, source_target_pairs={{0,2},{1,3},{2,0},{3,1},{4,6},{5,7},{6,4},{7,5},{8,10},{9,11},{10,... | collective-permute-start | bytes 294920 | tf_op jit(solution)/shard_map/ppermute | solution.py:800
  25.0 4.3 %collective-permute-done.4 = bf16[2,128,192]{2,1,0:T(8,128)(2,1)S(1)} collective-permute-done((bf16[2,128,192]{2,1,0:T(8,128)(2,1)S(1)}, bf16[2,128,192]{2,1,0:T(8,128)(2,1)S(1)}, u32[]{:S(2)}, u32[]{:S(2)}) %collective-permute-start.4) | collective-permute-done | bytes 98336 | tf_op jit(solution)/shard_map/ppermute | solution.py:800
  29.4 1.7 %collective-permute-done.5 = bf16[2,128,192]{2,1,0:T(8,128)(2,1)S(1)} collective-permute-done((bf16[2,128,192]{2,1,0:T(8,128)(2,1)S(1)}, bf16[2,128,192]{2,1,0:T(8,128)(2,1)S(1)}, u32[]{:S(2)}, u32[]{:S(2)}) %collective-permute-start.5) | collective-permute-done | bytes 98336 | tf_op jit(solution)/shard_map/ppermute | solution.py:800
  31.1 11.9 %rows_pass.1 = (bf16[256,768]{1,0:T(8,128)(2,1)}, f32[256,768]{1,0:T(8,128)}, bf16[256,1536]{1,0:T(8,128)(2,1)}, bf16[256,2304]{1,0:T(8,128)(2,1)}, bf16[256,384...) custom-call(s32[1]{0:T(128)} %bitcast.where, ...), custom_call_target="tpu_custom_call" | custom-call | flops 12650000384 | bytes 40590000 | tf_op jit(solution)/shard_map/rows_pass/pallas_call | solution.py:430
  43.5 1.7 %collective-permute-start.6 = (bf16[2,256,192]{2,1,0:T(8,128)(2,1)S(1)}, bf16[2,256,192]{2,1,0:T(8,128)(2,1)S(1)}, u32[]{:S(2)}, u32[]{:S(2)}) collective-permute-start(bf16[2,256,192]{2,1,0:T(8,128)(2,1)S(1)} %get-tuple-element.109), channel_id=1, source_target_pairs={{0,2},{1,3},{2,0},{3,1},{4,6},{5,7},{6,4},{7,5},{8,10},{9,11},{10,... | collective-permute-start | bytes 589832 | tf_op jit(solution)/shard_map/ppermute | solution.py:800
  46.1 3.1 %outer_grad.1 = (bf16[2,4,96,768]{3,2,1,0:T(8,128)(2,1)S(1)}, bf16[2,4,96,768]{3,2,1,0:T(8,128)(2,1)S(1)}, f32[8,128]{1,0:T(8,128)}) custom-call(s32[2]{0:T(128)S(1)} %pad_add_fusion.1.place.refs_0_, bf16[256,1536]{1,0:T(8,128)(2,1)} %get-tuple-element.110.active, bf16[256,2304]{1,0:T(8,128)(2,1)S(1)} %collective-permute-done.7.active_got.grad_got, ...), custom_call_target="tpu_custom_call" | custom-call | flops 34500001792 | bytes 110700000 | tf_op jit(solution)/shard_map/outer_grad/pallas_call | solution.py:472
  49.2 1.8 %collective-permute-start.15 = (bf16[2,4,96,768]{3,2,1,0:T(8,128)(2,1)S(1)}, bf16[2,4,96,768]{3,2,1,0:T(8,128)(2,1)S(1)}, u32[]{:S(2)}, u32[]{:S(2)}) collective-permute-start(bf16[2,4,96,768]{3,2,1,0:T(8,128)(2,1)S(1)} %get-tuple-element.129), channel_id=1, source_target_pairs={{0,4},{4,0},{8,12},{12,8},{16,20},{20,16},{24,28},{28,24},{1,5},{5... | collective-permute-start | bytes 3538952 | tf_op jit(solution)/shard_map/ppermute | solution.py:800
  52.2 5.7 %inner_grad.1 = (bf16[1,8,128,384]{3,2,1,0:T(8,128)(2,1)}, bf16[1,8,128,384]{3,2,1,0:T(8,128)(2,1)}, bf16[2,4,112,384]{3,2,1,0:T(8,128)(2,1)}, bf16[2,4,112,384]{3,2,1,0:T(8,128)(2,1)}, f32[8,128]{1,0:T(8,128)}) custom-call(s32[2]{0:T(128)S(1)} %pad_add_fusion.2.bit_b.bit_c.refs_0_.refs_1_, s32[2]{0:T(128)S(1)} %pad_add_fusion.2.bit_b.bit_c.refs_0_.refs_1_, ...), custom_call_target="tpu_custom_call" | custom-call | flops 4600000000 | bytes 14760000 | tf_op jit(solution)/shard_map/inner_grad/pallas_call | solution.py:565
  57.9 1.8 %collective-permute-start.14 = (bf16[1,8,128,384]{3,2,1,0:T(8,128)(2,1)}, bf16[1,8,128,384]{3,2,1,0:T(8,128)(2,1)}, u32[]{:S(2)}, u32[]{:S(2)}) collective-permute-start(bf16[1,8,128,384]{3,2,1,0:T(8,128)(2,1)} %get-tuple-element.127), channel_id=1, source_target_pairs={{0,2},{1,3},{2,0},{3,1},{4,6},{5,7},{6,4},{7,5},{8,10},{9,11},{10,... | collective-permute-start | bytes 2359304 | tf_op jit(solution)/shard_map/ppermute | solution.py:800
  59.7 1.6 collective-permute-start.13
  61.4 1.5 collective-permute-done.8
  62.9 12.1 %attend_back.1 = (bf16[2,2,128,768]{3,2,1,0:T(8,128)(2,1)}, bf16[2,2,128,768]{3,2,1,0:T(8,128)(2,1)}, bf16[1,4,96,640]{3,2,1,0:T(8,128)(2,1)S(1)}, bf16[1,4,96,640]{3,2,1,0:T(8,128)(2,1)}, f32[8,128]{1,0:T(8,128)}) custom-call(s32[2]{0:T(128)S(1)} %pad_add_fusion.place.refs_0_, bf16[2,512,768]{2,1,0:T(8,128)(2,1)} %get-tuple-element.105.refs_0_, ...), custom_call_target="tpu_custom_call" | custom-call | flops 1150000000 | bytes 3690000 | tf_op jit(solution)/shard_map/attend_back/pallas_call | solution.py:284
  75.0 1.6 collective-permute-start.12
  78.3 2.4 %collective-permute-start.20 = (bf16[1,4,96,768]{3,2,1,0:T(8,128)(2,1)S(1)}, bf16[1,4,96,768]{3,2,1,0:T(8,128)(2,1)S(1)}, u32[]{:S(2)}, u32[]{:S(2)}) collective-permute-start(bf16[1,4,96,768]{3,2,1,0:T(8,128)(2,1)S(1)} %get-tuple-element.139), channel_id=1, source_target_pairs={{0,2},{1,3},{2,0},{3,1},{4,6},{5,7},{6,4},{7,5},{8,10},{9,11},{10,... | collective-permute-start | bytes 1769480 | tf_op jit(solution)/shard_map/ppermute | solution.py:800
  80.6 1.3 sum_b.3
  81.9 1.6 collective-permute-start.17
  83.6 1.3 sum_c.3
  84.9 1.5 collective-permute-start.19
  86.4 2.7 %collective-permute-done.12.refs_2_ = bf16[1,4,96,640]{3,2,1,0:T(8,128)(2,1)S(1)} collective-permute-done((bf16[1,4,96,640]{3,2,1,0:T(8,128)(2,1)S(1)}, bf16[1,4,96,640]{3,2,1,0:T(8,128)(2,1)S(1)}, u32[]{:S(2)}, u32[]{:S(2)}) %collective-permute-start.12) | collective-permute-done | bytes 491552 | tf_op jit(solution)/shard_map/ppermute | solution.py:800
  89.7 2.6 %collective-permute-start.16 = (bf16[1,2,96,640]{3,2,1,0:T(8,128)(2,1)S(1)}, bf16[1,2,96,640]{3,2,1,0:T(8,128)(2,1)S(1)}, u32[]{:S(2)}, u32[]{:S(2)}) collective-permute-start(bf16[1,2,96,640]{3,2,1,0:T(8,128)(2,1)S(1)} %get-tuple-element.134), channel_id=1, source_target_pairs={{0,16},{4,20},{8,24},{12,28},{16,0},{20,4},{24,8},{28,12},{1,17},{... | collective-permute-start | bytes 737288 | tf_op jit(solution)/shard_map/ppermute | solution.py:800
  92.4 1.2 sum_b.4
  93.6 1.6 collective-permute-start.18
  95.9 1.4 collective-permute-start.24
  98.5 1.6 collective-permute-start.23
  100.1 1.3 sum_b.5
  101.4 2.4 %collective-permute-start.22 = (bf16[1,2,128,384]{3,2,1,0:T(8,128)(2,1)S(1)}, bf16[1,2,128,384]{3,2,1,0:T(8,128)(2,1)S(1)}, u32[]{:S(2)}, u32[]{:S(2)}) collective-permute-start(bf16[1,2,128,384]{3,2,1,0:T(8,128)(2,1)S(1)} %get-tuple-element.145.refs_1_), channel_id=1, source_target_pairs={{0,16},{4,20},{8,24},{12,28},{16,0},{20,4},{24,8},{28,12},{1,17},{... | collective-permute-start | bytes 589832 | tf_op jit(solution)/shard_map/ppermute | solution.py:800
  104.5 1.6 collective-permute-start.21
  106.1 9.1 %collective-permute-done.24.refs_4_ = bf16[1,2,96,768]{3,2,1,0:T(8,128)(2,1)S(1)} collective-permute-done((bf16[1,2,96,768]{3,2,1,0:T(8,128)(2,1)S(1)}, bf16[1,2,96,768]{3,2,1,0:T(8,128)(2,1)S(1)}, u32[]{:S(2)}, u32[]{:S(2)}) %collective-permute-start.24) | collective-permute-done | bytes 294944 | tf_op jit(solution)/shard_map/ppermute | solution.py:800
  115.9 1.2 sum_c.5
  117.2 2.9 %collective-permute-start.30 = (bf16[1,2,96,768]{3,2,1,0:T(8,128)(2,1)S(1)}, bf16[1,2,96,768]{3,2,1,0:T(8,128)(2,1)S(1)}, u32[]{:S(2)}, u32[]{:S(2)}) collective-permute-start(bf16[1,2,96,768]{3,2,1,0:T(8,128)(2,1)S(1)} %get-tuple-element.158.refs_1_), channel_id=1, source_target_pairs={{0,16},{4,20},{8,24},{12,28},{16,0},{20,4},{24,8},{28,12},{1,17},{... | collective-permute-start | bytes 884744 | tf_op jit(solution)/shard_map/ppermute | solution.py:800
  123.7 1.3 collective-permute-start.28
  125.1 2.1 %collective-permute-done.27 = bf16[2,24,640]{2,1,0:T(8,128)(2,1)S(1)} collective-permute-done((bf16[2,24,640]{2,1,0:T(8,128)(2,1)S(1)}, bf16[2,24,640]{2,1,0:T(8,128)(2,1)S(1)}, u32[]{:S(2)}, u32[]{:S(2)}) %collective-permute-start.27) | collective-permute-done | bytes 61472 | tf_op jit(solution)/shard_map/ppermute | solution.py:800
  129.2 2.1 %collective-permute-start.35 = (bf16[2,112,384]{2,1,0:T(8,128)(2,1)S(1)}, bf16[2,112,384]{2,1,0:T(8,128)(2,1)S(1)}, u32[]{:S(2)}, u32[]{:S(2)}) collective-permute-start(bf16[2,112,384]{2,1,0:T(8,128)(2,1)S(1)} %bitcast.52), channel_id=1, source_target_pairs={{0,4},{4,0},{8,12},{12,8},{16,20},{20,16},{24,28},{28,24},{1,5},{5... | collective-permute-start | bytes 516104 | tf_op jit(solution)/shard_map/ppermute | solution.py:800
  133.3 1.5 collective-permute-start.34
  134.7 2.1 %collective-permute-done.29.refs_1_ = bf16[2,96,640]{2,1,0:T(8,128)(2,1)S(1)} collective-permute-done((bf16[2,96,640]{2,1,0:T(8,128)(2,1)S(1)}, bf16[2,96,640]{2,1,0:T(8,128)(2,1)S(1)}, u32[]{:S(2)}, u32[]{:S(2)}) %collective-permute-start.29) | collective-permute-done | bytes 245792 | tf_op jit(solution)/shard_map/ppermute | solution.py:800
  137.5 1.4 collective-permute-start.33
  138.8 1.7 %collective-permute-done.35.refs_1_ = bf16[2,112,384]{2,1,0:T(8,128)(2,1)S(1)} collective-permute-done((bf16[2,112,384]{2,1,0:T(8,128)(2,1)S(1)}, bf16[2,112,384]{2,1,0:T(8,128)(2,1)S(1)}, u32[]{:S(2)}, u32[]{:S(2)}) %collective-permute-start.35) | collective-permute-done | bytes 172064 | tf_op jit(solution)/shard_map/ppermute | solution.py:800
  143.3 5.7 %collective-permute-done.34.refs_3_ = bf16[4,128,384]{2,1,0:T(8,128)(2,1)S(1)} collective-permute-done((bf16[4,128,384]{2,1,0:T(8,128)(2,1)S(1)}, bf16[4,128,384]{2,1,0:T(8,128)(2,1)S(1)}, u32[]{:S(2)}, u32[]{:S(2)}) %collective-permute-start.34) | collective-permute-done | bytes 393248 | tf_op jit(solution)/shard_map/ppermute | solution.py:800
  149.0 8.0 %collective-permute-done.36.refs_5_ = bf16[4,112,384]{2,1,0:T(8,128)(2,1)S(1)} collective-permute-done((bf16[4,112,384]{2,1,0:T(8,128)(2,1)S(1)}, bf16[4,112,384]{2,1,0:T(8,128)(2,1)S(1)}, u32[]{:S(2)}, u32[]{:S(2)}) %collective-permute-start.36) | collective-permute-done | bytes 344096 | tf_op jit(solution)/shard_map/ppermute | solution.py:800
  156.9 2.3 %inner_place.1 = (f32[192,3072]{1,0:T(8,128)}, f32[192,768]{1,0:T(8,128)}) custom-call(s32[2]{0:T(128)S(1)} %pad_add_fusion.2.bit_b.bit_c.refs_0_.refs_1_, s32[2]{0:T(128)S(1)} %pad_add_fusion.2.bit_b.bit_c.refs_0_.refs_1_, bf16[4,128,384]{2,1,0:T(8,128)(2,1)S(1)} %get-tuple-element.168.refs_2_, bf16[4,128,384]{2,1,0:T(8,128)(2,1)S(1)} %collective-permute-done.34.refs_3_, ...), custom_call_target="tpu_custom_call" | custom-call | flops 2300000000 | bytes 7380000 | tf_op jit(solution)/shard_map/inner_place/pallas_call | solution.py:673
  159.2 1.9 %collective-permute-done.33.refs_2_ = bf16[4,96,640]{2,1,0:T(8,128)(2,1)S(1)} collective-permute-done((bf16[4,96,640]{2,1,0:T(8,128)(2,1)S(1)}, bf16[4,96,640]{2,1,0:T(8,128)(2,1)S(1)}, u32[]{:S(2)}, u32[]{:S(2)}) %collective-permute-start.33) | collective-permute-done | bytes 491552 | tf_op jit(solution)/shard_map/ppermute | solution.py:800
  161.1 1.9 %project_place.1 = (f32[192,2304]{1,0:T(8,128)}, f32[16,192]{1,0:T(8,128)S(1)}) custom-call(s32[2]{0:T(128)S(1)} %pad_add_fusion.place.refs_0_, bf16[4,96,640]{2,1,0:T(8,128)(2,1)S(1)} %get-tuple-element.165.refs_1_, bf16[4,96,640]{2,1,0:T(8,128)(2,1)S(1)} %collective-permute-done.33.refs_2_), custom_call_target="tpu_custom_call" | custom-call | flops 2300000000 | bytes 7380000 | tf_op jit(solution)/shard_map/project_place/pallas_call | solution.py:715
  164.3 2.0 %outer_place.1 = f32[768,768]{1,0:T(8,128)} custom-call(s32[2]{0:T(128)S(1)} %pad_add_fusion.1.place.refs_0_, bf16[4,96,768]{2,1,0:T(8,128)(2,1)S(1)} %get-tuple-element.176.refs_1_, bf16[4,96,768]{2,1,0:T(8,128)(2,1)S(1)} %collective-permute-done.38.refs_2_), custom_call_target="tpu_custom_call" | custom-call | flops 2300000000 | bytes 7380000 | tf_op jit(solution)/shard_map/outer_place/pallas_call | solution.py:642
  (131 shorter events, 22.6 us)
Async XLA Ops:
  0.6 12.4 %collective-permute-start.1 = (bf16[2,128,768]{2,1,0:T(8,128)(2,1)}, bf16[2,128,768]{2,1,0:T(8,128)(2,1)S(1)}, u32[]{:S(2)}, u32[]{:S(2)}) collective-permute-start(bf16[2,128,768]{2,1,0:T(8,128)(2,1)} %x0.1), channel_id=1, source_target_pairs={{0,2},{1,3},{2,0},{3,1},{4,6},{5,7},{6,4},{7,5},{8,10},{9,11},{10,... | collective-permute-start | bytes 1179656 | tf_op jit(solution)/shard_map/ppermute | solution.py:800
  3.7 9.7 %collective-permute-start = (bf16[2,128,768]{2,1,0:T(8,128)(2,1)}, bf16[2,128,768]{2,1,0:T(8,128)(2,1)S(1)}, u32[]{:S(2)}, u32[]{:S(2)}) collective-permute-start(bf16[2,128,768]{2,1,0:T(8,128)(2,1)} %x0.1), channel_id=1, source_target_pairs={{0,1},{1,0},{2,3},{3,2},{4,5},{5,4},{6,7},{7,6},{8,9},{9,8},{10,11... | collective-permute-start | bytes 1179656 | tf_op jit(solution)/shard_map/ppermute | solution.py:800
  13.2 11.6 %copy-start.15 = (bf16[768]{0:T(1024)(128)(2,1)S(1)}, bf16[768]{0:T(1024)(128)(2,1)}, u32[]{:S(2)}) copy-start(bf16[768]{0:T(1024)(128)(2,1)} %param.22) | copy-start | bytes 4612
  13.2 11.6 %copy-start.17 = (bf16[768]{0:T(1024)(128)(2,1)S(1)}, bf16[768]{0:T(1024)(128)(2,1)}, u32[]{:S(2)}) copy-start(bf16[768]{0:T(1024)(128)(2,1)} %param.24) | copy-start | bytes 4612
  13.2 11.6 %copy-start.18 = (bf16[768]{0:T(1024)(128)(2,1)S(1)}, bf16[768]{0:T(1024)(128)(2,1)}, u32[]{:S(2)}) copy-start(bf16[768]{0:T(1024)(128)(2,1)} %param.28) | copy-start | bytes 4612
  13.3 11.6 %copy-start.19 = (bf16[768]{0:T(1024)(128)(2,1)S(1)}, bf16[768]{0:T(1024)(128)(2,1)}, u32[]{:S(2)}) copy-start(bf16[768]{0:T(1024)(128)(2,1)} %param.29) | copy-start | bytes 4612
  13.3 11.6 %copy-start.20 = (bf16[768]{0:T(1024)(128)(2,1)S(1)}, bf16[768]{0:T(1024)(128)(2,1)}, u32[]{:S(2)}) copy-start(bf16[768]{0:T(1024)(128)(2,1)} %param.30) | copy-start | bytes 4612
  13.3 11.7 %copy-start.14 = (bf16[3072]{0:T(1024)(128)(2,1)S(1)}, bf16[3072]{0:T(1024)(128)(2,1)}, u32[]{:S(2)}) copy-start(bf16[3072]{0:T(1024)(128)(2,1)} %param.26) | copy-start | bytes 18436
  13.3 17.8 %copy-start.5 = (bf16[768,768]{1,0:T(8,128)(2,1)S(1)}, bf16[768,768]{1,0:T(8,128)(2,1)}, u32[]{:S(2)}) copy-start(bf16[768,768]{1,0:T(8,128)(2,1)} %param.21) | copy-start | bytes 3538948
  13.3 17.8 %copy-start.7 = (bf16[2,128,768]{2,1,0:T(8,128)(2,1)S(1)}, bf16[2,128,768]{2,1,0:T(8,128)(2,1)}, u32[]{:S(2)}) copy-start(bf16[2,128,768]{2,1,0:T(8,128)(2,1)} %param.31) | copy-start | bytes 1179652
  13.3 1.8 %collective-permute-start.2 = (bf16[2,128,768]{2,1,0:T(8,128)(2,1)S(1)}, bf16[2,128,768]{2,1,0:T(8,128)(2,1)S(1)}, u32[]{:S(2)}, u32[]{:S(2)}) collective-permute-start(bf16[2,128,768]{2,1,0:T(8,128)(2,1)S(1)} %pass_on.1.x2), channel_id=1, source_target_pairs={{0,1},{1,0},{2,3},{3,2},{4,5},{5,4},{6,7},{7,6},{8,9},{9,8},{10,11... | collective-permute-start | bytes 1179656 | tf_op jit(solution)/shard_map/ppermute | solution.py:800
  22.8 2.2 %collective-permute-start.3 = (bf16[2,128,192]{2,1,0:T(8,128)(2,1)S(1)}, bf16[2,128,192]{2,1,0:T(8,128)(2,1)S(1)}, u32[]{:S(2)}, u32[]{:S(2)}) collective-permute-start(bf16[2,128,192]{2,1,0:T(8,128)(2,1)S(1)} %get-tuple-element.100), channel_id=1, source_target_pairs={{0,1},{1,0},{2,3},{3,2},{4,5},{5,4},{6,7},{7,6},{8,9},{9,8},{10,11... | collective-permute-start | bytes 294920 | tf_op jit(solution)/shard_map/ppermute | solution.py:800
  23.0 6.3 %collective-permute-start.4 = (bf16[2,128,192]{2,1,0:T(8,128)(2,1)S(1)}, bf16[2,128,192]{2,1,0:T(8,128)(2,1)S(1)}, u32[]{:S(2)}, u32[]{:S(2)}) collective-permute-start(bf16[2,128,192]{2,1,0:T(8,128)(2,1)S(1)} %get-tuple-element.101), channel_id=1, source_target_pairs={{0,2},{1,3},{2,0},{3,1},{4,6},{5,7},{6,4},{7,5},{8,10},{9,11},{10,... | collective-permute-start | bytes 294920 | tf_op jit(solution)/shard_map/ppermute | solution.py:800
  24.8 6.3 %collective-permute-start.5 = (bf16[2,128,192]{2,1,0:T(8,128)(2,1)S(1)}, bf16[2,128,192]{2,1,0:T(8,128)(2,1)S(1)}, u32[]{:S(2)}, u32[]{:S(2)}) collective-permute-start(bf16[2,128,192]{2,1,0:T(8,128)(2,1)S(1)} %get-tuple-element.102), channel_id=1, source_target_pairs={{0,3},{1,2},{2,1},{3,0},{4,7},{5,6},{6,5},{7,4},{8,11},{9,10},{10,... | collective-permute-start | bytes 294920 | tf_op jit(solution)/shard_map/ppermute | solution.py:800
  43.0 3.1 %collective-permute-start.7 = (bf16[256,2304]{1,0:T(8,128)(2,1)}, bf16[256,2304]{1,0:T(8,128)(2,1)S(1)}, u32[]{:S(2)}, u32[]{:S(2)}) collective-permute-start(bf16[256,2304]{1,0:T(8,128)(2,1)} %get-tuple-element.111.grad), channel_id=1, source_target_pairs={{0,1},{1,0},{2,3},{3,2},{4,5},{5,4},{6,7},{7,6},{8,9},{9,8},{10,11... | collective-permute-start | bytes 3538952 | tf_op jit(solution)/shard_map/ppermute | solution.py:800
  43.5 8.3 %collective-permute-start.6 = (bf16[2,256,192]{2,1,0:T(8,128)(2,1)S(1)}, bf16[2,256,192]{2,1,0:T(8,128)(2,1)S(1)}, u32[]{:S(2)}, u32[]{:S(2)}) collective-permute-start(bf16[2,256,192]{2,1,0:T(8,128)(2,1)S(1)} %get-tuple-element.109), channel_id=1, source_target_pairs={{0,2},{1,3},{2,0},{3,1},{4,6},{5,7},{6,4},{7,5},{8,10},{9,11},{10,... | collective-permute-start | bytes 589832 | tf_op jit(solution)/shard_map/ppermute | solution.py:800
  45.3 7.0 %collective-permute-start.9 = (bf16[4,192,256]{2,1,0:T(8,128)(2,1)}, bf16[4,192,256]{2,1,0:T(8,128)(2,1)S(1)}, u32[]{:S(2)}, u32[]{:S(2)}) collective-permute-start(bf16[4,192,256]{2,1,0:T(8,128)(2,1)} %get-tuple-element.117), channel_id=1, source_target_pairs={{0,1},{1,0},{2,3},{3,2},{4,5},{5,4},{6,7},{7,6},{8,9},{9,8},{10,11... | collective-permute-start | bytes 1179656 | tf_op jit(solution)/shard_map/ppermute | solution.py:800
  45.3 7.0 %collective-permute-start.10 = (bf16[256,3840]{1,0:T(8,128)(2,1)}, bf16[256,3840]{1,0:T(8,128)(2,1)S(1)}, u32[]{:S(2)}, u32[]{:S(2)}) collective-permute-start(bf16[256,3840]{1,0:T(8,128)(2,1)} %get-tuple-element.116.second_hbm), channel_id=1, source_target_pairs={{0,1},{1,0},{2,3},{3,2},{4,5},{5,4},{6,7},{7,6},{8,9},{9,8},{10,11... | collective-permute-start | bytes 5898248 | tf_op jit(solution)/shard_map/ppermute | solution.py:800
  49.2 28.3 %collective-permute-start.15 = (bf16[2,4,96,768]{3,2,1,0:T(8,128)(2,1)S(1)}, bf16[2,4,96,768]{3,2,1,0:T(8,128)(2,1)S(1)}, u32[]{:S(2)}, u32[]{:S(2)}) collective-permute-start(bf16[2,4,96,768]{3,2,1,0:T(8,128)(2,1)S(1)} %get-tuple-element.129), channel_id=1, source_target_pairs={{0,4},{4,0},{8,12},{12,8},{16,20},{20,16},{24,28},{28,24},{1,5},{5... | collective-permute-start | bytes 3538952 | tf_op jit(solution)/shard_map/ppermute | solution.py:800
  57.9 22.7 %collective-permute-start.14 = (bf16[1,8,128,384]{3,2,1,0:T(8,128)(2,1)}, bf16[1,8,128,384]{3,2,1,0:T(8,128)(2,1)}, u32[]{:S(2)}, u32[]{:S(2)}) collective-permute-start(bf16[1,8,128,384]{3,2,1,0:T(8,128)(2,1)} %get-tuple-element.127), channel_id=1, source_target_pairs={{0,2},{1,3},{2,0},{3,1},{4,6},{5,7},{6,4},{7,5},{8,10},{9,11},{10,... | collective-permute-start | bytes 2359304 | tf_op jit(solution)/shard_map/ppermute | solution.py:800
  59.7 23.8 %collective-permute-start.13 = (bf16[2,4,112,384]{3,2,1,0:T(8,128)(2,1)}, bf16[2,4,112,384]{3,2,1,0:T(8,128)(2,1)}, u32[]{:S(2)}, u32[]{:S(2)}) collective-permute-start(bf16[2,4,112,384]{3,2,1,0:T(8,128)(2,1)} %get-tuple-element.125), channel_id=1, source_target_pairs={{0,8},{4,12},{8,0},{12,4},{16,24},{20,28},{24,16},{28,20},{1,9},{5... | collective-permute-start | bytes 2064392 | tf_op jit(solution)/shard_map/ppermute | solution.py:800
  61.3 1.5 collective-permute-start.8
  62.9 14.7 %copy-start.9 = (bf16[2,4,96,768]{3,2,1,0:T(8,128)(2,1)S(1)}, bf16[2,4,96,768]{3,2,1,0:T(8,128)(2,1)}, u32[]{:S(2)}) copy-start(bf16[2,4,96,768]{3,2,1,0:T(8,128)(2,1)} %copy-done.8) | copy-start | bytes 3538948
  75.0 14.1 %collective-permute-start.12 = (bf16[1,4,96,640]{3,2,1,0:T(8,128)(2,1)S(1)}, bf16[1,4,96,640]{3,2,1,0:T(8,128)(2,1)S(1)}, u32[]{:S(2)}, u32[]{:S(2)}) collective-permute-start(bf16[1,4,96,640]{3,2,1,0:T(8,128)(2,1)S(1)} %get-tuple-element.123), channel_id=1, source_target_pairs={{0,4},{4,0},{8,12},{12,8},{16,20},{20,16},{24,28},{28,24},{1,5},{5... | collective-permute-start | bytes 1474568 | tf_op jit(solution)/shard_map/ppermute | solution.py:800
  76.5 20.8 %collective-permute-start.11 = (bf16[2,2,128,768]{3,2,1,0:T(8,128)(2,1)}, bf16[2,2,128,768]{3,2,1,0:T(8,128)(2,1)S(1)}, u32[]{:S(2)}, u32[]{:S(2)}) collective-permute-start(bf16[2,2,128,768]{3,2,1,0:T(8,128)(2,1)} %get-tuple-element.121), channel_id=1, source_target_pairs={{0,1},{1,0},{2,3},{3,2},{4,5},{5,4},{6,7},{7,6},{8,9},{9,8},{10,11... | collective-permute-start | bytes 2359304 | tf_op jit(solution)/shard_map/ppermute | solution.py:800
  78.3 16.9 %collective-permute-start.20 = (bf16[1,4,96,768]{3,2,1,0:T(8,128)(2,1)S(1)}, bf16[1,4,96,768]{3,2,1,0:T(8,128)(2,1)S(1)}, u32[]{:S(2)}, u32[]{:S(2)}) collective-permute-start(bf16[1,4,96,768]{3,2,1,0:T(8,128)(2,1)S(1)} %get-tuple-element.139), channel_id=1, source_target_pairs={{0,2},{1,3},{2,0},{3,1},{4,6},{5,7},{6,4},{7,5},{8,10},{9,11},{10,... | collective-permute-start | bytes 1769480 | tf_op jit(solution)/shard_map/ppermute | solution.py:800
  81.9 10.4 %collective-permute-start.17 = (bf16[1,4,128,384]{3,2,1,0:T(8,128)(2,1)S(1)}, bf16[1,4,128,384]{3,2,1,0:T(8,128)(2,1)S(1)}, u32[]{:S(2)}, u32[]{:S(2)}) collective-permute-start(bf16[1,4,128,384]{3,2,1,0:T(8,128)(2,1)S(1)} %get-tuple-element.135), channel_id=1, source_target_pairs={{0,8},{4,12},{8,0},{12,4},{16,24},{20,28},{24,16},{28,20},{1,9},{5... | collective-permute-start | bytes 1179656 | tf_op jit(solution)/shard_map/ppermute | solution.py:800
  84.9 12.5 %collective-permute-start.19 = (bf16[2,2,112,384]{3,2,1,0:T(8,128)(2,1)S(1)}, bf16[2,2,112,384]{3,2,1,0:T(8,128)(2,1)S(1)}, u32[]{:S(2)}, u32[]{:S(2)}) collective-permute-start(bf16[2,2,112,384]{3,2,1,0:T(8,128)(2,1)S(1)} %get-tuple-element.138), channel_id=1, source_target_pairs={{0,4},{4,0},{8,12},{12,8},{16,20},{20,16},{24,28},{28,24},{1,5},{5... | collective-permute-start | bytes 1032200 | tf_op jit(solution)/shard_map/ppermute | solution.py:800
  89.7 14.1 %collective-permute-start.16 = (bf16[1,2,96,640]{3,2,1,0:T(8,128)(2,1)S(1)}, bf16[1,2,96,640]{3,2,1,0:T(8,128)(2,1)S(1)}, u32[]{:S(2)}, u32[]{:S(2)}) collective-permute-start(bf16[1,2,96,640]{3,2,1,0:T(8,128)(2,1)S(1)} %get-tuple-element.134), channel_id=1, source_target_pairs={{0,16},{4,20},{8,24},{12,28},{16,0},{20,4},{24,8},{28,12},{1,17},{... | collective-permute-start | bytes 737288 | tf_op jit(solution)/shard_map/ppermute | solution.py:800
  93.6 6.5 %collective-permute-start.18 = (bf16[1,2,128,384]{3,2,1,0:T(8,128)(2,1)S(1)}, bf16[1,2,128,384]{3,2,1,0:T(8,128)(2,1)S(1)}, u32[]{:S(2)}, u32[]{:S(2)}) collective-permute-start(bf16[1,2,128,384]{3,2,1,0:T(8,128)(2,1)S(1)} %get-tuple-element.137), channel_id=1, source_target_pairs={{0,4},{4,0},{8,12},{12,8},{16,20},{20,16},{24,28},{28,24},{1,5},{5... | collective-permute-start | bytes 589832 | tf_op jit(solution)/shard_map/ppermute | solution.py:800
  95.9 19.3 %collective-permute-start.24 = (bf16[1,2,96,768]{3,2,1,0:T(8,128)(2,1)S(1)}, bf16[1,2,96,768]{3,2,1,0:T(8,128)(2,1)S(1)}, u32[]{:S(2)}, u32[]{:S(2)}) collective-permute-start(bf16[1,2,96,768]{3,2,1,0:T(8,128)(2,1)S(1)} %get-tuple-element.147), channel_id=1, source_target_pairs={{0,8},{4,12},{8,0},{12,4},{16,24},{20,28},{24,16},{28,20},{1,9},{5... | collective-permute-start | bytes 884744 | tf_op jit(solution)/shard_map/ppermute | solution.py:800
  98.5 17.4 %collective-permute-start.23 = (bf16[1,2,112,384]{3,2,1,0:T(8,128)(2,1)S(1)}, bf16[1,2,112,384]{3,2,1,0:T(8,128)(2,1)S(1)}, u32[]{:S(2)}, u32[]{:S(2)}) collective-permute-start(bf16[1,2,112,384]{3,2,1,0:T(8,128)(2,1)S(1)} %get-tuple-element.146), channel_id=1, source_target_pairs={{0,2},{1,3},{2,0},{3,1},{4,6},{5,7},{6,4},{7,5},{8,10},{9,11},{10,... | collective-permute-start | bytes 516104 | tf_op jit(solution)/shard_map/ppermute | solution.py:800
  101.4 18.7 %collective-permute-start.22 = (bf16[1,2,128,384]{3,2,1,0:T(8,128)(2,1)S(1)}, bf16[1,2,128,384]{3,2,1,0:T(8,128)(2,1)S(1)}, u32[]{:S(2)}, u32[]{:S(2)}) collective-permute-start(bf16[1,2,128,384]{3,2,1,0:T(8,128)(2,1)S(1)} %get-tuple-element.145.refs_1_), channel_id=1, source_target_pairs={{0,16},{4,20},{8,24},{12,28},{16,0},{20,4},{24,8},{28,12},{1,17},{... | collective-permute-start | bytes 589832 | tf_op jit(solution)/shard_map/ppermute | solution.py:800
  104.5 17.4 %collective-permute-start.21 = (bf16[1,2,96,640]{3,2,1,0:T(8,128)(2,1)S(1)}, bf16[1,2,96,640]{3,2,1,0:T(8,128)(2,1)S(1)}, u32[]{:S(2)}, u32[]{:S(2)}) collective-permute-start(bf16[1,2,96,640]{3,2,1,0:T(8,128)(2,1)S(1)} %get-tuple-element.144.refs_1_), channel_id=1, source_target_pairs={{0,8},{4,12},{8,0},{12,4},{16,24},{20,28},{24,16},{28,20},{1,9},{5... | collective-permute-start | bytes 737288 | tf_op jit(solution)/shard_map/ppermute | solution.py:800
  117.1 11.5 %collective-permute-start.31 = (bf16[1,2,112,384]{3,2,1,0:T(8,128)(2,1)S(1)}, bf16[1,2,112,384]{3,2,1,0:T(8,128)(2,1)S(1)}, u32[]{:S(2)}, u32[]{:S(2)}) collective-permute-start(bf16[1,2,112,384]{3,2,1,0:T(8,128)(2,1)S(1)} %get-tuple-element.159.refs_1_), channel_id=1, source_target_pairs={{0,16},{4,20},{8,24},{12,28},{16,0},{20,4},{24,8},{28,12},{1,17},{... | collective-permute-start | bytes 516104 | tf_op jit(solution)/shard_map/ppermute | solution.py:800
  117.2 14.5 %collective-permute-start.30 = (bf16[1,2,96,768]{3,2,1,0:T(8,128)(2,1)S(1)}, bf16[1,2,96,768]{3,2,1,0:T(8,128)(2,1)S(1)}, u32[]{:S(2)}, u32[]{:S(2)}) collective-permute-start(bf16[1,2,96,768]{3,2,1,0:T(8,128)(2,1)S(1)} %get-tuple-element.158.refs_1_), channel_id=1, source_target_pairs={{0,16},{4,20},{8,24},{12,28},{16,0},{20,4},{24,8},{28,12},{1,17},{... | collective-permute-start | bytes 884744 | tf_op jit(solution)/shard_map/ppermute | solution.py:800
  120.7 7.4 %collective-permute-start.32 = (bf16[2,128,384]{2,1,0:T(8,128)(2,1)S(1)}, bf16[2,128,384]{2,1,0:T(8,128)(2,1)S(1)}, u32[]{:S(2)}, u32[]{:S(2)}) collective-permute-start(bf16[2,128,384]{2,1,0:T(8,128)(2,1)S(1)} %bitcast.50), channel_id=1, source_target_pairs={{0,8},{4,12},{8,0},{12,4},{16,24},{20,28},{24,16},{28,20},{1,9},{5... | collective-permute-start | bytes 589832 | tf_op jit(solution)/shard_map/ppermute | solution.py:800
  122.4 1.3 collective-permute-start.26
  122.5 4.7 %collective-permute-start.27 = (bf16[2,24,640]{2,1,0:T(8,128)(2,1)S(1)}, bf16[2,24,640]{2,1,0:T(8,128)(2,1)S(1)}, u32[]{:S(2)}, u32[]{:S(2)}) collective-permute-start(bf16[2,24,640]{2,1,0:T(8,128)(2,1)S(1)} %get-tuple-element.156), channel_id=1, source_target_pairs={{0,2},{1,3},{2,0},{3,1},{4,6},{5,7},{6,4},{7,5},{8,10},{9,11},{10,... | collective-permute-start | bytes 184328 | tf_op jit(solution)/shard_map/ppermute | solution.py:800
  123.7 4.2 %collective-permute-start.28 = (bf16[2,24,640]{2,1,0:T(8,128)(2,1)S(1)}, bf16[2,24,640]{2,1,0:T(8,128)(2,1)S(1)}, u32[]{:S(2)}, u32[]{:S(2)}) collective-permute-start(bf16[2,24,640]{2,1,0:T(8,128)(2,1)S(1)} %get-tuple-element.157), channel_id=1, source_target_pairs={{0,3},{1,2},{2,1},{3,0},{4,7},{5,6},{6,5},{7,4},{8,11},{9,10},{10,... | collective-permute-start | bytes 184328 | tf_op jit(solution)/shard_map/ppermute | solution.py:800
  127.2 14.9 %collective-permute-start.25 = (bf16[1,1,256,768]{3,2,1,0:T(8,128)(2,1)S(1)}, bf16[1,1,256,768]{3,2,1,0:T(8,128)(2,1)S(1)}, u32[]{:S(2)}, u32[]{:S(2)}) collective-permute-start(bf16[1,1,256,768]{3,2,1,0:T(8,128)(2,1)S(1)} %get-tuple-element.153), channel_id=1, source_target_pairs={{0,2},{1,3},{2,0},{3,1},{4,6},{5,7},{6,4},{7,5},{8,10},{9,11},{10,... | collective-permute-start | bytes 1179656 | tf_op jit(solution)/shard_map/ppermute | solution.py:800
  128.0 8.9 %collective-permute-start.29 = (bf16[2,96,640]{2,1,0:T(8,128)(2,1)S(1)}, bf16[2,96,640]{2,1,0:T(8,128)(2,1)S(1)}, u32[]{:S(2)}, u32[]{:S(2)}) collective-permute-start(bf16[2,96,640]{2,1,0:T(8,128)(2,1)S(1)} %constant_dynamic-update-slice_fusion.refs_0_), channel_id=1, source_target_pairs={{0,4},{4,0},{8,12},{12,8},{16,20},{20,16},{24,28},{28,24},{1,5},{5... | collective-permute-start | bytes 737288 | tf_op jit(solution)/shard_map/ppermute | solution.py:800
  129.2 11.3 %collective-permute-start.35 = (bf16[2,112,384]{2,1,0:T(8,128)(2,1)S(1)}, bf16[2,112,384]{2,1,0:T(8,128)(2,1)S(1)}, u32[]{:S(2)}, u32[]{:S(2)}) collective-permute-start(bf16[2,112,384]{2,1,0:T(8,128)(2,1)S(1)} %bitcast.52), channel_id=1, source_target_pairs={{0,4},{4,0},{8,12},{12,8},{16,20},{20,16},{24,28},{28,24},{1,5},{5... | collective-permute-start | bytes 516104 | tf_op jit(solution)/shard_map/ppermute | solution.py:800
  132.3 10.7 %collective-permute-start.37 = (bf16[2,96,768]{2,1,0:T(8,128)(2,1)S(1)}, bf16[2,96,768]{2,1,0:T(8,128)(2,1)S(1)}, u32[]{:S(2)}, u32[]{:S(2)}) collective-permute-start(bf16[2,96,768]{2,1,0:T(8,128)(2,1)S(1)} %bitcast.48), channel_id=1, source_target_pairs={{0,8},{4,12},{8,0},{12,4},{16,24},{20,28},{24,16},{28,20},{1,9},{5... | collective-permute-start | bytes 884744 | tf_op jit(solution)/shard_map/ppermute | solution.py:800
  133.3 15.7 %collective-permute-start.34 = (bf16[4,128,384]{2,1,0:T(8,128)(2,1)S(1)}, bf16[4,128,384]{2,1,0:T(8,128)(2,1)S(1)}, u32[]{:S(2)}, u32[]{:S(2)}) collective-permute-start(bf16[4,128,384]{2,1,0:T(8,128)(2,1)S(1)} %get-tuple-element.168.refs_2_), channel_id=1, source_target_pairs={{0,4},{4,0},{8,12},{12,8},{16,20},{20,16},{24,28},{28,24},{1,5},{5... | collective-permute-start | bytes 1179656 | tf_op jit(solution)/shard_map/ppermute | solution.py:800
  137.5 23.6 %collective-permute-start.33 = (bf16[4,96,640]{2,1,0:T(8,128)(2,1)S(1)}, bf16[4,96,640]{2,1,0:T(8,128)(2,1)S(1)}, u32[]{:S(2)}, u32[]{:S(2)}) collective-permute-start(bf16[4,96,640]{2,1,0:T(8,128)(2,1)S(1)} %get-tuple-element.165.refs_1_), channel_id=1, source_target_pairs={{0,16},{4,20},{8,24},{12,28},{16,0},{20,4},{24,8},{28,12},{1,17},{... | collective-permute-start | bytes 1474568 | tf_op jit(solution)/shard_map/ppermute | solution.py:800
  141.0 15.9 %collective-permute-start.36 = (bf16[4,112,384]{2,1,0:T(8,128)(2,1)S(1)}, bf16[4,112,384]{2,1,0:T(8,128)(2,1)S(1)}, u32[]{:S(2)}, u32[]{:S(2)}) collective-permute-start(bf16[4,112,384]{2,1,0:T(8,128)(2,1)S(1)} %get-tuple-element.171.refs_4_), channel_id=1, source_target_pairs={{0,8},{4,12},{8,0},{12,4},{16,24},{20,28},{24,16},{28,20},{1,9},{5... | collective-permute-start | bytes 1032200 | tf_op jit(solution)/shard_map/ppermute | solution.py:800
  143.2 21.1 %collective-permute-start.38 = (bf16[4,96,768]{2,1,0:T(8,128)(2,1)S(1)}, bf16[4,96,768]{2,1,0:T(8,128)(2,1)S(1)}, u32[]{:S(2)}, u32[]{:S(2)}) collective-permute-start(bf16[4,96,768]{2,1,0:T(8,128)(2,1)S(1)} %get-tuple-element.176.refs_1_), channel_id=1, source_target_pairs={{0,4},{4,0},{8,12},{12,8},{16,20},{20,16},{24,28},{28,24},{1,5},{5... | collective-permute-start | bytes 1769480 | tf_op jit(solution)/shard_map/ppermute | solution.py:800
  (14 other events, 71.4 us)
